TPU v7x, 32 devices: a whole 2x2x4 slice. The times are simulated.
32 devices in a mesh: dp: 2 (over core), row: 4 (over y, x), col: 4 (over z).
Axes of the slice: x: 2, y: 2, z: 4, core: 2. Of those that a mesh axis runs over, the one named last changes fastest.
Arguments:
- images: bfloat16 [16, 4, 32, 2816], P('row', 'dp', None, 'col'), may hold values from -5 to 6.25
- cotangent: bfloat16 [16, 4, 32, 2816], P('row', 'dp', None, 'col'), may hold values from -6 to 6
- kernel: float32 [7, 7, 2816], P(None, None, 'col'), may hold values from -0.4 to 0.45
- w_in: bfloat16 [2816, 11264], P('col', ('row', 'dp')), may hold values from -0.109375 to 0.109375
- b_in: float32 [11264], P('row'), may hold values from -2.5 to 3
- grn_gamma: float32 [11264], P('row'), may hold values from -4 to 4
- grn_beta: float32 [11264], P('row'), may hold values from -3 to 3
- w_out: bfloat16 [11264, 2816], P(('row', 'dp'), 'col'), may hold values from -0.0546875 to 0.0546875
Outputs:
- result: bfloat16 [16, 4, 32, 2816], P('row', 'dp', None, 'col')
- x_grad: bfloat16 [16, 4, 32, 2816], P('row', 'dp', None, 'col')
- w_in_grad: float32 [2816, 11264], P('col', ('row', 'dp'))
- w_out_grad: float32 [11264, 2816], P(('row', 'dp'), 'col')
- kernel_grad: float32 [7, 7, 2816], P(None, None, 'col')
All inputs are finite; a program needn't handle non-finite values.
Results may differ from a plain program's by a relative error of at most 0.018.
Values may be sent and summed in bfloat16 or wider, within the bound.
No kernel may reach another device: no remote copies, remote signals or barrier semaphores. Data moves between devices by JAX's collectives and lax.ppermute only.
A program may use at most 128 MiB of HBM per device.

v0:
```python
import math

import jax
import jax.numpy as jnp
from jax import lax
from jax.sharding import PartitionSpec as P

C = 2816
FF = 11264


epsilon = 1e-06
root_half = 0.7071067811865476
inv_root_tau = 0.3989422804014327


def extended(block, sides, width):
    for axis, dim in sides:
        count = lax.axis_size(axis)
        forward = [(i, i + 1) for i in range(count - 1)]
        backward = [(target, source) for source, target in forward]
        low = lax.ppermute(
            lax.slice_in_dim(block, block.shape[dim] - width, None, axis=dim), axis, forward
        )
        high = lax.ppermute(lax.slice_in_dim(block, 0, width, axis=dim), axis, backward)
        block = jnp.concatenate([low, block, high], axis=dim)
    return block


def depthwise(padded, kernel, height, width):
    span = kernel.shape[0]
    result = jnp.zeros((height, padded.shape[1], width, padded.shape[3]), jnp.float32)
    for row_off in range(span):
        for col_off in range(span):
            window = padded[row_off : row_off + height, :, col_off : col_off + width, :]
            result = result + kernel[row_off, col_off] * window
    return result


def pad_width(tile_in, reach):
    return jnp.pad(tile_in, ((0, 0), (0, 0), (reach, reach), (0, 0)))


def gelu_slope(hidden_pre):
    cumul = 0.5 * (1.0 + lax.erf(hidden_pre * root_half))
    return cumul + hidden_pre * jnp.exp(-0.5 * hidden_pre * hidden_pre) * inv_root_tau


def local(images, cotangent, kernel, w_in, b_in, grn_gamma, grn_beta, w_out):
    height, batch, width, chans = images.shape
    span = kernel.shape[0]
    reach = span // 2
    col_count = lax.axis_size("col")
    row_count = lax.axis_size("row")
    data_count = lax.axis_size("dp")
    local_pix = height * batch * width
    group_pix = local_pix * row_count
    share_pix = group_pix // col_count
    hidden_blk = b_in.shape[0]
    scale_grad = 1.0 / math.sqrt(group_pix * data_count)
    contract_last = (((1,), (1,)), ((), ()))
    contract_first = (((0,), (0,)), ((), ()))
    halo_x = extended(images, (("row", 0),), reach)
    padded_x = pad_width(halo_x, reach).astype(jnp.float32)
    conv_out = depthwise(padded_x, kernel, height, width)
    mean_pix = lax.psum(jnp.sum(conv_out, axis=-1), "col") / C
    centred = conv_out - mean_pix[..., None]
    var_pix = lax.psum(jnp.sum(centred * centred, axis=-1), "col") / C
    inv_std = lax.rsqrt(var_pix + epsilon)[..., None]
    standard = centred * inv_std
    normed = standard.astype(jnp.bfloat16).reshape(local_pix, chans)
    w_in_full = lax.all_gather(w_in, "dp", axis=1, tiled=True)
    normed_all = lax.all_gather(normed, "row", axis=0, tiled=True)
    rows_in = normed_all
    hidden_pre = (
        lax.psum_scatter(
            jnp.dot(rows_in, w_in_full, preferred_element_type=jnp.float32).astype(jnp.bfloat16),
            "col",
            scatter_dimension=0,
            tiled=True,
        ).astype(jnp.float32)
        + b_in
    )
    hidden_act = jax.nn.gelu(hidden_pre, approximate=False)
    act_four = hidden_act.reshape(share_pix // (batch * width), batch, width, hidden_blk)
    sums_local = jnp.sum(act_four * act_four, axis=(0, 2))
    norm_chan = jnp.sqrt(lax.psum(sums_local, "col") + epsilon)
    mean_norm = lax.psum(jnp.sum(norm_chan, axis=-1), "row") / FF
    denom = (mean_norm + epsilon)[:, None]
    ratio_chan = norm_chan / denom
    gated = (grn_gamma * act_four * ratio_chan[None, :, None, :] + grn_beta + act_four).astype(
        jnp.bfloat16
    )
    gated_rows = gated.reshape(share_pix, hidden_blk)
    gated_all = lax.all_gather(gated_rows, "col", axis=0, tiled=True)
    w_out_full = lax.all_gather(w_out, "dp", axis=0, tiled=True)
    rows_in = gated_all
    branch = lax.psum_scatter(
        jnp.dot(rows_in, w_out_full, preferred_element_type=jnp.float32).astype(jnp.bfloat16),
        "row",
        scatter_dimension=0,
        tiled=True,
    ).astype(jnp.float32)
    result = (images.astype(jnp.float32) + branch.reshape(images.shape)).astype(jnp.bfloat16)
    cot_all = lax.all_gather(cotangent.reshape(local_pix, chans), "row", axis=0, tiled=True)
    w_in_back = lax.all_gather(w_in, "dp", axis=1, tiled=True)
    w_out_back = lax.all_gather(w_out, "dp", axis=0, tiled=True)
    rows_in = cot_all
    grad_gated = (
        lax.psum_scatter(
            lax.dot_general(
                rows_in, w_out_back, contract_last, preferred_element_type=jnp.float32
            ).astype(jnp.bfloat16),
            "col",
            scatter_dimension=0,
            tiled=True,
        )
        .astype(jnp.float32)
        .reshape(act_four.shape)
    )
    pull_local = jnp.sum(grad_gated * grn_gamma * act_four, axis=(0, 2))
    pull_chan = lax.psum(pull_local, "col")
    grad_norm = pull_chan / denom
    grad_act = (
        grad_gated * (grn_gamma * ratio_chan[None, :, None, :] + 1.0)
        + act_four * (grad_norm / norm_chan)[None, :, None, :]
    )
    grad_rows = (grad_act.reshape(share_pix, hidden_blk) * gelu_slope(hidden_pre)).astype(
        jnp.bfloat16
    )
    grad_pre_all = lax.all_gather(grad_rows, "col", axis=0, tiled=True)
    grad_w_out = lax.dot_general(
        gated_all, cot_all, contract_first, preferred_element_type=jnp.float32
    )
    grad_w_in = lax.dot_general(
        normed_all, grad_pre_all, contract_first, preferred_element_type=jnp.float32
    )
    rows_in = grad_pre_all
    grad_normed = (
        lax.psum_scatter(
            lax.dot_general(
                rows_in, w_in_back, contract_last, preferred_element_type=jnp.float32
            ).astype(jnp.bfloat16),
            "row",
            scatter_dimension=0,
            tiled=True,
        )
        .astype(jnp.float32)
        .reshape(conv_out.shape)
    )
    w_out_grad = (
        lax.psum_scatter(
            grad_w_out.astype(jnp.bfloat16), "dp", scatter_dimension=0, tiled=True
        ).astype(jnp.float32)
        * scale_grad
    )
    w_in_grad = (
        lax.psum_scatter(
            grad_w_in.astype(jnp.bfloat16), "dp", scatter_dimension=1, tiled=True
        ).astype(jnp.float32)
        * scale_grad
    )
    first_back, second_back = lax.psum(
        (jnp.sum(grad_normed, axis=-1), jnp.sum(grad_normed * standard, axis=-1)), "col"
    )
    grad_conv = inv_std * (
        grad_normed - (first_back / C)[..., None] - standard * (second_back / C)[..., None]
    )
    halo_cot = extended(grad_conv.astype(jnp.bfloat16), (("row", 0),), reach).astype(
        grad_conv.dtype
    )
    spread = depthwise(pad_width(halo_cot, reach), kernel[::-1, ::-1], height, width)
    x_grad = (cotangent.astype(jnp.float32) + spread).astype(jnp.bfloat16)
    kern_terms = []
    for row_off in range(span):
        for col_off in range(span):
            window = padded_x[row_off : row_off + height, :, col_off : col_off + width, :]
            kern_terms.append(jnp.sum(grad_conv * window, axis=(0, 1, 2)))
    kern_local = jnp.stack(kern_terms).reshape(span, span, chans)
    kernel_grad = (
        lax.psum(kern_local.astype(jnp.bfloat16), ("dp", "row")).astype(jnp.float32) * scale_grad
    )
    return (result, x_grad, w_in_grad, w_out_grad, kernel_grad)


def solution(mesh):
    return jax.shard_map(
        local,
        mesh=mesh,
        in_specs=(
            P("row", "dp", None, "col"),
            P("row", "dp", None, "col"),
            P(None, None, "col"),
            P("col", ("row", "dp")),
            P("row"),
            P("row"),
            P("row"),
            P(("row", "dp"), "col"),
        ),
        out_specs=(
            P("row", "dp", None, "col"),
            P("row", "dp", None, "col"),
            P("col", ("row", "dp")),
            P(("row", "dp"), "col"),
            P(None, None, "col"),
        ),
        check_vma=False,
    )
```

profile of v0, /device:TPU:0, one launch (start us, length us, event | category | flops | bytes accessed | tf_op | source)
XLA Modules:
  0.0 777.7 jit_solution(14633936844259891545)
XLA Ops:
  7.2 1.1 fusion.125
  8.3 4.9 collective-permute-start
  13.2 1.3 collective-permute-start.1
  14.5 1.1 slice_reduce_fusion.46
  15.6 1.4 slice_reduce_fusion.48
  17.0 1.4 slice_reduce_fusion.47
  18.7 0.8 collective-permute-done
  19.4 8.3 %collective-permute-done.1 = bf16[3,2,32,704]{3,2,1,0:T(8,128)(2,1)S(1)} collective-permute-done((bf16[3,2,32,704]{3,2,1,0:T(8,128)(2,1)S(1)}, bf16[3,2,32,704]{3,2,1,0:T(8,128)(2,1)S(1)}, u32[]{:S(2)}, u32[]{:S(2)}) %collective-permute-start.1) | collective-permute-done | bytes 270368 | tf_op jit(solution)/shard_map/ppermute | solution.py:25
  27.7 1.4 fusion.28
  29.1 6.5 fusion.123
  35.8 12.0 %psum.56 = f32[4,2,32]{2,1,0:T(2,128)S(1)} all-reduce(f32[4,2,32]{2,1,0:T(2,128)S(1)} %get-tuple-element.112), channel_id=1, replica_groups=mesh['dp'=2,'row'=4,'col'=4] {'col'}, use_global_device_ids=true, to_apply=%region_1.2 | all-reduce | flops 256 | bytes 2048 | tf_op jit(solution)/shard_map/psum | solution.py:66
  47.8 0.2 multiply_reduce_fusion.52
  48.0 8.4 %psum.57 = f32[4,2,32]{2,1,0:T(2,128)S(1)} all-reduce(f32[4,2,32]{2,1,0:T(2,128)S(1)} %multiply_reduce_fusion.52), channel_id=1, replica_groups=mesh['dp'=2,'row'=4,'col'=4] {'col'}, use_global_device_ids=true, to_apply=%region_3.4 | all-reduce | flops 256 | bytes 2048 | tf_op jit(solution)/shard_map/psum | solution.py:68
  56.4 0.9 fusion.121
  57.4 0.7 all-gather.9.cloned.1.call-update
  58.1 0.7 all-gather.15.cloned.1.call-update
  58.9 0.5 all-gather.13.cloned.1.call-update
  59.5 27.7 %all-gather.7.cloned.1.call-done = bf16[1024,704]{1,0:T(8,128)(2,1)} async-done(((bf16[256,704]{1,0:T(8,128)(2,1)}), bf16[1024,704]{1,0:T(8,128)(2,1)}) %all-gather.7.cloned.1.call-update) | async-done | bytes 1441808 | tf_op jit(solution)/shard_map/all_gather | solution.py:73
  87.2 14.9 %all-gather.9.cloned.1.call-done = bf16[704,2816]{1,0:T(8,128)(2,1)} async-done(((bf16[704,1408]{1,0:T(8,128)(2,1)}), bf16[704,2816]{1,0:T(8,128)(2,1)}) %all-gather.9.cloned.1.call-update) | async-done | bytes 3964944 | tf_op jit(solution)/shard_map/all_gather | solution.py:72
  102.1 9.7 %convolution_convert_fusion.1 = bf16[1024,2816]{1,0:T(8,128)(2,1)} fusion(bf16[1024,704]{1,0:T(8,128)(2,1)} %all-gather.7.cloned.1.call-done, bf16[704,2816]{1,0:T(8,128)(2,1)} %all-gather.9.cloned.1.call-done), kind=kOutput, calls=%fused_computation.43 | convolution fusion | flops 4062969856 | bytes 11173888 | tf_op jit(solution)/shard_map/dot_general | solution.py:77
  111.9 24.2 %all-gather.15.cloned.1.call-done = bf16[1024,704]{1,0:T(8,128)(2,1)} async-done(((bf16[256,704]{1,0:T(8,128)(2,1)}), bf16[1024,704]{1,0:T(8,128)(2,1)}) %all-gather.15.cloned.1.call-update) | async-done | bytes 1441808 | tf_op jit(solution)/shard_map/all_gather | solution.py:105
  136.1 14.7 %all-gather.13.cloned.1.call-done = bf16[2816,704]{0,1:T(8,128)(2,1)} async-done(((bf16[1408,704]{0,1:T(8,128)(2,1)}), bf16[2816,704]{0,1:T(8,128)(2,1)}) %all-gather.13.cloned.1.call-update) | async-done | bytes 3964944 | tf_op jit(solution)/shard_map/all_gather | solution.py:96
  150.8 10.0 %convolution_convert_fusion = bf16[1024,2816]{1,0:T(8,128)(2,1)} fusion(bf16[1024,704]{1,0:T(8,128)(2,1)} %all-gather.15.cloned.1.call-done, bf16[2816,704]{0,1:T(8,128)(2,1)} %all-gather.13.cloned.1.call-done), kind=kOutput, calls=%fused_computation.42 | convolution fusion | flops 4062969856 | bytes 11173888 | tf_op jit(solution)/shard_map/dot_general | solution.py:111
  160.9 0.2 all-gather.17.cloned.1.call-start
  161.1 95.3 %reduce-scatter.11.cloned.1.call-done = bf16[256,2816]{1,0:T(8,128)(2,1)} async-done(((bf16[1024,2816]{1,0:T(8,128)(2,1)}), bf16[256,2816]{1,0:T(8,128)(2,1)}) %reduce-scatter.11.cloned.1.call-update) | async-done | bytes 1441808 | tf_op jit(solution)/shard_map/reduce_scatter | solution.py:76
  256.4 8.2 %fusion.1 = f32[256,2816]{1,0:T(8,128)} fusion(bf16[256,2816]{1,0:T(8,128)(2,1)} %reduce-scatter.11.cloned.1.call-done, f32[2816]{0:T(1024)S(1)} %copy-done.3), kind=kLoop, calls=%fused_computation.53 | loop fusion | flops 47579136 | bytes 4336640 | tf_op jit(solution)/shard_map/mul | solution.py:84
  264.6 96.8 %reduce-scatter.15.cloned.1.call-done = bf16[256,2816]{1,0:T(8,128)(2,1)} async-done(((bf16[1024,2816]{1,0:T(8,128)(2,1)}), bf16[256,2816]{1,0:T(8,128)(2,1)}) %reduce-scatter.15.cloned.1.call-update) | async-done | bytes 1441808 | tf_op jit(solution)/shard_map/reduce_scatter | solution.py:110
  361.4 2.9 multiply_reduce_fusion
  364.3 18.7 %all-reduce.3 = (f32[2,2816]{1,0:T(2,128)S(1)}, f32[2,2816]{1,0:T(2,128)S(1)}) all-reduce(f32[2,2816]{1,0:T(2,128)S(1)} %get-tuple-element.55, f32[2,2816]{1,0:T(2,128)S(1)} %get-tuple-element.54), channel_id=1, replica_groups=mesh['dp'=2,'row'=4,'col'=4] {'col'}, use_global_device_ids=true, to_apply=%region_6.7 | all-reduce | flops 11264 | bytes 90112 | tf_op jit(solution)/shard_map/psum | solution.py:87
  383.1 10.1 %psum.59 = f32[2]{0:T(128)S(1)} all-reduce(f32[2]{0:T(128)S(1)} %fusion.122), channel_id=1, replica_groups=mesh['dp'=2,'row'=4,'col'=4] {'row'}, use_global_device_ids=true, to_apply=%region_8.9 | all-reduce | flops 2 | bytes 16 | tf_op jit(solution)/shard_map/psum | solution.py:88
  393.3 10.4 %fusion.7 = (bf16[256,2816]{1,0:T(8,128)(2,1)}, bf16[256,2816]{1,0:T(8,128)(2,1)}) fusion(bf16[256,2816]{1,0:T(8,128)(2,1)} %reduce-scatter.11.cloned.1.call-done, f32[2,2816]{1,0:T(2,128)S(1)} %get-tuple-element.121, f32[2,2816]{1,0:T(2,128)S(1)} %get-tuple-element.110, f32[2816]{0:T(1024)S(1)} %copy-done.3, ...), kind=kLoop, calls=%fused_computation.59 | loop fusion | flops 61276160 | bytes 5868544 | tf_op jit(solution)/shard_map/convert_element_type | solution.py:128
  403.7 0.7 all-gather.11.cloned.1.call-update
  404.5 102.4 %all-gather.17.cloned.1.call-done = bf16[1024,2816]{1,0:T(8,128)(2,1)} async-done(((bf16[256,2816]{1,0:T(8,128)(2,1)}), bf16[1024,2816]{1,0:T(8,128)(2,1)}) %all-gather.17.cloned.1.call-update) | async-done | bytes 5767184 | tf_op jit(solution)/shard_map/all_gather | solution.py:131
  506.9 9.2 %convolution_convert_fusion.4 = bf16[1024,704]{0,1:T(8,128)(2,1)} fusion(bf16[1024,2816]{1,0:T(8,128)(2,1)} %all-gather.17.cloned.1.call-done, bf16[704,2816]{1,0:T(8,128)(2,1)} %all-gather.9.cloned.1.call-done), kind=kOutput, calls=%fused_computation.88 | convolution fusion | flops 4060807168 | bytes 11173888 | tf_op jit(solution)/shard_map/dot_general | solution.py:141
  516.2 97.9 %all-gather.11.cloned.1.call-done = bf16[1024,2816]{1,0:T(8,128)(2,1)} async-done(((bf16[256,2816]{1,0:T(8,128)(2,1)}), bf16[1024,2816]{1,0:T(8,128)(2,1)}) %all-gather.11.cloned.1.call-update) | async-done | bytes 5767184 | tf_op jit(solution)/shard_map/all_gather | solution.py:95
  614.1 9.2 %convolution_convert_fusion.5 = bf16[1024,704]{0,1:T(8,128)(2,1)} fusion(bf16[1024,2816]{1,0:T(8,128)(2,1)} %all-gather.11.cloned.1.call-done, bf16[2816,704]{0,1:T(8,128)(2,1)} %all-gather.13.cloned.1.call-done), kind=kOutput, calls=%fused_computation.89 | convolution fusion | flops 4060807168 | bytes 11173888 | tf_op jit(solution)/shard_map/dot_general | solution.py:99
  623.4 22.7 %reduce-scatter.17.cloned.1.call-done = bf16[256,704]{0,1:T(8,128)(2,1)} async-done(((bf16[1024,704]{0,1:T(8,128)(2,1)}), bf16[256,704]{0,1:T(8,128)(2,1)}) %reduce-scatter.17.cloned.1.call-update) | async-done | bytes 360464 | tf_op jit(solution)/shard_map/reduce_scatter | solution.py:140
  646.0 1.1 convert_reduce_fusion
  647.2 2.0 copy.19
  649.3 1.4 multiply_reduce_fusion.51
  650.7 12.1 %all-reduce.2 = (f32[4,2,32]{2,1,0:T(2,128)S(1)}, f32[4,2,32]{2,1,0:T(2,128)S(1)}) all-reduce(f32[4,2,32]{2,1,0:T(2,128)S(1)} %multiply_reduce_fusion.51, f32[4,2,32]{2,1,0:T(2,128)S(1)} %reduce_sum.512), channel_id=1, replica_groups=mesh['dp'=2,'row'=4,'col'=4] {'col'}, use_global_device_ids=true, to_apply=%region_17.18 | all-reduce | flops 512 | bytes 4096 | tf_op jit(solution)/shard_map/psum | solution.py:163
  662.7 3.3 multiply_reduce_fusion.2
  666.3 1.2 multiply_reduce_fusion.38
  667.5 2.0 multiply_reduce_fusion.20
  669.9 0.4 stack.249
  670.2 0.7 convert_element_type.97
  671.0 9.6 %convolution_convert_fusion.3 = bf16[704,2816]{1,0:T(8,128)(2,1)} fusion(bf16[1024,704]{1,0:T(8,128)(2,1)} %all-gather.7.cloned.1.call-done, bf16[1024,2816]{1,0:T(8,128)(2,1)} %all-gather.17.cloned.1.call-done), kind=kOutput, calls=%fused_computation.45 | convolution fusion | flops 4062068736 | bytes 11173888 | tf_op jit(solution)/shard_map/dot_general | solution.py:135
  680.6 6.4 copy.20
  687.1 1.3 copy-done.47
  688.4 8.8 %convolution_convert_fusion.2 = bf16[2816,704]{0,1:T(8,128)(2,1)} fusion(bf16[1024,2816]{1,0:T(8,128)(2,1)} %all-gather.11.cloned.1.call-done, bf16[1024,704]{1,0:T(8,128)(2,1)S(1)} %copy-done.47), kind=kOutput, calls=%fused_computation.44 | convolution fusion | flops 4062068736 | bytes 11173888 | tf_op jit(solution)/shard_map/dot_general | solution.py:132
  697.2 6.3 copy.22
  703.6 3.5 collective-permute-start.2
  707.4 1.5 collective-permute-start.3
  709.0 1.2 copy.18
  710.1 0.8 add_convert_fusion
  711.0 23.3 %all-reduce.6.cloned.1.call-done = bf16[7,7,704]{2,1,0:T(8,128)(2,1)} async-done(((bf16[7,7,704]{2,1,0:T(8,128)(2,1)}), bf16[7,7,704]{2,1,0:T(8,128)(2,1)}) %all-reduce.6.cloned.1.call-update) | async-done | bytes 69008 | tf_op jit(solution)/shard_map/psum | solution.py:181
  734.3 1.6 convert_multiply_fusion.2
  736.2 7.0 fusion.116
  743.2 6.3 reduce-scatter.19.cloned.1.call-done
  749.5 3.1 copy.21
  752.6 2.3 convert_multiply_fusion.1
  754.9 10.4 %reduce-scatter.21.cloned.1.call-done = bf16[1408,704]{1,0:T(8,128)(2,1)} async-done(((bf16[2816,704]{1,0:T(8,128)(2,1)}), bf16[1408,704]{1,0:T(8,128)(2,1)}) %reduce-scatter.21.cloned.1.call-update) | async-done | bytes 1982480
  765.3 3.1 copy.23
  768.4 2.3 convert_multiply_fusion
  (177 shorter events, 1.7 us)
Async XLA Ops:
  7.2 80.0 %all-gather.7.cloned.1.call-start = ((), (), s32[]{:S(2)}) async-start(), calls=%async_computation.6 | async-start | bytes 1966080 | tf_op jit(solution)/shard_map/all_gather | solution.py:73
  8.3 11.1 %collective-permute-start = (bf16[3,2,32,704]{3,2,1,0:T(8,128)(2,1)S(1)}, bf16[3,2,32,704]{3,2,1,0:T(8,128)(2,1)S(1)}, u32[]{:S(2)}, u32[]{:S(2)}) collective-permute-start(bf16[3,2,32,704]{3,2,1,0:T(8,128)(2,1)S(1)} %get-tuple-element.119), channel_id=1, source_target_pairs={{0,4},{4,8},{8,12},{1,5},{5,9},{9,13},{2,6},{6,10},{10,14},{3,7},{... | collective-permute-start | bytes 811016 | tf_op jit(solution)/shard_map/ppermute | solution.py:22
  13.2 14.5 %collective-permute-start.1 = (bf16[3,2,32,704]{3,2,1,0:T(8,128)(2,1)S(1)}, bf16[3,2,32,704]{3,2,1,0:T(8,128)(2,1)S(1)}, u32[]{:S(2)}, u32[]{:S(2)}) collective-permute-start(bf16[3,2,32,704]{3,2,1,0:T(8,128)(2,1)S(1)} %get-tuple-element.120), channel_id=1, source_target_pairs={{4,0},{8,4},{12,8},{5,1},{9,5},{13,9},{6,2},{10,6},{14,10},{7,3},{... | collective-permute-start | bytes 811016 | tf_op jit(solution)/shard_map/ppermute | solution.py:25
  17.0 18.6 %copy-start.4 = (f32[704]{0:T(1024)}, f32[704]{0:T(1024)S(1)}, u32[]{:S(2)}) copy-start(f32[704]{0:T(1024)S(1)} %get-tuple-element.73) | copy-start | bytes 8452
  17.0 18.6 %copy-start.6 = (f32[704]{0:T(1024)}, f32[704]{0:T(1024)S(1)}, u32[]{:S(2)}) copy-start(f32[704]{0:T(1024)S(1)} %get-tuple-element.74) | copy-start | bytes 8452
  18.5 17.2 %copy-start.8 = (f32[704]{0:T(1024)}, f32[704]{0:T(1024)S(1)}, u32[]{:S(2)}) copy-start(f32[704]{0:T(1024)S(1)} %get-tuple-element.75) | copy-start | bytes 8452
  18.5 17.2 %copy-start.10 = (f32[704]{0:T(1024)}, f32[704]{0:T(1024)S(1)}, u32[]{:S(2)}) copy-start(f32[704]{0:T(1024)S(1)} %get-tuple-element.76) | copy-start | bytes 8452
  18.5 17.2 %copy-start.12 = (f32[704]{0:T(1024)}, f32[704]{0:T(1024)S(1)}, u32[]{:S(2)}) copy-start(f32[704]{0:T(1024)S(1)} %get-tuple-element.77) | copy-start | bytes 8452
  18.5 17.2 %copy-start.14 = (f32[704]{0:T(1024)}, f32[704]{0:T(1024)S(1)}, u32[]{:S(2)}) copy-start(f32[704]{0:T(1024)S(1)} %get-tuple-element.78) | copy-start | bytes 8452
  18.5 17.2 %copy-start.16 = (f32[704]{0:T(1024)}, f32[704]{0:T(1024)S(1)}, u32[]{:S(2)}) copy-start(f32[704]{0:T(1024)S(1)} %get-tuple-element.79) | copy-start | bytes 8452
  18.5 17.2 %copy-start.18 = (f32[704]{0:T(1024)}, f32[704]{0:T(1024)S(1)}, u32[]{:S(2)}) copy-start(f32[704]{0:T(1024)S(1)} %get-tuple-element.80) | copy-start | bytes 8452
  18.5 17.2 %copy-start.20 = (f32[704]{0:T(1024)}, f32[704]{0:T(1024)S(1)}, u32[]{:S(2)}) copy-start(f32[704]{0:T(1024)S(1)} %get-tuple-element.81) | copy-start | bytes 8452
  18.5 17.2 %copy-start.22 = (f32[704]{0:T(1024)}, f32[704]{0:T(1024)S(1)}, u32[]{:S(2)}) copy-start(f32[704]{0:T(1024)S(1)} %get-tuple-element.82) | copy-start | bytes 8452
  18.5 17.2 %copy-start.24 = (f32[704]{0:T(1024)}, f32[704]{0:T(1024)S(1)}, u32[]{:S(2)}) copy-start(f32[704]{0:T(1024)S(1)} %get-tuple-element.83) | copy-start | bytes 8452
  18.6 17.2 %copy-start.26 = (f32[704]{0:T(1024)}, f32[704]{0:T(1024)S(1)}, u32[]{:S(2)}) copy-start(f32[704]{0:T(1024)S(1)} %get-tuple-element.84) | copy-start | bytes 8452
  18.6 17.2 %copy-start.28 = (f32[704]{0:T(1024)}, f32[704]{0:T(1024)S(1)}, u32[]{:S(2)}) copy-start(f32[704]{0:T(1024)S(1)} %get-tuple-element.85) | copy-start | bytes 8452
  18.6 17.2 %copy-start.30 = (f32[704]{0:T(1024)}, f32[704]{0:T(1024)S(1)}, u32[]{:S(2)}) copy-start(f32[704]{0:T(1024)S(1)} %get-tuple-element.86) | copy-start | bytes 8452
  18.6 17.2 %copy-start.32 = (f32[704]{0:T(1024)}, f32[704]{0:T(1024)S(1)}, u32[]{:S(2)}) copy-start(f32[704]{0:T(1024)S(1)} %get-tuple-element.87) | copy-start | bytes 8452
  18.6 17.2 %copy-start.34 = (f32[704]{0:T(1024)}, f32[704]{0:T(1024)S(1)}, u32[]{:S(2)}) copy-start(f32[704]{0:T(1024)S(1)} %get-tuple-element.88) | copy-start | bytes 8452
  18.6 17.2 %copy-start.36 = (f32[704]{0:T(1024)}, f32[704]{0:T(1024)S(1)}, u32[]{:S(2)}) copy-start(f32[704]{0:T(1024)S(1)} %get-tuple-element.89) | copy-start | bytes 8452
  18.6 17.2 %copy-start.38 = (f32[704]{0:T(1024)}, f32[704]{0:T(1024)S(1)}, u32[]{:S(2)}) copy-start(f32[704]{0:T(1024)S(1)} %get-tuple-element.90) | copy-start | bytes 8452
  18.6 17.2 %copy-start.40 = (f32[704]{0:T(1024)}, f32[704]{0:T(1024)S(1)}, u32[]{:S(2)}) copy-start(f32[704]{0:T(1024)S(1)} %get-tuple-element.91) | copy-start | bytes 8452
  18.6 17.2 %copy-start.42 = (f32[704]{0:T(1024)}, f32[704]{0:T(1024)S(1)}, u32[]{:S(2)}) copy-start(f32[704]{0:T(1024)S(1)} %get-tuple-element.92) | copy-start | bytes 8452
  18.6 17.2 %copy-start.44 = (f32[704]{0:T(1024)}, f32[704]{0:T(1024)S(1)}, u32[]{:S(2)}) copy-start(f32[704]{0:T(1024)S(1)} %get-tuple-element.93) | copy-start | bytes 8452
  57.3 44.7 %all-gather.9.cloned.1.call-start = ((), (), s32[]{:S(2)}) async-start(), calls=%async_computation.7 | async-start | bytes 5947392 | tf_op jit(solution)/shard_map/all_gather | solution.py:72
  58.1 78.0 %all-gather.15.cloned.1.call-start = ((), (), s32[]{:S(2)}) async-start(), calls=%async_computation.12 | async-start | bytes 1966080 | tf_op jit(solution)/shard_map/all_gather | solution.py:105
  58.8 92.0 %all-gather.13.cloned.1.call-start = ((), (), s32[]{:S(2)}) async-start(), calls=%async_computation.10 | async-start | bytes 5947392 | tf_op jit(solution)/shard_map/all_gather | solution.py:96
  59.4 197.0 %reduce-scatter.11.cloned.1.call-start = ((), (), s32[]{:S(2)}) async-start(), calls=%async_computation.8 | async-start | bytes 7208960 | tf_op jit(solution)/shard_map/reduce_scatter | solution.py:76
  111.8 249.6 %reduce-scatter.15.cloned.1.call-start = ((), (), s32[]{:S(2)}) async-start(), calls=%async_computation.13 | async-start | bytes 7208960 | tf_op jit(solution)/shard_map/reduce_scatter | solution.py:110
  160.9 95.6 %copy-start.3 = (f32[2816]{0:T(1024)S(1)}, f32[2816]{0:T(1024)}, u32[]{:S(2)}) copy-start(f32[2816]{0:T(1024)} %param.12) | copy-start | bytes 33796
  160.9 200.5 %copy-start.2 = (f32[2816]{0:T(1024)S(1)}, f32[2816]{0:T(1024)}, u32[]{:S(2)}) copy-start(f32[2816]{0:T(1024)} %param.13) | copy-start | bytes 33796
  160.9 346.0 %all-gather.17.cloned.1.call-start = ((), (), s32[]{:S(2)}) async-start(), calls=%async_computation.14 | async-start | bytes 7208960 | tf_op jit(solution)/shard_map/all_gather | solution.py:131
  264.6 128.7 %copy-start.46 = (f32[2816]{0:T(1024)S(1)}, f32[2816]{0:T(1024)}, u32[]{:S(2)}) copy-start(f32[2816]{0:T(1024)} %param.14) | copy-start | bytes 33796
  403.7 210.4 %all-gather.11.cloned.1.call-start = ((), (), s32[]{:S(2)}) async-start(), calls=%async_computation.9 | async-start | bytes 7208960 | tf_op jit(solution)/shard_map/all_gather | solution.py:95
  404.4 241.6 %reduce-scatter.17.cloned.1.call-start = ((), (), s32[]{:S(2)}) async-start(), calls=%async_computation.15 | async-start | bytes 1802240 | tf_op jit(solution)/shard_map/reduce_scatter | solution.py:140
  516.1 192.8 %reduce-scatter.13.cloned.1.call-start = ((), (), s32[]{:S(2)}) async-start(), calls=%async_computation.11 | async-start | bytes 1802240 | tf_op jit(solution)/shard_map/reduce_scatter | solution.py:98
  623.3 111.0 %all-reduce.6.cloned.1.call-start = ((), (), s32[]{:S(2)}) async-start(), calls=%async_computation.16 | async-start | bytes 172032 | tf_op jit(solution)/shard_map/psum | solution.py:181
  670.9 78.6 %reduce-scatter.19.cloned.1.call-start = ((), (), s32[]{:S(2)}) async-start(), calls=%async_computation.17 | async-start | bytes 6488064
  687.0 78.3 %reduce-scatter.21.cloned.1.call-start = ((), (), s32[]{:S(2)}) async-start(), calls=%async_computation.18 | async-start | bytes 6488064
  703.6 6.6 copy-start
  703.6 32.2 %collective-permute-start.2 = (bf16[3,2,32,704]{3,2,1,0:T(8,128)(2,1)S(1)}, bf16[3,2,32,704]{3,2,1,0:T(8,128)(2,1)S(1)}, u32[]{:S(2)}, u32[]{:S(2)}) collective-permute-start(bf16[3,2,32,704]{3,2,1,0:T(8,128)(2,1)S(1)} %get-tuple-element.117), channel_id=1, source_target_pairs={{0,4},{4,8},{8,12},{1,5},{5,9},{9,13},{2,6},{6,10},{10,14},{3,7},{... | collective-permute-start | bytes 811016 | tf_op jit(solution)/shard_map/ppermute | solution.py:22
  707.2 28.9 %copy-start.1 = (bf16[4,2,32,704]{3,2,1,0:T(8,128)(2,1)S(1)}, bf16[4,2,32,704]{3,2,1,0:T(8,128)(2,1)}, u32[]{:S(2)}) copy-start(bf16[4,2,32,704]{3,2,1,0:T(8,128)(2,1)} %param.9) | copy-start | bytes 1081348
  707.2 28.9 %copy-start.5 = (f32[704]{0:T(1024)S(1)}, f32[704]{0:T(1024)}, u32[]{:S(2)}) copy-start(f32[704]{0:T(1024)} %copy-done.4) | copy-start | bytes 8452
  707.2 28.9 %copy-start.7 = (f32[704]{0:T(1024)S(1)}, f32[704]{0:T(1024)}, u32[]{:S(2)}) copy-start(f32[704]{0:T(1024)} %copy-done.6) | copy-start | bytes 8452
  707.2 28.9 %copy-start.9 = (f32[704]{0:T(1024)S(1)}, f32[704]{0:T(1024)}, u32[]{:S(2)}) copy-start(f32[704]{0:T(1024)} %copy-done.8) | copy-start | bytes 8452
  707.2 28.9 %copy-start.11 = (f32[704]{0:T(1024)S(1)}, f32[704]{0:T(1024)}, u32[]{:S(2)}) copy-start(f32[704]{0:T(1024)} %copy-done.10) | copy-start | bytes 8452
  707.2 28.9 %copy-start.13 = (f32[704]{0:T(1024)S(1)}, f32[704]{0:T(1024)}, u32[]{:S(2)}) copy-start(f32[704]{0:T(1024)} %copy-done.12) | copy-start | bytes 8452
  707.2 28.9 %copy-start.15 = (f32[704]{0:T(1024)S(1)}, f32[704]{0:T(1024)}, u32[]{:S(2)}) copy-start(f32[704]{0:T(1024)} %copy-done.14) | copy-start | bytes 8452
  707.2 28.9 %copy-start.17 = (f32[704]{0:T(1024)S(1)}, f32[704]{0:T(1024)}, u32[]{:S(2)}) copy-start(f32[704]{0:T(1024)} %copy-done.16) | copy-start | bytes 8452
  707.2 28.9 %copy-start.19 = (f32[704]{0:T(1024)S(1)}, f32[704]{0:T(1024)}, u32[]{:S(2)}) copy-start(f32[704]{0:T(1024)} %copy-done.18) | copy-start | bytes 8452
  707.2 28.9 %copy-start.21 = (f32[704]{0:T(1024)S(1)}, f32[704]{0:T(1024)}, u32[]{:S(2)}) copy-start(f32[704]{0:T(1024)} %copy-done.20) | copy-start | bytes 8452
  707.3 28.9 %copy-start.23 = (f32[704]{0:T(1024)S(1)}, f32[704]{0:T(1024)}, u32[]{:S(2)}) copy-start(f32[704]{0:T(1024)} %copy-done.22) | copy-start | bytes 8452
  707.3 28.9 %copy-start.25 = (f32[704]{0:T(1024)S(1)}, f32[704]{0:T(1024)}, u32[]{:S(2)}) copy-start(f32[704]{0:T(1024)} %copy-done.24) | copy-start | bytes 8452
  707.3 28.9 %copy-start.27 = (f32[704]{0:T(1024)S(1)}, f32[704]{0:T(1024)}, u32[]{:S(2)}) copy-start(f32[704]{0:T(1024)} %copy-done.26) | copy-start | bytes 8452
  707.3 28.9 %copy-start.29 = (f32[704]{0:T(1024)S(1)}, f32[704]{0:T(1024)}, u32[]{:S(2)}) copy-start(f32[704]{0:T(1024)} %copy-done.28) | copy-start | bytes 8452
  707.3 28.9 %copy-start.31 = (f32[704]{0:T(1024)S(1)}, f32[704]{0:T(1024)}, u32[]{:S(2)}) copy-start(f32[704]{0:T(1024)} %copy-done.30) | copy-start | bytes 8452
  707.3 28.9 %copy-start.33 = (f32[704]{0:T(1024)S(1)}, f32[704]{0:T(1024)}, u32[]{:S(2)}) copy-start(f32[704]{0:T(1024)} %copy-done.32) | copy-start | bytes 8452
  707.3 28.9 %copy-start.35 = (f32[704]{0:T(1024)S(1)}, f32[704]{0:T(1024)}, u32[]{:S(2)}) copy-start(f32[704]{0:T(1024)} %copy-done.34) | copy-start | bytes 8452
  707.3 28.9 %copy-start.37 = (f32[704]{0:T(1024)S(1)}, f32[704]{0:T(1024)}, u32[]{:S(2)}) copy-start(f32[704]{0:T(1024)} %copy-done.36) | copy-start | bytes 8452
  707.3 28.9 %copy-start.39 = (f32[704]{0:T(1024)S(1)}, f32[704]{0:T(1024)}, u32[]{:S(2)}) copy-start(f32[704]{0:T(1024)} %copy-done.38) | copy-start | bytes 8452
  707.3 28.9 %copy-start.41 = (f32[704]{0:T(1024)S(1)}, f32[704]{0:T(1024)}, u32[]{:S(2)}) copy-start(f32[704]{0:T(1024)} %copy-done.40) | copy-start | bytes 8452
  707.4 28.9 %copy-start.43 = (f32[704]{0:T(1024)S(1)}, f32[704]{0:T(1024)}, u32[]{:S(2)}) copy-start(f32[704]{0:T(1024)} %copy-done.42) | copy-start | bytes 8452
  707.4 28.9 %copy-start.45 = (f32[704]{0:T(1024)S(1)}, f32[704]{0:T(1024)}, u32[]{:S(2)}) copy-start(f32[704]{0:T(1024)} %copy-done.44) | copy-start | bytes 8452
  707.4 28.5 %collective-permute-start.3 = (bf16[3,2,32,704]{3,2,1,0:T(8,128)(2,1)S(1)}, bf16[3,2,32,704]{3,2,1,0:T(8,128)(2,1)S(1)}, u32[]{:S(2)}, u32[]{:S(2)}) collective-permute-start(bf16[3,2,32,704]{3,2,1,0:T(8,128)(2,1)S(1)} %get-tuple-element.118), channel_id=1, source_target_pairs={{4,0},{8,4},{12,8},{5,1},{9,5},{13,9},{6,2},{10,6},{14,10},{7,3},{... | collective-permute-start | bytes 811016 | tf_op jit(solution)/shard_map/ppermute | solution.py:25
  (1 other events, 1.4 us)
Sparse Core Ops, SparseCore 0:
  57.5 29.6 all-gather.6
  88.7 13.2 all-gather.8
  103.9 32.1 all-gather.14
  137.5 13.2 all-gather.12
  153.0 103.3 reduce-scatter.10
  258.6 102.7 reduce-scatter.14
  403.8 103.0 all-gather.16
  509.0 104.9 all-gather.10
  617.6 28.3 reduce-scatter.16
  649.7 30.1 reduce-scatter.12
  683.5 50.7 all-reduce.5
  736.6 12.9 reduce-scatter.18
  751.8 13.4 reduce-scatter.20
where the time goes:
time: 787 us; the launch traced here: 778 us
  waiting for transfers between devices  549 us (70%)
  blocking collectives  61.1 us (8%)
  matrix products  56.6 us (7%)
  other arithmetic  53.8 us (7%)
  local copies, waits for them, and re-layouts  30.1 us (4%)
  between operations  15.6 us (2%)
  starting transfers between devices  11.9 us (2%)
    all_gather x1, waiting for transfers between devices, local(): grad_pre_all = lax.all_gather(grad_rows, 'col', axis=0, tiled=True)  102 us
    all_gather x1, waiting for transfers between devices, local(): gated_all = lax.all_gather(gated_rows, 'col', axis=0, tiled=True)  97.9 us
    reduce_scatter x1, waiting for transfers between devices, local(): lax.psum_scatter(lax.dot_general(rows_in, w_out_back, contract_last, pref...  96.8 us
    reduce_scatter x1, waiting for transfers between devices, local(): lax.psum_scatter(jnp.dot(rows_in, w_in_full, preferred_element_type=jnp.f...  95.3 us
    all_gather x1, waiting for transfers between devices, local(): normed_all = lax.all_gather(normed, 'row', axis=0, tiled=True)  27.7 us
    all_gather x1, waiting for transfers between devices, local(): lax.all_gather(cotangent.reshape(local_pix, chans), 'row', axis=0, tiled=...  24.2 us
    psum x1, waiting for transfers between devices, local(): lax.psum(kern_local.astype(jnp.bfloat16), ('dp', 'row')).astype(jnp.float32)  23.3 us
    reduce_scatter x1, waiting for transfers between devices, local(): lax.psum_scatter(lax.dot_general(rows_in, w_in_back, contract_last, prefe...  22.7 us
  transfers between devices with their start and end apart: 17, of which 14 were waited for; matrix products, arithmetic and copies ran while one was open for 14% of the time, Pallas kernels for 0%

commit v1 on v0

v1 whole, which is shorter than its diff:
```python
import math

import jax
import jax.numpy as jnp
from jax import lax
from jax.sharding import PartitionSpec as P

epsilon = 1e-06
root_half = 0.7071067811865476
inv_root_tau = 0.3989422804014327
last_last = (((1,), (1,)), ((), ()))
first_first = (((0,), (0,)), ((), ()))
f32 = jnp.float32
bf16 = jnp.bfloat16


def swap(block, axis, bits):
    count = lax.axis_size(axis)
    return lax.ppermute(block, axis, [(i, i ^ bits) for i in range(count)])


def low_bit(m):
    return m & -m


def high_bit(m):
    return 1 << (m.bit_length() - 1)


def gather(block, axis, bit):
    held = [block]
    for m in range(1, lax.axis_size(axis)):
        step = bit(m)
        held.append(swap(held[m ^ step], axis, step))
    return held


def scatter_sum(parts, axis, bit):
    parts = list(parts)
    for m in range(lax.axis_size(axis) - 1, 0, -1):
        step = bit(m)
        got = swap(parts[m].astype(bf16), axis, step)
        parts[m ^ step] = parts[m ^ step].astype(f32) + got.astype(f32)
    return parts[0]


def gather_pixels(block):
    cols = gather(block, "col", low_bit)
    half = len(cols) // 2
    lower = gather(jnp.stack(cols[:half]), "row", low_bit)
    upper = gather(jnp.stack(cols[half:]), "row", high_bit)
    out = []
    for group in (lower, upper):
        for m in range(half):
            out.append(jnp.concatenate([piece[m] for piece in group], axis=0))
    return out


def scatter_pixels(blocks):
    half = len(blocks) // 2
    rows = lax.axis_size("row")
    done = []
    for group, bit in ((blocks[:half], low_bit), (blocks[half:], high_bit)):
        stacked = jnp.stack([b.reshape(rows, -1, b.shape[-1]) for b in group], axis=1)
        done.append(scatter_sum([stacked[q] for q in range(rows)], "row", bit))
    parts = [d[m].astype(bf16) for d in done for m in range(half)]
    return scatter_sum(parts, "col", low_bit)


def trade_pieces(pieces):
    return [pieces[0]] + [swap(pieces[m], "col", m) for m in range(1, len(pieces))]


def whole_weights(rows):
    count = lax.axis_size("col")
    share = rows.shape[0] // count
    me = lax.axis_index("col")
    pieces = [lax.dynamic_slice_in_dim(rows, (me ^ m) * share, share, axis=0) for m in range(count)]
    mine = jnp.stack(trade_pieces(pieces))
    other = swap(mine, "dp", 1)
    both = jnp.concatenate([mine, other], axis=1)
    return [both[m] for m in range(count)]


def whole_grads(blocks):
    count = len(blocks)
    share = blocks[0].shape[0] // 2
    me = lax.axis_index("col")
    stacked = jnp.stack(blocks)
    mine, other = stacked[:, :share], stacked[:, share:]
    got = swap(other, "dp", 1)
    total = (mine.astype(f32) + got.astype(f32)).astype(bf16)
    pieces = jnp.stack(trade_pieces([total[m] for m in range(count)]))
    return jnp.concatenate(
        [lax.dynamic_index_in_dim(pieces, me ^ j, 0, keepdims=False) for j in range(count)], axis=0
    )


def own_units(vector):
    count = lax.axis_size("col")
    span = vector.shape[0] // 2
    share = span // count
    me = lax.axis_index("col")
    side = lax.axis_index("dp")
    mine = lax.dynamic_slice_in_dim(vector, side * span + me * share, share)
    other = lax.dynamic_slice_in_dim(vector, (1 - side) * span + me * share, share)
    return jnp.concatenate([mine, other])


def add_over(value, axis):
    n = lax.axis_size(axis)
    step = 1
    while step < n:
        value = value + swap(value, axis, step)
        step *= 2
    return value


def extended(block, width):
    count = lax.axis_size("row")
    forward = [(i, i + 1) for i in range(count - 1)]
    backward = [(i + 1, i) for i in range(count - 1)]
    low = lax.ppermute(block[block.shape[0] - width :], "row", forward)
    high = lax.ppermute(block[:width], "row", backward)
    return jnp.concatenate([low, block, high], axis=0)


def depthwise(padded, kernel, height, width):
    span = kernel.shape[0]
    result = jnp.zeros((height, padded.shape[1], width, padded.shape[3]), f32)
    for row_off in range(span):
        for col_off in range(span):
            window = padded[row_off : row_off + height, :, col_off : col_off + width, :]
            result = result + kernel[row_off, col_off] * window
    return result


def pad_width(tile_in, reach):
    return jnp.pad(tile_in, ((0, 0), (0, 0), (reach, reach), (0, 0)))


def gelu_slope(hidden_pre):
    cumul = 0.5 * (1.0 + lax.erf(hidden_pre * root_half))
    return cumul + hidden_pre * jnp.exp(-0.5 * hidden_pre * hidden_pre) * inv_root_tau


def local(images, cotangent, kernel, w_in, b_in, grn_gamma, grn_beta, w_out):
    height, batch, width, chans = images.shape
    span = kernel.shape[0]
    reach = span // 2
    col_count = lax.axis_size("col")
    row_count = lax.axis_size("row")
    all_chans = chans * col_count
    all_units = b_in.shape[0] * row_count
    pixels = height * batch * width
    group_pix = pixels * row_count
    scale_grad = 1.0 / math.sqrt(group_pix * lax.axis_size("dp"))

    halo_x = extended(images, reach)
    w_in_all = whole_weights(w_in.T)
    cot_all = gather_pixels(cotangent.reshape(pixels, chans))
    w_out_all = whole_weights(w_out)
    bias, gamma, beta = own_units(b_in), own_units(grn_gamma), own_units(grn_beta)

    padded_x = pad_width(halo_x, reach).astype(f32)
    conv_out = depthwise(padded_x, kernel, height, width)
    mean_own = jnp.mean(conv_out, axis=-1)
    dev_own = conv_out - mean_own[..., None]
    stats = jnp.stack([mean_own, jnp.sum(dev_own * dev_own, axis=-1)])
    stats = [stats] + [swap(stats, "col", m) for m in range(1, col_count)]
    mean_pix = sum(s[0] for s in stats) / col_count
    var_pix = sum(s[1] + chans * (s[0] - mean_pix) ** 2 for s in stats) / all_chans
    inv_std = lax.rsqrt(var_pix + epsilon)[..., None]
    standard = (conv_out - mean_pix[..., None]) * inv_std
    normed_all = gather_pixels(standard.astype(bf16).reshape(pixels, chans))

    hidden_pre = bias + sum(
        lax.dot_general(x, w, last_last, preferred_element_type=f32)
        for x, w in zip(normed_all, w_in_all)
    )
    units = hidden_pre.shape[1]
    hidden_act = jax.nn.gelu(hidden_pre, approximate=False)
    act_four = hidden_act.reshape(-1, batch, width, units)
    norm_chan = jnp.sqrt(jnp.sum(act_four * act_four, axis=(0, 2)) + epsilon)
    norm_sum = add_over(add_over(jnp.sum(norm_chan, axis=-1), "row"), "col")
    denom = (norm_sum / all_units + epsilon)[:, None]
    ratio_chan = norm_chan / denom
    gated = (
        (gamma * act_four * ratio_chan[None, :, None, :] + beta + act_four)
        .astype(bf16)
        .reshape(group_pix, units)
    )
    branch = scatter_pixels(
        [jnp.dot(gated, w, preferred_element_type=f32).astype(bf16) for w in w_out_all]
    )
    result = (images.astype(f32) + branch.reshape(images.shape)).astype(bf16)

    grad_gated = sum(
        lax.dot_general(c, w, last_last, preferred_element_type=f32)
        for c, w in zip(cot_all, w_out_all)
    ).reshape(act_four.shape)
    pull_chan = jnp.sum(grad_gated * gamma * act_four, axis=(0, 2))
    grad_norm = pull_chan / denom
    grad_act = (
        grad_gated * (gamma * ratio_chan[None, :, None, :] + 1.0)
        + act_four * (grad_norm / norm_chan)[None, :, None, :]
    )
    grad_pre = (grad_act.reshape(group_pix, units) * gelu_slope(hidden_pre)).astype(bf16)
    grad_normed = scatter_pixels(
        [jnp.dot(grad_pre, w, preferred_element_type=f32).astype(bf16) for w in w_in_all]
    ).reshape(conv_out.shape)
    w_out_grad = (
        whole_grads(
            [
                lax.dot_general(gated, c, first_first, preferred_element_type=f32).astype(bf16)
                for c in cot_all
            ]
        ).astype(f32)
        * scale_grad
    )
    w_in_grad = (
        whole_grads(
            [
                lax.dot_general(grad_pre, x, first_first, preferred_element_type=f32).astype(bf16)
                for x in normed_all
            ]
        ).T.astype(f32)
        * scale_grad
    )

    sums = jnp.stack([jnp.sum(grad_normed, axis=-1), jnp.sum(grad_normed * standard, axis=-1)])
    sums = sum([swap(sums, "col", m) for m in range(1, col_count)], sums) / all_chans
    grad_conv = inv_std * (grad_normed - sums[0][..., None] - standard * sums[1][..., None])
    halo_cot = extended(grad_conv.astype(bf16), reach).astype(f32)
    spread = depthwise(pad_width(halo_cot, reach), kernel[::-1, ::-1], height, width)
    x_grad = (cotangent.astype(f32) + spread).astype(bf16)
    kern_terms = []
    for row_off in range(span):
        for col_off in range(span):
            window = padded_x[row_off : row_off + height, :, col_off : col_off + width, :]
            kern_terms.append(jnp.sum(grad_conv * window, axis=(0, 1, 2)))
    kern = jnp.stack(kern_terms).reshape(span, span, chans)
    for axis, step in (("dp", 1), ("row", 1), ("row", 2)):
        kern = kern.astype(bf16)
        kern = kern.astype(f32) + swap(kern, axis, step).astype(f32)
    kernel_grad = kern * scale_grad
    return (result, x_grad, w_in_grad, w_out_grad, kernel_grad)


def solution(mesh):
    return jax.shard_map(
        local,
        mesh=mesh,
        in_specs=(
            P("row", "dp", None, "col"),
            P("row", "dp", None, "col"),
            P(None, None, "col"),
            P("col", ("row", "dp")),
            P("row"),
            P("row"),
            P("row"),
            P(("row", "dp"), "col"),
        ),
        out_specs=(
            P("row", "dp", None, "col"),
            P("row", "dp", None, "col"),
            P("col", ("row", "dp")),
            P(("row", "dp"), "col"),
            P(None, None, "col"),
        ),
        check_vma=False,
    )
```

time: 787 us -> 654 us (0.83)
  waiting for transfers between devices: 549 us -> 261 us
  starting transfers between devices: 11.9 us -> 126 us
  local copies, waits for them, and re-layouts: 30.1 us -> 126 us
  blocking collectives: 61.1 us -> 0 us
  other arithmetic: 53.8 us -> 73.1 us
  between operations: 15.6 us -> 4.4 us
    all_gather x6 -> x0, waiting for transfers between devices: 282 us -> none  [the longest x1 102 us: local(): grad_pre_all = lax.all_gather(grad_rows, 'col', axis=0, tiled=True)]
    ppermute x4 -> x69, waiting for transfers between devices: 9.05 us -> 261 us  [the longest x65 261 us: swap(): return lax.ppermute(block, axis, [(i, i ^ bits) for i in range(count)])]
    reduce_scatter x4 -> x0, waiting for transfers between devices: 215 us -> none  [the longest x1 96.8 us: local(): lax.psum_scatter(lax.dot_general(rows_in, w_out_back, contract_last, pref...]
    ppermute x4 -> x69, starting transfers between devices: 11.2 us -> 126 us  [the longest x65 118 us: swap(): return lax.ppermute(block, axis, [(i, i ^ bits) for i in range(count)])]
    psum x5 -> x0, blocking collectives: 61.1 us -> none  [the longest x1 18.7 us: local(): norm_chan = jnp.sqrt(lax.psum(sums_local, 'col') + epsilon)]
    another operation x50 -> x69, local copies, waits for them, and re-layouts: 0.61 us -> 42 us  [the longest x12 28.9 us: scatter_pixels(): jnp.stack([b.reshape(rows, -1, b.shape[-1]) for b in group], axis=1)]
    psum x1 -> x0, waiting for transfers between devices: 23.3 us -> none  [local(): lax.psum(kern_local.astype(jnp.bfloat16), ('dp', 'row')).astype(jnp.float32)]
    unnamed x15 -> x0, waiting for transfers between devices: 19.4 us -> none
  transfers between devices with their start and end apart: 17 -> 69, of which waited for: 14 -> 31; matrix products, arithmetic and copies ran while one was open for 14% -> 23% of each run, Pallas kernels for 0% -> 0%
where the time goes in v1:
time: 654 us; the launch traced here: 649 us
  waiting for transfers between devices  261 us (40%)
  starting transfers between devices  126 us (19%)
  local copies, waits for them, and re-layouts  126 us (19%)
  other arithmetic  73.1 us (11%)
  matrix products  56.8 us (9%)
    ppermute x65, waiting for transfers between devices, swap(): return lax.ppermute(block, axis, [(i, i ^ bits) for i in range(count)])  261 us
    ppermute x65, starting transfers between devices, swap(): return lax.ppermute(block, axis, [(i, i ^ bits) for i in range(count)])  118 us
    another operation x12, local copies, waits for them, and re-layouts, scatter_pixels(): jnp.stack([b.reshape(rows, -1, b.shape[-1]) for b in group], axis=1)  28.9 us
    unnamed x358, local copies, waits for them, and re-layouts  20.7 us
    dot_general x4, matrix products, local(): lax.dot_general(x, w, last_last, preferred_element_type=f32)  15.4 us
  transfers between devices with their start and end apart: 69, of which 31 were waited for; matrix products, arithmetic and copies ran while one was open for 23% of the time, Pallas kernels for 0%

profile of v1, /device:TPU:0, one launch (start us, length us, event | category | flops | bytes accessed | tf_op | source)
XLA Modules:
  0.0 648.5 jit_solution(11959249537837701094)
XLA Ops:
  0.6 4.1 collective-permute-start.39
  7.5 3.4 collective-permute-start
  12.2 4.1 dynamic-slice_bitcast_fusion.12
  18.0 4.1 dynamic-slice_bitcast_fusion.8
  29.0 7.6 %fusion.174 = (f32[4,2,32]{2,1,0:T(2,128)S(1)}, f32[4,2,32,704]{3,2,1,0:T(8,128)S(1)}) fusion(f32[10,2,38,704]{3,2,1,0:T(8,128)S(1)} %fusion.41, f32[704]{0:T(1024)S(1)} %get-tuple-element.103, f32[704]{0:T(1024)S(1)} %get-tuple-element.104, f32[704]{0:T(1024)S(1)} %get-tuple-element.57, f32[704]{0:T(1024)S(1)} %get-tuple-element.58, ...), kind=kLoop, calls=%fused_computation.494 | loop fusion | flops 17661696 | bytes 36183808 | tf_op jit(solution)/shard_map/reduce_sum | solution.py:167
  44.2 9.5 %collective-permute-done.2 = f32[2,4,2,32]{3,2,1,0:T(2,128)S(1)} collective-permute-done((f32[2,4,2,32]{3,2,1,0:T(2,128)S(1)}, f32[2,4,2,32]{3,2,1,0:T(2,128)S(1)}, u32[]{:S(2)}, u32[]{:S(2)}) %collective-permute-start.2) | collective-permute-done | bytes 2080 | tf_op jit(solution)/shard_map/ppermute | solution.py:19
  53.7 4.5 collective-permute-start.10
  62.9 22.7 %collective-permute-start.13 = (bf16[256,704]{0,1:T(8,128)(2,1)}, bf16[256,704]{0,1:T(8,128)(2,1)}, u32[]{:S(2)}, u32[]{:S(2)}) collective-permute-start(bf16[256,704]{0,1:T(8,128)(2,1)} %copy.79), channel_id=1, source_target_pairs={{0,2},{1,3},{2,0},{3,1},{4,6},{5,7},{6,4},{7,5},{8,10},{9,11},{10,... | collective-permute-start | bytes 1081352 | tf_op jit(solution)/shard_map/ppermute | solution.py:19
  89.0 6.3 collective-permute-done.24
  95.3 3.4 collective-permute-start.37
  98.7 46.9 %collective-permute-done.23 = bf16[352,704]{0,1:T(8,128)(2,1)} collective-permute-done((bf16[352,704]{0,1:T(8,128)(2,1)}, bf16[352,704]{0,1:T(8,128)(2,1)}, u32[]{:S(2)}, u32[]{:S(2)}) %collective-permute-start.23) | collective-permute-done | bytes 495648 | tf_op jit(solution)/shard_map/ppermute | solution.py:19
  145.6 3.2 pad_maximum_fusion.4
  153.2 2.9 pad_maximum_fusion.5
  159.2 3.3 collective-permute-start.7
  182.8 5.8 collective-permute-done.6
  188.6 2.9 collective-permute-start.16
  199.4 4.7 collective-permute-done.41
  213.2 6.3 collective-permute-done.15
  219.5 2.9 collective-permute-start.43
  224.4 10.6 %collective-permute-done.38 = bf16[2,256,704]{1,2,0:T(8,128)(2,1)} collective-permute-done((bf16[2,256,704]{1,2,0:T(8,128)(2,1)}, bf16[2,256,704]{1,2,0:T(8,128)(2,1)}, u32[]{:S(2)}, u32[]{:S(2)}) %collective-permute-start.38) | collective-permute-done | bytes 720928 | tf_op jit(solution)/shard_map/ppermute | solution.py:19
  234.9 2.9 collective-permute-start.17
  240.8 9.4 %collective-permute-done.8 = bf16[2,256,704]{1,2,0:T(8,128)(2,1)} collective-permute-done((bf16[2,256,704]{1,2,0:T(8,128)(2,1)}, bf16[2,256,704]{1,2,0:T(8,128)(2,1)}, u32[]{:S(2)}, u32[]{:S(2)}) %collective-permute-start.8) | collective-permute-done | bytes 720928 | tf_op jit(solution)/shard_map/ppermute | solution.py:19
  256.4 4.3 pad_maximum_fusion.1
  266.4 10.3 %fusion.1 = (f32[1024,704]{0,1:T(8,128)S(1)}, f32[1024,704]{0,1:T(8,128)}) fusion(bf16[4,704,704]{1,2,0:T(8,128)(2,1)S(1)} %pad_maximum_fusion.1, bf16[256,704]{0,1:T(8,128)(2,1)S(1)} %get-tuple-element.165, bf16[256,704]{0,1:T(8,128)(2,1)S(1)} %copy-done.71, bf16[256,704]{0,1:T(8,128)(2,1)S(1)} %copy-done.75, ...), kind=kOutput, calls=%fused_computation.57 | convolution fusion | flops 1069809664 | bytes 16945152 | tf_op jit(solution)/shard_map/dot_general | solution.py:178
  276.6 2.6 copy.81
  279.3 3.9 pad_maximum_fusion
  285.4 2.5 fusion.47
  293.5 3.5 multiply_reduce_fusion
  300.7 2.7 collective-permute-start.19
  304.9 3.5 collective-permute-done.20
  308.5 4.4 collective-permute-done.21
  315.0 3.5 copy.104
  320.5 3.5 copy.82
  326.0 3.4 copy.106
  329.4 6.7 %fusion.7 = (bf16[1024,704]{0,1:T(8,128)(2,1)S(1)}, bf16[1024,704]{0,1:T(8,128)(2,1)S(1)}) fusion(f32[1024,704]{0,1:T(8,128)} %get-tuple-element.189, f32[1024,704]{0,1:T(8,128)} %copy-done.4, f32[1024,704]{0,1:T(8,128)} %copy.106, f32[1024,704]{0,1:T(8,128)S(1)} %add_add_fusion, f32[1024,704]{0,1:T(8,128)} %copy.104, f32[704]{0:T(1024)S(1)} %pad_maximum_fusion.40, ...), kind=kLoop, calls=%fused_computation.63 | loop fusion | flops 12976128 | bytes 20190720 | tf_op jit(solution)/shard_map/convert_element_type | solution.py:208
  338.5 3.8 convolution_convert_fusion.3
  359.6 4.0 stack_reshape.36
  365.5 4.2 stack_reshape.39
  373.2 4.0 stack_reshape.31
  377.2 2.6 copy_dynamic-update-slice_fusion.7
  379.9 4.0 stack_reshape.32
  383.9 4.0 stack_reshape.34
  387.9 4.0 stack_reshape.33
  410.3 2.4 fusion.37
  418.6 10.0 %collective-permute-done.30 = bf16[2,256,704]{1,2,0:T(8,128)(2,1)S(1)} collective-permute-done((bf16[2,256,704]{1,2,0:T(8,128)(2,1)S(1)}, bf16[2,256,704]{1,2,0:T(8,128)(2,1)S(1)}, u32[]{:S(2)}, u32[]{:S(2)}) %collective-permute-start.30) | collective-permute-done | bytes 720928 | tf_op jit(solution)/shard_map/ppermute | solution.py:19
  431.0 10.2 %collective-permute-done.48 = bf16[2,256,704]{1,2,0:T(8,128)(2,1)S(1)} collective-permute-done((bf16[2,256,704]{1,2,0:T(8,128)(2,1)S(1)}, bf16[2,256,704]{1,2,0:T(8,128)(2,1)S(1)}, u32[]{:S(2)}, u32[]{:S(2)}) %collective-permute-start.48) | collective-permute-done | bytes 720928 | tf_op jit(solution)/shard_map/ppermute | solution.py:19
  443.5 4.2 collective-permute-done.44
  451.2 11.9 %collective-permute-done.31 = bf16[2,256,704]{1,2,0:T(8,128)(2,1)S(1)} collective-permute-done((bf16[2,256,704]{1,2,0:T(8,128)(2,1)S(1)}, bf16[2,256,704]{1,2,0:T(8,128)(2,1)S(1)}, u32[]{:S(2)}, u32[]{:S(2)}) %collective-permute-start.31) | collective-permute-done | bytes 720928 | tf_op jit(solution)/shard_map/ppermute | solution.py:19
  465.6 4.4 collective-permute-done.47
  471.7 15.3 %collective-permute-done.49 = bf16[2,256,704]{1,2,0:T(8,128)(2,1)S(1)} collective-permute-done((bf16[2,256,704]{1,2,0:T(8,128)(2,1)S(1)}, bf16[2,256,704]{1,2,0:T(8,128)(2,1)S(1)}, u32[]{:S(2)}, u32[]{:S(2)}) %collective-permute-start.49) | collective-permute-done | bytes 720928 | tf_op jit(solution)/shard_map/ppermute | solution.py:19
  490.8 7.5 %collective-permute-done.32 = bf16[256,704]{0,1:T(8,128)(2,1)S(1)} collective-permute-done((bf16[256,704]{0,1:T(8,128)(2,1)S(1)}, bf16[256,704]{0,1:T(8,128)(2,1)S(1)}, u32[]{:S(2)}, u32[]{:S(2)}) %collective-permute-start.32) | collective-permute-done | bytes 360480 | tf_op jit(solution)/shard_map/ppermute | solution.py:19
  499.4 17.9 %collective-permute-done.50 = bf16[256,704]{0,1:T(8,128)(2,1)S(1)} collective-permute-done((bf16[256,704]{0,1:T(8,128)(2,1)S(1)}, bf16[256,704]{0,1:T(8,128)(2,1)S(1)}, u32[]{:S(2)}, u32[]{:S(2)}) %collective-permute-start.50) | collective-permute-done | bytes 360480 | tf_op jit(solution)/shard_map/ppermute | solution.py:19
  517.5 3.0 collective-permute-start.51
  522.9 28.6 %collective-permute-done.51 = bf16[256,704]{0,1:T(8,128)(2,1)S(1)} collective-permute-done((bf16[256,704]{0,1:T(8,128)(2,1)S(1)}, bf16[256,704]{0,1:T(8,128)(2,1)S(1)}, u32[]{:S(2)}, u32[]{:S(2)}) %collective-permute-start.51) | collective-permute-done | bytes 360480 | tf_op jit(solution)/shard_map/ppermute | solution.py:19
  574.7 2.7 collective-permute-start.56
  578.7 4.7 collective-permute-start.68
  584.2 3.5 collective-permute-done.68
  587.8 2.5 collective-permute-start.59
  593.3 2.8 collective-permute-start.64
  596.7 7.7 %fusion.135 = bf16[4,2,32,704]{3,2,1,0:T(8,128)(2,1)} fusion(f32[10,2,32,704]{3,2,1,0:T(8,128)S(1)} %maximum_convert_fusion, bf16[4,2,32,704]{3,2,1,0:T(8,128)(2,1)S(1)} %copy-done.30, f32[704]{0:T(1024)S(1)} %copy-done.112, f32[704]{0:T(1024)S(1)} %copy-done.114, f32[704]{0:T(1024)S(1)} %copy-done.118, f32[704]{0:T(1024)S(1)} %copy-done.120, ...), kind=kLoop, calls=%fused_computation.255 | loop fusion | flops 18022400 | bytes 8410112 | tf_op jit(solution)/shard_map/convert_element_type | solution.py:236
  607.5 3.0 concatenate.66
  612.8 4.3 collective-permute-done.65
  617.0 22.7 %collective-permute-done.64 = bf16[352,704]{0,1:T(8,128)(2,1)} collective-permute-done((bf16[352,704]{0,1:T(8,128)(2,1)}, bf16[352,704]{0,1:T(8,128)(2,1)}, u32[]{:S(2)}, u32[]{:S(2)}) %collective-permute-start.64) | collective-permute-done | bytes 495648 | tf_op jit(solution)/shard_map/ppermute | solution.py:19
  642.8 3.0 concatenate.67
  (632 shorter events, 214.9 us)
Async XLA Ops:
  0.6 57.6 %collective-permute-start.39 = (bf16[256,704]{1,0:T(8,128)(2,1)}, bf16[256,704]{1,0:T(8,128)(2,1)}, u32[]{:S(2)}, u32[]{:S(2)}) collective-permute-start(bf16[256,704]{1,0:T(8,128)(2,1)} %bitcast.361), channel_id=1, source_target_pairs={{0,2},{1,3},{2,0},{3,1},{4,6},{5,7},{6,4},{7,5},{8,10},{9,11},{10,... | collective-permute-start | bytes 1081352 | tf_op jit(solution)/shard_map/ppermute | solution.py:19
  4.7 53.6 %collective-permute-start.35 = (bf16[256,704]{1,0:T(8,128)(2,1)}, bf16[256,704]{1,0:T(8,128)(2,1)S(1)}, u32[]{:S(2)}, u32[]{:S(2)}) collective-permute-start(bf16[256,704]{1,0:T(8,128)(2,1)} %bitcast.362), channel_id=1, source_target_pairs={{0,1},{1,0},{2,3},{3,2},{4,5},{5,4},{6,7},{7,6},{8,9},{9,8},{10,11... | collective-permute-start | bytes 1081352 | tf_op jit(solution)/shard_map/ppermute | solution.py:19
  7.5 20.0 %collective-permute-start = (bf16[3,2,32,704]{3,2,1,0:T(8,128)(2,1)S(1)}, bf16[3,2,32,704]{3,2,1,0:T(8,128)(2,1)S(1)}, u32[]{:S(2)}, u32[]{:S(2)}) collective-permute-start(bf16[3,2,32,704]{3,2,1,0:T(8,128)(2,1)S(1)} %get-tuple-element.175), channel_id=1, source_target_pairs={{0,4},{4,8},{8,12},{1,5},{5,9},{9,13},{2,6},{6,10},{10,14},{3,7},{... | collective-permute-start | bytes 811016 | tf_op jit(solution)/shard_map/ppermute | solution.py:123
  10.9 16.6 %collective-permute-start.1 = (bf16[3,2,32,704]{3,2,1,0:T(8,128)(2,1)S(1)}, bf16[3,2,32,704]{3,2,1,0:T(8,128)(2,1)}, u32[]{:S(2)}, u32[]{:S(2)}) collective-permute-start(bf16[3,2,32,704]{3,2,1,0:T(8,128)(2,1)S(1)} %get-tuple-element.176), channel_id=1, source_target_pairs={{4,0},{8,4},{12,8},{5,1},{9,5},{13,9},{6,2},{10,6},{14,10},{7,3},{... | collective-permute-start | bytes 811016 | tf_op jit(solution)/shard_map/ppermute | solution.py:124
  16.3 43.5 %collective-permute-start.9 = (bf16[352,704]{0,1:T(8,128)(2,1)}, bf16[352,704]{0,1:T(8,128)(2,1)S(1)}, u32[]{:S(2)}, u32[]{:S(2)}) collective-permute-start(bf16[352,704]{0,1:T(8,128)(2,1)} %get-tuple-element.145), channel_id=1, source_target_pairs={{0,1},{1,0},{2,3},{3,2},{4,5},{5,4},{6,7},{7,6},{8,9},{9,8},{10,11... | collective-permute-start | bytes 1486856 | tf_op jit(solution)/shard_map/ppermute | solution.py:19
  37.1 5.6 collective-permute-start.4
  38.5 5.6 collective-permute-start.3
  42.7 20.2 %collective-permute-start.11 = (bf16[352,704]{0,1:T(8,128)(2,1)}, bf16[352,704]{0,1:T(8,128)(2,1)S(1)}, u32[]{:S(2)}, u32[]{:S(2)}) collective-permute-start(bf16[352,704]{0,1:T(8,128)(2,1)} %get-tuple-element.146), channel_id=1, source_target_pairs={{0,3},{1,2},{2,1},{3,0},{4,7},{5,6},{6,5},{7,4},{8,11},{9,10},{10,... | collective-permute-start | bytes 1486856 | tf_op jit(solution)/shard_map/ppermute | solution.py:19
  44.1 9.6 %collective-permute-start.2 = (f32[2,4,2,32]{3,2,1,0:T(2,128)S(1)}, f32[2,4,2,32]{3,2,1,0:T(2,128)S(1)}, u32[]{:S(2)}, u32[]{:S(2)}) collective-permute-start(f32[2,4,2,32]{3,2,1,0:T(2,128)S(1)} %pad_maximum_fusion.36), channel_id=1, source_target_pairs={{0,1},{1,0},{2,3},{3,2},{4,5},{5,4},{6,7},{7,6},{8,9},{9,8},{10,11... | collective-permute-start | bytes 6152 | tf_op jit(solution)/shard_map/ppermute | solution.py:19
  53.7 95.1 %collective-permute-start.10 = (bf16[352,704]{0,1:T(8,128)(2,1)}, bf16[352,704]{0,1:T(8,128)(2,1)}, u32[]{:S(2)}, u32[]{:S(2)}) collective-permute-start(bf16[352,704]{0,1:T(8,128)(2,1)} %get-tuple-element.147), channel_id=1, source_target_pairs={{0,2},{1,3},{2,0},{3,1},{4,6},{5,7},{6,4},{7,5},{8,10},{9,11},{10,... | collective-permute-start | bytes 1486856 | tf_op jit(solution)/shard_map/ppermute | solution.py:19
  58.3 30.6 %collective-permute-start.22 = (bf16[352,704]{0,1:T(8,128)(2,1)}, bf16[352,704]{0,1:T(8,128)(2,1)}, u32[]{:S(2)}, u32[]{:S(2)}) collective-permute-start(bf16[352,704]{0,1:T(8,128)(2,1)} %get-tuple-element.141), channel_id=1, source_target_pairs={{0,1},{1,0},{2,3},{3,2},{4,5},{5,4},{6,7},{7,6},{8,9},{9,8},{10,11... | collective-permute-start | bytes 1486856 | tf_op jit(solution)/shard_map/ppermute | solution.py:19
  58.4 36.9 %collective-permute-start.24 = (bf16[352,704]{0,1:T(8,128)(2,1)}, bf16[352,704]{0,1:T(8,128)(2,1)}, u32[]{:S(2)}, u32[]{:S(2)}) collective-permute-start(bf16[352,704]{0,1:T(8,128)(2,1)} %get-tuple-element.142), channel_id=1, source_target_pairs={{0,3},{1,2},{2,1},{3,0},{4,7},{5,6},{6,5},{7,4},{8,11},{9,10},{10,... | collective-permute-start | bytes 1486856 | tf_op jit(solution)/shard_map/ppermute | solution.py:19
  59.8 85.8 %collective-permute-start.23 = (bf16[352,704]{0,1:T(8,128)(2,1)}, bf16[352,704]{0,1:T(8,128)(2,1)}, u32[]{:S(2)}, u32[]{:S(2)}) collective-permute-start(bf16[352,704]{0,1:T(8,128)(2,1)} %get-tuple-element.143), channel_id=1, source_target_pairs={{0,2},{1,3},{2,0},{3,1},{4,6},{5,7},{6,4},{7,5},{8,10},{9,11},{10,... | collective-permute-start | bytes 1486856 | tf_op jit(solution)/shard_map/ppermute | solution.py:19
  62.9 88.2 %collective-permute-start.13 = (bf16[256,704]{0,1:T(8,128)(2,1)}, bf16[256,704]{0,1:T(8,128)(2,1)}, u32[]{:S(2)}, u32[]{:S(2)}) collective-permute-start(bf16[256,704]{0,1:T(8,128)(2,1)} %copy.79), channel_id=1, source_target_pairs={{0,2},{1,3},{2,0},{3,1},{4,6},{5,7},{6,4},{7,5},{8,10},{9,11},{10,... | collective-permute-start | bytes 1081352 | tf_op jit(solution)/shard_map/ppermute | solution.py:19
  88.9 67.2 %collective-permute-start.5 = (bf16[256,704]{0,1:T(8,128)(2,1)}, bf16[256,704]{0,1:T(8,128)(2,1)S(1)}, u32[]{:S(2)}, u32[]{:S(2)}) collective-permute-start(bf16[256,704]{0,1:T(8,128)(2,1)} %copy.79), channel_id=1, source_target_pairs={{0,1},{1,0},{2,3},{3,2},{4,5},{5,4},{6,7},{7,6},{8,9},{9,8},{10,11... | collective-permute-start | bytes 1081352 | tf_op jit(solution)/shard_map/ppermute | solution.py:19
  95.3 73.6 %collective-permute-start.37 = (bf16[2,256,704]{1,2,0:T(8,128)(2,1)}, bf16[2,256,704]{1,2,0:T(8,128)(2,1)}, u32[]{:S(2)}, u32[]{:S(2)}) collective-permute-start(bf16[2,256,704]{1,2,0:T(8,128)(2,1)} %copy.88), channel_id=1, source_target_pairs={{0,8},{4,12},{8,0},{12,4},{1,9},{5,13},{9,1},{13,5},{2,10},{6,14},... | collective-permute-start | bytes 2162696 | tf_op jit(solution)/shard_map/ppermute | solution.py:19
  145.6 13.6 %collective-permute-start.40 = (bf16[256,704]{1,0:T(8,128)(2,1)}, bf16[256,704]{1,0:T(8,128)(2,1)S(1)}, u32[]{:S(2)}, u32[]{:S(2)}) collective-permute-start(bf16[256,704]{1,0:T(8,128)(2,1)} %collective-permute-done.39), channel_id=1, source_target_pairs={{0,1},{1,0},{2,3},{3,2},{4,5},{5,4},{6,7},{7,6},{8,9},{9,8},{10,11... | collective-permute-start | bytes 1081352 | tf_op jit(solution)/shard_map/ppermute | solution.py:19
  148.8 25.5 %collective-permute-start.36 = (bf16[2,256,704]{1,2,0:T(8,128)(2,1)}, bf16[2,256,704]{1,2,0:T(8,128)(2,1)}, u32[]{:S(2)}, u32[]{:S(2)}) collective-permute-start(bf16[2,256,704]{1,2,0:T(8,128)(2,1)} %copy.88), channel_id=1, source_target_pairs={{0,4},{4,0},{8,12},{12,8},{1,5},{5,1},{9,13},{13,9},{2,6},{6,2},{1... | collective-permute-start | bytes 2162696 | tf_op jit(solution)/shard_map/ppermute | solution.py:19
  151.2 15.7 %collective-permute-start.14 = (bf16[256,704]{0,1:T(8,128)(2,1)}, bf16[256,704]{0,1:T(8,128)(2,1)}, u32[]{:S(2)}, u32[]{:S(2)}) collective-permute-start(bf16[256,704]{0,1:T(8,128)(2,1)} %collective-permute-done.13), channel_id=1, source_target_pairs={{0,1},{1,0},{2,3},{3,2},{4,5},{5,4},{6,7},{7,6},{8,9},{9,8},{10,11... | collective-permute-start | bytes 1081352 | tf_op jit(solution)/shard_map/ppermute | solution.py:19
  156.1 100.3 %collective-permute-start.12 = (bf16[4,352,704]{1,2,0:T(8,128)(2,1)}, bf16[4,352,704]{1,2,0:T(8,128)(2,1)}, u32[]{:S(2)}, u32[]{:S(2)}) collective-permute-start(bf16[4,352,704]{1,2,0:T(8,128)(2,1)} %pad_maximum_fusion.5), channel_id=1, source_target_pairs={{0,16},{16,0},{1,17},{17,1},{2,18},{18,2},{3,19},{19,3},{4,20},{20... | collective-permute-start | bytes 5947400 | tf_op jit(solution)/shard_map/ppermute | solution.py:19
  159.2 20.5 %collective-permute-start.7 = (bf16[2,256,704]{1,2,0:T(8,128)(2,1)}, bf16[2,256,704]{1,2,0:T(8,128)(2,1)}, u32[]{:S(2)}, u32[]{:S(2)}) collective-permute-start(bf16[2,256,704]{1,2,0:T(8,128)(2,1)} %pad_maximum_fusion.18), channel_id=1, source_target_pairs={{0,8},{4,12},{8,0},{12,4},{1,9},{5,13},{9,1},{13,5},{2,10},{6,14},... | collective-permute-start | bytes 2162696 | tf_op jit(solution)/shard_map/ppermute | solution.py:19
  166.9 112.4 %collective-permute-start.25 = (bf16[4,352,704]{1,2,0:T(8,128)(2,1)}, bf16[4,352,704]{1,2,0:T(8,128)(2,1)}, u32[]{:S(2)}, u32[]{:S(2)}) collective-permute-start(bf16[4,352,704]{1,2,0:T(8,128)(2,1)} %pad_maximum_fusion.4), channel_id=1, source_target_pairs={{0,16},{16,0},{1,17},{17,1},{2,18},{18,2},{3,19},{19,3},{4,20},{20... | collective-permute-start | bytes 5947400 | tf_op jit(solution)/shard_map/ppermute | solution.py:19
  168.9 19.7 %collective-permute-start.6 = (bf16[2,256,704]{1,2,0:T(8,128)(2,1)}, bf16[2,256,704]{1,2,0:T(8,128)(2,1)}, u32[]{:S(2)}, u32[]{:S(2)}) collective-permute-start(bf16[2,256,704]{1,2,0:T(8,128)(2,1)} %pad_maximum_fusion.18), channel_id=1, source_target_pairs={{0,4},{4,0},{8,12},{12,8},{1,5},{5,1},{9,13},{13,9},{2,6},{6,2},{1... | collective-permute-start | bytes 2162696 | tf_op jit(solution)/shard_map/ppermute | solution.py:19
  174.3 20.8 %collective-permute-start.42 = (bf16[2,256,704]{1,2,0:T(8,128)(2,1)}, bf16[2,256,704]{1,2,0:T(8,128)(2,1)}, u32[]{:S(2)}, u32[]{:S(2)}) collective-permute-start(bf16[2,256,704]{1,2,0:T(8,128)(2,1)} %copy.96), channel_id=1, source_target_pairs={{0,8},{4,12},{8,0},{12,4},{1,9},{5,13},{9,1},{13,5},{2,10},{6,14},... | collective-permute-start | bytes 2162696 | tf_op jit(solution)/shard_map/ppermute | solution.py:19
  179.7 24.4 %collective-permute-start.41 = (bf16[2,256,704]{1,2,0:T(8,128)(2,1)}, bf16[2,256,704]{1,2,0:T(8,128)(2,1)}, u32[]{:S(2)}, u32[]{:S(2)}) collective-permute-start(bf16[2,256,704]{1,2,0:T(8,128)(2,1)} %copy.96), channel_id=1, source_target_pairs={{0,4},{4,0},{8,12},{12,8},{1,5},{5,1},{9,13},{13,9},{2,6},{6,2},{1... | collective-permute-start | bytes 2162696 | tf_op jit(solution)/shard_map/ppermute | solution.py:19
  188.6 21.4 %collective-permute-start.16 = (bf16[2,256,704]{1,2,0:T(8,128)(2,1)}, bf16[2,256,704]{1,2,0:T(8,128)(2,1)}, u32[]{:S(2)}, u32[]{:S(2)}) collective-permute-start(bf16[2,256,704]{1,2,0:T(8,128)(2,1)} %pad_maximum_fusion.19), channel_id=1, source_target_pairs={{0,8},{4,12},{8,0},{12,4},{1,9},{5,13},{9,1},{13,5},{2,10},{6,14},... | collective-permute-start | bytes 2162696 | tf_op jit(solution)/shard_map/ppermute | solution.py:19
  195.1 24.4 %collective-permute-start.15 = (bf16[2,256,704]{1,2,0:T(8,128)(2,1)}, bf16[2,256,704]{1,2,0:T(8,128)(2,1)}, u32[]{:S(2)}, u32[]{:S(2)}) collective-permute-start(bf16[2,256,704]{1,2,0:T(8,128)(2,1)} %pad_maximum_fusion.19), channel_id=1, source_target_pairs={{0,4},{4,0},{8,12},{12,8},{1,5},{5,1},{9,13},{13,9},{2,6},{6,2},{1... | collective-permute-start | bytes 2162696 | tf_op jit(solution)/shard_map/ppermute | solution.py:19
  204.0 30.9 %collective-permute-start.38 = (bf16[2,256,704]{1,2,0:T(8,128)(2,1)}, bf16[2,256,704]{1,2,0:T(8,128)(2,1)}, u32[]{:S(2)}, u32[]{:S(2)}) collective-permute-start(bf16[2,256,704]{1,2,0:T(8,128)(2,1)} %collective-permute-done.37), channel_id=1, source_target_pairs={{0,4},{4,0},{8,12},{12,8},{1,5},{5,1},{9,13},{13,9},{2,6},{6,2},{1... | collective-permute-start | bytes 2162696 | tf_op jit(solution)/shard_map/ppermute | solution.py:19
  210.0 40.2 %collective-permute-start.8 = (bf16[2,256,704]{1,2,0:T(8,128)(2,1)}, bf16[2,256,704]{1,2,0:T(8,128)(2,1)}, u32[]{:S(2)}, u32[]{:S(2)}) collective-permute-start(bf16[2,256,704]{1,2,0:T(8,128)(2,1)} %collective-permute-done.7), channel_id=1, source_target_pairs={{0,4},{4,0},{8,12},{12,8},{1,5},{5,1},{9,13},{13,9},{2,6},{6,2},{1... | collective-permute-start | bytes 2162696 | tf_op jit(solution)/shard_map/ppermute | solution.py:19
  219.5 32.7 %collective-permute-start.43 = (bf16[2,256,704]{1,2,0:T(8,128)(2,1)}, bf16[2,256,704]{1,2,0:T(8,128)(2,1)}, u32[]{:S(2)}, u32[]{:S(2)}) collective-permute-start(bf16[2,256,704]{1,2,0:T(8,128)(2,1)} %collective-permute-done.41), channel_id=1, source_target_pairs={{0,8},{4,12},{8,0},{12,4},{1,9},{5,13},{9,1},{13,5},{2,10},{6,14},... | collective-permute-start | bytes 2162696 | tf_op jit(solution)/shard_map/ppermute | solution.py:19
  234.9 20.3 %collective-permute-start.17 = (bf16[2,256,704]{1,2,0:T(8,128)(2,1)}, bf16[2,256,704]{1,2,0:T(8,128)(2,1)}, u32[]{:S(2)}, u32[]{:S(2)}) collective-permute-start(bf16[2,256,704]{1,2,0:T(8,128)(2,1)} %collective-permute-done.15), channel_id=1, source_target_pairs={{0,8},{4,12},{8,0},{12,4},{1,9},{5,13},{9,1},{13,5},{2,10},{6,14},... | collective-permute-start | bytes 2162696 | tf_op jit(solution)/shard_map/ppermute | solution.py:19
  394.0 55.9 %collective-permute-start.29 = (bf16[2,256,704]{1,2,0:T(8,128)(2,1)S(1)}, bf16[2,256,704]{1,2,0:T(8,128)(2,1)S(1)}, u32[]{:S(2)}, u32[]{:S(2)}) collective-permute-start(bf16[2,256,704]{1,2,0:T(8,128)(2,1)S(1)} %get-tuple-element.120), channel_id=1, source_target_pairs={{0,8},{4,12},{8,0},{12,4},{1,9},{5,13},{9,1},{13,5},{2,10},{6,14},... | collective-permute-start | bytes 2162696 | tf_op jit(solution)/shard_map/ppermute | solution.py:19
  396.1 32.5 %collective-permute-start.30 = (bf16[2,256,704]{1,2,0:T(8,128)(2,1)S(1)}, bf16[2,256,704]{1,2,0:T(8,128)(2,1)S(1)}, u32[]{:S(2)}, u32[]{:S(2)}) collective-permute-start(bf16[2,256,704]{1,2,0:T(8,128)(2,1)S(1)} %get-tuple-element.121), channel_id=1, source_target_pairs={{0,8},{4,12},{8,0},{12,4},{1,9},{5,13},{9,1},{13,5},{2,10},{6,14},... | collective-permute-start | bytes 2162696 | tf_op jit(solution)/shard_map/ppermute | solution.py:19
  396.5 33.5 %collective-permute-start.26 = (bf16[2,256,704]{1,2,0:T(8,128)(2,1)S(1)}, bf16[2,256,704]{1,2,0:T(8,128)(2,1)S(1)}, u32[]{:S(2)}, u32[]{:S(2)}) collective-permute-start(bf16[2,256,704]{1,2,0:T(8,128)(2,1)S(1)} %get-tuple-element.122), channel_id=1, source_target_pairs={{0,4},{4,0},{8,12},{12,8},{1,5},{5,1},{9,13},{13,9},{2,6},{6,2},{1... | collective-permute-start | bytes 2162696 | tf_op jit(solution)/shard_map/ppermute | solution.py:19
  397.8 66.8 %collective-permute-start.28 = (bf16[2,256,704]{1,2,0:T(8,128)(2,1)S(1)}, bf16[2,256,704]{1,2,0:T(8,128)(2,1)S(1)}, u32[]{:S(2)}, u32[]{:S(2)}) collective-permute-start(bf16[2,256,704]{1,2,0:T(8,128)(2,1)S(1)} %get-tuple-element.123), channel_id=1, source_target_pairs={{0,4},{4,0},{8,12},{12,8},{1,5},{5,1},{9,13},{13,9},{2,6},{6,2},{1... | collective-permute-start | bytes 2162696 | tf_op jit(solution)/shard_map/ppermute | solution.py:19
  399.0 42.3 %collective-permute-start.48 = (bf16[2,256,704]{1,2,0:T(8,128)(2,1)S(1)}, bf16[2,256,704]{1,2,0:T(8,128)(2,1)S(1)}, u32[]{:S(2)}, u32[]{:S(2)}) collective-permute-start(bf16[2,256,704]{1,2,0:T(8,128)(2,1)S(1)} %get-tuple-element.115), channel_id=1, source_target_pairs={{0,8},{4,12},{8,0},{12,4},{1,9},{5,13},{9,1},{13,5},{2,10},{6,14},... | collective-permute-start | bytes 2162696 | tf_op jit(solution)/shard_map/ppermute | solution.py:19
  428.6 19.1 %collective-permute-start.44 = (bf16[2,256,704]{1,2,0:T(8,128)(2,1)S(1)}, bf16[2,256,704]{1,2,0:T(8,128)(2,1)S(1)}, u32[]{:S(2)}, u32[]{:S(2)}) collective-permute-start(bf16[2,256,704]{1,2,0:T(8,128)(2,1)S(1)} %get-tuple-element.116), channel_id=1, source_target_pairs={{0,4},{4,0},{8,12},{12,8},{1,5},{5,1},{9,13},{13,9},{2,6},{6,2},{1... | collective-permute-start | bytes 2162696 | tf_op jit(solution)/shard_map/ppermute | solution.py:19
  430.0 33.1 %collective-permute-start.31 = (bf16[2,256,704]{1,2,0:T(8,128)(2,1)S(1)}, bf16[2,256,704]{1,2,0:T(8,128)(2,1)S(1)}, u32[]{:S(2)}, u32[]{:S(2)}) collective-permute-start(bf16[2,256,704]{1,2,0:T(8,128)(2,1)S(1)} %fusion.22), channel_id=1, source_target_pairs={{0,4},{4,0},{8,12},{12,8},{1,5},{5,1},{9,13},{13,9},{2,6},{6,2},{1... | collective-permute-start | bytes 2162696 | tf_op jit(solution)/shard_map/ppermute | solution.py:19
  441.3 23.5 %collective-permute-start.27 = (bf16[2,256,704]{1,2,0:T(8,128)(2,1)S(1)}, bf16[2,256,704]{1,2,0:T(8,128)(2,1)S(1)}, u32[]{:S(2)}, u32[]{:S(2)}) collective-permute-start(bf16[2,256,704]{1,2,0:T(8,128)(2,1)S(1)} %fusion.25), channel_id=1, source_target_pairs={{0,8},{4,12},{8,0},{12,4},{1,9},{5,13},{9,1},{13,5},{2,10},{6,14},... | collective-permute-start | bytes 2162696 | tf_op jit(solution)/shard_map/ppermute | solution.py:19
  447.7 22.3 %collective-permute-start.47 = (bf16[2,256,704]{1,2,0:T(8,128)(2,1)S(1)}, bf16[2,256,704]{1,2,0:T(8,128)(2,1)S(1)}, u32[]{:S(2)}, u32[]{:S(2)}) collective-permute-start(bf16[2,256,704]{1,2,0:T(8,128)(2,1)S(1)} %get-tuple-element.114), channel_id=1, source_target_pairs={{0,8},{4,12},{8,0},{12,4},{1,9},{5,13},{9,1},{13,5},{2,10},{6,14},... | collective-permute-start | bytes 2162696 | tf_op jit(solution)/shard_map/ppermute | solution.py:19
  449.9 38.5 %collective-permute-start.46 = (bf16[2,256,704]{1,2,0:T(8,128)(2,1)S(1)}, bf16[2,256,704]{1,2,0:T(8,128)(2,1)S(1)}, u32[]{:S(2)}, u32[]{:S(2)}) collective-permute-start(bf16[2,256,704]{1,2,0:T(8,128)(2,1)S(1)} %get-tuple-element.117), channel_id=1, source_target_pairs={{0,4},{4,0},{8,12},{12,8},{1,5},{5,1},{9,13},{13,9},{2,6},{6,2},{1... | collective-permute-start | bytes 2162696 | tf_op jit(solution)/shard_map/ppermute | solution.py:19
  463.1 23.9 %collective-permute-start.49 = (bf16[2,256,704]{1,2,0:T(8,128)(2,1)S(1)}, bf16[2,256,704]{1,2,0:T(8,128)(2,1)S(1)}, u32[]{:S(2)}, u32[]{:S(2)}) collective-permute-start(bf16[2,256,704]{1,2,0:T(8,128)(2,1)S(1)} %fusion.16), channel_id=1, source_target_pairs={{0,4},{4,0},{8,12},{12,8},{1,5},{5,1},{9,13},{13,9},{2,6},{6,2},{1... | collective-permute-start | bytes 2162696 | tf_op jit(solution)/shard_map/ppermute | solution.py:19
  464.6 52.8 %collective-permute-start.58 = (bf16[4,352,704]{1,2,0:T(8,128)(2,1)S(1)}, bf16[4,352,704]{1,2,0:T(8,128)(2,1)S(1)}, u32[]{:S(2)}, u32[]{:S(2)}) collective-permute-start(bf16[4,352,704]{1,2,0:T(8,128)(2,1)S(1)} %slice.1196), channel_id=1, source_target_pairs={{0,16},{16,0},{1,17},{17,1},{2,18},{18,2},{3,19},{19,3},{4,20},{20... | collective-permute-start | bytes 5947400 | tf_op jit(solution)/shard_map/ppermute | solution.py:19
  464.7 57.6 %collective-permute-start.62 = (bf16[4,352,704]{1,2,0:T(8,128)(2,1)S(1)}, bf16[4,352,704]{1,2,0:T(8,128)(2,1)S(1)}, u32[]{:S(2)}, u32[]{:S(2)}) collective-permute-start(bf16[4,352,704]{1,2,0:T(8,128)(2,1)S(1)} %slice.1202), channel_id=1, source_target_pairs={{0,16},{16,0},{1,17},{17,1},{2,18},{18,2},{3,19},{19,3},{4,20},{20... | collective-permute-start | bytes 5947400 | tf_op jit(solution)/shard_map/ppermute | solution.py:19
  469.9 20.2 %collective-permute-start.45 = (bf16[2,256,704]{1,2,0:T(8,128)(2,1)S(1)}, bf16[2,256,704]{1,2,0:T(8,128)(2,1)S(1)}, u32[]{:S(2)}, u32[]{:S(2)}) collective-permute-start(bf16[2,256,704]{1,2,0:T(8,128)(2,1)S(1)} %fusion.19), channel_id=1, source_target_pairs={{0,8},{4,12},{8,0},{12,4},{1,9},{5,13},{9,1},{13,5},{2,10},{6,14},... | collective-permute-start | bytes 2162696 | tf_op jit(solution)/shard_map/ppermute | solution.py:19
  487.0 11.3 %collective-permute-start.32 = (bf16[256,704]{0,1:T(8,128)(2,1)S(1)}, bf16[256,704]{0,1:T(8,128)(2,1)S(1)}, u32[]{:S(2)}, u32[]{:S(2)}) collective-permute-start(bf16[256,704]{0,1:T(8,128)(2,1)S(1)} %slice_bitcast_fusion.51), channel_id=1, source_target_pairs={{0,1},{1,0},{2,3},{3,2},{4,5},{5,4},{6,7},{7,6},{8,9},{9,8},{10,11... | collective-permute-start | bytes 1081352 | tf_op jit(solution)/shard_map/ppermute | solution.py:19
  488.4 82.1 %collective-permute-start.34 = (bf16[256,704]{0,1:T(8,128)(2,1)}, bf16[256,704]{0,1:T(8,128)(2,1)}, u32[]{:S(2)}, u32[]{:S(2)}) collective-permute-start(bf16[256,704]{0,1:T(8,128)(2,1)} %slice_bitcast_fusion.50), channel_id=1, source_target_pairs={{0,1},{1,0},{2,3},{3,2},{4,5},{5,4},{6,7},{7,6},{8,9},{9,8},{10,11... | collective-permute-start | bytes 1081352 | tf_op jit(solution)/shard_map/ppermute | solution.py:19
  490.2 27.2 %collective-permute-start.50 = (bf16[256,704]{0,1:T(8,128)(2,1)S(1)}, bf16[256,704]{0,1:T(8,128)(2,1)S(1)}, u32[]{:S(2)}, u32[]{:S(2)}) collective-permute-start(bf16[256,704]{0,1:T(8,128)(2,1)S(1)} %slice_bitcast_fusion.47), channel_id=1, source_target_pairs={{0,1},{1,0},{2,3},{3,2},{4,5},{5,4},{6,7},{7,6},{8,9},{9,8},{10,11... | collective-permute-start | bytes 1081352 | tf_op jit(solution)/shard_map/ppermute | solution.py:19
  498.3 24.5 %collective-permute-start.52 = (bf16[256,704]{0,1:T(8,128)(2,1)S(1)}, bf16[256,704]{0,1:T(8,128)(2,1)S(1)}, u32[]{:S(2)}, u32[]{:S(2)}) collective-permute-start(bf16[256,704]{0,1:T(8,128)(2,1)S(1)} %slice_bitcast_fusion.46), channel_id=1, source_target_pairs={{0,1},{1,0},{2,3},{3,2},{4,5},{5,4},{6,7},{7,6},{8,9},{9,8},{10,11... | collective-permute-start | bytes 1081352 | tf_op jit(solution)/shard_map/ppermute | solution.py:19
  517.4 53.1 %collective-permute-start.33 = (bf16[256,704]{0,1:T(8,128)(2,1)}, bf16[256,704]{0,1:T(8,128)(2,1)}, u32[]{:S(2)}, u32[]{:S(2)}) collective-permute-start(bf16[256,704]{0,1:T(8,128)(2,1)} %fusion.142), channel_id=1, source_target_pairs={{0,2},{1,3},{2,0},{3,1},{4,6},{5,7},{6,4},{7,5},{8,10},{9,11},{10,... | collective-permute-start | bytes 1081352 | tf_op jit(solution)/shard_map/ppermute | solution.py:19
  517.5 33.9 %collective-permute-start.51 = (bf16[256,704]{0,1:T(8,128)(2,1)S(1)}, bf16[256,704]{0,1:T(8,128)(2,1)S(1)}, u32[]{:S(2)}, u32[]{:S(2)}) collective-permute-start(bf16[256,704]{0,1:T(8,128)(2,1)S(1)} %fusion.140), channel_id=1, source_target_pairs={{0,2},{1,3},{2,0},{3,1},{4,6},{5,7},{6,4},{7,5},{8,10},{9,11},{10,... | collective-permute-start | bytes 1081352 | tf_op jit(solution)/shard_map/ppermute | solution.py:19
  556.4 5.0 collective-permute-start.54
  556.4 6.9 %collective-permute-start.55 = (f32[2,4,2,32]{3,2,1,0:T(2,128)S(1)}, f32[2,4,2,32]{3,2,1,0:T(2,128)S(1)}, u32[]{:S(2)}, u32[]{:S(2)}) collective-permute-start(f32[2,4,2,32]{3,2,1,0:T(2,128)S(1)} %pad_maximum_fusion.37), channel_id=1, source_target_pairs={{0,3},{1,2},{2,1},{3,0},{4,7},{5,6},{6,5},{7,4},{8,11},{9,10},{10,... | collective-permute-start | bytes 6152 | tf_op jit(solution)/shard_map/ppermute | solution.py:19
  558.6 4.9 collective-permute-start.53
  561.3 43.1 %collective-permute-start.61 = (bf16[352,704]{0,1:T(8,128)(2,1)}, bf16[352,704]{0,1:T(8,128)(2,1)}, u32[]{:S(2)}, u32[]{:S(2)}) collective-permute-start(bf16[352,704]{0,1:T(8,128)(2,1)} %get-tuple-element.137), channel_id=1, source_target_pairs={{0,3},{1,2},{2,1},{3,0},{4,7},{5,6},{6,5},{7,4},{8,11},{9,10},{10,... | collective-permute-start | bytes 1486856 | tf_op jit(solution)/shard_map/ppermute | solution.py:19
  563.4 41.1 %collective-permute-start.60 = (bf16[352,704]{0,1:T(8,128)(2,1)}, bf16[352,704]{0,1:T(8,128)(2,1)}, u32[]{:S(2)}, u32[]{:S(2)}) collective-permute-start(bf16[352,704]{0,1:T(8,128)(2,1)} %get-tuple-element.138), channel_id=1, source_target_pairs={{0,2},{1,3},{2,0},{3,1},{4,6},{5,7},{6,4},{7,5},{8,10},{9,11},{10,... | collective-permute-start | bytes 1486856 | tf_op jit(solution)/shard_map/ppermute | solution.py:19
  572.9 5.7 collective-permute-start.67
  574.7 16.3 %collective-permute-start.56 = (bf16[3,2,32,704]{3,2,1,0:T(8,128)(2,1)S(1)}, bf16[3,2,32,704]{3,2,1,0:T(8,128)(2,1)S(1)}, u32[]{:S(2)}, u32[]{:S(2)}) collective-permute-start(bf16[3,2,32,704]{3,2,1,0:T(8,128)(2,1)S(1)} %get-tuple-element.173), channel_id=1, source_target_pairs={{0,4},{4,8},{8,12},{1,5},{5,9},{9,13},{2,6},{6,10},{10,14},{3,7},{... | collective-permute-start | bytes 811016 | tf_op jit(solution)/shard_map/ppermute | solution.py:123
  577.4 15.9 %collective-permute-start.57 = (bf16[3,2,32,704]{3,2,1,0:T(8,128)(2,1)S(1)}, bf16[3,2,32,704]{3,2,1,0:T(8,128)(2,1)S(1)}, u32[]{:S(2)}, u32[]{:S(2)}) collective-permute-start(bf16[3,2,32,704]{3,2,1,0:T(8,128)(2,1)S(1)} %get-tuple-element.174), channel_id=1, source_target_pairs={{4,0},{8,4},{12,8},{5,1},{9,5},{13,9},{6,2},{10,6},{14,10},{7,3},{... | collective-permute-start | bytes 811016 | tf_op jit(solution)/shard_map/ppermute | solution.py:124
  578.7 9.1 %collective-permute-start.68 = (bf16[7,7,704]{2,1,0:T(8,128)(2,1)S(1)}, bf16[7,7,704]{2,1,0:T(8,128)(2,1)S(1)}, u32[]{:S(2)}, u32[]{:S(2)}) collective-permute-start(bf16[7,7,704]{2,1,0:T(8,128)(2,1)S(1)} %add_convert_fusion.4), channel_id=1, source_target_pairs={{0,8},{4,12},{8,0},{12,4},{1,9},{5,13},{9,1},{13,5},{2,10},{6,14},... | collective-permute-start | bytes 206984 | tf_op jit(solution)/shard_map/ppermute | solution.py:19
  587.8 16.8 %collective-permute-start.59 = (bf16[352,704]{0,1:T(8,128)(2,1)S(1)}, bf16[352,704]{0,1:T(8,128)(2,1)S(1)}, u32[]{:S(2)}, u32[]{:S(2)}) collective-permute-start(bf16[352,704]{0,1:T(8,128)(2,1)S(1)} %copy-done.38), channel_id=1, source_target_pairs={{0,1},{1,0},{2,3},{3,2},{4,5},{5,4},{6,7},{7,6},{8,9},{9,8},{10,11... | collective-permute-start | bytes 1486856 | tf_op jit(solution)/shard_map/ppermute | solution.py:19
  591.0 26.0 %collective-permute-start.65 = (bf16[352,704]{0,1:T(8,128)(2,1)}, bf16[352,704]{0,1:T(8,128)(2,1)}, u32[]{:S(2)}, u32[]{:S(2)}) collective-permute-start(bf16[352,704]{0,1:T(8,128)(2,1)} %get-tuple-element.129), channel_id=1, source_target_pairs={{0,3},{1,2},{2,1},{3,0},{4,7},{5,6},{6,5},{7,4},{8,11},{9,10},{10,... | collective-permute-start | bytes 1486856 | tf_op jit(solution)/shard_map/ppermute | solution.py:19
  593.3 46.4 %collective-permute-start.64 = (bf16[352,704]{0,1:T(8,128)(2,1)}, bf16[352,704]{0,1:T(8,128)(2,1)}, u32[]{:S(2)}, u32[]{:S(2)}) collective-permute-start(bf16[352,704]{0,1:T(8,128)(2,1)} %get-tuple-element.130), channel_id=1, source_target_pairs={{0,2},{1,3},{2,0},{3,1},{4,6},{5,7},{6,4},{7,5},{8,10},{9,11},{10,... | collective-permute-start | bytes 1486856 | tf_op jit(solution)/shard_map/ppermute | solution.py:19
  604.4 35.3 %collective-permute-start.63 = (bf16[352,704]{0,1:T(8,128)(2,1)}, bf16[352,704]{0,1:T(8,128)(2,1)}, u32[]{:S(2)}, u32[]{:S(2)}) collective-permute-start(bf16[352,704]{0,1:T(8,128)(2,1)} %get-tuple-element.131), channel_id=1, source_target_pairs={{0,1},{1,0},{2,3},{3,2},{4,5},{5,4},{6,7},{7,6},{8,9},{9,8},{10,11... | collective-permute-start | bytes 1486856 | tf_op jit(solution)/shard_map/ppermute | solution.py:19
  (176 other events, 2002.4 us)

commit v2 on v1

v2 whole, which is shorter than its diff:
```python
import math

import jax
import jax.numpy as jnp
from jax import lax
from jax.experimental import pallas as pl
from jax.experimental.pallas import tpu as pltpu
from jax.sharding import PartitionSpec as P

epsilon = 1e-06
root_half = 0.7071067811865476
inv_root_tau = 0.3989422804014327
last_last = (((1,), (1,)), ((), ()))
first_first = (((0,), (0,)), ((), ()))
f32 = jnp.float32
bf16 = jnp.bfloat16


def swap(block, axis, bits):
    count = lax.axis_size(axis)
    return lax.ppermute(block, axis, [(i, i ^ bits) for i in range(count)])


def low_bit(m):
    return m & -m


def high_bit(m):
    return 1 << (m.bit_length() - 1)


def gather(block, axis, bit):
    held = [block]
    for m in range(1, lax.axis_size(axis)):
        step = bit(m)
        held.append(swap(held[m ^ step], axis, step))
    return held


def scatter_sum(parts, axis, bit):
    parts = list(parts)
    for m in range(lax.axis_size(axis) - 1, 0, -1):
        step = bit(m)
        got = swap(parts[m].astype(bf16), axis, step)
        parts[m ^ step] = parts[m ^ step].astype(f32) + got.astype(f32)
    return parts[0]


def gather_cols(block):
    cols = gather(block, "col", low_bit)
    half = len(cols) // 2
    return jnp.stack(cols[:half]), jnp.stack(cols[half:])


def gather_pixels(block):
    lower, upper = gather_cols(block)
    return gather(lower, "row", low_bit) + gather(upper, "row", high_bit)


def scatter_pixels(pieces):
    rows = lax.axis_size("row")
    done = [
        scatter_sum(pieces[:rows], "row", low_bit),
        scatter_sum(pieces[rows:], "row", high_bit),
    ]
    parts = [d[m].astype(bf16) for d in done for m in range(d.shape[0])]
    return scatter_sum(parts, "col", low_bit)


VMEM_BYTES = 44 * 2**20
in_vmem = pl.BlockSpec(memory_space=pltpu.VMEM)
in_smem = pl.BlockSpec(memory_space=pltpu.SMEM)


def call(body, outs, places, *operands, flops=0):
    moved = sum(math.prod(o.shape) * o.dtype.itemsize for o in list(operands) + list(outs))
    return pl.pallas_call(
        body,
        out_shape=outs,
        in_specs=[in_smem] + [in_vmem] * len(operands),
        out_specs=[in_vmem] * len(outs),
        compiler_params=pltpu.CompilerParams(vmem_limit_bytes=VMEM_BYTES),
        cost_estimate=pl.CostEstimate(flops=flops, bytes_accessed=moved, transcendentals=0),
    )(places, *operands)


def shape_of(dims, dtype):
    return jax.ShapeDtypeStruct(dims, dtype)


def piece_of(refs, places, rows, q, m):
    if len(refs) == 1:
        return refs[0][places[0] ^ q, m]
    half = refs[0].shape[0]
    return refs[q][m] if m < half else refs[rows + q][m - half]


def join_weights(places, mine, other):
    count, share, chans = mine.shape

    def body(places, mine, other, out):
        for m in range(count):
            out[m, :share, :] = mine[places[1] ^ m]
            out[m, share:, :] = other[places[1] ^ m]

    if share % 16:
        order = places[1] ^ jnp.arange(count)
        return jnp.concatenate([mine[order], other[order]], axis=1)
    return call(body, [shape_of((count, 2 * share, chans), bf16)], places, mine, other)[0]


def whole_weights(rows, places):
    count = lax.axis_size("col")
    mine = lax.all_to_all(rows.reshape(count, -1, rows.shape[1]), "col", 0, 0)
    return join_weights(places, mine, swap(mine, "dp", 1))


def hidden_kernel(places, pieces, weights, bias, dims):
    rows, height, batch, width = dims
    count, units, chans = weights.shape
    pixels = height * batch * width

    def body(places, *refs):
        xs = refs[: len(pieces)]
        w, b, act, slope, square = refs[len(pieces) :]
        total = jnp.zeros((batch, units), f32)
        for q in range(rows):
            pre = b[...]
            for m in range(count):
                pre = pre + lax.dot_general(
                    piece_of(xs, places, rows, q, m), w[m], last_last, preferred_element_type=f32
                )
            cumul = 0.5 * (1.0 + lax.erf(pre * root_half))
            value = pre * cumul
            act[q * pixels : (q + 1) * pixels, :] = value
            slope[q * pixels : (q + 1) * pixels, :] = cumul + pre * jnp.exp(-0.5 * pre * pre) * inv_root_tau
            total = total + jnp.sum((value * value).reshape(height, batch, width, units), axis=(0, 2))
        square[...] = total

    full = (rows * pixels, units)
    return call(
        body,
        [shape_of(full, f32), shape_of(full, f32), shape_of((batch, units), f32)],
        places,
        *pieces,
        weights,
        bias[None],
        flops=2 * rows * pixels * units * chans * count,
    )


def back_kernel(places, pieces, weights, act, dims):
    rows, height, batch, width = dims
    count, units, chans = weights.shape
    pixels = height * batch * width

    def body(places, *refs):
        xs = refs[: len(pieces)]
        w, act, grad, pull = refs[len(pieces) :]
        total = jnp.zeros((batch, units), f32)
        for q in range(rows):
            value = jnp.zeros((pixels, units), f32)
            for m in range(count):
                value = value + lax.dot_general(
                    piece_of(xs, places, rows, q, m), w[m], last_last, preferred_element_type=f32
                )
            grad[q * pixels : (q + 1) * pixels, :] = value
            both = value * act[q * pixels : (q + 1) * pixels, :]
            total = total + jnp.sum(both.reshape(height, batch, width, units), axis=(0, 2))
        pull[...] = total

    return call(
        body,
        [shape_of(act.shape, f32), shape_of((batch, units), f32)],
        places,
        *pieces,
        weights,
        act,
        flops=2 * rows * pixels * units * chans * count,
    )


def project_kernel(places, rows_of, operands, weights, dims, together):
    rows, height, batch, width = dims
    count, units, chans = weights.shape
    pixels = height * batch * width
    half = count // 2

    def body(places, *refs):
        ins = refs[: len(operands)]
        w, kept = refs[len(operands) : len(operands) + 2]
        outs = refs[len(operands) + 2 :]

        def spread(vector):
            wide = jnp.broadcast_to(vector[None, :, None, :], (height, batch, width, units))
            return wide.reshape(pixels, units)

        for q in range(rows):
            part = slice(q * pixels, (q + 1) * pixels)
            blocks = [r[part, :] if r.shape[0] == rows * pixels else r[...] for r in ins]
            made = rows_of(blocks, spread).astype(bf16)
            kept[part, :] = made
            for m in range(count):
                value = jnp.dot(made, w[m], preferred_element_type=f32).astype(bf16)
                if together:
                    outs[0][places[0] ^ q, m] = value
                elif m < half:
                    outs[q][m] = value
                else:
                    outs[rows + q][m - half] = value

    if together:
        outs = [shape_of((rows, count, pixels, chans), bf16)]
    else:
        outs = [shape_of((half, pixels, chans), bf16)] * (2 * rows)
    got = call(
        body,
        [shape_of((rows * pixels, units), bf16)] + outs,
        places,
        *operands,
        weights,
        flops=2 * rows * pixels * units * chans * count,
    )
    return got[0], got[1:]


def grads_kernel(places, left, pieces, dims, count, chans):
    rows, height, batch, width = dims
    units = left.shape[1]
    share = units // 2

    def body(places, left, *refs):
        xs = refs[: len(pieces)]
        mine, other = refs[len(pieces) :]
        turned = left[...].T
        for m in range(count):
            x = jnp.concatenate([piece_of(xs, places, rows, q, m) for q in range(rows)], axis=0)
            value = jnp.dot(turned, x, preferred_element_type=f32)
            mine[places[1] ^ m] = value[:share].astype(bf16)
            other[places[1] ^ m] = value[share:].astype(bf16)

    return call(
        body,
        [shape_of((count, share, chans), bf16)] * 2,
        places,
        left,
        *pieces,
        flops=2 * left.shape[0] * units * chans * count,
    )


def whole_grads(mine, other):
    total = (mine.astype(f32) + swap(other, "dp", 1).astype(f32)).astype(bf16)
    return lax.all_to_all(total, "col", 0, 0).reshape(-1, mine.shape[-1])


def own_units(vector):
    count = lax.axis_size("col")
    span = vector.shape[0] // 2
    share = span // count
    me = lax.axis_index("col")
    side = lax.axis_index("dp")
    mine = lax.dynamic_slice_in_dim(vector, side * span + me * share, share)
    other = lax.dynamic_slice_in_dim(vector, (1 - side) * span + me * share, share)
    return jnp.concatenate([mine, other])


def add_over(value, axis):
    n = lax.axis_size(axis)
    step = 1
    while step < n:
        value = value + swap(value, axis, step)
        step *= 2
    return value


def extended(block, width):
    count = lax.axis_size("row")
    forward = [(i, i + 1) for i in range(count - 1)]
    backward = [(i + 1, i) for i in range(count - 1)]
    low = lax.ppermute(block[block.shape[0] - width :], "row", forward)
    high = lax.ppermute(block[:width], "row", backward)
    return jnp.concatenate([low, block, high], axis=0)


def depthwise(padded, kernel, height, width):
    span = kernel.shape[0]
    result = jnp.zeros((height, padded.shape[1], width, padded.shape[3]), f32)
    for row_off in range(span):
        for col_off in range(span):
            window = padded[row_off : row_off + height, :, col_off : col_off + width, :]
            result = result + kernel[row_off, col_off] * window
    return result


def pad_width(tile_in, reach):
    return jnp.pad(tile_in, ((0, 0), (0, 0), (reach, reach), (0, 0)))


def local(images, cotangent, kernel, w_in, b_in, grn_gamma, grn_beta, w_out):
    height, batch, width, chans = images.shape
    span = kernel.shape[0]
    reach = span // 2
    col_count = lax.axis_size("col")
    row_count = lax.axis_size("row")
    all_chans = chans * col_count
    all_units = b_in.shape[0] * row_count
    pixels = height * batch * width
    group_pix = pixels * row_count
    scale_grad = 1.0 / math.sqrt(group_pix * lax.axis_size("dp"))

    places = jnp.stack([lax.axis_index("row"), lax.axis_index("col")]).astype(jnp.int32)
    dims = (row_count, height, batch, width)

    halo_x = extended(images, reach)
    w_in_all = whole_weights(w_in.T, places)
    cot_cols = jnp.concatenate(gather_cols(cotangent.reshape(pixels, chans)))
    cot_all = [lax.all_gather(cot_cols, "row")]
    w_out_all = whole_weights(w_out, places)
    bias, gamma, beta = own_units(b_in), own_units(grn_gamma), own_units(grn_beta)

    padded_x = pad_width(halo_x, reach).astype(f32)
    conv_out = depthwise(padded_x, kernel, height, width)
    mean_own = jnp.mean(conv_out, axis=-1)
    dev_own = conv_out - mean_own[..., None]
    stats = jnp.stack([mean_own, jnp.sum(dev_own * dev_own, axis=-1)])
    stats = [stats] + [swap(stats, "col", m) for m in range(1, col_count)]
    mean_pix = sum(s[0] for s in stats) / col_count
    var_pix = sum(s[1] + chans * (s[0] - mean_pix) ** 2 for s in stats) / all_chans
    inv_std = lax.rsqrt(var_pix + epsilon)[..., None]
    standard = (conv_out - mean_pix[..., None]) * inv_std
    normed_all = gather_pixels(standard.astype(bf16).reshape(pixels, chans))

    act, slope, square = hidden_kernel(places, normed_all, w_in_all, bias, dims)
    norm_chan = jnp.sqrt(square + epsilon)
    norm_sum = add_over(add_over(jnp.sum(norm_chan, axis=-1), "row"), "col")
    denom = (norm_sum / all_units + epsilon)[:, None]
    gain = gamma * (norm_chan / denom) + 1.0
    grad_gated, pull = back_kernel(places, cot_all, w_out_all, act, dims)
    share_back = gamma * pull / denom / norm_chan

    grad_pre, grad_parts = project_kernel(
        places,
        lambda b, spread: (b[0] * spread(b[3]) + b[1] * spread(b[4])) * b[2],
        [grad_gated, act, slope, gain, share_back],
        w_in_all,
        dims,
        False,
    )
    gated, out_parts = project_kernel(
        places,
        lambda b, spread: b[0] * spread(b[1]) + b[2],
        [act, gain, beta[None]],
        w_out_all,
        dims,
        True,
    )
    w_in_mine, w_in_other = grads_kernel(places, grad_pre, normed_all, dims, col_count, chans)
    w_out_mine, w_out_other = grads_kernel(places, gated, cot_all, dims, col_count, chans)
    w_in_grad = whole_grads(w_in_mine, w_in_other).T.astype(f32) * scale_grad
    w_out_grad = whole_grads(w_out_mine, w_out_other).astype(f32) * scale_grad

    grad_normed = scatter_pixels(grad_parts).reshape(conv_out.shape)
    branch_rows = lax.psum_scatter(
        out_parts[0].reshape(-1, chans), "row", scatter_dimension=0, tiled=True
    ).reshape(col_count, pixels, chans)
    branch = scatter_sum([branch_rows[m] for m in range(col_count)], "col", low_bit)
    result = (images.astype(f32) + branch.reshape(images.shape).astype(f32)).astype(bf16)

    sums = jnp.stack([jnp.sum(grad_normed, axis=-1), jnp.sum(grad_normed * standard, axis=-1)])
    sums = sum([swap(sums, "col", m) for m in range(1, col_count)], sums) / all_chans
    grad_conv = inv_std * (grad_normed - sums[0][..., None] - standard * sums[1][..., None])
    halo_cot = extended(grad_conv.astype(bf16), reach).astype(f32)
    spread = depthwise(pad_width(halo_cot, reach), kernel[::-1, ::-1], height, width)
    x_grad = (cotangent.astype(f32) + spread).astype(bf16)
    kern_terms = []
    for row_off in range(span):
        for col_off in range(span):
            window = padded_x[row_off : row_off + height, :, col_off : col_off + width, :]
            kern_terms.append(jnp.sum(grad_conv * window, axis=(0, 1, 2)))
    kern = jnp.stack(kern_terms).reshape(span, span, chans)
    steps = [("dp", 1)] + [("row", 1 << i) for i in range((row_count - 1).bit_length())]
    for axis, step in steps:
        kern = kern.astype(bf16)
        kern = kern.astype(f32) + swap(kern, axis, step).astype(f32)
    kernel_grad = kern * scale_grad
    return (result, x_grad, w_in_grad, w_out_grad, kernel_grad)


def solution(mesh):
    return jax.shard_map(
        local,
        mesh=mesh,
        in_specs=(
            P("row", "dp", None, "col"),
            P("row", "dp", None, "col"),
            P(None, None, "col"),
            P("col", ("row", "dp")),
            P("row"),
            P("row"),
            P("row"),
            P(("row", "dp"), "col"),
        ),
        out_specs=(
            P("row", "dp", None, "col"),
            P("row", "dp", None, "col"),
            P("col", ("row", "dp")),
            P(("row", "dp"), "col"),
            P(None, None, "col"),
        ),
        check_vma=False,
    )
```

time: 654 us -> 577 us (0.88)
  Pallas kernels: 0 us -> 57.8 us
  matrix products: 56.8 us -> 0 us
  starting transfers between devices: 126 us -> 73.3 us
  local copies, waits for them, and re-layouts: 126 us -> 100 us
  waiting for transfers between devices: 261 us -> 245 us
  between operations: 4.4 us -> 15.7 us
    ppermute x65 -> x41, starting transfers between devices: 118 us -> 46.1 us  [swap(): return lax.ppermute(block, axis, [(i, i ^ bits) for i in range(count)])]
    ppermute x65 -> x41, waiting for transfers between devices: 261 us -> 197 us  [swap(): return lax.ppermute(block, axis, [(i, i ^ bits) for i in range(count)])]
    pallas_call x0 -> x8, Pallas kernels: none -> 57.8 us  [call(): pl.pallas_call(body, out_shape=outs, in_specs=[in_smem] + [in_vmem] * len...]
    dot_general x24 -> x0, matrix products: 56.8 us -> none  [the longest x4 15.4 us: local(): lax.dot_general(x, w, last_last, preferred_element_type=f32)]
    another operation x18 -> x2, local copies, waits for them, and re-layouts: 41.3 us -> 3.4 us  [gather_cols(): return (jnp.stack(cols[:half]), jnp.stack(cols[half:]))]
    ppermute x0 -> x12, local copies, waits for them, and re-layouts: none -> 26.4 us  [swap(): return lax.ppermute(block, axis, [(i, i ^ bits) for i in range(count)])]
    ppermute x2, waiting for transfers between devices: 0.53 us -> 22.9 us  [extended(): high = lax.ppermute(block[:width], 'row', backward)]
    all_to_all x0 -> x4, starting transfers between devices: none -> 18.4 us  [the longest x2 10.1 us: whole_weights(): mine = lax.all_to_all(rows.reshape(count, -1, rows.shape[1]), 'col', 0, 0)]
  transfers between devices with their start and end apart: 69 -> 51, of which waited for: 31 -> 27; matrix products, arithmetic and copies ran while one was open for 23% -> 24% of each run, Pallas kernels for 0% -> 7%
where the time goes in v2:
time: 577 us; the launch traced here: 569 us
  waiting for transfers between devices  245 us (42%)
  local copies, waits for them, and re-layouts  100 us (17%)
  other arithmetic  76.9 us (13%)
  starting transfers between devices  73.3 us (13%)
  Pallas kernels  57.8 us (10%)
  between operations  15.7 us (3%)
    ppermute x41, waiting for transfers between devices, swap(): return lax.ppermute(block, axis, [(i, i ^ bits) for i in range(count)])  197 us
    pallas_call x8, Pallas kernels, call(): pl.pallas_call(body, out_shape=outs, in_specs=[in_smem] + [in_vmem] * len...  57.8 us
    ppermute x41, starting transfers between devices, swap(): return lax.ppermute(block, axis, [(i, i ^ bits) for i in range(count)])  46.1 us
    unnamed x102, local copies, waits for them, and re-layouts  33.8 us
    ppermute x12, local copies, waits for them, and re-layouts, swap(): return lax.ppermute(block, axis, [(i, i ^ bits) for i in range(count)])  26.4 us
    reduce_sum x1, other arithmetic, local(): mean_own = jnp.mean(conv_out, axis=-1)  25.4 us
    ppermute x2, waiting for transfers between devices, extended(): high = lax.ppermute(block[:width], 'row', backward)  22.9 us
    all_to_all x2, waiting for transfers between devices, whole_weights(): mine = lax.all_to_all(rows.reshape(count, -1, rows.shape[1]), 'col', 0, 0)  14.2 us
  transfers between devices with their start and end apart: 51, of which 27 were waited for; matrix products, arithmetic and copies ran while one was open for 24% of the time, Pallas kernels for 7%

profile of v2, /device:TPU:0, one launch (start us, length us, event | category | flops | bytes accessed | tf_op | source)
XLA Modules:
  0.0 568.6 jit_solution(15625581366254278612)
XLA Ops:
  7.2 4.1 collective-permute-start.24
  12.9 16.3 %collective-permute-done.24 = bf16[256,704]{1,0:T(8,128)(2,1)S(1)} collective-permute-done((bf16[256,704]{1,0:T(8,128)(2,1)}, bf16[256,704]{1,0:T(8,128)(2,1)S(1)}, u32[]{:S(2)}, u32[]{:S(2)}) %collective-permute-start.24) | collective-permute-done | bytes 360480 | tf_op jit(solution)/shard_map/ppermute | solution.py:21
  29.9 9.5 %collective-permute-done.25 = bf16[256,704]{1,0:T(8,128)(2,1)S(1)} collective-permute-done((bf16[256,704]{1,0:T(8,128)(2,1)S(1)}, bf16[256,704]{1,0:T(8,128)(2,1)S(1)}, u32[]{:S(2)}, u32[]{:S(2)}) %collective-permute-start.25) | collective-permute-done | bytes 360480 | tf_op jit(solution)/shard_map/ppermute | solution.py:21
  42.6 2.5 copy.56
  45.1 5.6 all-to-all-start
  51.5 3.4 collective-permute-start
  56.3 4.0 copy.63
  60.6 7.5 %collective-permute-done = bf16[3,2,32,704]{3,2,1,0:T(8,128)(2,1)S(1)} collective-permute-done((bf16[3,2,32,704]{3,2,1,0:T(8,128)(2,1)}, bf16[3,2,32,704]{3,2,1,0:T(8,128)(2,1)S(1)}, u32[]{:S(2)}, u32[]{:S(2)}) %collective-permute-start) | collective-permute-done | bytes 270368 | tf_op jit(solution)/shard_map/ppermute | solution.py:281
  68.1 14.6 %collective-permute-done.1 = bf16[3,2,32,704]{3,2,1,0:T(8,128)(2,1)} collective-permute-done((bf16[3,2,32,704]{3,2,1,0:T(8,128)(2,1)S(1)}, bf16[3,2,32,704]{3,2,1,0:T(8,128)(2,1)}, u32[]{:S(2)}, u32[]{:S(2)}) %collective-permute-start.1) | collective-permute-done | bytes 270368 | tf_op jit(solution)/shard_map/ppermute | solution.py:282
  82.7 2.8 fusion.6
  85.5 14.2 %all-to-all-done.mine = bf16[4,352,704]{2,1,0:T(8,128)(2,1)S(1)} async-done(((bf16[4,352,704]{2,1,0:T(8,128)(2,1)}), bf16[4,352,704]{2,1,0:T(8,128)(2,1)S(1)}, u32[]{:S(2)}, u32[]{:S(2)}) %all-to-all-start) | async-done | bytes 1982496 | tf_op jit(solution)/shard_map/all_to_all | solution.py:114
  99.7 4.5 all-to-all-start.1
  104.2 25.4 %fusion.115 = (f32[4,2,32]{2,1,0:T(2,128)S(1)}, f32[4,2,32,704]{3,2,1,0:T(8,128)S(1)}) fusion(f32[10,2,38,704]{3,2,1,0:T(8,128)} %fusion.6, f32[704]{0:T(1024)S(1)} %get-tuple-element.156, f32[704]{0:T(1024)S(1)} %get-tuple-element.157, f32[704]{0:T(1024)S(1)} %get-tuple-element.110, f32[704]{0:T(1024)S(1)} %get-tuple-element.111, ...), kind=kLoop, calls=%fused_computation.313 | loop fusion | flops 17661696 | bytes 36183808 | tf_op jit(solution)/shard_map/reduce_sum | solution.py:324
  129.9 3.8 collective-permute-start.4
  134.4 8.6 %collective-permute-done.4 = f32[2,4,2,32]{3,2,1,0:T(2,128)S(1)} collective-permute-done((f32[2,4,2,32]{3,2,1,0:T(2,128)S(1)}, f32[2,4,2,32]{3,2,1,0:T(2,128)S(1)}, u32[]{:S(2)}, u32[]{:S(2)}) %collective-permute-start.4) | collective-permute-done | bytes 2080 | tf_op jit(solution)/shard_map/ppermute | solution.py:21
  143.0 10.9 %collective-permute-done.3 = f32[2,4,2,32]{3,2,1,0:T(2,128)S(1)} collective-permute-done((f32[2,4,2,32]{3,2,1,0:T(2,128)S(1)}, f32[2,4,2,32]{3,2,1,0:T(2,128)S(1)}, u32[]{:S(2)}, u32[]{:S(2)}) %collective-permute-start.3) | collective-permute-done | bytes 2080 | tf_op jit(solution)/shard_map/ppermute | solution.py:21
  156.2 17.0 %collective-permute-done.9 = bf16[256,704]{1,0:T(8,128)(2,1)} collective-permute-done((bf16[256,704]{1,0:T(8,128)(2,1)S(1)}, bf16[256,704]{1,0:T(8,128)(2,1)}, u32[]{:S(2)}, u32[]{:S(2)}) %collective-permute-start.9) | collective-permute-done | bytes 360480 | tf_op jit(solution)/shard_map/ppermute | solution.py:21
  177.4 7.1 %collective-permute-done.10 = bf16[256,704]{1,0:T(8,128)(2,1)} collective-permute-done((bf16[256,704]{1,0:T(8,128)(2,1)}, bf16[256,704]{1,0:T(8,128)(2,1)}, u32[]{:S(2)}, u32[]{:S(2)}) %collective-permute-start.10) | collective-permute-done | bytes 360480 | tf_op jit(solution)/shard_map/ppermute | solution.py:21
  190.4 2.4 collective-permute-done.7
  196.8 14.0 %collective-permute-done.11 = bf16[2,256,704]{1,2,0:T(8,128)(2,1)} collective-permute-done((bf16[2,256,704]{1,2,0:T(8,128)(2,1)}, bf16[2,256,704]{1,2,0:T(8,128)(2,1)}, u32[]{:S(2)}, u32[]{:S(2)}) %collective-permute-start.11) | collective-permute-done | bytes 720928 | tf_op jit(solution)/shard_map/ppermute | solution.py:21
  213.9 2.3 copy.58.refs_2_
  218.4 2.3 copy.60.refs_5_
  220.7 2.3 copy.61.refs_6_
  233.6 9.7 %shard_map.120 = (f32[1024,704]{1,0:T(8,128)S(1)}, f32[1024,704]{1,0:T(8,128)}, f32[2,704]{1,0:T(2,128)S(1)}) custom-call(s32[2]{0:T(128)S(1)} %pad_add_fusion.places, bf16[2,256,704]{2,1,0:T(8,128)(2,1)S(1)} %pad_maximum_fusion.1.refs_0_, bf16[2,256,704]{2,1,0:T(8,128)(2,1)S(1)} %copy-done.8, bf16[2,256,704]{2,1,0:T(8,128)(2,1)S(1)} %copy-done.6, ...), custom_call_target="tpu_custom_call" | custom-call | flops 4060086272 | bytes 15507712 | tf_op jit(solution)/shard_map/pallas_call | solution.py:77
  245.0 2.6 shard_map.121.refs_3_.refs_1_
  250.0 3.0 collective-permute-done.16
  257.3 3.7 collective-permute-done.18
  261.1 8.6 %copy.65 = bf16[16,256,704]{2,1,0:T(8,128)(2,1)} copy(bf16[16,256,704]{1,2,0:T(8,128)(2,1)} %all-gather.3.cloned.1.call-done) | data formatting | bytes 11534336 | tf_op jit(solution)/shard_map/all_gather | solution.py:318
  271.6 9.3 %shard_map.123 = (f32[1024,704]{1,0:T(8,128)S(1)}, f32[2,704]{1,0:T(2,128)S(1)}) custom-call(s32[2]{0:T(128)S(1)} %pad_add_fusion.places, bf16[4,4,256,704]{3,2,1,0:T(8,128)(2,1)} %bitcast.108, bf16[4,704,704]{2,1,0:T(8,128)(2,1)} %copy-done.1, f32[1024,704]{1,0:T(8,128)S(1)} %copy-done.26), custom_call_target="tpu_custom_call" | custom-call | flops 4060086272 | bytes 15504896 | tf_op jit(solution)/shard_map/pallas_call | solution.py:77
  281.0 8.3 %shard_map.122 = (bf16[1024,704]{1,0:T(8,128)(2,1)S(1)}, bf16[4,4,256,704]{3,2,1,0:T(8,128)(2,1)}) custom-call(s32[2]{0:T(128)S(1)} %pad_add_fusion.places, f32[1024,704]{1,0:T(8,128)S(1)} %copy-done.26, f32[2,704]{1,0:T(2,128)S(1)} %get-tuple-element.179.refs_1_.refs_3_, f32[1,704]{1,0:T(1,128)S(1)} %broadcast_in_dim.5.refs_2_, ...), custom_call_target="tpu_custom_call" | custom-call | flops 4060086272 | bytes 14065920 | tf_op jit(solution)/shard_map/pallas_call | solution.py:77
  290.4 10.5 %shard_map.124 = (bf16[1024,704]{1,0:T(8,128)(2,1)S(1)}, bf16[2,256,704]{2,1,0:T(8,128)(2,1)S(1)}, bf16[2,256,704]{2,1,0:T(8,128)(2,1)S(1)}, bf16[2,256,704]{2,1...) custom-call(s32[2]{0:T(128)S(1)} %pad_add_fusion.places, ...), custom_call_target="tpu_custom_call" | custom-call | flops 4060086272 | bytes 19835904 | tf_op jit(solution)/shard_map/pallas_call | solution.py:77
  307.5 2.3 copy.74
  309.8 2.5 copy.66
  318.7 25.9 %collective-permute-done.30 = bf16[2,256,704]{1,2,0:T(8,128)(2,1)} collective-permute-done((bf16[2,256,704]{1,2,0:T(8,128)(2,1)}, bf16[2,256,704]{1,2,0:T(8,128)(2,1)}, u32[]{:S(2)}, u32[]{:S(2)}) %collective-permute-start.30) | collective-permute-done | bytes 720928 | tf_op jit(solution)/shard_map/ppermute | solution.py:21
  351.2 8.8 %shard_map.126 = (bf16[4,352,704]{2,1,0:T(8,128)(2,1)S(1)}, bf16[4,352,704]{2,1,0:T(8,128)(2,1)}) custom-call(s32[2]{0:T(128)S(1)} %pad_add_fusion.places, bf16[1024,704]{1,0:T(8,128)(2,1)S(1)} %copy-done.31, bf16[4,4,256,704]{3,2,1,0:T(8,128)(2,1)} %bitcast.109), custom_call_target="tpu_custom_call" | custom-call | flops 4060086272 | bytes 11173888 | tf_op jit(solution)/shard_map/pallas_call | solution.py:77
  360.0 3.9 collective-permute-done.26
  363.9 2.3 copy.67
  366.2 2.4 add_convert_fusion.5
  372.3 2.3 copy.73
  376.8 15.3 %collective-permute-done.31 = bf16[2,256,704]{1,2,0:T(8,128)(2,1)} collective-permute-done((bf16[2,256,704]{1,2,0:T(8,128)(2,1)}, bf16[2,256,704]{1,2,0:T(8,128)(2,1)}, u32[]{:S(2)}, u32[]{:S(2)}) %collective-permute-start.31) | collective-permute-done | bytes 720928 | tf_op jit(solution)/shard_map/ppermute | solution.py:21
  392.1 2.3 copy.77
  399.6 2.3 copy.69
  410.0 5.4 collective-permute-start.33
  415.5 3.5 add_convert_fusion
  418.9 4.7 all-to-all-start.3
  423.7 19.7 %collective-permute-done.33 = bf16[256,704]{1,0:T(8,128)(2,1)} collective-permute-done((bf16[256,704]{1,0:T(8,128)(2,1)}, bf16[256,704]{1,0:T(8,128)(2,1)}, u32[]{:S(2)}, u32[]{:S(2)}) %collective-permute-start.33) | collective-permute-done | bytes 360480 | tf_op jit(solution)/shard_map/ppermute | solution.py:21
  443.4 2.3 fusion.113
  447.6 3.4 collective-permute-start.35
  458.1 6.6 %shard_map.125 = (bf16[4,352,704]{2,1,0:T(8,128)(2,1)S(1)}, bf16[4,352,704]{2,1,0:T(8,128)(2,1)}) custom-call(s32[2]{0:T(128)S(1)} %pad_add_fusion.places, bf16[1024,704]{1,0:T(8,128)(2,1)S(1)} %copy-done.29, bf16[2,256,704]{2,1,0:T(8,128)(2,1)S(1)} %pad_maximum_fusion.1.refs_0_, bf16[2,256,704]{2,1,0:T(8,128)(2,1)S(1)} %copy-done.9, ...), custom_call_target="tpu_custom_call" | custom-call | flops 4060086272 | bytes 11173888 | tf_op jit(solution)/shard_map/pallas_call | solution.py:77
  464.7 10.2 %collective-permute-done.36 = f32[2,4,2,32]{3,2,1,0:T(2,128)S(1)} collective-permute-done((f32[2,4,2,32]{3,2,1,0:T(2,128)S(1)}, f32[2,4,2,32]{3,2,1,0:T(2,128)S(1)}, u32[]{:S(2)}, u32[]{:S(2)}) %collective-permute-start.36) | collective-permute-done | bytes 2080 | tf_op jit(solution)/shard_map/ppermute | solution.py:21
  475.0 2.3 multiply_reduce_fusion
  481.7 3.5 add_convert_fusion.1
  485.1 3.6 all-to-all-start.2
  488.9 4.9 collective-permute-done.43
  495.2 2.7 collective-permute-start.38
  500.0 3.8 collective-permute-done.38
  503.8 8.3 %collective-permute-done.39 = bf16[3,2,32,704]{3,2,1,0:T(8,128)(2,1)S(1)} collective-permute-done((bf16[3,2,32,704]{3,2,1,0:T(8,128)(2,1)S(1)}, bf16[3,2,32,704]{3,2,1,0:T(8,128)(2,1)S(1)}, u32[]{:S(2)}, u32[]{:S(2)}) %collective-permute-start.39) | collective-permute-done | bytes 270368 | tf_op jit(solution)/shard_map/ppermute | solution.py:282
  512.3 7.2 %fusion.94 = bf16[4,2,32,704]{3,2,1,0:T(8,128)(2,1)} fusion(f32[10,2,32,704]{3,2,1,0:T(8,128)S(1)} %maximum_convert_fusion, bf16[4,2,32,704]{3,2,1,0:T(8,128)(2,1)S(1)} %copy-done.41, f32[704]{0:T(1024)S(1)} %get-tuple-element.156, f32[704]{0:T(1024)S(1)} %get-tuple-element.157, f32[704]{0:T(1024)S(1)} %get-tuple-element.110, ...), kind=kLoop, calls=%fused_computation.148 | loop fusion | flops 18022400 | bytes 8425472 | tf_op jit(solution)/shard_map/convert_element_type | solution.py:375
  522.1 4.0 convert_multiply_fusion
  526.1 5.6 copy.85
  532.4 13.0 %collective-permute-done.20 = bf16[256,704]{1,0:T(8,128)(2,1)} collective-permute-done((bf16[256,704]{1,0:T(8,128)(2,1)S(1)}, bf16[256,704]{1,0:T(8,128)(2,1)}, u32[]{:S(2)}, u32[]{:S(2)}) %collective-permute-start.20) | collective-permute-done | bytes 360480 | tf_op jit(solution)/shard_map/ppermute | solution.py:21
  546.7 2.4 convert_multiply_fusion.1
  549.1 5.6 copy.84
  554.7 4.3 collective-permute-done.21
  (284 shorter events, 114.9 us)
Async XLA Ops:
  7.2 253.9 %all-gather.3.cloned.1.call-start = ((), (), s32[]{:S(2)}) async-start(), calls=%async_computation.6 | async-start | bytes 7208960 | tf_op jit(solution)/shard_map/all_gather | solution.py:318
  7.2 22.0 %collective-permute-start.24 = (bf16[256,704]{1,0:T(8,128)(2,1)}, bf16[256,704]{1,0:T(8,128)(2,1)S(1)}, u32[]{:S(2)}, u32[]{:S(2)}) collective-permute-start(bf16[256,704]{1,0:T(8,128)(2,1)} %bitcast.116), channel_id=1, source_target_pairs={{0,2},{1,3},{2,0},{3,1},{4,6},{5,7},{6,4},{7,5},{8,10},{9,11},{10,... | collective-permute-start | bytes 1081352 | tf_op jit(solution)/shard_map/ppermute | solution.py:21
  11.3 18.6 %collective-permute-start.23 = (bf16[256,704]{1,0:T(8,128)(2,1)}, bf16[256,704]{1,0:T(8,128)(2,1)S(1)}, u32[]{:S(2)}, u32[]{:S(2)}) collective-permute-start(bf16[256,704]{1,0:T(8,128)(2,1)} %bitcast.117), channel_id=1, source_target_pairs={{0,1},{1,0},{2,3},{3,2},{4,5},{5,4},{6,7},{7,6},{8,9},{9,8},{10,11... | collective-permute-start | bytes 1081352 | tf_op jit(solution)/shard_map/ppermute | solution.py:21
  29.2 10.2 %collective-permute-start.25 = (bf16[256,704]{1,0:T(8,128)(2,1)S(1)}, bf16[256,704]{1,0:T(8,128)(2,1)S(1)}, u32[]{:S(2)}, u32[]{:S(2)}) collective-permute-start(bf16[256,704]{1,0:T(8,128)(2,1)S(1)} %collective-permute-done.24), channel_id=1, source_target_pairs={{0,1},{1,0},{2,3},{3,2},{4,5},{5,4},{6,7},{7,6},{8,9},{9,8},{10,11... | collective-permute-start | bytes 1081352 | tf_op jit(solution)/shard_map/ppermute | solution.py:21
  45.1 54.6 %all-to-all-start = ((bf16[4,352,704]{2,1,0:T(8,128)(2,1)}), bf16[4,352,704]{2,1,0:T(8,128)(2,1)S(1)}, u32[]{:S(2)}, u32[]{:S(2)}) async-start(bf16[4,352,704]{2,1,0:T(8,128)(2,1)} %bitcast.105), calls=%async_computation | async-start | bytes 4325376 | tf_op jit(solution)/shard_map/all_to_all | solution.py:114
  51.5 16.6 %collective-permute-start = (bf16[3,2,32,704]{3,2,1,0:T(8,128)(2,1)}, bf16[3,2,32,704]{3,2,1,0:T(8,128)(2,1)S(1)}, u32[]{:S(2)}, u32[]{:S(2)}) collective-permute-start(bf16[3,2,32,704]{3,2,1,0:T(8,128)(2,1)} %get-tuple-element.170), channel_id=1, source_target_pairs={{0,4},{4,8},{8,12},{1,5},{5,9},{9,13},{2,6},{6,10},{10,14},{3,7},{... | collective-permute-start | bytes 811016 | tf_op jit(solution)/shard_map/ppermute | solution.py:281
  54.9 27.7 %collective-permute-start.1 = (bf16[3,2,32,704]{3,2,1,0:T(8,128)(2,1)S(1)}, bf16[3,2,32,704]{3,2,1,0:T(8,128)(2,1)}, u32[]{:S(2)}, u32[]{:S(2)}) collective-permute-start(bf16[3,2,32,704]{3,2,1,0:T(8,128)(2,1)S(1)} %get-tuple-element.171), channel_id=1, source_target_pairs={{4,0},{8,4},{12,8},{5,1},{9,5},{13,9},{6,2},{10,6},{14,10},{7,3},{... | collective-permute-start | bytes 811016 | tf_op jit(solution)/shard_map/ppermute | solution.py:282
  60.6 43.6 %copy-start.43 = (f32[704]{0:T(1024)}, f32[704]{0:T(1024)S(1)}, u32[]{:S(2)}) copy-start(f32[704]{0:T(1024)S(1)} %get-tuple-element.145) | copy-start | bytes 8452
  60.6 43.6 %copy-start.45 = (f32[704]{0:T(1024)}, f32[704]{0:T(1024)S(1)}, u32[]{:S(2)}) copy-start(f32[704]{0:T(1024)S(1)} %get-tuple-element.146) | copy-start | bytes 8452
  99.7 77.8 %all-to-all-start.1 = ((bf16[4,352,704]{2,1,0:T(8,128)(2,1)}), bf16[4,352,704]{2,1,0:T(8,128)(2,1)}, u32[]{:S(2)}, u32[]{:S(2)}) async-start(bf16[4,352,704]{2,1,0:T(8,128)(2,1)} %bitcast.104), calls=%async_computation.1 | async-start | bytes 4325376 | tf_op jit(solution)/shard_map/all_to_all | solution.py:114
  104.2 415.4 %reduce-scatter.2.cloned.1.call-start = ((), (), s32[]{:S(2)}) async-start(), calls=%async_computation.5 | async-start | bytes 7864320 | tf_op jit(solution)/shard_map/reduce_scatter | solution.py:364
  129.7 43.6 %copy-start.33 = (f32[4,2,32,704]{3,2,1,0:T(8,128)}, f32[4,2,32,704]{3,2,1,0:T(8,128)S(1)}, u32[]{:S(2)}) copy-start(f32[4,2,32,704]{3,2,1,0:T(8,128)S(1)} %get-tuple-element.164) | copy-start | bytes 2162692
  129.9 13.0 %collective-permute-start.4 = (f32[2,4,2,32]{3,2,1,0:T(2,128)S(1)}, f32[2,4,2,32]{3,2,1,0:T(2,128)S(1)}, u32[]{:S(2)}, u32[]{:S(2)}) collective-permute-start(f32[2,4,2,32]{3,2,1,0:T(2,128)S(1)} %pad_maximum_fusion.3), channel_id=1, source_target_pairs={{0,3},{1,2},{2,1},{3,0},{4,7},{5,6},{6,5},{7,4},{8,11},{9,10},{10,... | collective-permute-start | bytes 6152 | tf_op jit(solution)/shard_map/ppermute | solution.py:21
  133.7 20.2 %collective-permute-start.3 = (f32[2,4,2,32]{3,2,1,0:T(2,128)S(1)}, f32[2,4,2,32]{3,2,1,0:T(2,128)S(1)}, u32[]{:S(2)}, u32[]{:S(2)}) collective-permute-start(f32[2,4,2,32]{3,2,1,0:T(2,128)S(1)} %pad_maximum_fusion.3), channel_id=1, source_target_pairs={{0,2},{1,3},{2,0},{3,1},{4,6},{5,7},{6,4},{7,5},{8,10},{9,11},{10,... | collective-permute-start | bytes 6152 | tf_op jit(solution)/shard_map/ppermute | solution.py:21
  133.7 20.2 %collective-permute-start.2 = (f32[2,4,2,32]{3,2,1,0:T(2,128)S(1)}, f32[2,4,2,32]{3,2,1,0:T(2,128)S(1)}, u32[]{:S(2)}, u32[]{:S(2)}) collective-permute-start(f32[2,4,2,32]{3,2,1,0:T(2,128)S(1)} %pad_maximum_fusion.3), channel_id=1, source_target_pairs={{0,1},{1,0},{2,3},{3,2},{4,5},{5,4},{6,7},{7,6},{8,9},{9,8},{10,11... | collective-permute-start | bytes 6152 | tf_op jit(solution)/shard_map/ppermute | solution.py:21
  154.1 19.1 %collective-permute-start.9 = (bf16[256,704]{1,0:T(8,128)(2,1)S(1)}, bf16[256,704]{1,0:T(8,128)(2,1)}, u32[]{:S(2)}, u32[]{:S(2)}) collective-permute-start(bf16[256,704]{1,0:T(8,128)(2,1)S(1)} %bitcast.113), channel_id=1, source_target_pairs={{0,2},{1,3},{2,0},{3,1},{4,6},{5,7},{6,4},{7,5},{8,10},{9,11},{10,... | collective-permute-start | bytes 1081352 | tf_op jit(solution)/shard_map/ppermute | solution.py:21
  154.6 18.6 %collective-permute-start.5 = (bf16[256,704]{1,0:T(8,128)(2,1)S(1)}, bf16[256,704]{1,0:T(8,128)(2,1)S(1)}, u32[]{:S(2)}, u32[]{:S(2)}) collective-permute-start(bf16[256,704]{1,0:T(8,128)(2,1)S(1)} %bitcast.114), channel_id=1, source_target_pairs={{0,1},{1,0},{2,3},{3,2},{4,5},{5,4},{6,7},{7,6},{8,9},{9,8},{10,11... | collective-permute-start | bytes 1081352 | tf_op jit(solution)/shard_map/ppermute | solution.py:21
  156.2 73.3 %collective-permute-start.14 = (bf16[4,352,704]{2,1,0:T(8,128)(2,1)S(1)}, bf16[4,352,704]{2,1,0:T(8,128)(2,1)}, u32[]{:S(2)}, u32[]{:S(2)}) collective-permute-start(bf16[4,352,704]{2,1,0:T(8,128)(2,1)S(1)} %all-to-all-done.mine), channel_id=1, source_target_pairs={{0,16},{16,0},{1,17},{17,1},{2,18},{18,2},{3,19},{19,3},{4,20},{20... | collective-permute-start | bytes 5947400 | tf_op jit(solution)/shard_map/ppermute | solution.py:21
  173.2 11.4 %collective-permute-start.10 = (bf16[256,704]{1,0:T(8,128)(2,1)}, bf16[256,704]{1,0:T(8,128)(2,1)}, u32[]{:S(2)}, u32[]{:S(2)}) collective-permute-start(bf16[256,704]{1,0:T(8,128)(2,1)} %collective-permute-done.9), channel_id=1, source_target_pairs={{0,1},{1,0},{2,3},{3,2},{4,5},{5,4},{6,7},{7,6},{8,9},{9,8},{10,11... | collective-permute-start | bytes 1081352 | tf_op jit(solution)/shard_map/ppermute | solution.py:21
  174.4 18.4 %collective-permute-start.7 = (bf16[2,256,704]{1,2,0:T(8,128)(2,1)}, bf16[2,256,704]{1,2,0:T(8,128)(2,1)}, u32[]{:S(2)}, u32[]{:S(2)}) collective-permute-start(bf16[2,256,704]{1,2,0:T(8,128)(2,1)} %copy.52), channel_id=1, source_target_pairs={{0,8},{4,12},{8,0},{12,4},{1,9},{5,13},{9,1},{13,5},{2,10},{6,14},... | collective-permute-start | bytes 2162696 | tf_op jit(solution)/shard_map/ppermute | solution.py:21
  175.9 19.4 %collective-permute-start.6 = (bf16[2,256,704]{1,2,0:T(8,128)(2,1)}, bf16[2,256,704]{1,2,0:T(8,128)(2,1)}, u32[]{:S(2)}, u32[]{:S(2)}) collective-permute-start(bf16[2,256,704]{1,2,0:T(8,128)(2,1)} %copy.52), channel_id=1, source_target_pairs={{0,4},{4,0},{8,12},{12,8},{1,5},{5,1},{9,13},{13,9},{2,6},{6,2},{1... | collective-permute-start | bytes 2162696 | tf_op jit(solution)/shard_map/ppermute | solution.py:21
  177.4 67.5 %collective-permute-start.19 = (bf16[4,352,704]{2,1,0:T(8,128)(2,1)}, bf16[4,352,704]{2,1,0:T(8,128)(2,1)}, u32[]{:S(2)}, u32[]{:S(2)}) collective-permute-start(bf16[4,352,704]{2,1,0:T(8,128)(2,1)} %all-to-all-done.1.mine), channel_id=1, source_target_pairs={{0,16},{16,0},{1,17},{17,1},{2,18},{18,2},{3,19},{19,3},{4,20},{20... | collective-permute-start | bytes 5947400 | tf_op jit(solution)/shard_map/ppermute | solution.py:21
  188.9 21.9 %collective-permute-start.11 = (bf16[2,256,704]{1,2,0:T(8,128)(2,1)}, bf16[2,256,704]{1,2,0:T(8,128)(2,1)}, u32[]{:S(2)}, u32[]{:S(2)}) collective-permute-start(bf16[2,256,704]{1,2,0:T(8,128)(2,1)} %copy.54), channel_id=1, source_target_pairs={{0,4},{4,0},{8,12},{12,8},{1,5},{5,1},{9,13},{13,9},{2,6},{6,2},{1... | collective-permute-start | bytes 2162696 | tf_op jit(solution)/shard_map/ppermute | solution.py:21
  192.8 27.9 %collective-permute-start.12 = (bf16[2,256,704]{1,2,0:T(8,128)(2,1)}, bf16[2,256,704]{1,2,0:T(8,128)(2,1)}, u32[]{:S(2)}, u32[]{:S(2)}) collective-permute-start(bf16[2,256,704]{1,2,0:T(8,128)(2,1)} %copy.54), channel_id=1, source_target_pairs={{0,8},{4,12},{8,0},{12,4},{1,9},{5,13},{9,1},{13,5},{2,10},{6,14},... | collective-permute-start | bytes 2162696 | tf_op jit(solution)/shard_map/ppermute | solution.py:21
  195.3 29.6 %collective-permute-start.8 = (bf16[2,256,704]{1,2,0:T(8,128)(2,1)}, bf16[2,256,704]{1,2,0:T(8,128)(2,1)}, u32[]{:S(2)}, u32[]{:S(2)}) collective-permute-start(bf16[2,256,704]{1,2,0:T(8,128)(2,1)} %collective-permute-done.7), channel_id=1, source_target_pairs={{0,4},{4,0},{8,12},{12,8},{1,5},{5,1},{9,13},{13,9},{2,6},{6,2},{1... | collective-permute-start | bytes 2162696 | tf_op jit(solution)/shard_map/ppermute | solution.py:21
  210.8 16.5 %collective-permute-start.13 = (bf16[2,256,704]{1,2,0:T(8,128)(2,1)}, bf16[2,256,704]{1,2,0:T(8,128)(2,1)}, u32[]{:S(2)}, u32[]{:S(2)}) collective-permute-start(bf16[2,256,704]{1,2,0:T(8,128)(2,1)} %collective-permute-done.11), channel_id=1, source_target_pairs={{0,8},{4,12},{8,0},{12,4},{1,9},{5,13},{9,1},{13,5},{2,10},{6,14},... | collective-permute-start | bytes 2162696 | tf_op jit(solution)/shard_map/ppermute | solution.py:21
  243.4 6.1 %collective-permute-start.15 = (f32[2]{0:T(128)S(1)}, f32[2]{0:T(128)S(1)}, u32[]{:S(2)}, u32[]{:S(2)}) collective-permute-start(f32[2]{0:T(128)S(1)} %fusion.111), channel_id=1, source_target_pairs={{0,4},{4,0},{8,12},{12,8},{1,5},{5,1},{9,13},{13,9},{2,6},{6,2},{1... | collective-permute-start | bytes 32 | tf_op jit(solution)/shard_map/ppermute | solution.py:21
  249.5 3.5 collective-permute-start.16
  253.1 3.5 collective-permute-start.17
  256.6 4.4 collective-permute-start.18
  261.1 19.9 %slice-start = ((s8[4325376]{0:T(1024)(128)(4,1)}), s8[131072]{0:T(1024)(128)(4,1)S(1)}, s32[]{:S(2)}) async-start(s8[4325376]{0:T(1024)(128)(4,1)} %bitcast.100), calls=%async_computation.7 | async-start | bytes 262144
  309.8 34.7 %collective-permute-start.30 = (bf16[2,256,704]{1,2,0:T(8,128)(2,1)}, bf16[2,256,704]{1,2,0:T(8,128)(2,1)}, u32[]{:S(2)}, u32[]{:S(2)}) collective-permute-start(bf16[2,256,704]{1,2,0:T(8,128)(2,1)} %copy.74), channel_id=1, source_target_pairs={{0,8},{4,12},{8,0},{12,4},{1,9},{5,13},{9,1},{13,5},{2,10},{6,14},... | collective-permute-start | bytes 2162696 | tf_op jit(solution)/shard_map/ppermute | solution.py:21
  313.4 32.5 %copy-start.24 = (bf16[2,256,704]{2,1,0:T(8,128)(2,1)S(1)}, bf16[2,256,704]{2,1,0:T(8,128)(2,1)}, u32[]{:S(2)}) copy-start(bf16[2,256,704]{2,1,0:T(8,128)(2,1)} %copy-done.23) | copy-start | bytes 2162692
  314.6 57.7 %collective-permute-start.29 = (bf16[2,256,704]{1,2,0:T(8,128)(2,1)}, bf16[2,256,704]{1,2,0:T(8,128)(2,1)}, u32[]{:S(2)}, u32[]{:S(2)}) collective-permute-start(bf16[2,256,704]{1,2,0:T(8,128)(2,1)} %copy.72), channel_id=1, source_target_pairs={{0,8},{4,12},{8,0},{12,4},{1,9},{5,13},{9,1},{13,5},{2,10},{6,14},... | collective-permute-start | bytes 2162696 | tf_op jit(solution)/shard_map/ppermute | solution.py:21
  316.6 57.9 %collective-permute-start.28 = (bf16[2,256,704]{1,2,0:T(8,128)(2,1)}, bf16[2,256,704]{1,2,0:T(8,128)(2,1)}, u32[]{:S(2)}, u32[]{:S(2)}) collective-permute-start(bf16[2,256,704]{1,2,0:T(8,128)(2,1)} %copy.70), channel_id=1, source_target_pairs={{0,4},{4,0},{8,12},{12,8},{1,5},{5,1},{9,13},{13,9},{2,6},{6,2},{1... | collective-permute-start | bytes 2162696 | tf_op jit(solution)/shard_map/ppermute | solution.py:21
  317.1 46.8 %collective-permute-start.26 = (bf16[2,256,704]{1,2,0:T(8,128)(2,1)}, bf16[2,256,704]{1,2,0:T(8,128)(2,1)}, u32[]{:S(2)}, u32[]{:S(2)}) collective-permute-start(bf16[2,256,704]{1,2,0:T(8,128)(2,1)} %copy.66), channel_id=1, source_target_pairs={{0,4},{4,0},{8,12},{12,8},{1,5},{5,1},{9,13},{13,9},{2,6},{6,2},{1... | collective-permute-start | bytes 2162696 | tf_op jit(solution)/shard_map/ppermute | solution.py:21
  349.3 42.9 %collective-permute-start.31 = (bf16[2,256,704]{1,2,0:T(8,128)(2,1)}, bf16[2,256,704]{1,2,0:T(8,128)(2,1)}, u32[]{:S(2)}, u32[]{:S(2)}) collective-permute-start(bf16[2,256,704]{1,2,0:T(8,128)(2,1)} %copy.76), channel_id=1, source_target_pairs={{0,4},{4,0},{8,12},{12,8},{1,5},{5,1},{9,13},{13,9},{2,6},{6,2},{1... | collective-permute-start | bytes 2162696 | tf_op jit(solution)/shard_map/ppermute | solution.py:21
  360.0 55.4 %collective-permute-start.41 = (bf16[4,352,704]{2,1,0:T(8,128)(2,1)}, bf16[4,352,704]{2,1,0:T(8,128)(2,1)}, u32[]{:S(2)}, u32[]{:S(2)}) collective-permute-start(bf16[4,352,704]{2,1,0:T(8,128)(2,1)} %get-tuple-element.44), channel_id=1, source_target_pairs={{0,16},{16,0},{1,17},{17,1},{2,18},{18,2},{3,19},{19,3},{4,20},{20... | collective-permute-start | bytes 5947400 | tf_op jit(solution)/shard_map/ppermute | solution.py:21
  370.9 28.7 %collective-permute-start.27 = (bf16[2,256,704]{1,2,0:T(8,128)(2,1)}, bf16[2,256,704]{1,2,0:T(8,128)(2,1)}, u32[]{:S(2)}, u32[]{:S(2)}) collective-permute-start(bf16[2,256,704]{1,2,0:T(8,128)(2,1)} %copy.68), channel_id=1, source_target_pairs={{0,8},{4,12},{8,0},{12,4},{1,9},{5,13},{9,1},{13,5},{2,10},{6,14},... | collective-permute-start | bytes 2162696 | tf_op jit(solution)/shard_map/ppermute | solution.py:21
  398.1 10.1 %collective-permute-start.32 = (bf16[256,704]{1,0:T(8,128)(2,1)}, bf16[256,704]{1,0:T(8,128)(2,1)}, u32[]{:S(2)}, u32[]{:S(2)}) collective-permute-start(bf16[256,704]{1,0:T(8,128)(2,1)} %slice_bitcast_fusion.1), channel_id=1, source_target_pairs={{0,1},{1,0},{2,3},{3,2},{4,5},{5,4},{6,7},{7,6},{8,9},{9,8},{10,11... | collective-permute-start | bytes 1081352 | tf_op jit(solution)/shard_map/ppermute | solution.py:21
  405.5 18.2 %collective-permute-start.34 = (bf16[256,704]{1,0:T(8,128)(2,1)}, bf16[256,704]{1,0:T(8,128)(2,1)}, u32[]{:S(2)}, u32[]{:S(2)}) collective-permute-start(bf16[256,704]{1,0:T(8,128)(2,1)} %slice_bitcast_fusion), channel_id=1, source_target_pairs={{0,1},{1,0},{2,3},{3,2},{4,5},{5,4},{6,7},{7,6},{8,9},{9,8},{10,11... | collective-permute-start | bytes 1081352 | tf_op jit(solution)/shard_map/ppermute | solution.py:21
  410.0 33.4 %collective-permute-start.33 = (bf16[256,704]{1,0:T(8,128)(2,1)}, bf16[256,704]{1,0:T(8,128)(2,1)}, u32[]{:S(2)}, u32[]{:S(2)}) collective-permute-start(bf16[256,704]{1,0:T(8,128)(2,1)} %fusion.99), channel_id=1, source_target_pairs={{0,2},{1,3},{2,0},{3,1},{4,6},{5,7},{6,4},{7,5},{8,10},{9,11},{10,... | collective-permute-start | bytes 1081352 | tf_op jit(solution)/shard_map/ppermute | solution.py:21
  418.9 66.2 %all-to-all-start.3 = ((bf16[4,352,704]{2,1,0:T(8,128)(2,1)}), bf16[4,352,704]{2,1,0:T(8,128)(2,1)}, u32[]{:S(2)}, u32[]{:S(2)}) async-start(bf16[4,352,704]{2,1,0:T(8,128)(2,1)} %add_convert_fusion), calls=%async_computation.4 | async-start | bytes 4325376 | tf_op jit(solution)/shard_map/all_to_all | solution.py:254
  423.7 27.4 %copy-start.3 = (bf16[2,256,704]{2,1,0:T(8,128)(2,1)S(1)}, bf16[2,256,704]{2,1,0:T(8,128)(2,1)}, u32[]{:S(2)}) copy-start(bf16[2,256,704]{2,1,0:T(8,128)(2,1)} %pad_maximum_fusion.2.refs_4_) | copy-start | bytes 2162692
  423.7 27.4 %copy-start.7 = (bf16[2,256,704]{2,1,0:T(8,128)(2,1)S(1)}, bf16[2,256,704]{2,1,0:T(8,128)(2,1)}, u32[]{:S(2)}) copy-start(bf16[2,256,704]{2,1,0:T(8,128)(2,1)} %copy.58.refs_2_) | copy-start | bytes 2162692
  447.5 27.4 %collective-permute-start.36 = (f32[2,4,2,32]{3,2,1,0:T(2,128)S(1)}, f32[2,4,2,32]{3,2,1,0:T(2,128)S(1)}, u32[]{:S(2)}, u32[]{:S(2)}) collective-permute-start(f32[2,4,2,32]{3,2,1,0:T(2,128)S(1)} %pad_maximum_fusion.4), channel_id=1, source_target_pairs={{0,2},{1,3},{2,0},{3,1},{4,6},{5,7},{6,4},{7,5},{8,10},{9,11},{10,... | collective-permute-start | bytes 6152 | tf_op jit(solution)/shard_map/ppermute | solution.py:21
  447.6 27.3 %collective-permute-start.37 = (f32[2,4,2,32]{3,2,1,0:T(2,128)S(1)}, f32[2,4,2,32]{3,2,1,0:T(2,128)S(1)}, u32[]{:S(2)}, u32[]{:S(2)}) collective-permute-start(f32[2,4,2,32]{3,2,1,0:T(2,128)S(1)} %pad_maximum_fusion.4), channel_id=1, source_target_pairs={{0,3},{1,2},{2,1},{3,0},{4,7},{5,6},{6,5},{7,4},{8,11},{9,10},{10,... | collective-permute-start | bytes 6152 | tf_op jit(solution)/shard_map/ppermute | solution.py:21
  447.6 27.3 %collective-permute-start.35 = (f32[2,4,2,32]{3,2,1,0:T(2,128)S(1)}, f32[2,4,2,32]{3,2,1,0:T(2,128)S(1)}, u32[]{:S(2)}, u32[]{:S(2)}) collective-permute-start(f32[2,4,2,32]{3,2,1,0:T(2,128)S(1)} %pad_maximum_fusion.4), channel_id=1, source_target_pairs={{0,1},{1,0},{2,3},{3,2},{4,5},{5,4},{6,7},{7,6},{8,9},{9,8},{10,11... | collective-permute-start | bytes 6152 | tf_op jit(solution)/shard_map/ppermute | solution.py:21
  458.1 16.8 %copy-start.32 = (f32[10,2,38,704]{3,2,1,0:T(8,128)S(1)}, f32[10,2,38,704]{3,2,1,0:T(8,128)}, u32[]{:S(2)}) copy-start(f32[10,2,38,704]{3,2,1,0:T(8,128)} %fusion.6) | copy-start | bytes 6420484
  458.1 16.8 %copy-start.34 = (f32[4,2,32,704]{3,2,1,0:T(8,128)S(1)}, f32[4,2,32,704]{3,2,1,0:T(8,128)}, u32[]{:S(2)}) copy-start(f32[4,2,32,704]{3,2,1,0:T(8,128)} %copy-done.33) | copy-start | bytes 2162692
  458.1 16.8 %copy-start.35 = (f32[256,704]{1,0:T(8,128)S(1)}, f32[256,704]{1,0:T(8,128)}, u32[]{:S(2)}) copy-start(f32[256,704]{1,0:T(8,128)} %get-tuple-element.160) | copy-start | bytes 2162692
  464.7 16.9 %collective-permute-start.40 = (bf16[4,352,704]{2,1,0:T(8,128)(2,1)}, bf16[4,352,704]{2,1,0:T(8,128)(2,1)}, u32[]{:S(2)}, u32[]{:S(2)}) collective-permute-start(bf16[4,352,704]{2,1,0:T(8,128)(2,1)} %get-tuple-element.41), channel_id=1, source_target_pairs={{0,16},{16,0},{1,17},{17,1},{2,18},{18,2},{3,19},{19,3},{4,20},{20... | collective-permute-start | bytes 5947400 | tf_op jit(solution)/shard_map/ppermute | solution.py:21
  481.6 7.2 %collective-permute-start.42 = (bf16[7,7,704]{2,1,0:T(8,128)(2,1)S(1)}, bf16[7,7,704]{2,1,0:T(8,128)(2,1)S(1)}, u32[]{:S(2)}, u32[]{:S(2)}) collective-permute-start(bf16[7,7,704]{2,1,0:T(8,128)(2,1)S(1)} %convert_element_type.217), channel_id=1, source_target_pairs={{0,16},{16,0},{1,17},{17,1},{2,18},{18,2},{3,19},{19,3},{4,20},{20... | collective-permute-start | bytes 206984 | tf_op jit(solution)/shard_map/ppermute | solution.py:21
  485.1 61.6 %all-to-all-start.2 = ((bf16[4,352,704]{2,1,0:T(8,128)(2,1)}), bf16[4,352,704]{2,1,0:T(8,128)(2,1)S(1)}, u32[]{:S(2)}, u32[]{:S(2)}) async-start(bf16[4,352,704]{2,1,0:T(8,128)(2,1)} %add_convert_fusion.1), calls=%async_computation.3 | async-start | bytes 4325376 | tf_op jit(solution)/shard_map/all_to_all | solution.py:254
  488.8 5.0 collective-permute-start.43
  493.8 5.4 collective-permute-start.44
  495.1 17.1 %copy-start.41 = (bf16[4,2,32,704]{3,2,1,0:T(8,128)(2,1)S(1)}, bf16[4,2,32,704]{3,2,1,0:T(8,128)(2,1)}, u32[]{:S(2)}) copy-start(bf16[4,2,32,704]{3,2,1,0:T(8,128)(2,1)} %param.9) | copy-start | bytes 1081348
  495.2 17.1 %copy-start.44 = (f32[704]{0:T(1024)S(1)}, f32[704]{0:T(1024)}, u32[]{:S(2)}) copy-start(f32[704]{0:T(1024)} %copy-done.43) | copy-start | bytes 8452
  495.2 17.1 %copy-start.46 = (f32[704]{0:T(1024)S(1)}, f32[704]{0:T(1024)}, u32[]{:S(2)}) copy-start(f32[704]{0:T(1024)} %copy-done.45) | copy-start | bytes 8452
  495.2 8.5 %collective-permute-start.38 = (bf16[3,2,32,704]{3,2,1,0:T(8,128)(2,1)S(1)}, bf16[3,2,32,704]{3,2,1,0:T(8,128)(2,1)S(1)}, u32[]{:S(2)}, u32[]{:S(2)}) collective-permute-start(bf16[3,2,32,704]{3,2,1,0:T(8,128)(2,1)S(1)} %get-tuple-element.168), channel_id=1, source_target_pairs={{0,4},{4,8},{8,12},{1,5},{5,9},{9,13},{2,6},{6,10},{10,14},{3,7},{... | collective-permute-start | bytes 811016 | tf_op jit(solution)/shard_map/ppermute | solution.py:281
  497.9 14.1 %collective-permute-start.39 = (bf16[3,2,32,704]{3,2,1,0:T(8,128)(2,1)S(1)}, bf16[3,2,32,704]{3,2,1,0:T(8,128)(2,1)S(1)}, u32[]{:S(2)}, u32[]{:S(2)}) collective-permute-start(bf16[3,2,32,704]{3,2,1,0:T(8,128)(2,1)S(1)} %get-tuple-element.169), channel_id=1, source_target_pairs={{4,0},{8,4},{12,8},{5,1},{9,5},{13,9},{6,2},{10,6},{14,10},{7,3},{... | collective-permute-start | bytes 811016 | tf_op jit(solution)/shard_map/ppermute | solution.py:282
  520.7 24.7 %collective-permute-start.20 = (bf16[256,704]{1,0:T(8,128)(2,1)S(1)}, bf16[256,704]{1,0:T(8,128)(2,1)}, u32[]{:S(2)}, u32[]{:S(2)}) collective-permute-start(bf16[256,704]{1,0:T(8,128)(2,1)S(1)} %get-tuple-element.165), channel_id=1, source_target_pairs={{0,1},{1,0},{2,3},{3,2},{4,5},{5,4},{6,7},{7,6},{8,9},{9,8},{10,11... | collective-permute-start | bytes 1081352 | tf_op jit(solution)/shard_map/ppermute | solution.py:21
  531.8 22.9 %collective-permute-start.22 = (bf16[256,704]{1,0:T(8,128)(2,1)S(1)}, bf16[256,704]{1,0:T(8,128)(2,1)}, u32[]{:S(2)}, u32[]{:S(2)}) collective-permute-start(bf16[256,704]{1,0:T(8,128)(2,1)S(1)} %get-tuple-element.166), channel_id=1, source_target_pairs={{0,1},{1,0},{2,3},{3,2},{4,5},{5,4},{6,7},{7,6},{8,9},{9,8},{10,11... | collective-permute-start | bytes 1081352 | tf_op jit(solution)/shard_map/ppermute | solution.py:21
  546.6 12.5 %collective-permute-start.21 = (bf16[256,704]{1,0:T(8,128)(2,1)S(1)}, bf16[256,704]{1,0:T(8,128)(2,1)}, u32[]{:S(2)}, u32[]{:S(2)}) collective-permute-start(bf16[256,704]{1,0:T(8,128)(2,1)S(1)} %add_convert_fusion.7), channel_id=1, source_target_pairs={{0,2},{1,3},{2,0},{3,1},{4,6},{5,7},{6,4},{7,5},{8,10},{9,11},{10,... | collective-permute-start | bytes 1081352 | tf_op jit(solution)/shard_map/ppermute | solution.py:21
  (37 other events, 124.2 us)
Sparse Core Ops, SparseCore 0:
  42.4 79.7 all-gather.2
  290.6 105.0 reduce-scatter.1

commit v3 on v2

v3 whole, which is shorter than its diff:
```python
import math

import jax
import jax.numpy as jnp
from jax import lax
from jax.experimental import pallas as pl
from jax.experimental.layout import Layout, with_layout_constraint
from jax.experimental.pallas import tpu as pltpu
from jax.sharding import PartitionSpec as P

epsilon = 1e-06
root_half = 0.7071067811865476
inv_root_tau = 0.3989422804014327
last_last = (((1,), (1,)), ((), ()))
f32 = jnp.float32
bf16 = jnp.bfloat16


def swap(block, axis, bits):
    count = lax.axis_size(axis)
    return lax.ppermute(block, axis, [(i, i ^ bits) for i in range(count)])


def pin(block):
    return with_layout_constraint(block, Layout(tuple(range(block.ndim))))


def after(blocks, *earlier):
    kept, _ = lax.optimization_barrier((blocks, earlier))
    return kept


def first_hops(block, every=False):
    count = lax.axis_size("col")
    bits = range(1, count) if every else [1 << i for i in range((count - 1).bit_length())]
    return {bit: pin(swap(block, "col", bit)) for bit in bits}


def gather_cols(block, hops):
    held = {0: pin(block)} | hops
    count = lax.axis_size("col")
    for m in sorted(range(1, count), key=lambda m: m.bit_count()):
        if m not in held:
            held[m] = pin(swap(held[m & (m - 1)], "col", m & -m))
    return [held[m] for m in range(count)]


def stack_cols(blocks):
    return [pin(jnp.stack([blocks[m] for m in side])) for side in col_order(len(blocks))]


def gather_rows(block, bits):
    held = {0: block}
    for bit in bits:
        held.update({q ^ bit: pin(swap(held[q], "row", bit)) for q in list(held)})
    return [held[q] for q in range(lax.axis_size("row"))]


def row_bits():
    return [1 << i for i in range((lax.axis_size("row") - 1).bit_length())]


def col_order(count):
    held, step = [0], count // 2
    while step > 1:
        held = held + [m ^ step for m in held]
        step //= 2
    return held, [m ^ 1 for m in held]


def halve_sum(near, far, axis, bits, earlier=()):
    for place, bit in enumerate(bits):
        got = swap(pin(far.astype(bf16)), axis, bit)
        if earlier:
            got = after(got, *earlier)
        total = near.astype(f32) + got.astype(f32)
        half = total.shape[0] // 2
        near, far = total[:half], total[half:]
    return total[0]


VMEM_BYTES = 44 * 2**20
in_vmem = pl.BlockSpec(memory_space=pltpu.VMEM)
in_smem = pl.BlockSpec(memory_space=pltpu.SMEM)


def call(body, outs, places, *operands):
    return pl.pallas_call(
        body,
        out_shape=outs,
        in_specs=[in_smem] + [in_vmem] * len(operands),
        out_specs=[in_vmem] * len(outs),
        compiler_params=pltpu.CompilerParams(vmem_limit_bytes=VMEM_BYTES),
        cost_estimate=pl.CostEstimate(flops=0, bytes_accessed=0, transcendentals=0),
    )(places, *operands)


def shape_of(dims, dtype):
    return jax.ShapeDtypeStruct(dims, dtype)


def piece_of(refs, places, rows, q, m):
    half = refs[-1].shape[-3] if len(refs) > 1 else refs[0].shape[1] // 2
    side, place = m // half, m % half
    if len(refs) == 1:
        return refs[0][places[0] ^ q, m]
    return refs[side * rows + q][place]


def cut_units(w, out, count):
    share = w.shape[1] // count
    for j in range(count):
        out[j] = w[:, j * share : (j + 1) * share]


def prepare(places, images, cotangent, w_in, reach):
    height, batch, width, chans = cotangent.shape
    count = lax.axis_size("col")
    span = height * width

    def body(places, images, cot, w_in, pieces, turned, low, high):
        cut_units(w_in, pieces, count)
        for b in range(batch):
            turned[:, b * span : (b + 1) * span] = cot[:, b].reshape(span, chans).T
        low[...] = images[height - reach :]
        high[...] = images[:reach]

    edge = shape_of((reach, batch, width, chans), bf16)
    outs = [
        shape_of((count, chans, w_in.shape[1] // count), bf16),
        shape_of((chans, batch * span), bf16),
        edge,
        edge,
    ]
    return call(body, outs, places, images, cotangent, w_in)


def prepare_out(places, w_out_turned):
    count = lax.axis_size("col")
    chans, units = w_out_turned.shape

    def body(places, w, pieces):
        cut_units(w, pieces, count)

    return call(body, [shape_of((count, chans, units // count), bf16)], places, w_out_turned)[0]


def join_weights(places, mine, other):
    count, chans, share = mine.shape
    units = 2 * share
    order = sum(col_order(count), [])

    def body(places, mine, other, out, turned):
        for place, m in enumerate(order):
            j = places[1] ^ m
            both = jnp.concatenate([mine[j], other[j]], axis=1)
            turned[place] = both
            out[place] = both.T

    outs = [shape_of((count, units, chans), bf16), shape_of((count, chans, units), bf16)]
    return call(body, outs, places, mine, other)


def image_sums(value, batch):
    span = value.shape[1] // batch
    return [jnp.sum(value[:, b * span : (b + 1) * span], axis=1, keepdims=True) for b in range(batch)]


def hidden_kernel(places, pieces, weights, bias, dims):
    rows, batch, pixels = dims
    count, units, chans = weights.shape

    def body(places, *refs):
        xs = refs[: len(pieces)]
        w, b, act, slope, square = refs[len(pieces) :]
        total = jnp.zeros((units, batch), f32)
        for q in range(rows):
            pre = b[...]
            for m in range(count):
                pre = pre + jnp.dot(w[m], piece_of(xs, places, rows, q, m), preferred_element_type=f32)
            cumul = 0.5 * (1.0 + lax.erf(pre * root_half))
            value = pre * cumul
            part = slice(q * pixels, (q + 1) * pixels)
            act[:, part] = value
            slope[:, part] = cumul + pre * jnp.exp(-0.5 * pre * pre) * inv_root_tau
            total = total + jnp.concatenate(image_sums(value * value, batch), axis=1)
        square[...] = total

    full = (units, rows * pixels)
    return call(
        body,
        [shape_of(full, f32), shape_of(full, f32), shape_of((units, batch), f32)],
        places,
        *pieces,
        weights,
        bias[:, None],
    )


def back_kernel(places, pieces, weights, act, dims):
    rows, batch, pixels = dims
    count, units, chans = weights.shape

    def body(places, *refs):
        xs = refs[: len(pieces)]
        w, act, grad, pull = refs[len(pieces) :]
        total = jnp.zeros((units, batch), f32)
        for q in range(rows):
            value = jnp.zeros((units, pixels), f32)
            for m in range(count):
                value = value + jnp.dot(
                    w[m], piece_of(xs, places, rows, q, m), preferred_element_type=f32
                )
            part = slice(q * pixels, (q + 1) * pixels)
            grad[:, part] = value
            total = total + jnp.concatenate(image_sums(value * act[:, part], batch), axis=1)
        pull[...] = total

    return call(
        body,
        [shape_of(act.shape, f32), shape_of((units, batch), f32)],
        places,
        *pieces,
        weights,
        act,
    )


def project_kernel(places, made_of, operands, turned, dims, splits):
    rows, batch, pixels = dims
    count, chans, units = turned.shape
    half = count // 2

    def body(places, *refs):
        ins = refs[: len(operands)]
        w, kept = refs[len(operands) : len(operands) + 2]
        outs = refs[len(operands) + 2 :]

        def spread(vectors):
            span = (units, pixels // batch)
            return jnp.concatenate(
                [jnp.broadcast_to(vectors[:, b : b + 1], span) for b in range(batch)], axis=1
            )

        for q in range(rows):
            part = slice(q * pixels, (q + 1) * pixels)
            blocks = [r[:, part] if r.shape[1] == rows * pixels else r[...] for r in ins]
            made = made_of(blocks, spread).astype(bf16)
            kept[:, part] = made
            for m in range(count):
                value = jnp.dot(w[m], made, preferred_element_type=f32).astype(bf16)
                if not splits:
                    outs[0][places[0] ^ q, m] = value
                else:
                    side, place = m // half, m % half
                    bit = splits[side]
                    kind = 1 if q & bit else 0
                    outs[2 * side + kind][queue[side].index(q & ~bit), place] = value

    queue = [sorted({q & ~bit for q in range(rows)}) for bit in splits or []]
    if not splits:
        outs = [shape_of((rows, count, chans, pixels), bf16)]
    else:
        outs = [shape_of((rows // 2, half, chans, pixels), bf16)] * 4
    got = call(
        body, [shape_of((units, rows * pixels), bf16)] + outs, places, *operands, turned
    )
    return got[0], got[1:]


def grads_kernel(places, left, pieces, dims, count, chans):
    rows, batch, pixels = dims
    units = left.shape[0]
    share = units // 2
    order = sum(col_order(count), [])

    def body(places, left, *refs):
        xs = refs[: len(pieces)]
        mine, other = refs[len(pieces) :]
        for place, m in enumerate(order):
            x = jnp.concatenate([piece_of(xs, places, rows, q, place) for q in range(rows)], axis=1)
            value = lax.dot_general(x, left[...], last_last, preferred_element_type=f32).astype(bf16)
            mine[places[1] ^ m] = value[:, :share]
            other[places[1] ^ m] = value[:, share:]

    return call(body, [shape_of((count, chans, share), bf16)] * 2, places, left, *pieces)


def add_kernel(places, mine, got):
    def body(places, mine, got, out):
        for j in range(mine.shape[0]):
            out[j] = (mine[j].astype(f32) + got[j].astype(f32)).astype(bf16)

    return call(body, [shape_of(mine.shape, bf16)], places, mine, got)[0]


def finish_kernel(places, pieces, scale):
    count, chans, share = pieces.shape

    def body(places, pieces, out):
        wide = jnp.concatenate([pieces[j].astype(f32) for j in range(count)], axis=1)
        out[...] = wide * scale

    return call(body, [shape_of((chans, count * share), f32)], places, pieces)[0]


def own_units(vector):
    count = lax.axis_size("col")
    span = vector.shape[0] // 2
    share = span // count
    me = lax.axis_index("col")
    side = lax.axis_index("dp")
    mine = lax.dynamic_slice_in_dim(vector, side * span + me * share, share)
    other = lax.dynamic_slice_in_dim(vector, (1 - side) * span + me * share, share)
    return jnp.concatenate([mine, other])


def add_over(value, axis):
    n = lax.axis_size(axis)
    step = 1
    while step < n:
        value = value + swap(value, axis, step)
        step *= 2
    return value


def exchange_rows(low, high):
    count = lax.axis_size("row")
    forward = [(i, i + 1) for i in range(count - 1)]
    backward = [(i + 1, i) for i in range(count - 1)]
    return lax.ppermute(low, "row", forward), lax.ppermute(high, "row", backward)


EDGE = 8


def fill_padded(padded, low, mid, high):
    reach, height, width = low.shape[0], mid.shape[0], mid.shape[2]
    zeros = jnp.zeros(padded.shape[:2] + (EDGE, padded.shape[3]), f32)
    padded[:, :, :EDGE, :] = zeros
    padded[:, :, EDGE + width :, :] = zeros
    padded[:reach, :, EDGE : EDGE + width, :] = low[...].astype(f32)
    padded[reach : reach + height, :, EDGE : EDGE + width, :] = mid[...].astype(f32)
    padded[reach + height :, :, EDGE : EDGE + width, :] = high[...].astype(f32)


def lane_chunks(chans):
    return [slice(c, min(c + 128, chans)) for c in range(0, chans, 128)]


def depthwise(places, low, mid, high, kernel, extra, flip):
    height, batch, width, chans = mid.shape
    span = kernel.shape[0]
    reach = span // 2

    def body(places, low, mid, high, kern, *refs):
        out, padded = refs[-2:]
        fill_padded(padded, low, mid, high)

        @pl.loop(0, batch)
        def _(b):
            for lanes in lane_chunks(chans):
                sums = [None] * height
                for r in range(height + 2 * reach):
                    for j in range(span):
                        start = EDGE + j - reach
                        window = padded[r, b, start : start + width, lanes]
                        for h in range(max(0, r - span + 1), min(height, r + 1)):
                            i = r - h
                            tap = (span - 1 - i, span - 1 - j) if flip else (i, j)
                            term = kern[tap[0], tap[1] : tap[1] + 1, lanes] * window
                            sums[h] = term if sums[h] is None else sums[h] + term
                for h in range(height):
                    value = sums[h]
                    if extra is not None:
                        value = value + refs[0][h, b, :, lanes].astype(f32)
                    out[h, b, :, lanes] = value.astype(out.dtype)

    more = [] if extra is None else [extra]
    operands = [low, mid, high, kernel] + more
    return pl.pallas_call(
        body,
        out_shape=shape_of(mid.shape, f32 if extra is None else bf16),
        in_specs=[in_smem] + [in_vmem] * len(operands),
        out_specs=in_vmem,
        scratch_shapes=[pltpu.VMEM((height + 2 * reach, batch, width + 2 * EDGE, chans), f32)],
        compiler_params=pltpu.CompilerParams(vmem_limit_bytes=VMEM_BYTES),
        cost_estimate=pl.CostEstimate(flops=0, bytes_accessed=0, transcendentals=0),
    )(places, *operands)


def kernel_terms(places, low, mid, high, grad, span):
    height, batch, width, chans = mid.shape
    reach = span // 2

    def body(places, low, mid, high, grad, out, padded, sums):
        fill_padded(padded, low, mid, high)
        for lanes in lane_chunks(chans):
            for i in range(span):

                def step(b, total):
                    total = list(total)
                    for h in range(height):
                        piece = grad[h, b, :, lanes]
                        for j in range(span):
                            start = EDGE + j - reach
                            both = piece * padded[h + i, b, start : start + width, lanes]
                            total[j] = total[j] + jnp.sum(both.reshape(-1, 8, both.shape[1]), axis=0)
                    return tuple(total)

                zero = jnp.zeros((8, lanes.stop - lanes.start), f32)
                total = lax.fori_loop(0, batch, step, (zero,) * span)
                for j in range(span):
                    sums[i, j, :, lanes] = total[j]
        for i in range(span):
            out[i] = jnp.sum(sums[i], axis=1)

    operands = [low, mid, high, grad]
    return pl.pallas_call(
        body,
        out_shape=shape_of((span, span, chans), f32),
        in_specs=[in_smem] + [in_vmem] * len(operands),
        out_specs=in_vmem,
        scratch_shapes=[
            pltpu.VMEM((height + 2 * reach, batch, width + 2 * EDGE, chans), f32),
            pltpu.VMEM((span, span, 8, chans), f32),
        ],
        compiler_params=pltpu.CompilerParams(vmem_limit_bytes=VMEM_BYTES),
        cost_estimate=pl.CostEstimate(flops=0, bytes_accessed=0, transcendentals=0),
    )(places, *operands)


def local(images, cotangent, kernel, w_in, b_in, grn_gamma, grn_beta, w_out):
    height, batch, width, chans = images.shape
    span = kernel.shape[0]
    reach = span // 2
    col_count = lax.axis_size("col")
    row_count = lax.axis_size("row")
    all_chans = chans * col_count
    all_units = b_in.shape[0] * row_count
    pixels = height * batch * width
    group_pix = pixels * row_count
    scale_grad = 1.0 / math.sqrt(group_pix * lax.axis_size("dp"))

    places = jnp.stack([lax.axis_index("row"), lax.axis_index("col")]).astype(jnp.int32)
    dims = (row_count, batch, pixels)

    def turned(tile):
        return tile.transpose(3, 1, 0, 2).reshape(chans, pixels)

    def natural(block):
        return block.reshape(chans, batch, height, width).transpose(2, 1, 3, 0)


    pieces, cot_turned, low, high = prepare(places, images, cotangent, w_in, reach)
    cot_hops = first_hops(cot_turned, True)
    mine = lax.all_to_all(pieces, "col", 0, 0)
    w_in_all, w_in_turned = join_weights(places, mine, swap(mine, "dp", 1))
    w_in_there = mine
    low, high = exchange_rows(low, high)
    bias, gamma, beta = own_units(b_in), own_units(grn_gamma), own_units(grn_beta)

    conv_out = depthwise(places, low, images, high, kernel, None, False)
    mean_own = jnp.mean(conv_out, axis=-1)
    dev_own = conv_out - mean_own[..., None]
    stats = jnp.stack([mean_own, jnp.sum(dev_own * dev_own, axis=-1)])
    stats = after(stats, cot_hops)
    cot_cols = gather_cols(cot_turned, cot_hops)
    stats = [stats] + [swap(stats, "col", m) for m in range(1, col_count)]
    stats = after(stats, w_in_there)
    mean_pix = sum(s[0] for s in stats) / col_count
    var_pix = sum(s[1] + chans * (s[0] - mean_pix) ** 2 for s in stats) / all_chans
    inv_std = lax.rsqrt(var_pix + epsilon)[..., None]
    standard = (conv_out - mean_pix[..., None]) * inv_std
    bits = row_bits()
    normed = turned(standard.astype(bf16))
    normed_cols = gather_cols(normed, first_hops(normed))
    even, odd = stack_cols(normed_cols)
    normed_all = gather_rows(even, bits) + gather_rows(odd, bits[::-1])
    cot_all = [pin(lax.all_gather(pin(jnp.concatenate(stack_cols(cot_cols))), "row"))]
    pieces = after(prepare_out(places, w_out.T), normed_cols)
    w_out_there = lax.all_to_all(pieces, "col", 0, 0)
    act, slope, square = hidden_kernel(places, normed_all, w_in_all, bias, dims)
    w_out_there = after(w_out_there, normed_all)
    w_out_all, w_out_turned = join_weights(places, w_out_there, swap(w_out_there, "dp", 1))
    norm_chan = jnp.sqrt(square + epsilon)
    norm_sum = add_over(add_over(jnp.sum(norm_chan, axis=0), "row"), "col")
    denom = norm_sum / all_units + epsilon
    gamma, beta = gamma[:, None], beta[:, None]
    gain = gamma * (norm_chan / denom) + 1.0
    grad_gated, pull = back_kernel(places, cot_all, w_out_all, act, dims)
    share_back = gamma * pull / denom / norm_chan

    grad_pre, grad_parts = project_kernel(
        places,
        lambda b, spread: (b[0] * spread(b[3]) + b[1] * spread(b[4])) * b[2],
        [grad_gated, act, slope, gain, share_back],
        w_in_turned,
        dims,
        (bits[0], bits[-1]),
    )
    gated, out_parts = project_kernel(
        places,
        lambda b, spread: b[0] * spread(b[1]) + b[2],
        [act, gain, beta],
        w_out_turned,
        dims,
        (),
    )
    w_in_mine, w_in_other = grads_kernel(places, grad_pre, normed_all, dims, col_count, chans)
    w_out_mine, w_out_other = grads_kernel(places, gated, cot_all, dims, col_count, chans)
    w_out_sums = add_kernel(places, w_out_mine, swap(w_out_other, "dp", 1))
    w_out_back = lax.all_to_all(w_out_sums, "col", 0, 0)
    w_out_grad = finish_kernel(places, w_out_back, scale_grad).T
    w_in_sums = add_kernel(places, w_in_mine, swap(w_in_other, "dp", 1))

    near_a, far_a, near_b, far_b = grad_parts
    even = halve_sum(near_a, far_a, "row", bits, (w_in_other,))
    odd = halve_sum(near_b, far_b, "row", bits[::-1], (w_in_other,))
    down = [1 << i for i in range((col_count - 1).bit_length())]
    branch_rows = pin(
        lax.psum_scatter(
            pin(after(out_parts[0], even, odd).reshape(-1, pixels)), "row", scatter_dimension=0, tiled=True
        )
    ).reshape(col_count, chans, pixels)
    odd = after(odd, w_out_back)
    grad_normed = natural(pin(halve_sum(even, odd, "col", down)))

    sums = jnp.stack([jnp.sum(grad_normed, axis=-1), jnp.sum(grad_normed * standard, axis=-1)])
    sums = sum([swap(sums, "col", m) for m in range(1, col_count)], sums) / all_chans
    branch_rows = after(branch_rows, sums)
    w_in_sums = after(w_in_sums, sums)
    w_in_grad = finish_kernel(places, lax.all_to_all(w_in_sums, "col", 0, 0), scale_grad)
    grad_conv = inv_std * (grad_normed - sums[0][..., None] - standard * sums[1][..., None])
    edge = grad_conv.astype(bf16)
    low_grad, high_grad = exchange_rows(edge[height - reach :], edge[:reach])
    x_grad = depthwise(places, low_grad, grad_conv, high_grad, kernel, cotangent, True)
    kern = kernel_terms(places, low, images, high, after(grad_conv, low_grad, high_grad), span)
    steps = [("dp", 1)] + [("row", 1 << i) for i in range((row_count - 1).bit_length())]
    for axis, step in steps:
        kern = kern.astype(bf16)
        kern = kern.astype(f32) + swap(kern, axis, step).astype(f32)
    kernel_grad = kern * scale_grad
    branch = halve_sum(branch_rows[: col_count // 2], branch_rows[col_count // 2 :], "col", down, (x_grad, kern))
    branch = natural(pin(branch))
    result = (images.astype(f32) + branch.astype(f32)).astype(bf16)
    return (result, x_grad, w_in_grad, w_out_grad, kernel_grad)


def solution(mesh):
    return jax.shard_map(
        local,
        mesh=mesh,
        in_specs=(
            P("row", "dp", None, "col"),
            P("row", "dp", None, "col"),
            P(None, None, "col"),
            P("col", ("row", "dp")),
            P("row"),
            P("row"),
            P("row"),
            P(("row", "dp"), "col"),
        ),
        out_specs=(
            P("row", "dp", None, "col"),
            P("row", "dp", None, "col"),
            P("col", ("row", "dp")),
            P(("row", "dp"), "col"),
            P(None, None, "col"),
        ),
        check_vma=False,
    )
```

time: 577 us -> 498 us (0.86)
  other arithmetic: 76.9 us -> 23 us
  local copies, waits for them, and re-layouts: 100 us -> 46.3 us
  Pallas kernels: 57.8 us -> 96.5 us
  waiting for transfers between devices: 245 us -> 226 us
  starting transfers between devices: 73.3 us -> 84.5 us
    ppermute x12 -> x0, local copies, waits for them, and re-layouts: 26.4 us -> none  [swap(): return lax.ppermute(block, axis, [(i, i ^ bits) for i in range(count)])]
    reduce_sum x1, other arithmetic: 25.4 us -> 0.12 us  [local(): mean_own = jnp.mean(conv_out, axis=-1)]
    convert_element_type x11 -> x2, other arithmetic: 24.7 us -> 1.55 us  [the longest x1 1.47 us: local(): edge = grad_conv.astype(bf16)]
    pallas_call x0 -> x3, Pallas kernels: none -> 21.7 us  [the longest x2 14.9 us: depthwise(): pl.pallas_call(body, out_shape=shape_of(mid.shape, f32 if extra is None e...]
    pallas_call x8 -> x14, Pallas kernels: 57.8 us -> 74.9 us  [call(): pl.pallas_call(body, out_shape=outs, in_specs=[in_smem] + [in_vmem] * len...]
    all_to_all x4, waiting for transfers between devices: 14.2 us -> 0.01 us  [the longest x1 0.01 us: local(): mine = lax.all_to_all(pieces, 'col', 0, 0)]
    ppermute x41 -> x37, starting transfers between devices: 46.1 us -> 56.6 us  [swap(): return lax.ppermute(block, axis, [(i, i ^ bits) for i in range(count)])]
    all_gather x1 -> x0, local copies, waits for them, and re-layouts: 8.59 us -> none  [local(): cot_all = [lax.all_gather(cot_cols, 'row')]]
  transfers between devices with their start and end apart: 51 -> 47, of which waited for: 27 -> 26; matrix products, arithmetic and copies ran while one was open for 24% -> 6% of each run, Pallas kernels for 7% -> 14%
where the time goes in v3:
time: 498 us; the launch traced here: 492 us
  waiting for transfers between devices  226 us (45%)
  Pallas kernels  96.5 us (19%)
  starting transfers between devices  84.5 us (17%)
  local copies, waits for them, and re-layouts  46.3 us (9%)
  other arithmetic  23 us (5%)
  between operations  15.2 us (3%)
    ppermute x37, waiting for transfers between devices, swap(): return lax.ppermute(block, axis, [(i, i ^ bits) for i in range(count)])  192 us
    pallas_call x14, Pallas kernels, call(): pl.pallas_call(body, out_shape=outs, in_specs=[in_smem] + [in_vmem] * len...  74.9 us
    ppermute x37, starting transfers between devices, swap(): return lax.ppermute(block, axis, [(i, i ^ bits) for i in range(count)])  56.6 us
    unnamed x131, local copies, waits for them, and re-layouts  33.9 us
    ppermute x2, waiting for transfers between devices, exchange_rows(): lax.ppermute(high, 'row', backward)  21 us
    pallas_call x2, Pallas kernels, depthwise(): pl.pallas_call(body, out_shape=shape_of(mid.shape, f32 if extra is None e...  14.9 us
    ppermute x2, waiting for transfers between devices, exchange_rows(): lax.ppermute(low, 'row', forward)  12.6 us
  transfers between devices with their start and end apart: 47, of which 26 were waited for; matrix products, arithmetic and copies ran while one was open for 6% of the time, Pallas kernels for 14%

profile of v3, /device:TPU:0, one launch (start us, length us, event | category | flops | bytes accessed | tf_op | source)
XLA Modules:
  0.0 491.7 jit_solution(11750881241869615595)
XLA Ops:
  14.2 3.0 collective-permute-start.2
  17.2 2.6 collective-permute-start.3
  19.8 5.1 %all-to-all-start = ((bf16[4,704,352]{2,1,0:T(8,128)(2,1)}), bf16[4,704,352]{2,1,0:T(8,128)(2,1)S(1)}, u32[]{:S(2)}, u32[]{:S(2)}) async-start(bf16[4,704,352]{2,1,0:T(8,128)(2,1)} %copy-done.41), calls=%async_computation | async-start | bytes 4325376 | tf_op jit(solution)/shard_map/all_to_all | solution.py:457
  24.9 8.5 %collective-permute-done.2 = bf16[704,256]{1,0:T(8,128)(2,1)S(1)} collective-permute-done((bf16[704,256]{1,0:T(8,128)(2,1)S(1)}, bf16[704,256]{1,0:T(8,128)(2,1)S(1)}, u32[]{:S(2)}, u32[]{:S(2)}) %collective-permute-start.2) | collective-permute-done | bytes 360480 | tf_op jit(solution)/shard_map/ppermute | solution.py:21
  33.4 23.2 %collective-permute-done.3 = bf16[704,256]{1,0:T(8,128)(2,1)} collective-permute-done((bf16[704,256]{1,0:T(8,128)(2,1)S(1)}, bf16[704,256]{1,0:T(8,128)(2,1)}, u32[]{:S(2)}, u32[]{:S(2)}) %collective-permute-start.3) | collective-permute-done | bytes 360480 | tf_op jit(solution)/shard_map/ppermute | solution.py:21
  56.6 2.5 maximum_maximum_fusion
  59.1 3.4 collective-permute-start
  63.9 3.2 collective-permute-done.low
  67.1 5.0 %collective-permute-done.1.high = bf16[3,2,32,704]{3,2,1,0:T(8,128)(2,1)S(1)} collective-permute-done((bf16[3,2,32,704]{3,2,1,0:T(8,128)(2,1)S(1)}, bf16[3,2,32,704]{3,2,1,0:T(8,128)(2,1)S(1)}, u32[]{:S(2)}, u32[]{:S(2)}) %collective-permute-start.1) | collective-permute-done | bytes 270368 | tf_op jit(solution)/shard_map/ppermute | solution.py:331
  72.1 6.9 %shard_map.120 = f32[4,2,32,704]{3,2,1,0:T(8,128)S(1)} custom-call(s32[2]{0:T(128)S(1)} %pad_add_fusion.places, bf16[3,2,32,704]{3,2,1,0:T(8,128)(2,1)S(1)} %collective-permute-done.low, bf16[4,2,32,704]{3,2,1,0:T(8,128)(2,1)S(1)} %copy-done.14, bf16[3,2,32,704]{3,2,1,0:T(8,128)(2,1)S(1)} %collective-permute-done.1.high, f32[7,7,704]{2,1,0:T(8,128)S(1)} %copy-done.52), custom_call_target="tpu_custom_call" | custom-call | tf_op jit(solution)/shard_map/pallas_call | solution.py:381
  80.9 19.9 %collective-permute-start.5 = (f32[2,4,2,32]{3,2,1,0:T(2,128)S(1)}, f32[2,4,2,32]{3,2,1,0:T(2,128)S(1)}, u32[]{:S(2)}, u32[]{:S(2)}) collective-permute-start(f32[2,4,2,32]{3,2,1,0:T(2,128)S(1)} %pad_maximum_fusion.2), channel_id=1, source_target_pairs={{0,1},{1,0},{2,3},{3,2},{4,5},{5,4},{6,7},{7,6},{8,9},{9,8},{10,11... | collective-permute-start | bytes 6152 | tf_op jit(solution)/shard_map/ppermute | solution.py:21
  100.8 2.4 collective-permute-start.7
  103.2 4.6 collective-permute-done.6
  108.8 1.9 copy.27
  112.3 11.0 %collective-permute-done.8 = bf16[704,256]{1,0:T(8,128)(2,1)S(1)} collective-permute-done((bf16[704,256]{1,0:T(8,128)(2,1)}, bf16[704,256]{1,0:T(8,128)(2,1)S(1)}, u32[]{:S(2)}, u32[]{:S(2)}) %collective-permute-start.8) | collective-permute-done | bytes 360480 | tf_op jit(solution)/shard_map/ppermute | solution.py:21
  127.4 3.3 collective-permute-done.13
  130.8 4.9 %all-to-all-start.1 = ((bf16[4,704,352]{2,1,0:T(8,128)(2,1)}), bf16[4,704,352]{2,1,0:T(8,128)(2,1)}, u32[]{:S(2)}, u32[]{:S(2)}) async-start(bf16[4,704,352]{2,1,0:T(8,128)(2,1)} %copy-done.4), calls=%async_computation.1 | async-start | bytes 4325376 | tf_op jit(solution)/shard_map/all_to_all | solution.py:482
  139.7 2.0 collective-permute-start.10
  143.1 12.9 %collective-permute-done.9.refs_1_ = bf16[2,704,256]{2,1,0:T(8,128)(2,1)S(1)} collective-permute-done((bf16[2,704,256]{2,1,0:T(8,128)(2,1)S(1)}, bf16[2,704,256]{2,1,0:T(8,128)(2,1)S(1)}, u32[]{:S(2)}, u32[]{:S(2)}) %collective-permute-start.9) | collective-permute-done | bytes 720928 | tf_op jit(solution)/shard_map/ppermute | solution.py:21
  160.1 14.0 %collective-permute-done.10.refs_2_ = bf16[2,704,256]{2,1,0:T(8,128)(2,1)S(1)} collective-permute-done((bf16[2,704,256]{2,1,0:T(8,128)(2,1)S(1)}, bf16[2,704,256]{2,1,0:T(8,128)(2,1)S(1)}, u32[]{:S(2)}, u32[]{:S(2)}) %collective-permute-start.10) | collective-permute-done | bytes 720928 | tf_op jit(solution)/shard_map/ppermute | solution.py:21
  176.0 9.1 %collective-permute-done.11.refs_3_ = bf16[2,704,256]{2,1,0:T(8,128)(2,1)S(1)} collective-permute-done((bf16[2,704,256]{2,1,0:T(8,128)(2,1)S(1)}, bf16[2,704,256]{2,1,0:T(8,128)(2,1)S(1)}, u32[]{:S(2)}, u32[]{:S(2)}) %collective-permute-start.11) | collective-permute-done | bytes 720928 | tf_op jit(solution)/shard_map/ppermute | solution.py:21
  189.9 5.4 %shard_map.121 = (bf16[4,704,704]{2,1,0:T(8,128)(2,1)S(1)}, bf16[4,704,704]{2,1,0:T(8,128)(2,1)}) custom-call(s32[2]{0:T(128)S(1)} %pad_add_fusion.places, bf16[4,704,352]{2,1,0:T(8,128)(2,1)S(1)} %all-to-all-done.mine, bf16[4,704,352]{2,1,0:T(8,128)(2,1)} %collective-permute-done.17.other), custom_call_target="tpu_custom_call" | custom-call | tf_op jit(solution)/shard_map/pallas_call | solution.py:88
  195.3 2.1 copy-done.17
  198.6 9.2 %shard_map.122 = (f32[704,1024]{1,0:T(8,128)S(1)}, f32[704,1024]{1,0:T(8,128)}, f32[704,2]{1,0:T(8,128)S(1)}) custom-call(s32[2]{0:T(128)S(1)} %pad_add_fusion.places, bf16[2,704,256]{2,1,0:T(8,128)(2,1)S(1)} %copy-done.8, bf16[2,704,256]{2,1,0:T(8,128)(2,1)S(1)} %copy-done.22, bf16[2,704,256]{2,1,0:T(8,128)(2,1)S(1)} %copy-done.28, ...), custom_call_target="tpu_custom_call" | custom-call | tf_op jit(solution)/shard_map/pallas_call | solution.py:88
  210.1 3.1 collective-permute-done.18
  213.1 1.7 collective-permute-start.19
  214.9 1.8 collective-permute-done.19
  218.3 1.9 collective-permute-done.20
  220.2 2.5 collective-permute-start.21
  222.7 1.9 collective-permute-done.21
  224.7 6.0 %shard_map.124 = (bf16[4,704,704]{2,1,0:T(8,128)(2,1)S(1)}, bf16[4,704,704]{2,1,0:T(8,128)(2,1)}) custom-call(s32[2]{0:T(128)S(1)} %pad_add_fusion.places, bf16[4,704,352]{2,1,0:T(8,128)(2,1)} %all-to-all-done.1.mine, bf16[4,704,352]{2,1,0:T(8,128)(2,1)} %collective-permute-done.22.other), custom_call_target="tpu_custom_call" | custom-call | tf_op jit(solution)/shard_map/pallas_call | solution.py:88
  230.7 2.0 copy-done.15
  232.7 1.8 copy-done.1
  234.5 9.1 %shard_map.126 = (f32[704,1024]{1,0:T(8,128)S(1)}, f32[704,2]{1,0:T(8,128)S(1)}) custom-call(s32[2]{0:T(128)S(1)} %pad_add_fusion.places, bf16[4,4,704,256]{3,2,1,0:T(8,128)(2,1)} %bitcast.127, bf16[4,704,704]{2,1,0:T(8,128)(2,1)} %copy-done.15, f32[704,1024]{1,0:T(8,128)S(1)} %copy-done.1), custom_call_target="tpu_custom_call" | custom-call | tf_op jit(solution)/shard_map/pallas_call | solution.py:88
  244.8 8.2 %shard_map.125 = (bf16[704,1024]{1,0:T(8,128)(2,1)S(1)}, bf16[4,4,704,256]{3,2,1,0:T(8,128)(2,1)}) custom-call(s32[2]{0:T(128)S(1)} %pad_add_fusion.places, f32[704,1024]{1,0:T(8,128)S(1)} %copy-done.1, f32[704,2]{1,0:T(8,128)S(1)} %get-tuple-element.110.refs_1_.refs_3_, f32[704,1]{1,0:T(8,128)S(1)} %copy-done.46, bf16[4,704,704]{2,1,0:T(8,128)(2,1)S(1)} %copy-done.16), custom_call_target="tpu_custom_call" | custom-call | tf_op jit(solution)/shard_map/pallas_call | solution.py:88
  253.0 7.4 %shard_map.129 = (bf16[4,704,352]{2,1,0:T(8,128)(2,1)S(1)}, bf16[4,704,352]{2,1,0:T(8,128)(2,1)S(1)}) custom-call(s32[2]{0:T(128)S(1)} %pad_add_fusion.places, bf16[704,1024]{1,0:T(8,128)(2,1)S(1)} %get-tuple-element.79.left, bf16[4,4,704,256]{3,2,1,0:T(8,128)(2,1)} %bitcast.128), custom_call_target="tpu_custom_call" | custom-call | tf_op jit(solution)/shard_map/pallas_call | solution.py:88
  260.5 4.2 collective-permute-done.27.got
  267.2 4.7 all-to-all-start.2
  274.2 9.8 %shard_map.127 = (bf16[704,1024]{1,0:T(8,128)(2,1)S(1)}, bf16[2,2,704,256]{3,2,1,0:T(8,128)(2,1)S(1)}, bf16[2,2,704,256]{3,2,1,0:T(8,128)(2,1)S(1)}, bf16[2,2,70...) custom-call(s32[2]{0:T(128)S(1)} %pad_add_fusion.places, f32[704,1024]{1,0:T(8,128)} %copy-done.20, ...), custom_call_target="tpu_custom_call" | custom-call | tf_op jit(solution)/shard_map/pallas_call | solution.py:88
  284.0 1.8 collective-permute-start.25
  286.3 6.6 %shard_map.128 = (bf16[4,704,352]{2,1,0:T(8,128)(2,1)S(1)}, bf16[4,704,352]{2,1,0:T(8,128)(2,1)}) custom-call(s32[2]{0:T(128)S(1)} %pad_add_fusion.places, bf16[704,1024]{1,0:T(8,128)(2,1)S(1)} %get-tuple-element.70.left, bf16[2,704,256]{2,1,0:T(8,128)(2,1)S(1)} %copy-done.9, bf16[2,704,256]{2,1,0:T(8,128)(2,1)S(1)} %copy-done.23, ...), custom_call_target="tpu_custom_call" | custom-call | tf_op jit(solution)/shard_map/pallas_call | solution.py:88
  293.0 24.5 %collective-permute-done.25 = bf16[2,2,704,256]{3,2,1,0:T(8,128)(2,1)} collective-permute-done((bf16[2,2,704,256]{3,2,1,0:T(8,128)(2,1)S(1)}, bf16[2,2,704,256]{3,2,1,0:T(8,128)(2,1)}, u32[]{:S(2)}, u32[]{:S(2)}) %collective-permute-start.25) | collective-permute-done | bytes 1441824 | tf_op jit(solution)/shard_map/ppermute | solution.py:21
  322.6 1.7 collective-permute-start.24
  324.3 12.1 %collective-permute-done.26 = bf16[1,2,704,256]{3,2,1,0:T(8,128)(2,1)S(1)} collective-permute-done((bf16[1,2,704,256]{3,2,1,0:T(8,128)(2,1)S(1)}, bf16[1,2,704,256]{3,2,1,0:T(8,128)(2,1)S(1)}, u32[]{:S(2)}, u32[]{:S(2)}) %collective-permute-start.26) | collective-permute-done | bytes 720928 | tf_op jit(solution)/shard_map/ppermute | solution.py:21
  339.7 14.2 %collective-permute-done.28 = bf16[2,704,256]{2,1,0:T(8,128)(2,1)S(1)} collective-permute-done((bf16[2,704,256]{2,1,0:T(8,128)(2,1)}, bf16[2,704,256]{2,1,0:T(8,128)(2,1)S(1)}, u32[]{:S(2)}, u32[]{:S(2)}) %collective-permute-start.28) | collective-permute-done | bytes 720928 | tf_op jit(solution)/shard_map/ppermute | solution.py:21
  353.9 3.0 convert_add_fusion.3
  358.1 2.1 collective-permute-start.29
  360.2 17.4 %collective-permute-done.29 = bf16[1,704,256]{2,1,0:T(8,128)(2,1)S(1)} collective-permute-done((bf16[1,704,256]{2,1,0:T(8,128)(2,1)S(1)}, bf16[1,704,256]{2,1,0:T(8,128)(2,1)S(1)}, u32[]{:S(2)}, u32[]{:S(2)}) %collective-permute-start.29) | collective-permute-done | bytes 360480 | tf_op jit(solution)/shard_map/ppermute | solution.py:21
  377.6 2.1 fusion.6
  379.7 2.3 copy.32
  383.6 3.2 collective-permute-start.31
  389.5 2.2 shard_map.133
  393.2 4.5 all-to-all-start.3
  399.2 2.2 collective-permute-start.34
  403.0 9.4 %collective-permute-done.34.low = bf16[3,2,32,704]{3,2,1,0:T(8,128)(2,1)S(1)} collective-permute-done((bf16[3,2,32,704]{3,2,1,0:T(8,128)(2,1)S(1)}, bf16[3,2,32,704]{3,2,1,0:T(8,128)(2,1)S(1)}, u32[]{:S(2)}, u32[]{:S(2)}) %collective-permute-start.34) | collective-permute-done | bytes 270368 | tf_op jit(solution)/shard_map/ppermute | solution.py:331
  413.1 16.0 %collective-permute-done.35.high = bf16[3,2,32,704]{3,2,1,0:T(8,128)(2,1)S(1)} collective-permute-done((bf16[3,2,32,704]{3,2,1,0:T(8,128)(2,1)S(1)}, bf16[3,2,32,704]{3,2,1,0:T(8,128)(2,1)S(1)}, u32[]{:S(2)}, u32[]{:S(2)}) %collective-permute-start.35) | collective-permute-done | bytes 270368 | tf_op jit(solution)/shard_map/ppermute | solution.py:331
  429.1 6.7 %shard_map.132 = f32[7,7,704]{2,1,0:T(8,128)S(1)} custom-call(s32[2]{0:T(128)S(1)} %pad_add_fusion.places, bf16[3,2,32,704]{3,2,1,0:T(8,128)(2,1)S(1)} %copy-done.49, bf16[4,2,32,704]{3,2,1,0:T(8,128)(2,1)S(1)} %copy-done.14, bf16[3,2,32,704]{3,2,1,0:T(8,128)(2,1)S(1)} %copy-done.51, f32[4,2,32,704]{3,2,1,0:T(8,128)S(1)} %get-tuple-element.84.mid.grad), custom_call_target="tpu_custom_call" | custom-call | tf_op jit(solution)/shard_map/pallas_call | solution.py:419
  437.9 2.0 collective-permute-start.33
  441.0 4.5 collective-permute-done.37
  445.7 8.0 %shard_map.131 = bf16[4,2,32,704]{3,2,1,0:T(8,128)(2,1)} custom-call(s32[2]{0:T(128)S(1)} %pad_add_fusion.places, bf16[3,2,32,704]{3,2,1,0:T(8,128)(2,1)S(1)} %copy-done.55, f32[4,2,32,704]{3,2,1,0:T(8,128)S(1)} %copy-done.6, bf16[3,2,32,704]{3,2,1,0:T(8,128)(2,1)S(1)} %copy-done.57, f32[7,7,704]{2,1,0:T(8,128)S(1)} %copy-done.53, ...), custom_call_target="tpu_custom_call" | custom-call | tf_op jit(solution)/shard_map/pallas_call | solution.py:381
  453.7 8.2 %collective-permute-done.33 = bf16[2,704,256]{2,1,0:T(8,128)(2,1)S(1)} collective-permute-done((bf16[2,704,256]{2,1,0:T(8,128)(2,1)S(1)}, bf16[2,704,256]{2,1,0:T(8,128)(2,1)S(1)}, u32[]{:S(2)}, u32[]{:S(2)}) %collective-permute-start.33) | collective-permute-done | bytes 720928 | tf_op jit(solution)/shard_map/ppermute | solution.py:21
  463.9 3.1 shard_map.135
  467.7 4.3 shard_map.134
  472.0 10.3 %collective-permute-done.39 = bf16[1,704,256]{2,1,0:T(8,128)(2,1)} collective-permute-done((bf16[1,704,256]{2,1,0:T(8,128)(2,1)}, bf16[1,704,256]{2,1,0:T(8,128)(2,1)}, u32[]{:S(2)}, u32[]{:S(2)}) %collective-permute-start.39) | collective-permute-done | bytes 360480 | tf_op jit(solution)/shard_map/ppermute | solution.py:21
  (230 shorter events, 71.6 us)
Async XLA Ops:
  14.2 19.2 %collective-permute-start.2 = (bf16[704,256]{1,0:T(8,128)(2,1)S(1)}, bf16[704,256]{1,0:T(8,128)(2,1)S(1)}, u32[]{:S(2)}, u32[]{:S(2)}) collective-permute-start(bf16[704,256]{1,0:T(8,128)(2,1)S(1)} %get-tuple-element.49), channel_id=1, source_target_pairs={{0,1},{1,0},{2,3},{3,2},{4,5},{5,4},{6,7},{7,6},{8,9},{9,8},{10,11... | collective-permute-start | bytes 1081352 | tf_op jit(solution)/shard_map/ppermute | solution.py:21
  17.2 39.4 %collective-permute-start.3 = (bf16[704,256]{1,0:T(8,128)(2,1)S(1)}, bf16[704,256]{1,0:T(8,128)(2,1)}, u32[]{:S(2)}, u32[]{:S(2)}) collective-permute-start(bf16[704,256]{1,0:T(8,128)(2,1)S(1)} %get-tuple-element.49), channel_id=1, source_target_pairs={{0,2},{1,3},{2,0},{3,1},{4,6},{5,7},{6,4},{7,5},{8,10},{9,11},{10,... | collective-permute-start | bytes 1081352 | tf_op jit(solution)/shard_map/ppermute | solution.py:21
  19.8 36.8 %collective-permute-start.4 = (bf16[704,256]{1,0:T(8,128)(2,1)S(1)}, bf16[704,256]{1,0:T(8,128)(2,1)}, u32[]{:S(2)}, u32[]{:S(2)}) collective-permute-start(bf16[704,256]{1,0:T(8,128)(2,1)S(1)} %get-tuple-element.49), channel_id=1, source_target_pairs={{0,3},{1,2},{2,1},{3,0},{4,7},{5,6},{6,5},{7,4},{8,11},{9,10},{10,... | collective-permute-start | bytes 1081352 | tf_op jit(solution)/shard_map/ppermute | solution.py:21
  19.8 88.1 %all-to-all-start = ((bf16[4,704,352]{2,1,0:T(8,128)(2,1)}), bf16[4,704,352]{2,1,0:T(8,128)(2,1)S(1)}, u32[]{:S(2)}, u32[]{:S(2)}) async-start(bf16[4,704,352]{2,1,0:T(8,128)(2,1)} %copy-done.41), calls=%async_computation | async-start | bytes 4325376 | tf_op jit(solution)/shard_map/all_to_all | solution.py:457
  24.9 207.8 %all-gather.3.cloned.1.call-start = ((), (), s32[]{:S(2)}) async-start(), calls=%async_computation.6 | async-start | bytes 7208960 | tf_op jit(solution)/shard_map/all_gather | solution.py:480
  33.4 23.2 %copy-start.63 = (bf16[704,256]{1,0:T(8,128)(2,1)}, bf16[704,256]{1,0:T(8,128)(2,1)S(1)}, u32[]{:S(2)}) copy-start(bf16[704,256]{1,0:T(8,128)(2,1)S(1)} %collective-permute-done.2) | copy-start | bytes 1081348
  56.6 15.5 %copy-start.14 = (bf16[4,2,32,704]{3,2,1,0:T(8,128)(2,1)S(1)}, bf16[4,2,32,704]{3,2,1,0:T(8,128)(2,1)}, u32[]{:S(2)}) copy-start(bf16[4,2,32,704]{3,2,1,0:T(8,128)(2,1)} %mid.3) | copy-start | bytes 1081348
  56.6 15.5 %copy-start.52 = (f32[7,7,704]{2,1,0:T(8,128)S(1)}, f32[7,7,704]{2,1,0:T(8,128)}, u32[]{:S(2)}) copy-start(f32[7,7,704]{2,1,0:T(8,128)} %kern.3) | copy-start | bytes 413956
  59.1 7.9 %collective-permute-start = (bf16[3,2,32,704]{3,2,1,0:T(8,128)(2,1)}, bf16[3,2,32,704]{3,2,1,0:T(8,128)(2,1)S(1)}, u32[]{:S(2)}, u32[]{:S(2)}) collective-permute-start(bf16[3,2,32,704]{3,2,1,0:T(8,128)(2,1)} %copy-done.58), channel_id=1, source_target_pairs={{0,4},{4,8},{8,12},{1,5},{5,9},{9,13},{2,6},{6,10},{10,14},{3,7},{... | collective-permute-start | bytes 811016 | tf_op jit(solution)/shard_map/ppermute | solution.py:331
  62.6 9.5 %collective-permute-start.1 = (bf16[3,2,32,704]{3,2,1,0:T(8,128)(2,1)S(1)}, bf16[3,2,32,704]{3,2,1,0:T(8,128)(2,1)S(1)}, u32[]{:S(2)}, u32[]{:S(2)}) collective-permute-start(bf16[3,2,32,704]{3,2,1,0:T(8,128)(2,1)S(1)} %get-tuple-element.48), channel_id=1, source_target_pairs={{4,0},{8,4},{12,8},{5,1},{9,5},{13,9},{6,2},{10,6},{14,10},{7,3},{... | collective-permute-start | bytes 811016 | tf_op jit(solution)/shard_map/ppermute | solution.py:331
  80.9 22.4 %collective-permute-start.5 = (f32[2,4,2,32]{3,2,1,0:T(2,128)S(1)}, f32[2,4,2,32]{3,2,1,0:T(2,128)S(1)}, u32[]{:S(2)}, u32[]{:S(2)}) collective-permute-start(f32[2,4,2,32]{3,2,1,0:T(2,128)S(1)} %pad_maximum_fusion.2), channel_id=1, source_target_pairs={{0,1},{1,0},{2,3},{3,2},{4,5},{5,4},{6,7},{7,6},{8,9},{9,8},{10,11... | collective-permute-start | bytes 6152 | tf_op jit(solution)/shard_map/ppermute | solution.py:21
  100.8 7.1 %collective-permute-start.6 = (f32[2,4,2,32]{3,2,1,0:T(2,128)S(1)}, f32[2,4,2,32]{3,2,1,0:T(2,128)S(1)}, u32[]{:S(2)}, u32[]{:S(2)}) collective-permute-start(f32[2,4,2,32]{3,2,1,0:T(2,128)S(1)} %pad_maximum_fusion.2), channel_id=1, source_target_pairs={{0,2},{1,3},{2,0},{3,1},{4,6},{5,7},{6,4},{7,5},{8,10},{9,11},{10,... | collective-permute-start | bytes 6152 | tf_op jit(solution)/shard_map/ppermute | solution.py:21
  100.8 7.1 %collective-permute-start.7 = (f32[2,4,2,32]{3,2,1,0:T(2,128)S(1)}, f32[2,4,2,32]{3,2,1,0:T(2,128)S(1)}, u32[]{:S(2)}, u32[]{:S(2)}) collective-permute-start(f32[2,4,2,32]{3,2,1,0:T(2,128)S(1)} %pad_maximum_fusion.2), channel_id=1, source_target_pairs={{0,3},{1,2},{2,1},{3,0},{4,7},{5,6},{6,5},{7,4},{8,11},{9,10},{10,... | collective-permute-start | bytes 6152 | tf_op jit(solution)/shard_map/ppermute | solution.py:21
  110.7 12.5 %collective-permute-start.8 = (bf16[704,256]{1,0:T(8,128)(2,1)}, bf16[704,256]{1,0:T(8,128)(2,1)S(1)}, u32[]{:S(2)}, u32[]{:S(2)}) collective-permute-start(bf16[704,256]{1,0:T(8,128)(2,1)} %copy.27), channel_id=1, source_target_pairs={{0,2},{1,3},{2,0},{3,1},{4,6},{5,7},{6,4},{7,5},{8,10},{9,11},{10,... | collective-permute-start | bytes 1081352 | tf_op jit(solution)/shard_map/ppermute | solution.py:21
  111.8 15.6 %collective-permute-start.12 = (bf16[704,256]{1,0:T(8,128)(2,1)}, bf16[704,256]{1,0:T(8,128)(2,1)}, u32[]{:S(2)}, u32[]{:S(2)}) collective-permute-start(bf16[704,256]{1,0:T(8,128)(2,1)} %copy.27), channel_id=1, source_target_pairs={{0,1},{1,0},{2,3},{3,2},{4,5},{5,4},{6,7},{7,6},{8,9},{9,8},{10,11... | collective-permute-start | bytes 1081352 | tf_op jit(solution)/shard_map/ppermute | solution.py:21
  123.2 7.5 %collective-permute-start.13 = (bf16[704,256]{1,0:T(8,128)(2,1)S(1)}, bf16[704,256]{1,0:T(8,128)(2,1)}, u32[]{:S(2)}, u32[]{:S(2)}) collective-permute-start(bf16[704,256]{1,0:T(8,128)(2,1)S(1)} %collective-permute-done.8), channel_id=1, source_target_pairs={{0,1},{1,0},{2,3},{3,2},{4,5},{5,4},{6,7},{7,6},{8,9},{9,8},{10,11... | collective-permute-start | bytes 1081352 | tf_op jit(solution)/shard_map/ppermute | solution.py:21
  130.8 56.1 %all-to-all-start.1 = ((bf16[4,704,352]{2,1,0:T(8,128)(2,1)}), bf16[4,704,352]{2,1,0:T(8,128)(2,1)}, u32[]{:S(2)}, u32[]{:S(2)}) async-start(bf16[4,704,352]{2,1,0:T(8,128)(2,1)} %copy-done.4), calls=%async_computation.1 | async-start | bytes 4325376 | tf_op jit(solution)/shard_map/all_to_all | solution.py:482
  136.9 21.9 %copy-start.7 = (bf16[2,704,256]{2,1,0:T(8,128)(2,1)}, bf16[2,704,256]{2,1,0:T(8,128)(2,1)S(1)}, u32[]{:S(2)}) copy-start(bf16[2,704,256]{2,1,0:T(8,128)(2,1)S(1)} %pad_maximum_fusion.refs_0_) | copy-start | bytes 2162692
  136.9 19.1 %collective-permute-start.9 = (bf16[2,704,256]{2,1,0:T(8,128)(2,1)S(1)}, bf16[2,704,256]{2,1,0:T(8,128)(2,1)S(1)}, u32[]{:S(2)}, u32[]{:S(2)}) collective-permute-start(bf16[2,704,256]{2,1,0:T(8,128)(2,1)S(1)} %pad_maximum_fusion.refs_0_), channel_id=1, source_target_pairs={{0,4},{4,0},{8,12},{12,8},{1,5},{5,1},{9,13},{13,9},{2,6},{6,2},{1... | collective-permute-start | bytes 2162696 | tf_op jit(solution)/shard_map/ppermute | solution.py:21
  139.6 19.1 %collective-permute-start.15 = (bf16[2,704,256]{2,1,0:T(8,128)(2,1)S(1)}, bf16[2,704,256]{2,1,0:T(8,128)(2,1)S(1)}, u32[]{:S(2)}, u32[]{:S(2)}) collective-permute-start(bf16[2,704,256]{2,1,0:T(8,128)(2,1)S(1)} %pad_maximum_fusion.1.refs_4_), channel_id=1, source_target_pairs={{0,8},{4,12},{8,0},{12,4},{1,9},{5,13},{9,1},{13,5},{2,10},{6,14},... | collective-permute-start | bytes 2162696 | tf_op jit(solution)/shard_map/ppermute | solution.py:21
  139.7 34.5 %collective-permute-start.10 = (bf16[2,704,256]{2,1,0:T(8,128)(2,1)S(1)}, bf16[2,704,256]{2,1,0:T(8,128)(2,1)S(1)}, u32[]{:S(2)}, u32[]{:S(2)}) collective-permute-start(bf16[2,704,256]{2,1,0:T(8,128)(2,1)S(1)} %pad_maximum_fusion.refs_0_), channel_id=1, source_target_pairs={{0,8},{4,12},{8,0},{12,4},{1,9},{5,13},{9,1},{13,5},{2,10},{6,14},... | collective-permute-start | bytes 2162696 | tf_op jit(solution)/shard_map/ppermute | solution.py:21
  141.7 33.4 %collective-permute-start.14 = (bf16[2,704,256]{2,1,0:T(8,128)(2,1)S(1)}, bf16[2,704,256]{2,1,0:T(8,128)(2,1)S(1)}, u32[]{:S(2)}, u32[]{:S(2)}) collective-permute-start(bf16[2,704,256]{2,1,0:T(8,128)(2,1)S(1)} %pad_maximum_fusion.1.refs_4_), channel_id=1, source_target_pairs={{0,4},{4,0},{8,12},{12,8},{1,5},{5,1},{9,13},{13,9},{2,6},{6,2},{1... | collective-permute-start | bytes 2162696 | tf_op jit(solution)/shard_map/ppermute | solution.py:21
  156.0 29.0 %collective-permute-start.11 = (bf16[2,704,256]{2,1,0:T(8,128)(2,1)S(1)}, bf16[2,704,256]{2,1,0:T(8,128)(2,1)S(1)}, u32[]{:S(2)}, u32[]{:S(2)}) collective-permute-start(bf16[2,704,256]{2,1,0:T(8,128)(2,1)S(1)} %collective-permute-done.9.refs_1_), channel_id=1, source_target_pairs={{0,8},{4,12},{8,0},{12,4},{1,9},{5,13},{9,1},{13,5},{2,10},{6,14},... | collective-permute-start | bytes 2162696 | tf_op jit(solution)/shard_map/ppermute | solution.py:21
  158.8 27.2 %collective-permute-start.16 = (bf16[2,704,256]{2,1,0:T(8,128)(2,1)S(1)}, bf16[2,704,256]{2,1,0:T(8,128)(2,1)S(1)}, u32[]{:S(2)}, u32[]{:S(2)}) collective-permute-start(bf16[2,704,256]{2,1,0:T(8,128)(2,1)S(1)} %collective-permute-done.15.refs_6_), channel_id=1, source_target_pairs={{0,4},{4,0},{8,12},{12,8},{1,5},{5,1},{9,13},{13,9},{2,6},{6,2},{1... | collective-permute-start | bytes 2162696 | tf_op jit(solution)/shard_map/ppermute | solution.py:21
  160.1 29.8 %collective-permute-start.17 = (bf16[4,704,352]{2,1,0:T(8,128)(2,1)S(1)}, bf16[4,704,352]{2,1,0:T(8,128)(2,1)}, u32[]{:S(2)}, u32[]{:S(2)}) collective-permute-start(bf16[4,704,352]{2,1,0:T(8,128)(2,1)S(1)} %all-to-all-done.mine), channel_id=1, source_target_pairs={{0,16},{16,0},{1,17},{17,1},{2,18},{18,2},{3,19},{19,3},{4,20},{20... | collective-permute-start | bytes 5947400 | tf_op jit(solution)/shard_map/ppermute | solution.py:21
  186.9 37.8 %collective-permute-start.22 = (bf16[4,704,352]{2,1,0:T(8,128)(2,1)}, bf16[4,704,352]{2,1,0:T(8,128)(2,1)}, u32[]{:S(2)}, u32[]{:S(2)}) collective-permute-start(bf16[4,704,352]{2,1,0:T(8,128)(2,1)} %all-to-all-done.1.mine), channel_id=1, source_target_pairs={{0,16},{16,0},{1,17},{17,1},{2,18},{18,2},{3,19},{19,3},{4,20},{20... | collective-permute-start | bytes 5947400 | tf_op jit(solution)/shard_map/ppermute | solution.py:21
  209.5 3.6 collective-permute-start.18
  213.1 3.5 collective-permute-start.19
  216.7 3.5 collective-permute-start.20
  220.2 4.4 collective-permute-start.21
  260.4 4.3 collective-permute-start.27
  267.2 70.2 %all-to-all-start.2 = ((bf16[4,704,352]{2,1,0:T(8,128)(2,1)}), bf16[4,704,352]{2,1,0:T(8,128)(2,1)S(1)}, u32[]{:S(2)}, u32[]{:S(2)}) async-start(bf16[4,704,352]{2,1,0:T(8,128)(2,1)} %copy-done.3), calls=%async_computation.3 | async-start | bytes 4325376 | tf_op jit(solution)/shard_map/all_to_all | solution.py:513
  272.0 164.6 %reduce-scatter.2.cloned.1.call-start = ((), (), s32[]{:S(2)}) async-start(), calls=%async_computation.5 | async-start | bytes 7208960 | tf_op jit(solution)/shard_map/reduce_scatter | solution.py:522
  274.2 12.1 %copy-start.23 = (bf16[2,704,256]{2,1,0:T(8,128)(2,1)S(1)}, bf16[2,704,256]{2,1,0:T(8,128)(2,1)}, u32[]{:S(2)}) copy-start(bf16[2,704,256]{2,1,0:T(8,128)(2,1)} %copy-done.21) | copy-start | bytes 2162692
  274.2 12.1 %copy-start.26 = (bf16[2,704,256]{2,1,0:T(8,128)(2,1)S(1)}, bf16[2,704,256]{2,1,0:T(8,128)(2,1)}, u32[]{:S(2)}) copy-start(bf16[2,704,256]{2,1,0:T(8,128)(2,1)} %copy-done.24) | copy-start | bytes 2162692
  274.2 12.1 %copy-start.29 = (bf16[2,704,256]{2,1,0:T(8,128)(2,1)S(1)}, bf16[2,704,256]{2,1,0:T(8,128)(2,1)}, u32[]{:S(2)}) copy-start(bf16[2,704,256]{2,1,0:T(8,128)(2,1)} %copy-done.27) | copy-start | bytes 2162692
  274.2 12.1 %copy-start.32 = (bf16[2,704,256]{2,1,0:T(8,128)(2,1)S(1)}, bf16[2,704,256]{2,1,0:T(8,128)(2,1)}, u32[]{:S(2)}) copy-start(bf16[2,704,256]{2,1,0:T(8,128)(2,1)} %copy-done.30) | copy-start | bytes 2162692
  274.2 12.1 %copy-start.35 = (bf16[2,704,256]{2,1,0:T(8,128)(2,1)S(1)}, bf16[2,704,256]{2,1,0:T(8,128)(2,1)}, u32[]{:S(2)}) copy-start(bf16[2,704,256]{2,1,0:T(8,128)(2,1)} %copy-done.33) | copy-start | bytes 2162692
  274.2 12.1 %copy-start.38 = (bf16[2,704,256]{2,1,0:T(8,128)(2,1)S(1)}, bf16[2,704,256]{2,1,0:T(8,128)(2,1)}, u32[]{:S(2)}) copy-start(bf16[2,704,256]{2,1,0:T(8,128)(2,1)} %copy-done.36) | copy-start | bytes 2162692
  284.0 33.5 %collective-permute-start.25 = (bf16[2,2,704,256]{3,2,1,0:T(8,128)(2,1)S(1)}, bf16[2,2,704,256]{3,2,1,0:T(8,128)(2,1)}, u32[]{:S(2)}, u32[]{:S(2)}) collective-permute-start(bf16[2,2,704,256]{3,2,1,0:T(8,128)(2,1)S(1)} %get-tuple-element.75), channel_id=1, source_target_pairs={{0,8},{4,12},{8,0},{12,4},{1,9},{5,13},{9,1},{13,5},{2,10},{6,14},... | collective-permute-start | bytes 4325384 | tf_op jit(solution)/shard_map/ppermute | solution.py:21
  285.8 34.1 %collective-permute-start.23 = (bf16[2,2,704,256]{3,2,1,0:T(8,128)(2,1)S(1)}, bf16[2,2,704,256]{3,2,1,0:T(8,128)(2,1)}, u32[]{:S(2)}, u32[]{:S(2)}) collective-permute-start(bf16[2,2,704,256]{3,2,1,0:T(8,128)(2,1)S(1)} %get-tuple-element.69), channel_id=1, source_target_pairs={{0,4},{4,0},{8,12},{12,8},{1,5},{5,1},{9,13},{13,9},{2,6},{6,2},{1... | collective-permute-start | bytes 4325384 | tf_op jit(solution)/shard_map/ppermute | solution.py:21
  293.0 26.2 %copy-start.39 = (bf16[4,704,352]{2,1,0:T(8,128)(2,1)}, bf16[4,704,352]{2,1,0:T(8,128)(2,1)S(1)}, u32[]{:S(2)}) copy-start(bf16[4,704,352]{2,1,0:T(8,128)(2,1)S(1)} %get-tuple-element.87.mine) | copy-start | bytes 5947396
  319.3 17.1 %collective-permute-start.26 = (bf16[1,2,704,256]{3,2,1,0:T(8,128)(2,1)S(1)}, bf16[1,2,704,256]{3,2,1,0:T(8,128)(2,1)S(1)}, u32[]{:S(2)}, u32[]{:S(2)}) collective-permute-start(bf16[1,2,704,256]{3,2,1,0:T(8,128)(2,1)S(1)} %slice.139), channel_id=1, source_target_pairs={{0,4},{4,0},{8,12},{12,8},{1,5},{5,1},{9,13},{13,9},{2,6},{6,2},{1... | collective-permute-start | bytes 2162696 | tf_op jit(solution)/shard_map/ppermute | solution.py:21
  321.5 14.9 %copy-start.59 = (f32[2,2,704,256]{3,2,1,0:T(8,128)}, f32[2,2,704,256]{3,2,1,0:T(8,128)S(1)}, u32[]{:S(2)}) copy-start(f32[2,2,704,256]{3,2,1,0:T(8,128)S(1)} %convert_add_fusion.1) | copy-start | bytes 8650756
  322.6 17.1 %collective-permute-start.24 = (bf16[1,2,704,256]{3,2,1,0:T(8,128)(2,1)}, bf16[1,2,704,256]{3,2,1,0:T(8,128)(2,1)}, u32[]{:S(2)}, u32[]{:S(2)}) collective-permute-start(bf16[1,2,704,256]{3,2,1,0:T(8,128)(2,1)} %slice.140), channel_id=1, source_target_pairs={{0,8},{4,12},{8,0},{12,4},{1,9},{5,13},{9,1},{13,5},{2,10},{6,14},... | collective-permute-start | bytes 2162696 | tf_op jit(solution)/shard_map/ppermute | solution.py:21
  337.5 16.4 %collective-permute-start.28 = (bf16[2,704,256]{2,1,0:T(8,128)(2,1)}, bf16[2,704,256]{2,1,0:T(8,128)(2,1)S(1)}, u32[]{:S(2)}, u32[]{:S(2)}) collective-permute-start(bf16[2,704,256]{2,1,0:T(8,128)(2,1)} %fusion), channel_id=1, source_target_pairs={{0,1},{1,0},{2,3},{3,2},{4,5},{5,4},{6,7},{7,6},{8,9},{9,8},{10,11... | collective-permute-start | bytes 2162696 | tf_op jit(solution)/shard_map/ppermute | solution.py:21
  356.9 31.1 %collective-permute-start.40 = (bf16[4,704,352]{2,1,0:T(8,128)(2,1)}, bf16[4,704,352]{2,1,0:T(8,128)(2,1)}, u32[]{:S(2)}, u32[]{:S(2)}) collective-permute-start(bf16[4,704,352]{2,1,0:T(8,128)(2,1)} %get-tuple-element.71), channel_id=1, source_target_pairs={{0,16},{16,0},{1,17},{17,1},{2,18},{18,2},{3,19},{19,3},{4,20},{20... | collective-permute-start | bytes 5947400 | tf_op jit(solution)/shard_map/ppermute | solution.py:21
  358.1 19.5 %collective-permute-start.29 = (bf16[1,704,256]{2,1,0:T(8,128)(2,1)S(1)}, bf16[1,704,256]{2,1,0:T(8,128)(2,1)S(1)}, u32[]{:S(2)}, u32[]{:S(2)}) collective-permute-start(bf16[1,704,256]{2,1,0:T(8,128)(2,1)S(1)} %slice.142), channel_id=1, source_target_pairs={{0,2},{1,3},{2,0},{3,1},{4,6},{5,7},{6,4},{7,5},{8,10},{9,11},{10,... | collective-permute-start | bytes 1081352 | tf_op jit(solution)/shard_map/ppermute | solution.py:21
  383.5 9.7 %collective-permute-start.30 = (f32[2,4,2,32]{3,2,1,0:T(2,128)S(1)}, f32[2,4,2,32]{3,2,1,0:T(2,128)S(1)}, u32[]{:S(2)}, u32[]{:S(2)}) collective-permute-start(f32[2,4,2,32]{3,2,1,0:T(2,128)S(1)} %pad_maximum_fusion.3), channel_id=1, source_target_pairs={{0,1},{1,0},{2,3},{3,2},{4,5},{5,4},{6,7},{7,6},{8,9},{9,8},{10,11... | collective-permute-start | bytes 6152 | tf_op jit(solution)/shard_map/ppermute | solution.py:21
  383.6 9.5 %collective-permute-start.31 = (f32[2,4,2,32]{3,2,1,0:T(2,128)S(1)}, f32[2,4,2,32]{3,2,1,0:T(2,128)S(1)}, u32[]{:S(2)}, u32[]{:S(2)}) collective-permute-start(f32[2,4,2,32]{3,2,1,0:T(2,128)S(1)} %pad_maximum_fusion.3), channel_id=1, source_target_pairs={{0,2},{1,3},{2,0},{3,1},{4,6},{5,7},{6,4},{7,5},{8,10},{9,11},{10,... | collective-permute-start | bytes 6152 | tf_op jit(solution)/shard_map/ppermute | solution.py:21
  386.8 6.3 %collective-permute-start.32 = (f32[2,4,2,32]{3,2,1,0:T(2,128)S(1)}, f32[2,4,2,32]{3,2,1,0:T(2,128)S(1)}, u32[]{:S(2)}, u32[]{:S(2)}) collective-permute-start(f32[2,4,2,32]{3,2,1,0:T(2,128)S(1)} %pad_maximum_fusion.3), channel_id=1, source_target_pairs={{0,3},{1,2},{2,1},{3,0},{4,7},{5,6},{6,5},{7,4},{8,11},{9,10},{10,... | collective-permute-start | bytes 6152 | tf_op jit(solution)/shard_map/ppermute | solution.py:21
  393.2 74.5 %all-to-all-start.3 = ((bf16[4,704,352]{2,1,0:T(8,128)(2,1)}), bf16[4,704,352]{2,1,0:T(8,128)(2,1)}, u32[]{:S(2)}, u32[]{:S(2)}) async-start(bf16[4,704,352]{2,1,0:T(8,128)(2,1)} %copy-done.2), calls=%async_computation.4 | async-start | bytes 4325376 | tf_op jit(solution)/shard_map/all_to_all | solution.py:533
  397.7 31.5 %copy-start.49 = (bf16[3,2,32,704]{3,2,1,0:T(8,128)(2,1)S(1)}, bf16[3,2,32,704]{3,2,1,0:T(8,128)(2,1)}, u32[]{:S(2)}) copy-start(bf16[3,2,32,704]{3,2,1,0:T(8,128)(2,1)} %copy-done.48) | copy-start | bytes 811012
  397.7 31.5 %copy-start.51 = (bf16[3,2,32,704]{3,2,1,0:T(8,128)(2,1)S(1)}, bf16[3,2,32,704]{3,2,1,0:T(8,128)(2,1)}, u32[]{:S(2)}) copy-start(bf16[3,2,32,704]{3,2,1,0:T(8,128)(2,1)} %copy-done.50) | copy-start | bytes 811012
  399.1 30.0 %copy-start.5 = (f32[4,2,32,704]{3,2,1,0:T(8,128)}, f32[4,2,32,704]{3,2,1,0:T(8,128)S(1)}, u32[]{:S(2)}) copy-start(f32[4,2,32,704]{3,2,1,0:T(8,128)S(1)} %get-tuple-element.84.mid.grad) | copy-start | bytes 2162692
  399.2 13.2 %collective-permute-start.34 = (bf16[3,2,32,704]{3,2,1,0:T(8,128)(2,1)S(1)}, bf16[3,2,32,704]{3,2,1,0:T(8,128)(2,1)S(1)}, u32[]{:S(2)}, u32[]{:S(2)}) collective-permute-start(bf16[3,2,32,704]{3,2,1,0:T(8,128)(2,1)S(1)} %get-tuple-element.108), channel_id=1, source_target_pairs={{0,4},{4,8},{8,12},{1,5},{5,9},{9,13},{2,6},{6,10},{10,14},{3,7},{... | collective-permute-start | bytes 811016 | tf_op jit(solution)/shard_map/ppermute | solution.py:331
  401.5 27.7 %collective-permute-start.35 = (bf16[3,2,32,704]{3,2,1,0:T(8,128)(2,1)S(1)}, bf16[3,2,32,704]{3,2,1,0:T(8,128)(2,1)S(1)}, u32[]{:S(2)}, u32[]{:S(2)}) collective-permute-start(bf16[3,2,32,704]{3,2,1,0:T(8,128)(2,1)S(1)} %get-tuple-element.107), channel_id=1, source_target_pairs={{4,0},{8,4},{12,8},{5,1},{9,5},{13,9},{6,2},{10,6},{14,10},{7,3},{... | collective-permute-start | bytes 811016 | tf_op jit(solution)/shard_map/ppermute | solution.py:331
  436.6 3.3 collective-permute-start.36
  436.6 25.3 %copy-start.62 = (bf16[2816,256]{1,0:T(8,128)(2,1)S(1)}, bf16[2816,256]{1,0:T(8,128)(2,1)}, u32[]{:S(2)}) copy-start(bf16[2816,256]{1,0:T(8,128)(2,1)} %reduce-scatter.2.cloned.1.call-done) | copy-start | bytes 4325380
  437.9 24.0 %collective-permute-start.33 = (bf16[2,704,256]{2,1,0:T(8,128)(2,1)S(1)}, bf16[2,704,256]{2,1,0:T(8,128)(2,1)S(1)}, u32[]{:S(2)}, u32[]{:S(2)}) collective-permute-start(bf16[2,704,256]{2,1,0:T(8,128)(2,1)S(1)} %slice.89), channel_id=1, source_target_pairs={{0,1},{1,0},{2,3},{3,2},{4,5},{5,4},{6,7},{7,6},{8,9},{9,8},{10,11... | collective-permute-start | bytes 2162696 | tf_op jit(solution)/shard_map/ppermute | solution.py:21
  440.8 4.7 collective-permute-start.37
  445.5 8.1 %collective-permute-start.38 = (bf16[7,7,704]{2,1,0:T(8,128)(2,1)S(1)}, bf16[7,7,704]{2,1,0:T(8,128)(2,1)S(1)}, u32[]{:S(2)}, u32[]{:S(2)}) collective-permute-start(bf16[7,7,704]{2,1,0:T(8,128)(2,1)S(1)} %add_convert_fusion.1), channel_id=1, source_target_pairs={{0,8},{4,12},{8,0},{12,4},{1,9},{5,13},{9,1},{13,5},{2,10},{6,14},... | collective-permute-start | bytes 206984 | tf_op jit(solution)/shard_map/ppermute | solution.py:21
  463.9 18.3 %collective-permute-start.39 = (bf16[1,704,256]{2,1,0:T(8,128)(2,1)}, bf16[1,704,256]{2,1,0:T(8,128)(2,1)}, u32[]{:S(2)}, u32[]{:S(2)}) collective-permute-start(bf16[1,704,256]{2,1,0:T(8,128)(2,1)} %slice.141), channel_id=1, source_target_pairs={{0,2},{1,3},{2,0},{3,1},{4,6},{5,7},{6,4},{7,5},{8,10},{9,11},{10,... | collective-permute-start | bytes 1081352 | tf_op jit(solution)/shard_map/ppermute | solution.py:21
  467.7 14.6 %copy-start.61 = (f32[2,704,256]{2,1,0:T(8,128)S(1)}, f32[2,704,256]{2,1,0:T(8,128)}, u32[]{:S(2)}) copy-start(f32[2,704,256]{2,1,0:T(8,128)} %copy-done.60) | copy-start | bytes 4325380
  (48 other events, 206.0 us)
Sparse Core Ops, SparseCore 0:
  59.3 75.4 all-gather.2
  357.0 76.5 reduce-scatter.1

commit v4 on v3

--- a/solution.py
+++ b/solution.py
@@ -197,6 +197,26 @@
     )
 
 
+def spread_images(vectors, units, span):
+    count = vectors.shape[1]
+    return jnp.concatenate(
+        [jnp.broadcast_to(vectors[:, b : b + 1], (units, span)) for b in range(count)], axis=1
+    )
+
+
+def gated_kernel(places, act, gain, beta, dims):
+    rows, batch, pixels = dims
+    units = act.shape[0]
+
+    def body(places, act, gain, beta, out):
+        for q in range(rows):
+            part = slice(q * pixels, (q + 1) * pixels)
+            wide = spread_images(gain[...], units, pixels // batch)
+            out[:, part] = (act[:, part] * wide + beta[...]).astype(bf16)
+
+    return call(body, [shape_of(act.shape, bf16)], places, act, gain, beta)[0]
+
+
 def back_kernel(places, pieces, weights, act, dims):
     rows, batch, pixels = dims
     count, units, chans = weights.shape
@@ -237,10 +257,7 @@
         outs = refs[len(operands) + 2 :]
 
         def spread(vectors):
-            span = (units, pixels // batch)
-            return jnp.concatenate(
-                [jnp.broadcast_to(vectors[:, b : b + 1], span) for b in range(batch)], axis=1
-            )
+            return spread_images(vectors, units, pixels // batch)
 
         for q in range(rows):
             part = slice(q * pixels, (q + 1) * pixels)
@@ -454,9 +471,6 @@
 
     pieces, cot_turned, low, high = prepare(places, images, cotangent, w_in, reach)
     cot_hops = first_hops(cot_turned, True)
-    mine = lax.all_to_all(pieces, "col", 0, 0)
-    w_in_all, w_in_turned = join_weights(places, mine, swap(mine, "dp", 1))
-    w_in_there = mine
     low, high = exchange_rows(low, high)
     bias, gamma, beta = own_units(b_in), own_units(grn_gamma), own_units(grn_beta)
 
@@ -464,10 +478,8 @@
     mean_own = jnp.mean(conv_out, axis=-1)
     dev_own = conv_out - mean_own[..., None]
     stats = jnp.stack([mean_own, jnp.sum(dev_own * dev_own, axis=-1)])
-    stats = after(stats, cot_hops)
-    cot_cols = gather_cols(cot_turned, cot_hops)
+    cot_cols = after(gather_cols(cot_turned, cot_hops), stats)
     stats = [stats] + [swap(stats, "col", m) for m in range(1, col_count)]
-    stats = after(stats, w_in_there)
     mean_pix = sum(s[0] for s in stats) / col_count
     var_pix = sum(s[1] + chans * (s[0] - mean_pix) ** 2 for s in stats) / all_chans
     inv_std = lax.rsqrt(var_pix + epsilon)[..., None]
@@ -478,16 +490,25 @@
     even, odd = stack_cols(normed_cols)
     normed_all = gather_rows(even, bits) + gather_rows(odd, bits[::-1])
     cot_all = [pin(lax.all_gather(pin(jnp.concatenate(stack_cols(cot_cols))), "row"))]
-    pieces = after(prepare_out(places, w_out.T), normed_cols)
+    w_in_there = lax.all_to_all(after(pieces, normed_cols), "col", 0, 0)
+    near_rows = [normed_all[side + bit] for side in (0, row_count) for bit in bits]
+    w_in_there = after(w_in_there, near_rows)
+    w_in_all, w_in_turned = join_weights(places, w_in_there, swap(w_in_there, "dp", 1))
+    pieces = after(prepare_out(places, w_out.T), w_in_there)
     w_out_there = lax.all_to_all(pieces, "col", 0, 0)
     act, slope, square = hidden_kernel(places, normed_all, w_in_all, bias, dims)
-    w_out_there = after(w_out_there, normed_all)
-    w_out_all, w_out_turned = join_weights(places, w_out_there, swap(w_out_there, "dp", 1))
     norm_chan = jnp.sqrt(square + epsilon)
     norm_sum = add_over(add_over(jnp.sum(norm_chan, axis=0), "row"), "col")
     denom = norm_sum / all_units + epsilon
     gamma, beta = gamma[:, None], beta[:, None]
     gain = gamma * (norm_chan / denom) + 1.0
+    gated = gated_kernel(places, act, gain, beta, dims)
+    w_out_mine, w_out_other = grads_kernel(places, gated, cot_all, dims, col_count, chans)
+    w_out_sums = add_kernel(places, w_out_mine, swap(w_out_other, "dp", 1))
+    w_out_there = after(w_out_there, w_out_sums)
+    w_out_all, w_out_turned = join_weights(places, w_out_there, swap(w_out_there, "dp", 1))
+    w_out_back = lax.all_to_all(after(w_out_sums, w_out_there), "col", 0, 0)
+    w_out_grad = finish_kernel(places, w_out_back, scale_grad).T
     grad_gated, pull = back_kernel(places, cot_all, w_out_all, act, dims)
     share_back = gamma * pull / denom / norm_chan
 
@@ -499,38 +520,28 @@
         dims,
         (bits[0], bits[-1]),
     )
-    gated, out_parts = project_kernel(
-        places,
-        lambda b, spread: b[0] * spread(b[1]) + b[2],
-        [act, gain, beta],
-        w_out_turned,
-        dims,
-        (),
+    _, out_parts = project_kernel(
+        places, lambda b, spread: b[0], [gated], w_out_turned, dims, (bits[0], bits[-1])
     )
     w_in_mine, w_in_other = grads_kernel(places, grad_pre, normed_all, dims, col_count, chans)
-    w_out_mine, w_out_other = grads_kernel(places, gated, cot_all, dims, col_count, chans)
-    w_out_sums = add_kernel(places, w_out_mine, swap(w_out_other, "dp", 1))
-    w_out_back = lax.all_to_all(w_out_sums, "col", 0, 0)
-    w_out_grad = finish_kernel(places, w_out_back, scale_grad).T
     w_in_sums = add_kernel(places, w_in_mine, swap(w_in_other, "dp", 1))
 
     near_a, far_a, near_b, far_b = grad_parts
-    even = halve_sum(near_a, far_a, "row", bits, (w_in_other,))
-    odd = halve_sum(near_b, far_b, "row", bits[::-1], (w_in_other,))
+    even = halve_sum(near_a, far_a, "row", bits, (w_in_other, out_parts[0]))
+    odd = halve_sum(near_b, far_b, "row", bits[::-1], (w_in_other, out_parts[0]))
     down = [1 << i for i in range((col_count - 1).bit_length())]
-    branch_rows = pin(
-        lax.psum_scatter(
-            pin(after(out_parts[0], even, odd).reshape(-1, pixels)), "row", scatter_dimension=0, tiled=True
-        )
-    ).reshape(col_count, chans, pixels)
+    near_a, far_a, near_b, far_b = out_parts
+    far_a, far_b = after((far_a, far_b), even, odd)
+    out_even = halve_sum(near_a, far_a, "row", bits)
+    out_odd = halve_sum(near_b, far_b, "row", bits[::-1])
     odd = after(odd, w_out_back)
     grad_normed = natural(pin(halve_sum(even, odd, "col", down)))
 
     sums = jnp.stack([jnp.sum(grad_normed, axis=-1), jnp.sum(grad_normed * standard, axis=-1)])
     sums = sum([swap(sums, "col", m) for m in range(1, col_count)], sums) / all_chans
-    branch_rows = after(branch_rows, sums)
-    w_in_sums = after(w_in_sums, sums)
-    w_in_grad = finish_kernel(places, lax.all_to_all(w_in_sums, "col", 0, 0), scale_grad)
+    out_odd = after(out_odd, sums)
+    w_in_back = lax.all_to_all(after(w_in_sums, sums), "col", 0, 0)
+    w_in_grad = finish_kernel(places, w_in_back, scale_grad)
     grad_conv = inv_std * (grad_normed - sums[0][..., None] - standard * sums[1][..., None])
     edge = grad_conv.astype(bf16)
     low_grad, high_grad = exchange_rows(edge[height - reach :], edge[:reach])
@@ -541,7 +552,7 @@
         kern = kern.astype(bf16)
         kern = kern.astype(f32) + swap(kern, axis, step).astype(f32)
     kernel_grad = kern * scale_grad
-    branch = halve_sum(branch_rows[: col_count // 2], branch_rows[col_count // 2 :], "col", down, (x_grad, kern))
+    branch = halve_sum(out_even, out_odd, "col", down, (x_grad,))
     branch = natural(pin(branch))
     result = (images.astype(f32) + branch.astype(f32)).astype(bf16)
     return (result, x_grad, w_in_grad, w_out_grad, kernel_grad)

time: 498 us -> 469 us (0.942)
  waiting for transfers between devices: 226 us -> 208 us
  local copies, waits for them, and re-layouts: 46.3 us -> 34.3 us
  Pallas kernels: 96.5 us -> 103 us
    ppermute x2, waiting for transfers between devices: 12.6 us -> 3.38 us  [exchange_rows(): lax.ppermute(low, 'row', forward)]
    unnamed x131 -> x95, local copies, waits for them, and re-layouts: 33.9 us -> 26.2 us
    pallas_call x14 -> x15, Pallas kernels: 74.9 us -> 81.1 us  [call(): pl.pallas_call(body, out_shape=outs, in_specs=[in_smem] + [in_vmem] * len...]
    ppermute x2, waiting for transfers between devices: 21 us -> 16 us  [exchange_rows(): lax.ppermute(high, 'row', backward)]
    ppermute x37 -> x41, waiting for transfers between devices: 192 us -> 188 us  [swap(): return lax.ppermute(block, axis, [(i, i ^ bits) for i in range(count)])]
    ppermute x37 -> x41, starting transfers between devices: 56.6 us -> 53.5 us  [swap(): return lax.ppermute(block, axis, [(i, i ^ bits) for i in range(count)])]
  transfers between devices with their start and end apart: 47 -> 50, of which waited for: 26 -> 27; matrix products, arithmetic and copies ran while one was open for 6% -> 6% of each run, Pallas kernels for 14% -> 21%
where the time goes in v4:
time: 469 us; the launch traced here: 462 us
  waiting for transfers between devices  208 us (44%)
  Pallas kernels  103 us (22%)
  starting transfers between devices  81.4 us (17%)
  local copies, waits for them, and re-layouts  34.3 us (7%)
  other arithmetic  20.7 us (4%)
  between operations  15.2 us (3%)
    ppermute x41, waiting for transfers between devices, swap(): return lax.ppermute(block, axis, [(i, i ^ bits) for i in range(count)])  188 us
    pallas_call x15, Pallas kernels, call(): pl.pallas_call(body, out_shape=outs, in_specs=[in_smem] + [in_vmem] * len...  81.1 us
    ppermute x41, starting transfers between devices, swap(): return lax.ppermute(block, axis, [(i, i ^ bits) for i in range(count)])  53.5 us
    unnamed x95, local copies, waits for them, and re-layouts  26.2 us
    ppermute x2, waiting for transfers between devices, exchange_rows(): lax.ppermute(high, 'row', backward)  16 us
    pallas_call x2, Pallas kernels, depthwise(): pl.pallas_call(body, out_shape=shape_of(mid.shape, f32 if extra is None e...  14.9 us
  transfers between devices with their start and end apart: 50, of which 27 were waited for; matrix products, arithmetic and copies ran while one was open for 6% of the time, Pallas kernels for 21%

profile of v4, /device:TPU:0, one launch (start us, length us, event | category | flops | bytes accessed | tf_op | source)
XLA Modules:
  0.0 462.2 jit_solution(10610837523426866140)
XLA Ops:
  13.5 4.8 %collective-permute-start = (bf16[3,2,32,704]{3,2,1,0:T(8,128)(2,1)S(1)}, bf16[3,2,32,704]{3,2,1,0:T(8,128)(2,1)S(1)}, u32[]{:S(2)}, u32[]{:S(2)}) collective-permute-start(bf16[3,2,32,704]{3,2,1,0:T(8,128)(2,1)S(1)} %get-tuple-element.52), channel_id=1, source_target_pairs={{0,4},{4,8},{8,12},{1,5},{5,9},{9,13},{2,6},{6,10},{10,14},{3,7},{... | collective-permute-start | bytes 811016 | tf_op jit(solution)/shard_map/ppermute | solution.py:348
  19.6 1.6 collective-permute-start.19
  21.3 2.6 collective-permute-start.20
  24.6 8.3 %collective-permute-done.1.high = bf16[3,2,32,704]{3,2,1,0:T(8,128)(2,1)S(1)} collective-permute-done((bf16[3,2,32,704]{3,2,1,0:T(8,128)(2,1)S(1)}, bf16[3,2,32,704]{3,2,1,0:T(8,128)(2,1)S(1)}, u32[]{:S(2)}, u32[]{:S(2)}) %collective-permute-start.1) | collective-permute-done | bytes 270368 | tf_op jit(solution)/shard_map/ppermute | solution.py:348
  32.9 6.9 %shard_map.120 = f32[4,2,32,704]{3,2,1,0:T(8,128)S(1)} custom-call(s32[2]{0:T(128)S(1)} %pad_add_fusion.places, bf16[3,2,32,704]{3,2,1,0:T(8,128)(2,1)S(1)} %collective-permute-done.low, bf16[4,2,32,704]{3,2,1,0:T(8,128)(2,1)S(1)} %copy-done.11, bf16[3,2,32,704]{3,2,1,0:T(8,128)(2,1)S(1)} %collective-permute-done.1.high, f32[7,7,704]{2,1,0:T(8,128)S(1)} %copy-done.37), custom_call_target="tpu_custom_call" | custom-call | tf_op jit(solution)/shard_map/pallas_call | solution.py:398
  41.6 7.4 %collective-permute-done.20 = bf16[704,256]{1,0:T(8,128)(2,1)S(1)} collective-permute-done((bf16[704,256]{1,0:T(8,128)(2,1)S(1)}, bf16[704,256]{1,0:T(8,128)(2,1)S(1)}, u32[]{:S(2)}, u32[]{:S(2)}) %collective-permute-start.20) | collective-permute-done | bytes 360480 | tf_op jit(solution)/shard_map/ppermute | solution.py:21
  50.3 6.6 %collective-permute-start.2 = (f32[2,4,2,32]{3,2,1,0:T(2,128)S(1)}, f32[2,4,2,32]{3,2,1,0:T(2,128)S(1)}, u32[]{:S(2)}, u32[]{:S(2)}) collective-permute-start(f32[2,4,2,32]{3,2,1,0:T(2,128)S(1)} %pad_maximum_fusion.2), channel_id=1, source_target_pairs={{0,1},{1,0},{2,3},{3,2},{4,5},{5,4},{6,7},{7,6},{8,9},{9,8},{10,11... | collective-permute-start | bytes 6152 | tf_op jit(solution)/shard_map/ppermute | solution.py:21
  59.4 2.1 collective-permute-done.3
  61.4 2.0 collective-permute-done.4
  63.9 1.9 collective-permute-start.9
  65.9 13.3 %collective-permute-done.5 = bf16[704,256]{1,0:T(8,128)(2,1)S(1)} collective-permute-done((bf16[704,256]{1,0:T(8,128)(2,1)S(1)}, bf16[704,256]{1,0:T(8,128)(2,1)S(1)}, u32[]{:S(2)}, u32[]{:S(2)}) %collective-permute-start.5) | collective-permute-done | bytes 360480 | tf_op jit(solution)/shard_map/ppermute | solution.py:21
  79.1 9.7 %collective-permute-done.10 = bf16[704,256]{1,0:T(8,128)(2,1)S(1)} collective-permute-done((bf16[704,256]{1,0:T(8,128)(2,1)S(1)}, bf16[704,256]{1,0:T(8,128)(2,1)S(1)}, u32[]{:S(2)}, u32[]{:S(2)}) %collective-permute-start.10) | collective-permute-done | bytes 360480 | tf_op jit(solution)/shard_map/ppermute | solution.py:21
  89.6 3.8 all-to-all-start
  94.6 1.8 collective-permute-start.6
  100.3 28.7 %collective-permute-done.6.refs_1_ = bf16[2,704,256]{2,1,0:T(8,128)(2,1)S(1)} collective-permute-done((bf16[2,704,256]{2,1,0:T(8,128)(2,1)S(1)}, bf16[2,704,256]{2,1,0:T(8,128)(2,1)S(1)}, u32[]{:S(2)}, u32[]{:S(2)}) %collective-permute-start.6) | collective-permute-done | bytes 720928 | tf_op jit(solution)/shard_map/ppermute | solution.py:21
  129.1 1.7 collective-permute-done.7.refs_2_
  131.6 21.2 %collective-permute-done.11.refs_5_ = bf16[2,704,256]{2,1,0:T(8,128)(2,1)S(1)} collective-permute-done((bf16[2,704,256]{2,1,0:T(8,128)(2,1)S(1)}, bf16[2,704,256]{2,1,0:T(8,128)(2,1)S(1)}, u32[]{:S(2)}, u32[]{:S(2)}) %collective-permute-start.11) | collective-permute-done | bytes 720928 | tf_op jit(solution)/shard_map/ppermute | solution.py:21
  160.8 5.0 %all-to-all-start.1 = ((bf16[4,704,352]{2,1,0:T(8,128)(2,1)}), bf16[4,704,352]{2,1,0:T(8,128)(2,1)}, u32[]{:S(2)}, u32[]{:S(2)}) async-start(bf16[4,704,352]{2,1,0:T(8,128)(2,1)} %copy-done.3), calls=%async_computation.1 | async-start | bytes 4325376 | tf_op jit(solution)/shard_map/all_to_all | solution.py:498
  167.3 5.6 %shard_map.121 = (bf16[4,704,704]{2,1,0:T(8,128)(2,1)S(1)}, bf16[4,704,704]{2,1,0:T(8,128)(2,1)}) custom-call(s32[2]{0:T(128)S(1)} %pad_add_fusion.places, bf16[4,704,352]{2,1,0:T(8,128)(2,1)S(1)} %all-to-all-done.mine, bf16[4,704,352]{2,1,0:T(8,128)(2,1)} %collective-permute-done.14.other), custom_call_target="tpu_custom_call" | custom-call | tf_op jit(solution)/shard_map/pallas_call | solution.py:88
  172.8 2.0 copy-done.13
  174.9 9.9 %shard_map.122 = (f32[704,1024]{1,0:T(8,128)S(1)}, f32[704,1024]{1,0:T(8,128)}, f32[704,2]{1,0:T(8,128)S(1)}) custom-call(s32[2]{0:T(128)S(1)} %pad_add_fusion.places, bf16[2,704,256]{2,1,0:T(8,128)(2,1)S(1)} %copy-done.5, bf16[2,704,256]{2,1,0:T(8,128)(2,1)S(1)} %copy-done.16, bf16[2,704,256]{2,1,0:T(8,128)(2,1)S(1)} %copy-done.19, ...), custom_call_target="tpu_custom_call" | custom-call | tf_op jit(solution)/shard_map/pallas_call | solution.py:88
  186.5 2.1 collective-permute-done.15
  189.2 2.9 collective-permute-done.16
  192.1 2.0 collective-permute-start.17
  194.1 6.5 %collective-permute-done.17 = f32[2]{0:T(128)S(1)} collective-permute-done((f32[2]{0:T(128)S(1)}, f32[2]{0:T(128)S(1)}, u32[]{:S(2)}, u32[]{:S(2)}) %collective-permute-start.17) | collective-permute-done | bytes 40 | tf_op jit(solution)/shard_map/ppermute | solution.py:21
  200.6 4.5 collective-permute-start.18
  205.1 10.2 %collective-permute-done.18 = f32[2]{0:T(128)S(1)} collective-permute-done((f32[2]{0:T(128)S(1)}, f32[2]{0:T(128)S(1)}, u32[]{:S(2)}, u32[]{:S(2)}) %collective-permute-start.18) | collective-permute-done | bytes 40 | tf_op jit(solution)/shard_map/ppermute | solution.py:21
  215.4 1.7 shard_map.123.left.refs_0_
  217.2 1.6 copy-done
  218.8 7.4 %shard_map.125 = (bf16[4,704,352]{2,1,0:T(8,128)(2,1)S(1)}, bf16[4,704,352]{2,1,0:T(8,128)(2,1)S(1)}) custom-call(s32[2]{0:T(128)S(1)} %pad_add_fusion.places, bf16[704,1024]{1,0:T(8,128)(2,1)S(1)} %shard_map.123.left.refs_0_, bf16[4,4,704,256]{3,2,1,0:T(8,128)(2,1)} %bitcast.112), custom_call_target="tpu_custom_call" | custom-call | tf_op jit(solution)/shard_map/pallas_call | solution.py:88
  226.2 4.2 collective-permute-done.22.got
  233.2 4.5 all-to-all-start.2
  237.7 6.1 %shard_map.127 = (bf16[4,704,704]{2,1,0:T(8,128)(2,1)S(1)}, bf16[4,704,704]{2,1,0:T(8,128)(2,1)}) custom-call(s32[2]{0:T(128)S(1)} %pad_add_fusion.places, bf16[4,704,352]{2,1,0:T(8,128)(2,1)} %all-to-all-done.1.mine, bf16[4,704,352]{2,1,0:T(8,128)(2,1)} %collective-permute-done.23.other), custom_call_target="tpu_custom_call" | custom-call | tf_op jit(solution)/shard_map/pallas_call | solution.py:88
  243.8 2.0 copy-done.12
  245.8 8.8 %shard_map.129 = (f32[704,1024]{1,0:T(8,128)S(1)}, f32[704,2]{1,0:T(8,128)S(1)}) custom-call(s32[2]{0:T(128)S(1)} %pad_add_fusion.places, bf16[4,4,704,256]{3,2,1,0:T(8,128)(2,1)} %bitcast.113, bf16[4,704,704]{2,1,0:T(8,128)(2,1)} %copy-done.12, f32[704,1024]{1,0:T(8,128)S(1)} %copy-done.1), custom_call_target="tpu_custom_call" | custom-call | tf_op jit(solution)/shard_map/pallas_call | solution.py:88
  256.3 10.8 %shard_map.130 = (bf16[704,1024]{1,0:T(8,128)(2,1)S(1)}, bf16[2,2,704,256]{3,2,1,0:T(8,128)(2,1)S(1)}, bf16[2,2,704,256]{3,2,1,0:T(8,128)(2,1)S(1)}, bf16[2,2,70...) custom-call(s32[2]{0:T(128)S(1)} %pad_add_fusion.places, f32[704,1024]{1,0:T(8,128)} %copy-done.14, f32[704,1024]{1,0:T(8,128)} %copy-done, ...), custom_call_target="tpu_custom_call" | custom-call | tf_op jit(solution)/shard_map/pallas_call | solution.py:88
  269.2 8.3 %shard_map.128 = (bf16[704,1024]{1,0:T(8,128)(2,1)}, bf16[2,2,704,256]{3,2,1,0:T(8,128)(2,1)S(1)}, bf16[2,2,704,256]{3,2,1,0:T(8,128)(2,1)}, bf16[2,2,704,256]{3...) custom-call(s32[2]{0:T(128)S(1)} %pad_add_fusion.places, bf16[704,1024]{1,0:T(8,128)(2,1)S(1)} %shard_map.123.left.refs_0_, ...), custom_call_target="tpu_custom_call" | custom-call | tf_op jit(solution)/shard_map/pallas_call | solution.py:88
  278.7 8.1 %shard_map.131 = (bf16[4,704,352]{2,1,0:T(8,128)(2,1)S(1)}, bf16[4,704,352]{2,1,0:T(8,128)(2,1)}) custom-call(s32[2]{0:T(128)S(1)} %pad_add_fusion.places, bf16[704,1024]{1,0:T(8,128)(2,1)S(1)} %get-tuple-element.80.left, bf16[2,704,256]{2,1,0:T(8,128)(2,1)S(1)} %copy-done.6, bf16[2,704,256]{2,1,0:T(8,128)(2,1)S(1)} %copy-done.17, ...), custom_call_target="tpu_custom_call" | custom-call | tf_op jit(solution)/shard_map/pallas_call | solution.py:88
  286.9 14.5 %collective-permute-done.26 = bf16[2,2,704,256]{3,2,1,0:T(8,128)(2,1)} collective-permute-done((bf16[2,2,704,256]{3,2,1,0:T(8,128)(2,1)}, bf16[2,2,704,256]{3,2,1,0:T(8,128)(2,1)}, u32[]{:S(2)}, u32[]{:S(2)}) %collective-permute-start.26) | collective-permute-done | bytes 1441824 | tf_op jit(solution)/shard_map/ppermute | solution.py:21
  301.3 1.7 convert_add_fusion.2
  304.6 1.7 convert_add_fusion.3
  309.3 11.4 %collective-permute-done.27 = bf16[1,2,704,256]{3,2,1,0:T(8,128)(2,1)S(1)} collective-permute-done((bf16[1,2,704,256]{3,2,1,0:T(8,128)(2,1)S(1)}, bf16[1,2,704,256]{3,2,1,0:T(8,128)(2,1)S(1)}, u32[]{:S(2)}, u32[]{:S(2)}) %collective-permute-start.27) | collective-permute-done | bytes 720928 | tf_op jit(solution)/shard_map/ppermute | solution.py:21
  323.2 3.3 collective-permute-done.25
  326.4 12.4 %collective-permute-done.32 = bf16[2,704,256]{2,1,0:T(8,128)(2,1)S(1)} collective-permute-done((bf16[2,704,256]{2,1,0:T(8,128)(2,1)}, bf16[2,704,256]{2,1,0:T(8,128)(2,1)S(1)}, u32[]{:S(2)}, u32[]{:S(2)}) %collective-permute-start.32) | collective-permute-done | bytes 720928 | tf_op jit(solution)/shard_map/ppermute | solution.py:21
  338.8 1.9 convert_add_fusion.4
  341.4 2.0 collective-permute-start.33
  344.8 13.2 %collective-permute-done.33 = bf16[1,704,256]{2,1,0:T(8,128)(2,1)S(1)} collective-permute-done((bf16[1,704,256]{2,1,0:T(8,128)(2,1)S(1)}, bf16[1,704,256]{2,1,0:T(8,128)(2,1)S(1)}, u32[]{:S(2)}, u32[]{:S(2)}) %collective-permute-start.33) | collective-permute-done | bytes 360480 | tf_op jit(solution)/shard_map/ppermute | solution.py:21
  358.9 2.3 copy.32
  362.8 3.0 collective-permute-start.35
  367.2 3.6 shard_map.133
  372.4 1.7 convert_add_fusion
  378.0 3.8 all-to-all-start.3
  383.4 1.8 convert_add_fusion.1
  386.0 6.4 %collective-permute-done.31 = bf16[1,2,704,256]{3,2,1,0:T(8,128)(2,1)} collective-permute-done((bf16[1,2,704,256]{3,2,1,0:T(8,128)(2,1)}, bf16[1,2,704,256]{3,2,1,0:T(8,128)(2,1)}, u32[]{:S(2)}, u32[]{:S(2)}) %collective-permute-start.31) | collective-permute-done | bytes 720928 | tf_op jit(solution)/shard_map/ppermute | solution.py:21
  393.8 3.4 collective-permute-start.38
  398.5 2.9 collective-permute-done.38.low
  401.5 7.7 %collective-permute-done.39.high = bf16[3,2,32,704]{3,2,1,0:T(8,128)(2,1)S(1)} collective-permute-done((bf16[3,2,32,704]{3,2,1,0:T(8,128)(2,1)S(1)}, bf16[3,2,32,704]{3,2,1,0:T(8,128)(2,1)S(1)}, u32[]{:S(2)}, u32[]{:S(2)}) %collective-permute-start.39) | collective-permute-done | bytes 270368 | tf_op jit(solution)/shard_map/ppermute | solution.py:348
  409.2 7.0 %shard_map.136 = f32[7,7,704]{2,1,0:T(8,128)S(1)} custom-call(s32[2]{0:T(128)S(1)} %pad_add_fusion.places, bf16[3,2,32,704]{3,2,1,0:T(8,128)(2,1)S(1)} %copy-done.34, bf16[4,2,32,704]{3,2,1,0:T(8,128)(2,1)S(1)} %copy-done.11, bf16[3,2,32,704]{3,2,1,0:T(8,128)(2,1)S(1)} %copy-done.36, f32[4,2,32,704]{3,2,1,0:T(8,128)S(1)} %get-tuple-element.98.mid.grad), custom_call_target="tpu_custom_call" | custom-call | tf_op jit(solution)/shard_map/pallas_call | solution.py:436
  416.3 8.0 %shard_map.132 = bf16[4,2,32,704]{3,2,1,0:T(8,128)(2,1)} custom-call(s32[2]{0:T(128)S(1)} %pad_add_fusion.places, bf16[3,2,32,704]{3,2,1,0:T(8,128)(2,1)S(1)} %collective-permute-done.38.low, f32[4,2,32,704]{3,2,1,0:T(8,128)S(1)} %get-tuple-element.98.mid.grad, bf16[3,2,32,704]{3,2,1,0:T(8,128)(2,1)S(1)} %collective-permute-done.39.high, ...), custom_call_target="tpu_custom_call" | custom-call | tf_op jit(solution)/shard_map/pallas_call | solution.py:398
  425.8 6.0 %collective-permute-done.37 = bf16[2,704,256]{2,1,0:T(8,128)(2,1)S(1)} collective-permute-done((bf16[2,704,256]{2,1,0:T(8,128)(2,1)S(1)}, bf16[2,704,256]{2,1,0:T(8,128)(2,1)S(1)}, u32[]{:S(2)}, u32[]{:S(2)}) %collective-permute-start.37) | collective-permute-done | bytes 720928 | tf_op jit(solution)/shard_map/ppermute | solution.py:21
  432.0 3.4 collective-permute-start.40
  436.4 4.1 shard_map.135
  441.2 7.4 %collective-permute-done.40 = bf16[1,704,256]{2,1,0:T(8,128)(2,1)S(1)} collective-permute-done((bf16[1,704,256]{2,1,0:T(8,128)(2,1)S(1)}, bf16[1,704,256]{2,1,0:T(8,128)(2,1)S(1)}, u32[]{:S(2)}, u32[]{:S(2)}) %collective-permute-start.40) | collective-permute-done | bytes 360480 | tf_op jit(solution)/shard_map/ppermute | solution.py:21
  451.8 3.1 shard_map.134
  (205 shorter events, 70.7 us)
Async XLA Ops:
  7.2 211.6 %all-gather.3.cloned.1.call-start = ((), (), s32[]{:S(2)}) async-start(), calls=%async_computation.4 | async-start | bytes 7208960 | tf_op jit(solution)/shard_map/all_gather | solution.py:492
  10.8 22.0 %copy-start.11 = (bf16[4,2,32,704]{3,2,1,0:T(8,128)(2,1)S(1)}, bf16[4,2,32,704]{3,2,1,0:T(8,128)(2,1)}, u32[]{:S(2)}) copy-start(bf16[4,2,32,704]{3,2,1,0:T(8,128)(2,1)} %mid.3) | copy-start | bytes 1081348
  10.8 22.0 %copy-start.37 = (f32[7,7,704]{2,1,0:T(8,128)S(1)}, f32[7,7,704]{2,1,0:T(8,128)}, u32[]{:S(2)}) copy-start(f32[7,7,704]{2,1,0:T(8,128)} %kern.3) | copy-start | bytes 413956
  13.5 11.1 %collective-permute-start = (bf16[3,2,32,704]{3,2,1,0:T(8,128)(2,1)S(1)}, bf16[3,2,32,704]{3,2,1,0:T(8,128)(2,1)S(1)}, u32[]{:S(2)}, u32[]{:S(2)}) collective-permute-start(bf16[3,2,32,704]{3,2,1,0:T(8,128)(2,1)S(1)} %get-tuple-element.52), channel_id=1, source_target_pairs={{0,4},{4,8},{8,12},{1,5},{5,9},{9,13},{2,6},{6,10},{10,14},{3,7},{... | collective-permute-start | bytes 811016 | tf_op jit(solution)/shard_map/ppermute | solution.py:348
  18.3 14.5 %collective-permute-start.1 = (bf16[3,2,32,704]{3,2,1,0:T(8,128)(2,1)S(1)}, bf16[3,2,32,704]{3,2,1,0:T(8,128)(2,1)S(1)}, u32[]{:S(2)}, u32[]{:S(2)}) collective-permute-start(bf16[3,2,32,704]{3,2,1,0:T(8,128)(2,1)S(1)} %get-tuple-element.53), channel_id=1, source_target_pairs={{4,0},{8,4},{12,8},{5,1},{9,5},{13,9},{6,2},{10,6},{14,10},{7,3},{... | collective-permute-start | bytes 811016 | tf_op jit(solution)/shard_map/ppermute | solution.py:348
  19.6 22.0 %collective-permute-start.19 = (bf16[704,256]{1,0:T(8,128)(2,1)S(1)}, bf16[704,256]{1,0:T(8,128)(2,1)S(1)}, u32[]{:S(2)}, u32[]{:S(2)}) collective-permute-start(bf16[704,256]{1,0:T(8,128)(2,1)S(1)} %get-tuple-element.62), channel_id=1, source_target_pairs={{0,1},{1,0},{2,3},{3,2},{4,5},{5,4},{6,7},{7,6},{8,9},{9,8},{10,11... | collective-permute-start | bytes 1081352 | tf_op jit(solution)/shard_map/ppermute | solution.py:21
  21.3 27.7 %collective-permute-start.20 = (bf16[704,256]{1,0:T(8,128)(2,1)S(1)}, bf16[704,256]{1,0:T(8,128)(2,1)S(1)}, u32[]{:S(2)}, u32[]{:S(2)}) collective-permute-start(bf16[704,256]{1,0:T(8,128)(2,1)S(1)} %get-tuple-element.62), channel_id=1, source_target_pairs={{0,2},{1,3},{2,0},{3,1},{4,6},{5,7},{6,4},{7,5},{8,10},{9,11},{10,... | collective-permute-start | bytes 1081352 | tf_op jit(solution)/shard_map/ppermute | solution.py:21
  23.9 25.1 %collective-permute-start.21 = (bf16[704,256]{1,0:T(8,128)(2,1)S(1)}, bf16[704,256]{1,0:T(8,128)(2,1)S(1)}, u32[]{:S(2)}, u32[]{:S(2)}) collective-permute-start(bf16[704,256]{1,0:T(8,128)(2,1)S(1)} %get-tuple-element.62), channel_id=1, source_target_pairs={{0,3},{1,2},{2,1},{3,0},{4,7},{5,6},{6,5},{7,4},{8,11},{9,10},{10,... | collective-permute-start | bytes 1081352 | tf_op jit(solution)/shard_map/ppermute | solution.py:21
  50.3 9.1 %collective-permute-start.2 = (f32[2,4,2,32]{3,2,1,0:T(2,128)S(1)}, f32[2,4,2,32]{3,2,1,0:T(2,128)S(1)}, u32[]{:S(2)}, u32[]{:S(2)}) collective-permute-start(f32[2,4,2,32]{3,2,1,0:T(2,128)S(1)} %pad_maximum_fusion.2), channel_id=1, source_target_pairs={{0,1},{1,0},{2,3},{3,2},{4,5},{5,4},{6,7},{7,6},{8,9},{9,8},{10,11... | collective-permute-start | bytes 6152 | tf_op jit(solution)/shard_map/ppermute | solution.py:21
  56.9 4.5 collective-permute-start.3
  58.0 5.4 %collective-permute-start.4 = (f32[2,4,2,32]{3,2,1,0:T(2,128)S(1)}, f32[2,4,2,32]{3,2,1,0:T(2,128)S(1)}, u32[]{:S(2)}, u32[]{:S(2)}) collective-permute-start(f32[2,4,2,32]{3,2,1,0:T(2,128)S(1)} %pad_maximum_fusion.2), channel_id=1, source_target_pairs={{0,3},{1,2},{2,1},{3,0},{4,7},{5,6},{6,5},{7,4},{8,11},{9,10},{10,... | collective-permute-start | bytes 6152 | tf_op jit(solution)/shard_map/ppermute | solution.py:21
  63.8 25.0 %copy-start.41 = (bf16[704,256]{1,0:T(8,128)(2,1)}, bf16[704,256]{1,0:T(8,128)(2,1)S(1)}, u32[]{:S(2)}) copy-start(bf16[704,256]{1,0:T(8,128)(2,1)S(1)} %copy.27) | copy-start | bytes 1081348
  63.8 15.3 %collective-permute-start.5 = (bf16[704,256]{1,0:T(8,128)(2,1)S(1)}, bf16[704,256]{1,0:T(8,128)(2,1)S(1)}, u32[]{:S(2)}, u32[]{:S(2)}) collective-permute-start(bf16[704,256]{1,0:T(8,128)(2,1)S(1)} %copy.27), channel_id=1, source_target_pairs={{0,2},{1,3},{2,0},{3,1},{4,6},{5,7},{6,4},{7,5},{8,10},{9,11},{10,... | collective-permute-start | bytes 1081352 | tf_op jit(solution)/shard_map/ppermute | solution.py:21
  63.9 15.2 %collective-permute-start.9 = (bf16[704,256]{1,0:T(8,128)(2,1)S(1)}, bf16[704,256]{1,0:T(8,128)(2,1)S(1)}, u32[]{:S(2)}, u32[]{:S(2)}) collective-permute-start(bf16[704,256]{1,0:T(8,128)(2,1)S(1)} %copy.27), channel_id=1, source_target_pairs={{0,1},{1,0},{2,3},{3,2},{4,5},{5,4},{6,7},{7,6},{8,9},{9,8},{10,11... | collective-permute-start | bytes 1081352 | tf_op jit(solution)/shard_map/ppermute | solution.py:21
  79.1 9.7 %copy-start.44 = (bf16[704,256]{1,0:T(8,128)(2,1)}, bf16[704,256]{1,0:T(8,128)(2,1)S(1)}, u32[]{:S(2)}) copy-start(bf16[704,256]{1,0:T(8,128)(2,1)S(1)} %collective-permute-done.5) | copy-start | bytes 1081348
  79.1 9.7 %collective-permute-start.10 = (bf16[704,256]{1,0:T(8,128)(2,1)S(1)}, bf16[704,256]{1,0:T(8,128)(2,1)S(1)}, u32[]{:S(2)}, u32[]{:S(2)}) collective-permute-start(bf16[704,256]{1,0:T(8,128)(2,1)S(1)} %collective-permute-done.5), channel_id=1, source_target_pairs={{0,1},{1,0},{2,3},{3,2},{4,5},{5,4},{6,7},{7,6},{8,9},{9,8},{10,11... | collective-permute-start | bytes 1081352 | tf_op jit(solution)/shard_map/ppermute | solution.py:21
  79.1 9.7 %copy-start.42 = (bf16[704,256]{1,0:T(8,128)(2,1)}, bf16[704,256]{1,0:T(8,128)(2,1)S(1)}, u32[]{:S(2)}) copy-start(bf16[704,256]{1,0:T(8,128)(2,1)S(1)} %collective-permute-done.9) | copy-start | bytes 1081348
  89.6 64.2 %all-to-all-start = ((bf16[4,704,352]{2,1,0:T(8,128)(2,1)}), bf16[4,704,352]{2,1,0:T(8,128)(2,1)S(1)}, u32[]{:S(2)}, u32[]{:S(2)}) async-start(bf16[4,704,352]{2,1,0:T(8,128)(2,1)} %copy-done.24), calls=%async_computation | async-start | bytes 4325376 | tf_op jit(solution)/shard_map/all_to_all | solution.py:493
  94.6 58.3 %copy-start.4 = (bf16[2,704,256]{2,1,0:T(8,128)(2,1)}, bf16[2,704,256]{2,1,0:T(8,128)(2,1)S(1)}, u32[]{:S(2)}) copy-start(bf16[2,704,256]{2,1,0:T(8,128)(2,1)S(1)} %pad_maximum_fusion.refs_0_) | copy-start | bytes 2162692
  94.6 34.5 %collective-permute-start.6 = (bf16[2,704,256]{2,1,0:T(8,128)(2,1)S(1)}, bf16[2,704,256]{2,1,0:T(8,128)(2,1)S(1)}, u32[]{:S(2)}, u32[]{:S(2)}) collective-permute-start(bf16[2,704,256]{2,1,0:T(8,128)(2,1)S(1)} %pad_maximum_fusion.refs_0_), channel_id=1, source_target_pairs={{0,4},{4,0},{8,12},{12,8},{1,5},{5,1},{9,13},{13,9},{2,6},{6,2},{1... | collective-permute-start | bytes 2162696 | tf_op jit(solution)/shard_map/ppermute | solution.py:21
  96.3 34.4 %collective-permute-start.7 = (bf16[2,704,256]{2,1,0:T(8,128)(2,1)S(1)}, bf16[2,704,256]{2,1,0:T(8,128)(2,1)S(1)}, u32[]{:S(2)}, u32[]{:S(2)}) collective-permute-start(bf16[2,704,256]{2,1,0:T(8,128)(2,1)S(1)} %pad_maximum_fusion.refs_0_), channel_id=1, source_target_pairs={{0,8},{4,12},{8,0},{12,4},{1,9},{5,13},{9,1},{13,5},{2,10},{6,14},... | collective-permute-start | bytes 2162696 | tf_op jit(solution)/shard_map/ppermute | solution.py:21
  97.9 54.9 %collective-permute-start.11 = (bf16[2,704,256]{2,1,0:T(8,128)(2,1)S(1)}, bf16[2,704,256]{2,1,0:T(8,128)(2,1)S(1)}, u32[]{:S(2)}, u32[]{:S(2)}) collective-permute-start(bf16[2,704,256]{2,1,0:T(8,128)(2,1)S(1)} %pad_maximum_fusion.1.refs_4_), channel_id=1, source_target_pairs={{0,4},{4,0},{8,12},{12,8},{1,5},{5,1},{9,13},{13,9},{2,6},{6,2},{1... | collective-permute-start | bytes 2162696 | tf_op jit(solution)/shard_map/ppermute | solution.py:21
  99.4 54.3 %collective-permute-start.12 = (bf16[2,704,256]{2,1,0:T(8,128)(2,1)S(1)}, bf16[2,704,256]{2,1,0:T(8,128)(2,1)}, u32[]{:S(2)}, u32[]{:S(2)}) collective-permute-start(bf16[2,704,256]{2,1,0:T(8,128)(2,1)S(1)} %pad_maximum_fusion.1.refs_4_), channel_id=1, source_target_pairs={{0,8},{4,12},{8,0},{12,4},{1,9},{5,13},{9,1},{13,5},{2,10},{6,14},... | collective-permute-start | bytes 2162696 | tf_op jit(solution)/shard_map/ppermute | solution.py:21
  129.0 23.8 %copy-start.15 = (bf16[2,704,256]{2,1,0:T(8,128)(2,1)}, bf16[2,704,256]{2,1,0:T(8,128)(2,1)S(1)}, u32[]{:S(2)}) copy-start(bf16[2,704,256]{2,1,0:T(8,128)(2,1)S(1)} %collective-permute-done.6.refs_1_) | copy-start | bytes 2162692
  153.8 13.5 %collective-permute-start.14 = (bf16[4,704,352]{2,1,0:T(8,128)(2,1)S(1)}, bf16[4,704,352]{2,1,0:T(8,128)(2,1)}, u32[]{:S(2)}, u32[]{:S(2)}) collective-permute-start(bf16[4,704,352]{2,1,0:T(8,128)(2,1)S(1)} %all-to-all-done.mine), channel_id=1, source_target_pairs={{0,16},{16,0},{1,17},{17,1},{2,18},{18,2},{3,19},{19,3},{4,20},{20... | collective-permute-start | bytes 5947400 | tf_op jit(solution)/shard_map/ppermute | solution.py:21
  153.8 21.1 %collective-permute-start.8 = (bf16[2,704,256]{2,1,0:T(8,128)(2,1)}, bf16[2,704,256]{2,1,0:T(8,128)(2,1)}, u32[]{:S(2)}, u32[]{:S(2)}) collective-permute-start(bf16[2,704,256]{2,1,0:T(8,128)(2,1)} %copy-done.15), channel_id=1, source_target_pairs={{0,8},{4,12},{8,0},{12,4},{1,9},{5,13},{9,1},{13,5},{2,10},{6,14},... | collective-permute-start | bytes 2162696 | tf_op jit(solution)/shard_map/ppermute | solution.py:21
  155.3 19.5 %collective-permute-start.13 = (bf16[2,704,256]{2,1,0:T(8,128)(2,1)}, bf16[2,704,256]{2,1,0:T(8,128)(2,1)}, u32[]{:S(2)}, u32[]{:S(2)}) collective-permute-start(bf16[2,704,256]{2,1,0:T(8,128)(2,1)} %collective-permute-done.12.refs_6_), channel_id=1, source_target_pairs={{0,4},{4,0},{8,12},{12,8},{1,5},{5,1},{9,13},{13,9},{2,6},{6,2},{1... | collective-permute-start | bytes 2162696 | tf_op jit(solution)/shard_map/ppermute | solution.py:21
  160.8 72.1 %all-to-all-start.1 = ((bf16[4,704,352]{2,1,0:T(8,128)(2,1)}), bf16[4,704,352]{2,1,0:T(8,128)(2,1)}, u32[]{:S(2)}, u32[]{:S(2)}) async-start(bf16[4,704,352]{2,1,0:T(8,128)(2,1)} %copy-done.3), calls=%async_computation.1 | async-start | bytes 4325376 | tf_op jit(solution)/shard_map/all_to_all | solution.py:498
  185.0 3.6 collective-permute-start.15
  188.6 3.5 collective-permute-start.16
  192.1 8.5 %collective-permute-start.17 = (f32[2]{0:T(128)S(1)}, f32[2]{0:T(128)S(1)}, u32[]{:S(2)}, u32[]{:S(2)}) collective-permute-start(f32[2]{0:T(128)S(1)} %add.212), channel_id=1, source_target_pairs={{0,1},{1,0},{2,3},{3,2},{4,5},{5,4},{6,7},{7,6},{8,9},{9,8},{10,11... | collective-permute-start | bytes 32 | tf_op jit(solution)/shard_map/ppermute | solution.py:21
  200.6 14.6 %collective-permute-start.18 = (f32[2]{0:T(128)S(1)}, f32[2]{0:T(128)S(1)}, u32[]{:S(2)}, u32[]{:S(2)}) collective-permute-start(f32[2]{0:T(128)S(1)} %add.213), channel_id=1, source_target_pairs={{0,2},{1,3},{2,0},{3,1},{4,6},{5,7},{6,4},{7,5},{8,10},{9,11},{10,... | collective-permute-start | bytes 32 | tf_op jit(solution)/shard_map/ppermute | solution.py:21
  226.1 4.3 collective-permute-start.22
  232.8 4.8 %collective-permute-start.23 = (bf16[4,704,352]{2,1,0:T(8,128)(2,1)}, bf16[4,704,352]{2,1,0:T(8,128)(2,1)}, u32[]{:S(2)}, u32[]{:S(2)}) collective-permute-start(bf16[4,704,352]{2,1,0:T(8,128)(2,1)} %all-to-all-done.1.mine), channel_id=1, source_target_pairs={{0,16},{16,0},{1,17},{17,1},{2,18},{18,2},{3,19},{19,3},{4,20},{20... | collective-permute-start | bytes 5947400 | tf_op jit(solution)/shard_map/ppermute | solution.py:21
  233.2 88.6 %all-to-all-start.2 = ((bf16[4,704,352]{2,1,0:T(8,128)(2,1)}), bf16[4,704,352]{2,1,0:T(8,128)(2,1)}, u32[]{:S(2)}, u32[]{:S(2)}) async-start(bf16[4,704,352]{2,1,0:T(8,128)(2,1)} %copy-done.2), calls=%async_computation.2 | async-start | bytes 4325376 | tf_op jit(solution)/shard_map/all_to_all | solution.py:510
  267.1 34.2 %collective-permute-start.26 = (bf16[2,2,704,256]{3,2,1,0:T(8,128)(2,1)}, bf16[2,2,704,256]{3,2,1,0:T(8,128)(2,1)}, u32[]{:S(2)}, u32[]{:S(2)}) collective-permute-start(bf16[2,2,704,256]{3,2,1,0:T(8,128)(2,1)} %get-tuple-element.85), channel_id=1, source_target_pairs={{0,8},{4,12},{8,0},{12,4},{1,9},{5,13},{9,1},{13,5},{2,10},{6,14},... | collective-permute-start | bytes 4325384 | tf_op jit(solution)/shard_map/ppermute | solution.py:21
  267.8 36.8 %collective-permute-start.24 = (bf16[2,2,704,256]{3,2,1,0:T(8,128)(2,1)S(1)}, bf16[2,2,704,256]{3,2,1,0:T(8,128)(2,1)}, u32[]{:S(2)}, u32[]{:S(2)}) collective-permute-start(bf16[2,2,704,256]{3,2,1,0:T(8,128)(2,1)S(1)} %get-tuple-element.79), channel_id=1, source_target_pairs={{0,4},{4,0},{8,12},{12,8},{1,5},{5,1},{9,13},{13,9},{2,6},{6,2},{1... | collective-permute-start | bytes 4325384 | tf_op jit(solution)/shard_map/ppermute | solution.py:21
  269.2 9.5 %copy-start.9 = (bf16[2,704,256]{2,1,0:T(8,128)(2,1)S(1)}, bf16[2,704,256]{2,1,0:T(8,128)(2,1)}, u32[]{:S(2)}) copy-start(bf16[2,704,256]{2,1,0:T(8,128)(2,1)} %copy-done.7) | copy-start | bytes 2162692
  269.2 9.5 %copy-start.17 = (bf16[2,704,256]{2,1,0:T(8,128)(2,1)S(1)}, bf16[2,704,256]{2,1,0:T(8,128)(2,1)}, u32[]{:S(2)}) copy-start(bf16[2,704,256]{2,1,0:T(8,128)(2,1)} %copy-done.15) | copy-start | bytes 2162692
  269.2 9.5 %copy-start.20 = (bf16[2,704,256]{2,1,0:T(8,128)(2,1)S(1)}, bf16[2,704,256]{2,1,0:T(8,128)(2,1)}, u32[]{:S(2)}) copy-start(bf16[2,704,256]{2,1,0:T(8,128)(2,1)} %copy-done.18) | copy-start | bytes 2162692
  269.2 9.5 %copy-start.23 = (bf16[2,704,256]{2,1,0:T(8,128)(2,1)S(1)}, bf16[2,704,256]{2,1,0:T(8,128)(2,1)}, u32[]{:S(2)}) copy-start(bf16[2,704,256]{2,1,0:T(8,128)(2,1)} %copy-done.21) | copy-start | bytes 2162692
  303.1 17.7 %collective-permute-start.27 = (bf16[1,2,704,256]{3,2,1,0:T(8,128)(2,1)S(1)}, bf16[1,2,704,256]{3,2,1,0:T(8,128)(2,1)S(1)}, u32[]{:S(2)}, u32[]{:S(2)}) collective-permute-start(bf16[1,2,704,256]{3,2,1,0:T(8,128)(2,1)S(1)} %slice.193), channel_id=1, source_target_pairs={{0,4},{4,0},{8,12},{12,8},{1,5},{5,1},{9,13},{13,9},{2,6},{6,2},{1... | collective-permute-start | bytes 2162696 | tf_op jit(solution)/shard_map/ppermute | solution.py:21
  308.8 17.6 %collective-permute-start.25 = (bf16[1,2,704,256]{3,2,1,0:T(8,128)(2,1)}, bf16[1,2,704,256]{3,2,1,0:T(8,128)(2,1)}, u32[]{:S(2)}, u32[]{:S(2)}) collective-permute-start(bf16[1,2,704,256]{3,2,1,0:T(8,128)(2,1)} %slice.194), channel_id=1, source_target_pairs={{0,8},{4,12},{8,0},{12,4},{1,9},{5,13},{9,1},{13,5},{2,10},{6,14},... | collective-permute-start | bytes 2162696 | tf_op jit(solution)/shard_map/ppermute | solution.py:21
  321.8 17.0 %collective-permute-start.32 = (bf16[2,704,256]{2,1,0:T(8,128)(2,1)}, bf16[2,704,256]{2,1,0:T(8,128)(2,1)S(1)}, u32[]{:S(2)}, u32[]{:S(2)}) collective-permute-start(bf16[2,704,256]{2,1,0:T(8,128)(2,1)} %fusion.3), channel_id=1, source_target_pairs={{0,1},{1,0},{2,3},{3,2},{4,5},{5,4},{6,7},{7,6},{8,9},{9,8},{10,11... | collective-permute-start | bytes 2162696 | tf_op jit(solution)/shard_map/ppermute | solution.py:21
  323.2 42.7 %collective-permute-start.41 = (bf16[4,704,352]{2,1,0:T(8,128)(2,1)}, bf16[4,704,352]{2,1,0:T(8,128)(2,1)}, u32[]{:S(2)}, u32[]{:S(2)}) collective-permute-start(bf16[4,704,352]{2,1,0:T(8,128)(2,1)} %get-tuple-element.81), channel_id=1, source_target_pairs={{0,16},{16,0},{1,17},{17,1},{2,18},{18,2},{3,19},{19,3},{4,20},{20... | collective-permute-start | bytes 5947400 | tf_op jit(solution)/shard_map/ppermute | solution.py:21
  340.7 31.7 %collective-permute-start.30 = (bf16[2,2,704,256]{3,2,1,0:T(8,128)(2,1)}, bf16[2,2,704,256]{3,2,1,0:T(8,128)(2,1)}, u32[]{:S(2)}, u32[]{:S(2)}) collective-permute-start(bf16[2,2,704,256]{3,2,1,0:T(8,128)(2,1)} %get-tuple-element.90), channel_id=1, source_target_pairs={{0,8},{4,12},{8,0},{12,4},{1,9},{5,13},{9,1},{13,5},{2,10},{6,14},... | collective-permute-start | bytes 4325384 | tf_op jit(solution)/shard_map/ppermute | solution.py:21
  341.4 16.6 %collective-permute-start.33 = (bf16[1,704,256]{2,1,0:T(8,128)(2,1)S(1)}, bf16[1,704,256]{2,1,0:T(8,128)(2,1)S(1)}, u32[]{:S(2)}, u32[]{:S(2)}) collective-permute-start(bf16[1,704,256]{2,1,0:T(8,128)(2,1)S(1)} %slice.196), channel_id=1, source_target_pairs={{0,2},{1,3},{2,0},{3,1},{4,6},{5,7},{6,4},{7,5},{8,10},{9,11},{10,... | collective-permute-start | bytes 1081352 | tf_op jit(solution)/shard_map/ppermute | solution.py:21
  343.4 39.8 %collective-permute-start.28 = (bf16[2,2,704,256]{3,2,1,0:T(8,128)(2,1)}, bf16[2,2,704,256]{3,2,1,0:T(8,128)(2,1)}, u32[]{:S(2)}, u32[]{:S(2)}) collective-permute-start(bf16[2,2,704,256]{3,2,1,0:T(8,128)(2,1)} %get-tuple-element.88), channel_id=1, source_target_pairs={{0,4},{4,0},{8,12},{12,8},{1,5},{5,1},{9,13},{13,9},{2,6},{6,2},{1... | collective-permute-start | bytes 4325384 | tf_op jit(solution)/shard_map/ppermute | solution.py:21
  362.7 8.0 %collective-permute-start.34 = (f32[2,4,2,32]{3,2,1,0:T(2,128)S(1)}, f32[2,4,2,32]{3,2,1,0:T(2,128)S(1)}, u32[]{:S(2)}, u32[]{:S(2)}) collective-permute-start(f32[2,4,2,32]{3,2,1,0:T(2,128)S(1)} %pad_maximum_fusion.3), channel_id=1, source_target_pairs={{0,1},{1,0},{2,3},{3,2},{4,5},{5,4},{6,7},{7,6},{8,9},{9,8},{10,11... | collective-permute-start | bytes 6152 | tf_op jit(solution)/shard_map/ppermute | solution.py:21
  362.8 8.0 %collective-permute-start.35 = (f32[2,4,2,32]{3,2,1,0:T(2,128)S(1)}, f32[2,4,2,32]{3,2,1,0:T(2,128)S(1)}, u32[]{:S(2)}, u32[]{:S(2)}) collective-permute-start(f32[2,4,2,32]{3,2,1,0:T(2,128)S(1)} %pad_maximum_fusion.3), channel_id=1, source_target_pairs={{0,2},{1,3},{2,0},{3,1},{4,6},{5,7},{6,4},{7,5},{8,10},{9,11},{10,... | collective-permute-start | bytes 6152 | tf_op jit(solution)/shard_map/ppermute | solution.py:21
  365.8 5.4 %collective-permute-start.36 = (f32[2,4,2,32]{3,2,1,0:T(2,128)S(1)}, f32[2,4,2,32]{3,2,1,0:T(2,128)S(1)}, u32[]{:S(2)}, u32[]{:S(2)}) collective-permute-start(f32[2,4,2,32]{3,2,1,0:T(2,128)S(1)} %pad_maximum_fusion.3), channel_id=1, source_target_pairs={{0,3},{1,2},{2,1},{3,0},{4,7},{5,6},{6,5},{7,4},{8,11},{9,10},{10,... | collective-permute-start | bytes 6152 | tf_op jit(solution)/shard_map/ppermute | solution.py:21
  376.6 15.8 %collective-permute-start.31 = (bf16[1,2,704,256]{3,2,1,0:T(8,128)(2,1)}, bf16[1,2,704,256]{3,2,1,0:T(8,128)(2,1)}, u32[]{:S(2)}, u32[]{:S(2)}) collective-permute-start(bf16[1,2,704,256]{3,2,1,0:T(8,128)(2,1)} %slice.191), channel_id=1, source_target_pairs={{0,4},{4,0},{8,12},{12,8},{1,5},{5,1},{9,13},{13,9},{2,6},{6,2},{1... | collective-permute-start | bytes 2162696 | tf_op jit(solution)/shard_map/ppermute | solution.py:21
  378.0 73.8 %all-to-all-start.3 = ((bf16[4,704,352]{2,1,0:T(8,128)(2,1)}), bf16[4,704,352]{2,1,0:T(8,128)(2,1)S(1)}, u32[]{:S(2)}, u32[]{:S(2)}) async-start(bf16[4,704,352]{2,1,0:T(8,128)(2,1)} %shard_map.133), calls=%async_computation.3 | async-start | bytes 4325376 | tf_op jit(solution)/shard_map/all_to_all | solution.py:543
  385.3 23.9 %copy-start.34 = (bf16[3,2,32,704]{3,2,1,0:T(8,128)(2,1)S(1)}, bf16[3,2,32,704]{3,2,1,0:T(8,128)(2,1)}, u32[]{:S(2)}) copy-start(bf16[3,2,32,704]{3,2,1,0:T(8,128)(2,1)} %copy-done.33) | copy-start | bytes 811012
  385.3 23.9 %copy-start.36 = (bf16[3,2,32,704]{3,2,1,0:T(8,128)(2,1)S(1)}, bf16[3,2,32,704]{3,2,1,0:T(8,128)(2,1)}, u32[]{:S(2)}) copy-start(bf16[3,2,32,704]{3,2,1,0:T(8,128)(2,1)} %copy-done.35) | copy-start | bytes 811012
  385.3 46.4 %collective-permute-start.29 = (bf16[1,2,704,256]{3,2,1,0:T(8,128)(2,1)S(1)}, bf16[1,2,704,256]{3,2,1,0:T(8,128)(2,1)S(1)}, u32[]{:S(2)}, u32[]{:S(2)}) collective-permute-start(bf16[1,2,704,256]{3,2,1,0:T(8,128)(2,1)S(1)} %slice.192), channel_id=1, source_target_pairs={{0,8},{4,12},{8,0},{12,4},{1,9},{5,13},{9,1},{13,5},{2,10},{6,14},... | collective-permute-start | bytes 2162696 | tf_op jit(solution)/shard_map/ppermute | solution.py:21
  393.7 38.0 %collective-permute-start.37 = (bf16[2,704,256]{2,1,0:T(8,128)(2,1)S(1)}, bf16[2,704,256]{2,1,0:T(8,128)(2,1)S(1)}, u32[]{:S(2)}, u32[]{:S(2)}) collective-permute-start(bf16[2,704,256]{2,1,0:T(8,128)(2,1)S(1)} %fusion), channel_id=1, source_target_pairs={{0,1},{1,0},{2,3},{3,2},{4,5},{5,4},{6,7},{7,6},{8,9},{9,8},{10,11... | collective-permute-start | bytes 2162696 | tf_op jit(solution)/shard_map/ppermute | solution.py:21
  393.8 22.5 %copy-start.28 = (bf16[4,2,32,704]{3,2,1,0:T(8,128)(2,1)S(1)}, bf16[4,2,32,704]{3,2,1,0:T(8,128)(2,1)}, u32[]{:S(2)}) copy-start(bf16[4,2,32,704]{3,2,1,0:T(8,128)(2,1)} %refs_0_.1) | copy-start | bytes 1081348
  393.8 7.6 %collective-permute-start.38 = (bf16[3,2,32,704]{3,2,1,0:T(8,128)(2,1)S(1)}, bf16[3,2,32,704]{3,2,1,0:T(8,128)(2,1)S(1)}, u32[]{:S(2)}, u32[]{:S(2)}) collective-permute-start(bf16[3,2,32,704]{3,2,1,0:T(8,128)(2,1)S(1)} %get-tuple-element.118), channel_id=1, source_target_pairs={{0,4},{4,8},{8,12},{1,5},{5,9},{9,13},{2,6},{6,10},{10,14},{3,7},{... | collective-permute-start | bytes 811016 | tf_op jit(solution)/shard_map/ppermute | solution.py:348
  397.2 11.9 %collective-permute-start.39 = (bf16[3,2,32,704]{3,2,1,0:T(8,128)(2,1)S(1)}, bf16[3,2,32,704]{3,2,1,0:T(8,128)(2,1)S(1)}, u32[]{:S(2)}, u32[]{:S(2)}) collective-permute-start(bf16[3,2,32,704]{3,2,1,0:T(8,128)(2,1)S(1)} %get-tuple-element.117), channel_id=1, source_target_pairs={{4,0},{8,4},{12,8},{5,1},{9,5},{13,9},{6,2},{10,6},{14,10},{7,3},{... | collective-permute-start | bytes 811016 | tf_op jit(solution)/shard_map/ppermute | solution.py:348
  416.2 8.1 %collective-permute-start.42 = (bf16[7,7,704]{2,1,0:T(8,128)(2,1)S(1)}, bf16[7,7,704]{2,1,0:T(8,128)(2,1)S(1)}, u32[]{:S(2)}, u32[]{:S(2)}) collective-permute-start(bf16[7,7,704]{2,1,0:T(8,128)(2,1)S(1)} %convert_element_type.121), channel_id=1, source_target_pairs={{0,16},{16,0},{1,17},{17,1},{2,18},{18,2},{3,19},{19,3},{4,20},{20... | collective-permute-start | bytes 206984 | tf_op jit(solution)/shard_map/ppermute | solution.py:21
  424.3 11.1 %collective-permute-start.43 = (bf16[7,7,704]{2,1,0:T(8,128)(2,1)S(1)}, bf16[7,7,704]{2,1,0:T(8,128)(2,1)S(1)}, u32[]{:S(2)}, u32[]{:S(2)}) collective-permute-start(bf16[7,7,704]{2,1,0:T(8,128)(2,1)S(1)} %add_convert_fusion.2), channel_id=1, source_target_pairs={{0,4},{4,0},{8,12},{12,8},{1,5},{5,1},{9,13},{13,9},{2,6},{6,2},{1... | collective-permute-start | bytes 206984 | tf_op jit(solution)/shard_map/ppermute | solution.py:21
  432.0 16.6 %collective-permute-start.40 = (bf16[1,704,256]{2,1,0:T(8,128)(2,1)S(1)}, bf16[1,704,256]{2,1,0:T(8,128)(2,1)S(1)}, u32[]{:S(2)}, u32[]{:S(2)}) collective-permute-start(bf16[1,704,256]{2,1,0:T(8,128)(2,1)S(1)} %slice.195), channel_id=1, source_target_pairs={{0,2},{1,3},{2,0},{3,1},{4,6},{5,7},{6,4},{7,5},{8,10},{9,11},{10,... | collective-permute-start | bytes 1081352 | tf_op jit(solution)/shard_map/ppermute | solution.py:21
  435.5 5.1 %collective-permute-start.44 = (bf16[7,7,704]{2,1,0:T(8,128)(2,1)S(1)}, bf16[7,7,704]{2,1,0:T(8,128)(2,1)S(1)}, u32[]{:S(2)}, u32[]{:S(2)}) collective-permute-start(bf16[7,7,704]{2,1,0:T(8,128)(2,1)S(1)} %add_convert_fusion.1), channel_id=1, source_target_pairs={{0,8},{4,12},{8,0},{12,4},{1,9},{5,13},{9,1},{13,5},{2,10},{6,14},... | collective-permute-start | bytes 206984 | tf_op jit(solution)/shard_map/ppermute | solution.py:21
  (33 other events, 114.5 us)
Sparse Core Ops, SparseCore 0:
  50.4 97.3 all-gather.2

commit v5 on v4

--- a/solution.py
+++ b/solution.py
@@ -46,14 +46,20 @@
 
 
 def stack_cols(blocks):
-    return [pin(jnp.stack([blocks[m] for m in side])) for side in col_order(len(blocks))]
-
-
-def gather_rows(block, bits):
-    held = {0: block}
-    for bit in bits:
-        held.update({q ^ bit: pin(swap(held[q], "row", bit)) for q in list(held)})
-    return [held[q] for q in range(lax.axis_size("row"))]
+    return pin(jnp.stack([blocks[m] for side in col_order(len(blocks)) for m in side]))
+
+
+def gather_rows(stacked):
+    half = stacked.shape[0] // 2
+    one = pin(swap(stacked, "row", 1))
+    two = pin(swap(stacked, "row", 2))
+    return [
+        stacked,
+        one,
+        two,
+        pin(swap(pin(one[:half]), "row", 2)),
+        pin(swap(pin(two[half:]), "row", 1)),
+    ]
 
 
 def row_bits():
@@ -69,7 +75,7 @@
 
 
 def halve_sum(near, far, axis, bits, earlier=()):
-    for place, bit in enumerate(bits):
+    for bit in bits:
         got = swap(pin(far.astype(bf16)), axis, bit)
         if earlier:
             got = after(got, *earlier)
@@ -100,11 +106,10 @@
 
 
 def piece_of(refs, places, rows, q, m):
-    half = refs[-1].shape[-3] if len(refs) > 1 else refs[0].shape[1] // 2
-    side, place = m // half, m % half
-    if len(refs) == 1:
-        return refs[0][places[0] ^ q, m]
-    return refs[side * rows + q][place]
+    if q < rows - 1:
+        return refs[q][m]
+    half = refs[-1].shape[0]
+    return refs[rows - 1 + m // half][m % half]
 
 
 def cut_units(w, out, count):
@@ -478,7 +483,8 @@
     mean_own = jnp.mean(conv_out, axis=-1)
     dev_own = conv_out - mean_own[..., None]
     stats = jnp.stack([mean_own, jnp.sum(dev_own * dev_own, axis=-1)])
-    cot_cols = after(gather_cols(cot_turned, cot_hops), stats)
+    stats = after(stats, cot_hops)
+    cot_all = gather_rows(stack_cols(gather_cols(cot_turned, cot_hops)))
     stats = [stats] + [swap(stats, "col", m) for m in range(1, col_count)]
     mean_pix = sum(s[0] for s in stats) / col_count
     var_pix = sum(s[1] + chans * (s[0] - mean_pix) ** 2 for s in stats) / all_chans
@@ -487,12 +493,10 @@
     bits = row_bits()
     normed = turned(standard.astype(bf16))
     normed_cols = gather_cols(normed, first_hops(normed))
-    even, odd = stack_cols(normed_cols)
-    normed_all = gather_rows(even, bits) + gather_rows(odd, bits[::-1])
-    cot_all = [pin(lax.all_gather(pin(jnp.concatenate(stack_cols(cot_cols))), "row"))]
-    w_in_there = lax.all_to_all(after(pieces, normed_cols), "col", 0, 0)
-    near_rows = [normed_all[side + bit] for side in (0, row_count) for bit in bits]
-    w_in_there = after(w_in_there, near_rows)
+    normed_stack = after(stack_cols(normed_cols), cot_all[1], cot_all[2])
+    normed_all = gather_rows(normed_stack)
+    w_in_there = lax.all_to_all(after(pieces, normed_stack), "col", 0, 0)
+    w_in_there = after(w_in_there, normed_all[1], normed_all[2], cot_all[3], cot_all[4])
     w_in_all, w_in_turned = join_weights(places, w_in_there, swap(w_in_there, "dp", 1))
     pieces = after(prepare_out(places, w_out.T), w_in_there)
     w_out_there = lax.all_to_all(pieces, "col", 0, 0)
@@ -506,9 +510,9 @@
     w_out_mine, w_out_other = grads_kernel(places, gated, cot_all, dims, col_count, chans)
     w_out_sums = add_kernel(places, w_out_mine, swap(w_out_other, "dp", 1))
     w_out_there = after(w_out_there, w_out_sums)
-    w_out_all, w_out_turned = join_weights(places, w_out_there, swap(w_out_there, "dp", 1))
     w_out_back = lax.all_to_all(after(w_out_sums, w_out_there), "col", 0, 0)
     w_out_grad = finish_kernel(places, w_out_back, scale_grad).T
+    w_out_all, w_out_turned = join_weights(places, w_out_there, swap(w_out_there, "dp", 1))
     grad_gated, pull = back_kernel(places, cot_all, w_out_all, act, dims)
     share_back = gamma * pull / denom / norm_chan
 
@@ -523,12 +527,15 @@
     _, out_parts = project_kernel(
         places, lambda b, spread: b[0], [gated], w_out_turned, dims, (bits[0], bits[-1])
     )
-    w_in_mine, w_in_other = grads_kernel(places, grad_pre, normed_all, dims, col_count, chans)
+    w_in_mine, w_in_other = grads_kernel(
+        places, grad_pre, normed_all, dims, col_count, chans
+    )
     w_in_sums = add_kernel(places, w_in_mine, swap(w_in_other, "dp", 1))
 
     near_a, far_a, near_b, far_b = grad_parts
-    even = halve_sum(near_a, far_a, "row", bits, (w_in_other, out_parts[0]))
-    odd = halve_sum(near_b, far_b, "row", bits[::-1], (w_in_other, out_parts[0]))
+    shade = (w_in_other, out_parts[0])
+    even = halve_sum(near_a, far_a, "row", bits, shade)
+    odd = halve_sum(near_b, far_b, "row", bits[::-1], shade)
     down = [1 << i for i in range((col_count - 1).bit_length())]
     near_a, far_a, near_b, far_b = out_parts
     far_a, far_b = after((far_a, far_b), even, odd)

time: 469 us -> 457 us (0.974)
  waiting for transfers between devices: 208 us -> 192 us
  between operations: 15.2 us -> 1.68 us
  starting transfers between devices: 81.4 us -> 89.1 us
  local copies, waits for them, and re-layouts: 34.3 us -> 40.1 us
    ppermute x41 -> x43, waiting for transfers between devices: 188 us -> 174 us  [swap(): return lax.ppermute(block, axis, [(i, i ^ bits) for i in range(count)])]
    ppermute x41 -> x43, starting transfers between devices: 53.5 us -> 60.3 us  [swap(): return lax.ppermute(block, axis, [(i, i ^ bits) for i in range(count)])]
    slice x0 -> x4, local copies, waits for them, and re-layouts: none -> 6.34 us  [the longest x2 3.17 us: gather_rows(): one[:half]]
    unnamed x95 -> x77, local copies, waits for them, and re-layouts: 26.2 us -> 24.9 us
  transfers between devices with their start and end apart: 50 -> 51, of which waited for: 27 -> 25; matrix products, arithmetic and copies ran while one was open for 6% -> 8% of each run, Pallas kernels for 21% -> 22%
where the time goes in v5:
time: 457 us; the launch traced here: 450 us
  waiting for transfers between devices  192 us (42%)
  Pallas kernels  105 us (23%)
  starting transfers between devices  89.1 us (19%)
  local copies, waits for them, and re-layouts  40.1 us (9%)
  other arithmetic  21.9 us (5%)
    ppermute x43, waiting for transfers between devices, swap(): return lax.ppermute(block, axis, [(i, i ^ bits) for i in range(count)])  174 us
    pallas_call x15, Pallas kernels, call(): pl.pallas_call(body, out_shape=outs, in_specs=[in_smem] + [in_vmem] * len...  82.9 us
    ppermute x43, starting transfers between devices, swap(): return lax.ppermute(block, axis, [(i, i ^ bits) for i in range(count)])  60.3 us
    unnamed x77, local copies, waits for them, and re-layouts  24.9 us
    pallas_call x2, Pallas kernels, depthwise(): pl.pallas_call(body, out_shape=shape_of(mid.shape, f32 if extra is None e...  14.9 us
    ppermute x2, waiting for transfers between devices, exchange_rows(): lax.ppermute(high, 'row', backward)  14.8 us
  transfers between devices with their start and end apart: 51, of which 25 were waited for; matrix products, arithmetic and copies ran while one was open for 8% of the time, Pallas kernels for 22%

profile of v5, /device:TPU:0, one launch (start us, length us, event | category | flops | bytes accessed | tf_op | source)
XLA Modules:
  0.0 449.7 jit_solution(17032092041534965191)
XLA Ops:
  6.9 4.8 %collective-permute-start = (bf16[3,2,32,704]{3,2,1,0:T(8,128)(2,1)S(1)}, bf16[3,2,32,704]{3,2,1,0:T(8,128)(2,1)S(1)}, u32[]{:S(2)}, u32[]{:S(2)}) collective-permute-start(bf16[3,2,32,704]{3,2,1,0:T(8,128)(2,1)S(1)} %get-tuple-element.50), channel_id=1, source_target_pairs={{0,4},{4,8},{8,12},{1,5},{5,9},{9,13},{2,6},{6,10},{10,14},{3,7},{... | collective-permute-start | bytes 811016 | tf_op jit(solution)/shard_map/ppermute | solution.py:353
  14.7 2.6 collective-permute-start.3
  18.0 8.3 %collective-permute-done.1.high = bf16[3,2,32,704]{3,2,1,0:T(8,128)(2,1)S(1)} collective-permute-done((bf16[3,2,32,704]{3,2,1,0:T(8,128)(2,1)S(1)}, bf16[3,2,32,704]{3,2,1,0:T(8,128)(2,1)S(1)}, u32[]{:S(2)}, u32[]{:S(2)}) %collective-permute-start.1) | collective-permute-done | bytes 270368 | tf_op jit(solution)/shard_map/ppermute | solution.py:353
  26.3 6.9 %shard_map.120 = f32[4,2,32,704]{3,2,1,0:T(8,128)S(1)} custom-call(s32[2]{0:T(128)S(1)} %pad_add_fusion.places, bf16[3,2,32,704]{3,2,1,0:T(8,128)(2,1)S(1)} %collective-permute-done.low, bf16[4,2,32,704]{3,2,1,0:T(8,128)(2,1)S(1)} %copy-done.8, bf16[3,2,32,704]{3,2,1,0:T(8,128)(2,1)S(1)} %collective-permute-done.1.high, f32[7,7,704]{2,1,0:T(8,128)S(1)} %copy-done.31), custom_call_target="tpu_custom_call" | custom-call | tf_op jit(solution)/shard_map/pallas_call | solution.py:403
  35.0 7.4 %collective-permute-done.3 = bf16[704,256]{1,0:T(8,128)(2,1)S(1)} collective-permute-done((bf16[704,256]{1,0:T(8,128)(2,1)S(1)}, bf16[704,256]{1,0:T(8,128)(2,1)S(1)}, u32[]{:S(2)}, u32[]{:S(2)}) %collective-permute-start.3) | collective-permute-done | bytes 360480 | tf_op jit(solution)/shard_map/ppermute | solution.py:21
  44.6 2.7 collective-permute-start.11
  48.9 6.2 %collective-permute-start.5 = (f32[2,4,2,32]{3,2,1,0:T(2,128)S(1)}, f32[2,4,2,32]{3,2,1,0:T(2,128)S(1)}, u32[]{:S(2)}, u32[]{:S(2)}) collective-permute-start(f32[2,4,2,32]{3,2,1,0:T(2,128)S(1)} %pad_maximum_fusion.2), channel_id=1, source_target_pairs={{0,1},{1,0},{2,3},{3,2},{4,5},{5,4},{6,7},{7,6},{8,9},{9,8},{10,11... | collective-permute-start | bytes 6152 | tf_op jit(solution)/shard_map/ppermute | solution.py:21
  57.5 2.1 collective-permute-done.6
  59.6 2.0 collective-permute-done.7
  62.8 1.9 collective-permute-start.9
  64.7 13.0 %collective-permute-done.8 = bf16[704,256]{1,0:T(8,128)(2,1)S(1)} collective-permute-done((bf16[704,256]{1,0:T(8,128)(2,1)}, bf16[704,256]{1,0:T(8,128)(2,1)S(1)}, u32[]{:S(2)}, u32[]{:S(2)}) %collective-permute-start.8) | collective-permute-done | bytes 360480 | tf_op jit(solution)/shard_map/ppermute | solution.py:21
  77.7 9.3 %collective-permute-done.10 = bf16[704,256]{1,0:T(8,128)(2,1)S(1)} collective-permute-done((bf16[704,256]{1,0:T(8,128)(2,1)S(1)}, bf16[704,256]{1,0:T(8,128)(2,1)S(1)}, u32[]{:S(2)}, u32[]{:S(2)}) %collective-permute-start.10) | collective-permute-done | bytes 360480 | tf_op jit(solution)/shard_map/ppermute | solution.py:21
  87.0 2.3 pad_maximum_fusion.refs_0_
  89.3 4.5 all-to-all-start
  100.3 41.8 %collective-permute-done.17.refs_3_ = bf16[2,704,256]{2,1,0:T(8,128)(2,1)S(1)} collective-permute-done((bf16[2,704,256]{2,1,0:T(8,128)(2,1)S(1)}, bf16[2,704,256]{2,1,0:T(8,128)(2,1)S(1)}, u32[]{:S(2)}, u32[]{:S(2)}) %collective-permute-start.17) | collective-permute-done | bytes 720928 | tf_op jit(solution)/shard_map/ppermute | solution.py:21
  143.2 2.0 slice.128
  146.1 2.0 slice.129
  153.4 5.1 %all-to-all-start.1 = ((bf16[4,704,352]{2,1,0:T(8,128)(2,1)}), bf16[4,704,352]{2,1,0:T(8,128)(2,1)}, u32[]{:S(2)}, u32[]{:S(2)}) async-start(bf16[4,704,352]{2,1,0:T(8,128)(2,1)} %copy-done.6), calls=%async_computation.1 | async-start | bytes 4325376 | tf_op jit(solution)/shard_map/all_to_all | solution.py:502
  159.9 6.1 %shard_map.121 = (bf16[4,704,704]{2,1,0:T(8,128)(2,1)S(1)}, bf16[4,704,704]{2,1,0:T(8,128)(2,1)}) custom-call(s32[2]{0:T(128)S(1)} %pad_add_fusion.places, bf16[4,704,352]{2,1,0:T(8,128)(2,1)} %all-to-all-done.mine, bf16[4,704,352]{2,1,0:T(8,128)(2,1)} %collective-permute-done.19.other), custom_call_target="tpu_custom_call" | custom-call | tf_op jit(solution)/shard_map/pallas_call | solution.py:94
  166.0 2.1 copy-done.10
  168.1 10.5 %shard_map.122 = (f32[704,1024]{1,0:T(8,128)S(1)}, f32[704,1024]{1,0:T(8,128)}, f32[704,2]{1,0:T(8,128)S(1)}) custom-call(s32[2]{0:T(128)S(1)} %pad_add_fusion.places, bf16[4,704,256]{2,1,0:T(8,128)(2,1)S(1)} %copy-done.1, bf16[4,704,256]{2,1,0:T(8,128)(2,1)} %collective-permute-done.13.refs_1_, bf16[4,704,256]{2,1,0:T(8,128)(2,1)} %collective-permute-done.14.refs_2_, ...), custom_call_target="tpu_custom_call" | custom-call | tf_op jit(solution)/shard_map/pallas_call | solution.py:94
  178.8 1.8 collective-permute-start.20
  180.6 1.8 collective-permute-done.20
  183.8 2.1 collective-permute-done.21
  185.9 2.0 collective-permute-start.22
  187.9 5.8 %collective-permute-done.22 = f32[2]{0:T(128)S(1)} collective-permute-done((f32[2]{0:T(128)S(1)}, f32[2]{0:T(128)S(1)}, u32[]{:S(2)}, u32[]{:S(2)}) %collective-permute-start.22) | collective-permute-done | bytes 40 | tf_op jit(solution)/shard_map/ppermute | solution.py:21
  193.8 4.5 collective-permute-start.23
  198.2 10.2 %collective-permute-done.23 = f32[2]{0:T(128)S(1)} collective-permute-done((f32[2]{0:T(128)S(1)}, f32[2]{0:T(128)S(1)}, u32[]{:S(2)}, u32[]{:S(2)}) %collective-permute-start.23) | collective-permute-done | bytes 40 | tf_op jit(solution)/shard_map/ppermute | solution.py:21
  208.6 1.7 shard_map.123.left.refs_0_
  211.9 8.4 %shard_map.125 = (bf16[4,704,352]{2,1,0:T(8,128)(2,1)S(1)}, bf16[4,704,352]{2,1,0:T(8,128)(2,1)}) custom-call(s32[2]{0:T(128)S(1)} %pad_add_fusion.places, bf16[704,1024]{1,0:T(8,128)(2,1)S(1)} %shard_map.123.left.refs_0_, bf16[4,704,256]{2,1,0:T(8,128)(2,1)S(1)} %pad_maximum_fusion.1.refs_0_, bf16[4,704,256]{2,1,0:T(8,128)(2,1)} %collective-permute-done.11.refs_1_, ...), custom_call_target="tpu_custom_call" | custom-call | tf_op jit(solution)/shard_map/pallas_call | solution.py:94
  220.4 4.5 collective-permute-done.24.got
  227.4 4.7 %all-to-all-start.2 = ((bf16[4,704,352]{2,1,0:T(8,128)(2,1)}), bf16[4,704,352]{2,1,0:T(8,128)(2,1)}, u32[]{:S(2)}, u32[]{:S(2)}) async-start(bf16[4,704,352]{2,1,0:T(8,128)(2,1)} %copy-done.5), calls=%async_computation.2 | async-start | bytes 4325376 | tf_op jit(solution)/shard_map/all_to_all | solution.py:513
  232.1 6.1 %shard_map.127 = (bf16[4,704,704]{2,1,0:T(8,128)(2,1)S(1)}, bf16[4,704,704]{2,1,0:T(8,128)(2,1)}) custom-call(s32[2]{0:T(128)S(1)} %pad_add_fusion.places, bf16[4,704,352]{2,1,0:T(8,128)(2,1)} %all-to-all-done.1.mine, bf16[4,704,352]{2,1,0:T(8,128)(2,1)} %collective-permute-done.25.other), custom_call_target="tpu_custom_call" | custom-call | tf_op jit(solution)/shard_map/pallas_call | solution.py:94
  238.2 2.1 copy-done.9
  240.3 8.8 %shard_map.129 = (f32[704,1024]{1,0:T(8,128)S(1)}, f32[704,2]{1,0:T(8,128)S(1)}) custom-call(s32[2]{0:T(128)S(1)} %pad_add_fusion.places, bf16[4,704,256]{2,1,0:T(8,128)(2,1)S(1)} %pad_maximum_fusion.1.refs_0_, bf16[4,704,256]{2,1,0:T(8,128)(2,1)} %collective-permute-done.11.refs_1_, bf16[4,704,256]{2,1,0:T(8,128)(2,1)} %collective-permute-done.12.refs_2_, ...), custom_call_target="tpu_custom_call" | custom-call | tf_op jit(solution)/shard_map/pallas_call | solution.py:94
  250.9 9.7 %shard_map.130 = (bf16[704,1024]{1,0:T(8,128)(2,1)S(1)}, bf16[2,2,704,256]{3,2,1,0:T(8,128)(2,1)S(1)}, bf16[2,2,704,256]{3,2,1,0:T(8,128)(2,1)S(1)}, bf16[2,2,70...) custom-call(s32[2]{0:T(128)S(1)} %pad_add_fusion.places, f32[704,1024]{1,0:T(8,128)} %copy-done.17, ...), custom_call_target="tpu_custom_call" | custom-call | tf_op jit(solution)/shard_map/pallas_call | solution.py:94
  263.5 8.3 %shard_map.128 = (bf16[704,1024]{1,0:T(8,128)(2,1)}, bf16[2,2,704,256]{3,2,1,0:T(8,128)(2,1)S(1)}, bf16[2,2,704,256]{3,2,1,0:T(8,128)(2,1)}, bf16[2,2,704,256]{3...) custom-call(s32[2]{0:T(128)S(1)} %pad_add_fusion.places, bf16[704,1024]{1,0:T(8,128)(2,1)S(1)} %copy-done.4, ...), custom_call_target="tpu_custom_call" | custom-call | tf_op jit(solution)/shard_map/pallas_call | solution.py:94
  273.0 8.8 %shard_map.131 = (bf16[4,704,352]{2,1,0:T(8,128)(2,1)S(1)}, bf16[4,704,352]{2,1,0:T(8,128)(2,1)}) custom-call(s32[2]{0:T(128)S(1)} %pad_add_fusion.places, bf16[704,1024]{1,0:T(8,128)(2,1)S(1)} %get-tuple-element.76.left, bf16[4,704,256]{2,1,0:T(8,128)(2,1)S(1)} %copy-done.2, bf16[4,704,256]{2,1,0:T(8,128)(2,1)} %collective-permute-done.13.refs_1_, ...), custom_call_target="tpu_custom_call" | custom-call | tf_op jit(solution)/shard_map/pallas_call | solution.py:94
  281.8 12.9 %collective-permute-done.28 = bf16[2,2,704,256]{3,2,1,0:T(8,128)(2,1)} collective-permute-done((bf16[2,2,704,256]{3,2,1,0:T(8,128)(2,1)S(1)}, bf16[2,2,704,256]{3,2,1,0:T(8,128)(2,1)}, u32[]{:S(2)}, u32[]{:S(2)}) %collective-permute-start.28) | collective-permute-done | bytes 1441824 | tf_op jit(solution)/shard_map/ppermute | solution.py:21
  296.4 1.7 collective-permute-start.29
  303.5 10.6 %collective-permute-done.29 = bf16[1,2,704,256]{3,2,1,0:T(8,128)(2,1)S(1)} collective-permute-done((bf16[1,2,704,256]{3,2,1,0:T(8,128)(2,1)S(1)}, bf16[1,2,704,256]{3,2,1,0:T(8,128)(2,1)S(1)}, u32[]{:S(2)}, u32[]{:S(2)}) %collective-permute-start.29) | collective-permute-done | bytes 720928 | tf_op jit(solution)/shard_map/ppermute | solution.py:21
  316.6 3.4 collective-permute-done.27
  320.0 12.2 %collective-permute-done.34 = bf16[2,704,256]{2,1,0:T(8,128)(2,1)S(1)} collective-permute-done((bf16[2,704,256]{2,1,0:T(8,128)(2,1)}, bf16[2,704,256]{2,1,0:T(8,128)(2,1)S(1)}, u32[]{:S(2)}, u32[]{:S(2)}) %collective-permute-start.34) | collective-permute-done | bytes 720928 | tf_op jit(solution)/shard_map/ppermute | solution.py:21
  332.2 1.9 convert_add_fusion.4
  335.6 2.0 collective-permute-start.35
  339.0 13.2 %collective-permute-done.35 = bf16[1,704,256]{2,1,0:T(8,128)(2,1)S(1)} collective-permute-done((bf16[1,704,256]{2,1,0:T(8,128)(2,1)S(1)}, bf16[1,704,256]{2,1,0:T(8,128)(2,1)S(1)}, u32[]{:S(2)}, u32[]{:S(2)}) %collective-permute-start.35) | collective-permute-done | bytes 360480 | tf_op jit(solution)/shard_map/ppermute | solution.py:21
  353.1 2.4 copy.21
  356.9 3.0 collective-permute-start.37
  361.3 3.6 shard_map.133
  370.0 1.7 collective-permute-start.33
  371.7 3.8 all-to-all-start.3
  377.1 1.8 convert_add_fusion.1
  380.2 6.4 %collective-permute-done.33 = bf16[1,2,704,256]{3,2,1,0:T(8,128)(2,1)} collective-permute-done((bf16[1,2,704,256]{3,2,1,0:T(8,128)(2,1)}, bf16[1,2,704,256]{3,2,1,0:T(8,128)(2,1)}, u32[]{:S(2)}, u32[]{:S(2)}) %collective-permute-start.33) | collective-permute-done | bytes 720928 | tf_op jit(solution)/shard_map/ppermute | solution.py:21
  388.0 3.4 collective-permute-start.40
  392.7 2.9 collective-permute-done.40.low
  395.6 6.5 %collective-permute-done.41.high = bf16[3,2,32,704]{3,2,1,0:T(8,128)(2,1)S(1)} collective-permute-done((bf16[3,2,32,704]{3,2,1,0:T(8,128)(2,1)S(1)}, bf16[3,2,32,704]{3,2,1,0:T(8,128)(2,1)S(1)}, u32[]{:S(2)}, u32[]{:S(2)}) %collective-permute-start.41) | collective-permute-done | bytes 270368 | tf_op jit(solution)/shard_map/ppermute | solution.py:353
  402.1 7.0 %shard_map.136 = f32[7,7,704]{2,1,0:T(8,128)S(1)} custom-call(s32[2]{0:T(128)S(1)} %pad_add_fusion.places, bf16[3,2,32,704]{3,2,1,0:T(8,128)(2,1)S(1)} %copy-done.28, bf16[4,2,32,704]{3,2,1,0:T(8,128)(2,1)S(1)} %copy-done.8, bf16[3,2,32,704]{3,2,1,0:T(8,128)(2,1)S(1)} %copy-done.30, f32[4,2,32,704]{3,2,1,0:T(8,128)S(1)} %get-tuple-element.94.mid.grad), custom_call_target="tpu_custom_call" | custom-call | tf_op jit(solution)/shard_map/pallas_call | solution.py:441
  409.2 8.0 %shard_map.132 = bf16[4,2,32,704]{3,2,1,0:T(8,128)(2,1)} custom-call(s32[2]{0:T(128)S(1)} %pad_add_fusion.places, bf16[3,2,32,704]{3,2,1,0:T(8,128)(2,1)S(1)} %collective-permute-done.40.low, f32[4,2,32,704]{3,2,1,0:T(8,128)S(1)} %get-tuple-element.94.mid.grad, bf16[3,2,32,704]{3,2,1,0:T(8,128)(2,1)S(1)} %collective-permute-done.41.high, ...), custom_call_target="tpu_custom_call" | custom-call | tf_op jit(solution)/shard_map/pallas_call | solution.py:403
  417.3 1.7 collective-permute-start.45
  419.0 6.9 %collective-permute-done.39 = bf16[2,704,256]{2,1,0:T(8,128)(2,1)S(1)} collective-permute-done((bf16[2,704,256]{2,1,0:T(8,128)(2,1)S(1)}, bf16[2,704,256]{2,1,0:T(8,128)(2,1)S(1)}, u32[]{:S(2)}, u32[]{:S(2)}) %collective-permute-start.39) | collective-permute-done | bytes 720928 | tf_op jit(solution)/shard_map/ppermute | solution.py:21
  426.2 3.1 collective-permute-start.42
  430.6 4.1 shard_map.135
  435.5 7.5 %collective-permute-done.42 = bf16[1,704,256]{2,1,0:T(8,128)(2,1)S(1)} collective-permute-done((bf16[1,704,256]{2,1,0:T(8,128)(2,1)S(1)}, bf16[1,704,256]{2,1,0:T(8,128)(2,1)S(1)}, u32[]{:S(2)}, u32[]{:S(2)}) %collective-permute-start.42) | collective-permute-done | bytes 360480 | tf_op jit(solution)/shard_map/ppermute | solution.py:21
  446.2 3.1 shard_map.134
  (191 shorter events, 78.3 us)
Async XLA Ops:
  4.3 22.0 %copy-start.8 = (bf16[4,2,32,704]{3,2,1,0:T(8,128)(2,1)S(1)}, bf16[4,2,32,704]{3,2,1,0:T(8,128)(2,1)}, u32[]{:S(2)}) copy-start(bf16[4,2,32,704]{3,2,1,0:T(8,128)(2,1)} %mid.3) | copy-start | bytes 1081348
  4.3 22.0 %copy-start.31 = (f32[7,7,704]{2,1,0:T(8,128)S(1)}, f32[7,7,704]{2,1,0:T(8,128)}, u32[]{:S(2)}) copy-start(f32[7,7,704]{2,1,0:T(8,128)} %kern.3) | copy-start | bytes 413956
  6.9 11.1 %collective-permute-start = (bf16[3,2,32,704]{3,2,1,0:T(8,128)(2,1)S(1)}, bf16[3,2,32,704]{3,2,1,0:T(8,128)(2,1)S(1)}, u32[]{:S(2)}, u32[]{:S(2)}) collective-permute-start(bf16[3,2,32,704]{3,2,1,0:T(8,128)(2,1)S(1)} %get-tuple-element.50), channel_id=1, source_target_pairs={{0,4},{4,8},{8,12},{1,5},{5,9},{9,13},{2,6},{6,10},{10,14},{3,7},{... | collective-permute-start | bytes 811016 | tf_op jit(solution)/shard_map/ppermute | solution.py:353
  11.8 14.5 %collective-permute-start.1 = (bf16[3,2,32,704]{3,2,1,0:T(8,128)(2,1)S(1)}, bf16[3,2,32,704]{3,2,1,0:T(8,128)(2,1)S(1)}, u32[]{:S(2)}, u32[]{:S(2)}) collective-permute-start(bf16[3,2,32,704]{3,2,1,0:T(8,128)(2,1)S(1)} %get-tuple-element.51), channel_id=1, source_target_pairs={{4,0},{8,4},{12,8},{5,1},{9,5},{13,9},{6,2},{10,6},{14,10},{7,3},{... | collective-permute-start | bytes 811016 | tf_op jit(solution)/shard_map/ppermute | solution.py:353
  13.1 21.9 %collective-permute-start.2 = (bf16[704,256]{1,0:T(8,128)(2,1)S(1)}, bf16[704,256]{1,0:T(8,128)(2,1)S(1)}, u32[]{:S(2)}, u32[]{:S(2)}) collective-permute-start(bf16[704,256]{1,0:T(8,128)(2,1)S(1)} %get-tuple-element.52), channel_id=1, source_target_pairs={{0,1},{1,0},{2,3},{3,2},{4,5},{5,4},{6,7},{7,6},{8,9},{9,8},{10,11... | collective-permute-start | bytes 1081352 | tf_op jit(solution)/shard_map/ppermute | solution.py:21
  14.7 27.7 %collective-permute-start.3 = (bf16[704,256]{1,0:T(8,128)(2,1)S(1)}, bf16[704,256]{1,0:T(8,128)(2,1)S(1)}, u32[]{:S(2)}, u32[]{:S(2)}) collective-permute-start(bf16[704,256]{1,0:T(8,128)(2,1)S(1)} %get-tuple-element.52), channel_id=1, source_target_pairs={{0,2},{1,3},{2,0},{3,1},{4,6},{5,7},{6,4},{7,5},{8,10},{9,11},{10,... | collective-permute-start | bytes 1081352 | tf_op jit(solution)/shard_map/ppermute | solution.py:21
  17.3 25.1 %collective-permute-start.4 = (bf16[704,256]{1,0:T(8,128)(2,1)S(1)}, bf16[704,256]{1,0:T(8,128)(2,1)S(1)}, u32[]{:S(2)}, u32[]{:S(2)}) collective-permute-start(bf16[704,256]{1,0:T(8,128)(2,1)S(1)} %get-tuple-element.52), channel_id=1, source_target_pairs={{0,3},{1,2},{2,1},{3,0},{4,7},{5,6},{6,5},{7,4},{8,11},{9,10},{10,... | collective-permute-start | bytes 1081352 | tf_op jit(solution)/shard_map/ppermute | solution.py:21
  44.6 44.6 %collective-permute-start.11 = (bf16[4,704,256]{2,1,0:T(8,128)(2,1)S(1)}, bf16[4,704,256]{2,1,0:T(8,128)(2,1)}, u32[]{:S(2)}, u32[]{:S(2)}) collective-permute-start(bf16[4,704,256]{2,1,0:T(8,128)(2,1)S(1)} %pad_maximum_fusion.1.refs_0_), channel_id=1, source_target_pairs={{0,4},{4,0},{8,12},{12,8},{1,5},{5,1},{9,13},{13,9},{2,6},{6,2},{1... | collective-permute-start | bytes 4325384 | tf_op jit(solution)/shard_map/ppermute | solution.py:21
  47.4 41.9 %collective-permute-start.12 = (bf16[4,704,256]{2,1,0:T(8,128)(2,1)S(1)}, bf16[4,704,256]{2,1,0:T(8,128)(2,1)}, u32[]{:S(2)}, u32[]{:S(2)}) collective-permute-start(bf16[4,704,256]{2,1,0:T(8,128)(2,1)S(1)} %pad_maximum_fusion.1.refs_0_), channel_id=1, source_target_pairs={{0,8},{4,12},{8,0},{12,4},{1,9},{5,13},{9,1},{13,5},{2,10},{6,14},... | collective-permute-start | bytes 4325384 | tf_op jit(solution)/shard_map/ppermute | solution.py:21
  48.9 8.7 %collective-permute-start.5 = (f32[2,4,2,32]{3,2,1,0:T(2,128)S(1)}, f32[2,4,2,32]{3,2,1,0:T(2,128)S(1)}, u32[]{:S(2)}, u32[]{:S(2)}) collective-permute-start(f32[2,4,2,32]{3,2,1,0:T(2,128)S(1)} %pad_maximum_fusion.2), channel_id=1, source_target_pairs={{0,1},{1,0},{2,3},{3,2},{4,5},{5,4},{6,7},{7,6},{8,9},{9,8},{10,11... | collective-permute-start | bytes 6152 | tf_op jit(solution)/shard_map/ppermute | solution.py:21
  55.1 4.5 %collective-permute-start.6 = (f32[2,4,2,32]{3,2,1,0:T(2,128)S(1)}, f32[2,4,2,32]{3,2,1,0:T(2,128)S(1)}, u32[]{:S(2)}, u32[]{:S(2)}) collective-permute-start(f32[2,4,2,32]{3,2,1,0:T(2,128)S(1)} %pad_maximum_fusion.2), channel_id=1, source_target_pairs={{0,2},{1,3},{2,0},{3,1},{4,6},{5,7},{6,4},{7,5},{8,10},{9,11},{10,... | collective-permute-start | bytes 6152 | tf_op jit(solution)/shard_map/ppermute | solution.py:21
  56.1 5.4 %collective-permute-start.7 = (f32[2,4,2,32]{3,2,1,0:T(2,128)S(1)}, f32[2,4,2,32]{3,2,1,0:T(2,128)S(1)}, u32[]{:S(2)}, u32[]{:S(2)}) collective-permute-start(f32[2,4,2,32]{3,2,1,0:T(2,128)S(1)} %pad_maximum_fusion.2), channel_id=1, source_target_pairs={{0,3},{1,2},{2,1},{3,0},{4,7},{5,6},{6,5},{7,4},{8,11},{9,10},{10,... | collective-permute-start | bytes 6152 | tf_op jit(solution)/shard_map/ppermute | solution.py:21
  62.7 15.0 %collective-permute-start.8 = (bf16[704,256]{1,0:T(8,128)(2,1)}, bf16[704,256]{1,0:T(8,128)(2,1)S(1)}, u32[]{:S(2)}, u32[]{:S(2)}) collective-permute-start(bf16[704,256]{1,0:T(8,128)(2,1)} %copy.16), channel_id=1, source_target_pairs={{0,2},{1,3},{2,0},{3,1},{4,6},{5,7},{6,4},{7,5},{8,10},{9,11},{10,... | collective-permute-start | bytes 1081352 | tf_op jit(solution)/shard_map/ppermute | solution.py:21
  62.8 14.9 %collective-permute-start.9 = (bf16[704,256]{1,0:T(8,128)(2,1)}, bf16[704,256]{1,0:T(8,128)(2,1)S(1)}, u32[]{:S(2)}, u32[]{:S(2)}) collective-permute-start(bf16[704,256]{1,0:T(8,128)(2,1)} %copy.16), channel_id=1, source_target_pairs={{0,1},{1,0},{2,3},{3,2},{4,5},{5,4},{6,7},{7,6},{8,9},{9,8},{10,11... | collective-permute-start | bytes 1081352 | tf_op jit(solution)/shard_map/ppermute | solution.py:21
  77.7 9.3 %collective-permute-start.10 = (bf16[704,256]{1,0:T(8,128)(2,1)S(1)}, bf16[704,256]{1,0:T(8,128)(2,1)S(1)}, u32[]{:S(2)}, u32[]{:S(2)}) collective-permute-start(bf16[704,256]{1,0:T(8,128)(2,1)S(1)} %collective-permute-done.8), channel_id=1, source_target_pairs={{0,1},{1,0},{2,3},{3,2},{4,5},{5,4},{6,7},{7,6},{8,9},{9,8},{10,11... | collective-permute-start | bytes 1081352 | tf_op jit(solution)/shard_map/ppermute | solution.py:21
  89.3 53.8 %all-to-all-start = ((bf16[4,704,352]{2,1,0:T(8,128)(2,1)}), bf16[4,704,352]{2,1,0:T(8,128)(2,1)}, u32[]{:S(2)}, u32[]{:S(2)}) async-start(bf16[4,704,352]{2,1,0:T(8,128)(2,1)} %copy-done.18), calls=%async_computation | async-start | bytes 4325376 | tf_op jit(solution)/shard_map/all_to_all | solution.py:498
  93.7 49.4 %collective-permute-start.13 = (bf16[4,704,256]{2,1,0:T(8,128)(2,1)}, bf16[4,704,256]{2,1,0:T(8,128)(2,1)}, u32[]{:S(2)}, u32[]{:S(2)}) collective-permute-start(bf16[4,704,256]{2,1,0:T(8,128)(2,1)} %pad_maximum_fusion.refs_0_), channel_id=1, source_target_pairs={{0,4},{4,0},{8,12},{12,8},{1,5},{5,1},{9,13},{13,9},{2,6},{6,2},{1... | collective-permute-start | bytes 4325384 | tf_op jit(solution)/shard_map/ppermute | solution.py:21
  95.2 47.9 %collective-permute-start.14 = (bf16[4,704,256]{2,1,0:T(8,128)(2,1)}, bf16[4,704,256]{2,1,0:T(8,128)(2,1)}, u32[]{:S(2)}, u32[]{:S(2)}) collective-permute-start(bf16[4,704,256]{2,1,0:T(8,128)(2,1)} %pad_maximum_fusion.refs_0_), channel_id=1, source_target_pairs={{0,8},{4,12},{8,0},{12,4},{1,9},{5,13},{9,1},{13,5},{2,10},{6,14},... | collective-permute-start | bytes 4325384 | tf_op jit(solution)/shard_map/ppermute | solution.py:21
  97.0 45.1 %collective-permute-start.17 = (bf16[2,704,256]{2,1,0:T(8,128)(2,1)S(1)}, bf16[2,704,256]{2,1,0:T(8,128)(2,1)S(1)}, u32[]{:S(2)}, u32[]{:S(2)}) collective-permute-start(bf16[2,704,256]{2,1,0:T(8,128)(2,1)S(1)} %slice.130), channel_id=1, source_target_pairs={{0,8},{4,12},{8,0},{12,4},{1,9},{5,13},{9,1},{13,5},{2,10},{6,14},... | collective-permute-start | bytes 2162696 | tf_op jit(solution)/shard_map/ppermute | solution.py:21
  99.6 42.5 %collective-permute-start.18 = (bf16[2,704,256]{2,1,0:T(8,128)(2,1)S(1)}, bf16[2,704,256]{2,1,0:T(8,128)(2,1)S(1)}, u32[]{:S(2)}, u32[]{:S(2)}) collective-permute-start(bf16[2,704,256]{2,1,0:T(8,128)(2,1)S(1)} %slice.131), channel_id=1, source_target_pairs={{0,4},{4,0},{8,12},{12,8},{1,5},{5,1},{9,13},{13,9},{2,6},{6,2},{1... | collective-permute-start | bytes 2162696 | tf_op jit(solution)/shard_map/ppermute | solution.py:21
  143.1 16.8 %collective-permute-start.19 = (bf16[4,704,352]{2,1,0:T(8,128)(2,1)}, bf16[4,704,352]{2,1,0:T(8,128)(2,1)}, u32[]{:S(2)}, u32[]{:S(2)}) collective-permute-start(bf16[4,704,352]{2,1,0:T(8,128)(2,1)} %all-to-all-done.mine), channel_id=1, source_target_pairs={{0,16},{16,0},{1,17},{17,1},{2,18},{18,2},{3,19},{19,3},{4,20},{20... | collective-permute-start | bytes 5947400 | tf_op jit(solution)/shard_map/ppermute | solution.py:21
  145.2 22.9 %collective-permute-start.15 = (bf16[2,704,256]{2,1,0:T(8,128)(2,1)}, bf16[2,704,256]{2,1,0:T(8,128)(2,1)}, u32[]{:S(2)}, u32[]{:S(2)}) collective-permute-start(bf16[2,704,256]{2,1,0:T(8,128)(2,1)} %slice.128), channel_id=1, source_target_pairs={{0,8},{4,12},{8,0},{12,4},{1,9},{5,13},{9,1},{13,5},{2,10},{6,14},... | collective-permute-start | bytes 2162696 | tf_op jit(solution)/shard_map/ppermute | solution.py:21
  148.1 20.0 %collective-permute-start.16 = (bf16[2,704,256]{2,1,0:T(8,128)(2,1)}, bf16[2,704,256]{2,1,0:T(8,128)(2,1)}, u32[]{:S(2)}, u32[]{:S(2)}) collective-permute-start(bf16[2,704,256]{2,1,0:T(8,128)(2,1)} %slice.129), channel_id=1, source_target_pairs={{0,4},{4,0},{8,12},{12,8},{1,5},{5,1},{9,13},{13,9},{2,6},{6,2},{1... | collective-permute-start | bytes 2162696 | tf_op jit(solution)/shard_map/ppermute | solution.py:21
  153.4 73.8 %all-to-all-start.1 = ((bf16[4,704,352]{2,1,0:T(8,128)(2,1)}), bf16[4,704,352]{2,1,0:T(8,128)(2,1)}, u32[]{:S(2)}, u32[]{:S(2)}) async-start(bf16[4,704,352]{2,1,0:T(8,128)(2,1)} %copy-done.6), calls=%async_computation.1 | async-start | bytes 4325376 | tf_op jit(solution)/shard_map/all_to_all | solution.py:502
  159.9 8.2 %copy-start.1 = (bf16[4,704,256]{2,1,0:T(8,128)(2,1)S(1)}, bf16[4,704,256]{2,1,0:T(8,128)(2,1)}, u32[]{:S(2)}) copy-start(bf16[4,704,256]{2,1,0:T(8,128)(2,1)} %pad_maximum_fusion.refs_0_) | copy-start | bytes 4325380
  178.8 3.6 collective-permute-start.20
  182.4 3.5 collective-permute-start.21
  185.9 7.9 %collective-permute-start.22 = (f32[2]{0:T(128)S(1)}, f32[2]{0:T(128)S(1)}, u32[]{:S(2)}, u32[]{:S(2)}) collective-permute-start(f32[2]{0:T(128)S(1)} %add.212), channel_id=1, source_target_pairs={{0,1},{1,0},{2,3},{3,2},{4,5},{5,4},{6,7},{7,6},{8,9},{9,8},{10,11... | collective-permute-start | bytes 32 | tf_op jit(solution)/shard_map/ppermute | solution.py:21
  193.8 14.6 %collective-permute-start.23 = (f32[2]{0:T(128)S(1)}, f32[2]{0:T(128)S(1)}, u32[]{:S(2)}, u32[]{:S(2)}) collective-permute-start(f32[2]{0:T(128)S(1)} %add.213), channel_id=1, source_target_pairs={{0,2},{1,3},{2,0},{3,1},{4,6},{5,7},{6,4},{7,5},{8,10},{9,11},{10,... | collective-permute-start | bytes 32 | tf_op jit(solution)/shard_map/ppermute | solution.py:21
  211.9 8.4 %copy-start.3 = (bf16[704,1024]{1,0:T(8,128)(2,1)}, bf16[704,1024]{1,0:T(8,128)(2,1)S(1)}, u32[]{:S(2)}) copy-start(bf16[704,1024]{1,0:T(8,128)(2,1)S(1)} %shard_map.123.left.refs_0_) | copy-start | bytes 4325380
  220.4 4.5 collective-permute-start.24
  227.3 4.8 %collective-permute-start.25 = (bf16[4,704,352]{2,1,0:T(8,128)(2,1)}, bf16[4,704,352]{2,1,0:T(8,128)(2,1)}, u32[]{:S(2)}, u32[]{:S(2)}) collective-permute-start(bf16[4,704,352]{2,1,0:T(8,128)(2,1)} %all-to-all-done.1.mine), channel_id=1, source_target_pairs={{0,16},{16,0},{1,17},{17,1},{2,18},{18,2},{3,19},{19,3},{4,20},{20... | collective-permute-start | bytes 5947400 | tf_op jit(solution)/shard_map/ppermute | solution.py:21
  227.4 87.8 %all-to-all-start.2 = ((bf16[4,704,352]{2,1,0:T(8,128)(2,1)}), bf16[4,704,352]{2,1,0:T(8,128)(2,1)}, u32[]{:S(2)}, u32[]{:S(2)}) async-start(bf16[4,704,352]{2,1,0:T(8,128)(2,1)} %copy-done.5), calls=%async_computation.2 | async-start | bytes 4325376 | tf_op jit(solution)/shard_map/all_to_all | solution.py:513
  232.1 8.2 %copy-start.13 = (bf16[2,704,256]{2,1,0:T(8,128)(2,1)S(1)}, bf16[2,704,256]{2,1,0:T(8,128)(2,1)}, u32[]{:S(2)}) copy-start(bf16[2,704,256]{2,1,0:T(8,128)(2,1)} %copy-done.11) | copy-start | bytes 2162692
  232.1 8.2 %copy-start.16 = (bf16[2,704,256]{2,1,0:T(8,128)(2,1)S(1)}, bf16[2,704,256]{2,1,0:T(8,128)(2,1)}, u32[]{:S(2)}) copy-start(bf16[2,704,256]{2,1,0:T(8,128)(2,1)} %copy-done.14) | copy-start | bytes 2162692
  250.9 12.6 %copy-start.4 = (bf16[704,1024]{1,0:T(8,128)(2,1)S(1)}, bf16[704,1024]{1,0:T(8,128)(2,1)}, u32[]{:S(2)}) copy-start(bf16[704,1024]{1,0:T(8,128)(2,1)} %copy-done.3) | copy-start | bytes 4325380
  260.6 34.0 %collective-permute-start.28 = (bf16[2,2,704,256]{3,2,1,0:T(8,128)(2,1)S(1)}, bf16[2,2,704,256]{3,2,1,0:T(8,128)(2,1)}, u32[]{:S(2)}, u32[]{:S(2)}) collective-permute-start(bf16[2,2,704,256]{3,2,1,0:T(8,128)(2,1)S(1)} %get-tuple-element.81), channel_id=1, source_target_pairs={{0,8},{4,12},{8,0},{12,4},{1,9},{5,13},{9,1},{13,5},{2,10},{6,14},... | collective-permute-start | bytes 4325384 | tf_op jit(solution)/shard_map/ppermute | solution.py:21
  262.1 36.1 %collective-permute-start.26 = (bf16[2,2,704,256]{3,2,1,0:T(8,128)(2,1)S(1)}, bf16[2,2,704,256]{3,2,1,0:T(8,128)(2,1)}, u32[]{:S(2)}, u32[]{:S(2)}) collective-permute-start(bf16[2,2,704,256]{3,2,1,0:T(8,128)(2,1)S(1)} %get-tuple-element.75), channel_id=1, source_target_pairs={{0,4},{4,0},{8,12},{12,8},{1,5},{5,1},{9,13},{13,9},{2,6},{6,2},{1... | collective-permute-start | bytes 4325384 | tf_op jit(solution)/shard_map/ppermute | solution.py:21
  263.5 9.4 %copy-start.2 = (bf16[4,704,256]{2,1,0:T(8,128)(2,1)S(1)}, bf16[4,704,256]{2,1,0:T(8,128)(2,1)}, u32[]{:S(2)}) copy-start(bf16[4,704,256]{2,1,0:T(8,128)(2,1)} %pad_maximum_fusion.refs_0_) | copy-start | bytes 4325380
  273.0 8.8 %copy-start.23 = (bf16[2,2,704,256]{3,2,1,0:T(8,128)(2,1)}, bf16[2,2,704,256]{3,2,1,0:T(8,128)(2,1)S(1)}, u32[]{:S(2)}) copy-start(bf16[2,2,704,256]{3,2,1,0:T(8,128)(2,1)S(1)} %get-tuple-element.66) | copy-start | bytes 4325380
  296.4 17.7 %collective-permute-start.29 = (bf16[1,2,704,256]{3,2,1,0:T(8,128)(2,1)S(1)}, bf16[1,2,704,256]{3,2,1,0:T(8,128)(2,1)S(1)}, u32[]{:S(2)}, u32[]{:S(2)}) collective-permute-start(bf16[1,2,704,256]{3,2,1,0:T(8,128)(2,1)S(1)} %slice.227), channel_id=1, source_target_pairs={{0,4},{4,0},{8,12},{12,8},{1,5},{5,1},{9,13},{13,9},{2,6},{6,2},{1... | collective-permute-start | bytes 2162696 | tf_op jit(solution)/shard_map/ppermute | solution.py:21
  302.4 17.6 %collective-permute-start.27 = (bf16[1,2,704,256]{3,2,1,0:T(8,128)(2,1)}, bf16[1,2,704,256]{3,2,1,0:T(8,128)(2,1)}, u32[]{:S(2)}, u32[]{:S(2)}) collective-permute-start(bf16[1,2,704,256]{3,2,1,0:T(8,128)(2,1)} %slice.228), channel_id=1, source_target_pairs={{0,8},{4,12},{8,0},{12,4},{1,9},{5,13},{9,1},{13,5},{2,10},{6,14},... | collective-permute-start | bytes 2162696 | tf_op jit(solution)/shard_map/ppermute | solution.py:21
  315.2 17.0 %collective-permute-start.34 = (bf16[2,704,256]{2,1,0:T(8,128)(2,1)}, bf16[2,704,256]{2,1,0:T(8,128)(2,1)S(1)}, u32[]{:S(2)}, u32[]{:S(2)}) collective-permute-start(bf16[2,704,256]{2,1,0:T(8,128)(2,1)} %fusion.3), channel_id=1, source_target_pairs={{0,1},{1,0},{2,3},{3,2},{4,5},{5,4},{6,7},{7,6},{8,9},{9,8},{10,11... | collective-permute-start | bytes 2162696 | tf_op jit(solution)/shard_map/ppermute | solution.py:21
  316.6 43.4 %collective-permute-start.43 = (bf16[4,704,352]{2,1,0:T(8,128)(2,1)}, bf16[4,704,352]{2,1,0:T(8,128)(2,1)}, u32[]{:S(2)}, u32[]{:S(2)}) collective-permute-start(bf16[4,704,352]{2,1,0:T(8,128)(2,1)} %get-tuple-element.77), channel_id=1, source_target_pairs={{0,16},{16,0},{1,17},{17,1},{2,18},{18,2},{3,19},{19,3},{4,20},{20... | collective-permute-start | bytes 5947400 | tf_op jit(solution)/shard_map/ppermute | solution.py:21
  334.1 31.7 %collective-permute-start.32 = (bf16[2,2,704,256]{3,2,1,0:T(8,128)(2,1)}, bf16[2,2,704,256]{3,2,1,0:T(8,128)(2,1)}, u32[]{:S(2)}, u32[]{:S(2)}) collective-permute-start(bf16[2,2,704,256]{3,2,1,0:T(8,128)(2,1)} %get-tuple-element.86), channel_id=1, source_target_pairs={{0,8},{4,12},{8,0},{12,4},{1,9},{5,13},{9,1},{13,5},{2,10},{6,14},... | collective-permute-start | bytes 4325384 | tf_op jit(solution)/shard_map/ppermute | solution.py:21
  335.6 16.6 %collective-permute-start.35 = (bf16[1,704,256]{2,1,0:T(8,128)(2,1)S(1)}, bf16[1,704,256]{2,1,0:T(8,128)(2,1)S(1)}, u32[]{:S(2)}, u32[]{:S(2)}) collective-permute-start(bf16[1,704,256]{2,1,0:T(8,128)(2,1)S(1)} %slice.230), channel_id=1, source_target_pairs={{0,2},{1,3},{2,0},{3,1},{4,6},{5,7},{6,4},{7,5},{8,10},{9,11},{10,... | collective-permute-start | bytes 1081352 | tf_op jit(solution)/shard_map/ppermute | solution.py:21
  337.5 39.4 %collective-permute-start.30 = (bf16[2,2,704,256]{3,2,1,0:T(8,128)(2,1)}, bf16[2,2,704,256]{3,2,1,0:T(8,128)(2,1)}, u32[]{:S(2)}, u32[]{:S(2)}) collective-permute-start(bf16[2,2,704,256]{3,2,1,0:T(8,128)(2,1)} %get-tuple-element.84), channel_id=1, source_target_pairs={{0,4},{4,0},{8,12},{12,8},{1,5},{5,1},{9,13},{13,9},{2,6},{6,2},{1... | collective-permute-start | bytes 4325384 | tf_op jit(solution)/shard_map/ppermute | solution.py:21
  356.8 8.0 %collective-permute-start.36 = (f32[2,4,2,32]{3,2,1,0:T(2,128)S(1)}, f32[2,4,2,32]{3,2,1,0:T(2,128)S(1)}, u32[]{:S(2)}, u32[]{:S(2)}) collective-permute-start(f32[2,4,2,32]{3,2,1,0:T(2,128)S(1)} %pad_maximum_fusion.3), channel_id=1, source_target_pairs={{0,1},{1,0},{2,3},{3,2},{4,5},{5,4},{6,7},{7,6},{8,9},{9,8},{10,11... | collective-permute-start | bytes 6152 | tf_op jit(solution)/shard_map/ppermute | solution.py:21
  356.9 8.0 %collective-permute-start.37 = (f32[2,4,2,32]{3,2,1,0:T(2,128)S(1)}, f32[2,4,2,32]{3,2,1,0:T(2,128)S(1)}, u32[]{:S(2)}, u32[]{:S(2)}) collective-permute-start(f32[2,4,2,32]{3,2,1,0:T(2,128)S(1)} %pad_maximum_fusion.3), channel_id=1, source_target_pairs={{0,2},{1,3},{2,0},{3,1},{4,6},{5,7},{6,4},{7,5},{8,10},{9,11},{10,... | collective-permute-start | bytes 6152 | tf_op jit(solution)/shard_map/ppermute | solution.py:21
  360.0 5.4 %collective-permute-start.38 = (f32[2,4,2,32]{3,2,1,0:T(2,128)S(1)}, f32[2,4,2,32]{3,2,1,0:T(2,128)S(1)}, u32[]{:S(2)}, u32[]{:S(2)}) collective-permute-start(f32[2,4,2,32]{3,2,1,0:T(2,128)S(1)} %pad_maximum_fusion.3), channel_id=1, source_target_pairs={{0,3},{1,2},{2,1},{3,0},{4,7},{5,6},{6,5},{7,4},{8,11},{9,10},{10,... | collective-permute-start | bytes 6152 | tf_op jit(solution)/shard_map/ppermute | solution.py:21
  370.0 16.6 %collective-permute-start.33 = (bf16[1,2,704,256]{3,2,1,0:T(8,128)(2,1)}, bf16[1,2,704,256]{3,2,1,0:T(8,128)(2,1)}, u32[]{:S(2)}, u32[]{:S(2)}) collective-permute-start(bf16[1,2,704,256]{3,2,1,0:T(8,128)(2,1)} %slice.225), channel_id=1, source_target_pairs={{0,4},{4,0},{8,12},{12,8},{1,5},{5,1},{9,13},{13,9},{2,6},{6,2},{1... | collective-permute-start | bytes 2162696 | tf_op jit(solution)/shard_map/ppermute | solution.py:21
  371.7 74.5 %all-to-all-start.3 = ((bf16[4,704,352]{2,1,0:T(8,128)(2,1)}), bf16[4,704,352]{2,1,0:T(8,128)(2,1)S(1)}, u32[]{:S(2)}, u32[]{:S(2)}) async-start(bf16[4,704,352]{2,1,0:T(8,128)(2,1)} %shard_map.133), calls=%async_computation.3 | async-start | bytes 4325376 | tf_op jit(solution)/shard_map/all_to_all | solution.py:550
  377.1 9.5 %copy-start.33 = (f32[2,2,704,256]{3,2,1,0:T(8,128)S(1)}, f32[2,2,704,256]{3,2,1,0:T(8,128)}, u32[]{:S(2)}) copy-start(f32[2,2,704,256]{3,2,1,0:T(8,128)} %copy-done.32) | copy-start | bytes 8650756
  379.0 23.2 %copy-start.28 = (bf16[3,2,32,704]{3,2,1,0:T(8,128)(2,1)S(1)}, bf16[3,2,32,704]{3,2,1,0:T(8,128)(2,1)}, u32[]{:S(2)}) copy-start(bf16[3,2,32,704]{3,2,1,0:T(8,128)(2,1)} %copy-done.27) | copy-start | bytes 811012
  379.0 23.2 %copy-start.30 = (bf16[3,2,32,704]{3,2,1,0:T(8,128)(2,1)S(1)}, bf16[3,2,32,704]{3,2,1,0:T(8,128)(2,1)}, u32[]{:S(2)}) copy-start(bf16[3,2,32,704]{3,2,1,0:T(8,128)(2,1)} %copy-done.29) | copy-start | bytes 811012
  379.0 47.0 %collective-permute-start.31 = (bf16[1,2,704,256]{3,2,1,0:T(8,128)(2,1)S(1)}, bf16[1,2,704,256]{3,2,1,0:T(8,128)(2,1)S(1)}, u32[]{:S(2)}, u32[]{:S(2)}) collective-permute-start(bf16[1,2,704,256]{3,2,1,0:T(8,128)(2,1)S(1)} %slice.226), channel_id=1, source_target_pairs={{0,8},{4,12},{8,0},{12,4},{1,9},{5,13},{9,1},{13,5},{2,10},{6,14},... | collective-permute-start | bytes 2162696 | tf_op jit(solution)/shard_map/ppermute | solution.py:21
  387.8 38.1 %collective-permute-start.39 = (bf16[2,704,256]{2,1,0:T(8,128)(2,1)S(1)}, bf16[2,704,256]{2,1,0:T(8,128)(2,1)S(1)}, u32[]{:S(2)}, u32[]{:S(2)}) collective-permute-start(bf16[2,704,256]{2,1,0:T(8,128)(2,1)S(1)} %fusion), channel_id=1, source_target_pairs={{0,1},{1,0},{2,3},{3,2},{4,5},{5,4},{6,7},{7,6},{8,9},{9,8},{10,11... | collective-permute-start | bytes 2162696 | tf_op jit(solution)/shard_map/ppermute | solution.py:21
  387.9 21.3 %copy-start.22 = (bf16[4,2,32,704]{3,2,1,0:T(8,128)(2,1)S(1)}, bf16[4,2,32,704]{3,2,1,0:T(8,128)(2,1)}, u32[]{:S(2)}) copy-start(bf16[4,2,32,704]{3,2,1,0:T(8,128)(2,1)} %refs_0_.1) | copy-start | bytes 1081348
  388.0 7.7 %collective-permute-start.40 = (bf16[3,2,32,704]{3,2,1,0:T(8,128)(2,1)S(1)}, bf16[3,2,32,704]{3,2,1,0:T(8,128)(2,1)S(1)}, u32[]{:S(2)}, u32[]{:S(2)}) collective-permute-start(bf16[3,2,32,704]{3,2,1,0:T(8,128)(2,1)S(1)} %get-tuple-element.109), channel_id=1, source_target_pairs={{0,4},{4,8},{8,12},{1,5},{5,9},{9,13},{2,6},{6,10},{10,14},{3,7},{... | collective-permute-start | bytes 811016 | tf_op jit(solution)/shard_map/ppermute | solution.py:353
  391.4 10.7 %collective-permute-start.41 = (bf16[3,2,32,704]{3,2,1,0:T(8,128)(2,1)S(1)}, bf16[3,2,32,704]{3,2,1,0:T(8,128)(2,1)S(1)}, u32[]{:S(2)}, u32[]{:S(2)}) collective-permute-start(bf16[3,2,32,704]{3,2,1,0:T(8,128)(2,1)S(1)} %get-tuple-element.108), channel_id=1, source_target_pairs={{4,0},{8,4},{12,8},{5,1},{9,5},{13,9},{6,2},{10,6},{14,10},{7,3},{... | collective-permute-start | bytes 811016 | tf_op jit(solution)/shard_map/ppermute | solution.py:353
  409.2 8.1 %collective-permute-start.44 = (bf16[7,7,704]{2,1,0:T(8,128)(2,1)S(1)}, bf16[7,7,704]{2,1,0:T(8,128)(2,1)S(1)}, u32[]{:S(2)}, u32[]{:S(2)}) collective-permute-start(bf16[7,7,704]{2,1,0:T(8,128)(2,1)S(1)} %convert_element_type.121), channel_id=1, source_target_pairs={{0,16},{16,0},{1,17},{17,1},{2,18},{18,2},{3,19},{19,3},{4,20},{20... | collective-permute-start | bytes 206984 | tf_op jit(solution)/shard_map/ppermute | solution.py:21
  417.3 12.0 %collective-permute-start.45 = (bf16[7,7,704]{2,1,0:T(8,128)(2,1)S(1)}, bf16[7,7,704]{2,1,0:T(8,128)(2,1)S(1)}, u32[]{:S(2)}, u32[]{:S(2)}) collective-permute-start(bf16[7,7,704]{2,1,0:T(8,128)(2,1)S(1)} %add_convert_fusion.2), channel_id=1, source_target_pairs={{0,4},{4,0},{8,12},{12,8},{1,5},{5,1},{9,13},{13,9},{2,6},{6,2},{1... | collective-permute-start | bytes 206984 | tf_op jit(solution)/shard_map/ppermute | solution.py:21
  426.2 16.8 %collective-permute-start.42 = (bf16[1,704,256]{2,1,0:T(8,128)(2,1)S(1)}, bf16[1,704,256]{2,1,0:T(8,128)(2,1)S(1)}, u32[]{:S(2)}, u32[]{:S(2)}) collective-permute-start(bf16[1,704,256]{2,1,0:T(8,128)(2,1)S(1)} %slice.229), channel_id=1, source_target_pairs={{0,2},{1,3},{2,0},{3,1},{4,6},{5,7},{6,4},{7,5},{8,10},{9,11},{10,... | collective-permute-start | bytes 1081352 | tf_op jit(solution)/shard_map/ppermute | solution.py:21
  429.3 5.5 %collective-permute-start.46 = (bf16[7,7,704]{2,1,0:T(8,128)(2,1)S(1)}, bf16[7,7,704]{2,1,0:T(8,128)(2,1)S(1)}, u32[]{:S(2)}, u32[]{:S(2)}) collective-permute-start(bf16[7,7,704]{2,1,0:T(8,128)(2,1)S(1)} %add_convert_fusion.1), channel_id=1, source_target_pairs={{0,8},{4,12},{8,0},{12,4},{1,9},{5,13},{9,1},{13,5},{2,10},{6,14},... | collective-permute-start | bytes 206984 | tf_op jit(solution)/shard_map/ppermute | solution.py:21
  (25 other events, 51.0 us)

commit v6 on v5

--- a/solution.py
+++ b/solution.py
@@ -502,17 +502,13 @@
     w_out_there = lax.all_to_all(pieces, "col", 0, 0)
     act, slope, square = hidden_kernel(places, normed_all, w_in_all, bias, dims)
     norm_chan = jnp.sqrt(square + epsilon)
-    norm_sum = add_over(add_over(jnp.sum(norm_chan, axis=0), "row"), "col")
+    norm_rows = add_over(jnp.sum(norm_chan, axis=0), "row")
+    w_out_there = after(w_out_there, norm_rows)
+    w_out_all, w_out_turned = join_weights(places, w_out_there, swap(w_out_there, "dp", 1))
+    norm_sum = add_over(norm_rows, "col")
     denom = norm_sum / all_units + epsilon
     gamma, beta = gamma[:, None], beta[:, None]
     gain = gamma * (norm_chan / denom) + 1.0
-    gated = gated_kernel(places, act, gain, beta, dims)
-    w_out_mine, w_out_other = grads_kernel(places, gated, cot_all, dims, col_count, chans)
-    w_out_sums = add_kernel(places, w_out_mine, swap(w_out_other, "dp", 1))
-    w_out_there = after(w_out_there, w_out_sums)
-    w_out_back = lax.all_to_all(after(w_out_sums, w_out_there), "col", 0, 0)
-    w_out_grad = finish_kernel(places, w_out_back, scale_grad).T
-    w_out_all, w_out_turned = join_weights(places, w_out_there, swap(w_out_there, "dp", 1))
     grad_gated, pull = back_kernel(places, cot_all, w_out_all, act, dims)
     share_back = gamma * pull / denom / norm_chan
 
@@ -524,6 +520,11 @@
         dims,
         (bits[0], bits[-1]),
     )
+    gated = gated_kernel(places, after(act, grad_parts), gain, beta, dims)
+    w_out_mine, w_out_other = grads_kernel(places, gated, cot_all, dims, col_count, chans)
+    w_out_sums = add_kernel(places, w_out_mine, swap(w_out_other, "dp", 1))
+    w_out_back = lax.all_to_all(after(w_out_sums, w_out_there), "col", 0, 0)
+    w_out_grad = finish_kernel(places, w_out_back, scale_grad).T
     _, out_parts = project_kernel(
         places, lambda b, spread: b[0], [gated], w_out_turned, dims, (bits[0], bits[-1])
     )
@@ -533,7 +534,7 @@
     w_in_sums = add_kernel(places, w_in_mine, swap(w_in_other, "dp", 1))
 
     near_a, far_a, near_b, far_b = grad_parts
-    shade = (w_in_other, out_parts[0])
+    shade = (w_out_other, w_in_other, out_parts[0])
     even = halve_sum(near_a, far_a, "row", bits, shade)
     odd = halve_sum(near_b, far_b, "row", bits[::-1], shade)
     down = [1 << i for i in range((col_count - 1).bit_length())]

time: 457 us -> 451 us (0.987)
  starting transfers between devices: 89.1 us -> 78.4 us
  waiting for transfers between devices: 192 us -> 199 us
    ppermute x43, starting transfers between devices: 60.3 us -> 49.1 us  [swap(): return lax.ppermute(block, axis, [(i, i ^ bits) for i in range(count)])]
    all_to_all x1, waiting for transfers between devices: 0.01 us -> 4.64 us  [local(): w_out_there = lax.all_to_all(pieces, 'col', 0, 0)]
    unnamed x77 -> x85, local copies, waits for them, and re-layouts: 24.9 us -> 27.5 us
  transfers between devices with their start and end apart: 51 -> 51, of which waited for: 25 -> 28; matrix products, arithmetic and copies ran while one was open for 8% -> 8% of each run, Pallas kernels for 22% -> 14%
where the time goes in v6:
time: 451 us; the launch traced here: 444 us
  waiting for transfers between devices  199 us (44%)
  Pallas kernels  104 us (23%)
  starting transfers between devices  78.4 us (17%)
  local copies, waits for them, and re-layouts  42.9 us (10%)
  other arithmetic  19.1 us (4%)
    ppermute x43, waiting for transfers between devices, swap(): return lax.ppermute(block, axis, [(i, i ^ bits) for i in range(count)])  175 us
    pallas_call x15, Pallas kernels, call(): pl.pallas_call(body, out_shape=outs, in_specs=[in_smem] + [in_vmem] * len...  81.9 us
    ppermute x43, starting transfers between devices, swap(): return lax.ppermute(block, axis, [(i, i ^ bits) for i in range(count)])  49.1 us
    unnamed x85, local copies, waits for them, and re-layouts  27.5 us
    ppermute x2, waiting for transfers between devices, exchange_rows(): lax.ppermute(high, 'row', backward)  16 us
    pallas_call x2, Pallas kernels, depthwise(): pl.pallas_call(body, out_shape=shape_of(mid.shape, f32 if extra is None e...  14.9 us
  transfers between devices with their start and end apart: 51, of which 28 were waited for; matrix products, arithmetic and copies ran while one was open for 8% of the time, Pallas kernels for 14%

profile of v6, /device:TPU:0, one launch (start us, length us, event | category | flops | bytes accessed | tf_op | source)
XLA Modules:
  0.0 444.3 jit_solution(16901890769147303458)
XLA Ops:
  6.9 4.8 %collective-permute-start = (bf16[3,2,32,704]{3,2,1,0:T(8,128)(2,1)S(1)}, bf16[3,2,32,704]{3,2,1,0:T(8,128)(2,1)S(1)}, u32[]{:S(2)}, u32[]{:S(2)}) collective-permute-start(bf16[3,2,32,704]{3,2,1,0:T(8,128)(2,1)S(1)} %get-tuple-element.51), channel_id=1, source_target_pairs={{0,4},{4,8},{8,12},{1,5},{5,9},{9,13},{2,6},{6,10},{10,14},{3,7},{... | collective-permute-start | bytes 811016 | tf_op jit(solution)/shard_map/ppermute | solution.py:353
  13.1 1.6 collective-permute-start.2
  14.7 2.6 collective-permute-start.3
  18.0 8.3 %collective-permute-done.1.high = bf16[3,2,32,704]{3,2,1,0:T(8,128)(2,1)S(1)} collective-permute-done((bf16[3,2,32,704]{3,2,1,0:T(8,128)(2,1)S(1)}, bf16[3,2,32,704]{3,2,1,0:T(8,128)(2,1)S(1)}, u32[]{:S(2)}, u32[]{:S(2)}) %collective-permute-start.1) | collective-permute-done | bytes 270368 | tf_op jit(solution)/shard_map/ppermute | solution.py:353
  26.3 6.9 %shard_map.120 = f32[4,2,32,704]{3,2,1,0:T(8,128)S(1)} custom-call(s32[2]{0:T(128)S(1)} %pad_add_fusion.places, bf16[3,2,32,704]{3,2,1,0:T(8,128)(2,1)S(1)} %collective-permute-done.low, bf16[4,2,32,704]{3,2,1,0:T(8,128)(2,1)S(1)} %copy-done.8, bf16[3,2,32,704]{3,2,1,0:T(8,128)(2,1)S(1)} %collective-permute-done.1.high, f32[7,7,704]{2,1,0:T(8,128)S(1)} %copy-done.34), custom_call_target="tpu_custom_call" | custom-call | tf_op jit(solution)/shard_map/pallas_call | solution.py:403
  35.0 7.4 %collective-permute-done.3 = bf16[704,256]{1,0:T(8,128)(2,1)S(1)} collective-permute-done((bf16[704,256]{1,0:T(8,128)(2,1)S(1)}, bf16[704,256]{1,0:T(8,128)(2,1)S(1)}, u32[]{:S(2)}, u32[]{:S(2)}) %collective-permute-start.3) | collective-permute-done | bytes 360480 | tf_op jit(solution)/shard_map/ppermute | solution.py:21
  44.5 2.7 collective-permute-start.11
  48.8 6.2 %collective-permute-start.5 = (f32[2,4,2,32]{3,2,1,0:T(2,128)S(1)}, f32[2,4,2,32]{3,2,1,0:T(2,128)S(1)}, u32[]{:S(2)}, u32[]{:S(2)}) collective-permute-start(f32[2,4,2,32]{3,2,1,0:T(2,128)S(1)} %pad_maximum_fusion.2), channel_id=1, source_target_pairs={{0,1},{1,0},{2,3},{3,2},{4,5},{5,4},{6,7},{7,6},{8,9},{9,8},{10,11... | collective-permute-start | bytes 6152 | tf_op jit(solution)/shard_map/ppermute | solution.py:21
  57.4 2.1 collective-permute-done.6
  59.5 2.1 collective-permute-done.7
  62.0 1.9 collective-permute-start.9
  64.0 12.8 %collective-permute-done.8 = bf16[704,256]{1,0:T(8,128)(2,1)S(1)} collective-permute-done((bf16[704,256]{1,0:T(8,128)(2,1)S(1)}, bf16[704,256]{1,0:T(8,128)(2,1)S(1)}, u32[]{:S(2)}, u32[]{:S(2)}) %collective-permute-start.8) | collective-permute-done | bytes 360480 | tf_op jit(solution)/shard_map/ppermute | solution.py:21
  76.8 9.3 %collective-permute-done.10 = bf16[704,256]{1,0:T(8,128)(2,1)S(1)} collective-permute-done((bf16[704,256]{1,0:T(8,128)(2,1)S(1)}, bf16[704,256]{1,0:T(8,128)(2,1)S(1)}, u32[]{:S(2)}, u32[]{:S(2)}) %collective-permute-start.10) | collective-permute-done | bytes 360480 | tf_op jit(solution)/shard_map/ppermute | solution.py:21
  87.5 4.5 %all-to-all-start = ((bf16[4,704,352]{2,1,0:T(8,128)(2,1)}), bf16[4,704,352]{2,1,0:T(8,128)(2,1)}, u32[]{:S(2)}, u32[]{:S(2)}) async-start(bf16[4,704,352]{2,1,0:T(8,128)(2,1)} %copy-done.15), calls=%async_computation | async-start | bytes 4325376 | tf_op jit(solution)/shard_map/all_to_all | solution.py:498
  95.0 1.6 collective-permute-start.17
  101.0 39.3 %collective-permute-done.17.refs_3_ = bf16[2,704,256]{2,1,0:T(8,128)(2,1)S(1)} collective-permute-done((bf16[2,704,256]{2,1,0:T(8,128)(2,1)S(1)}, bf16[2,704,256]{2,1,0:T(8,128)(2,1)S(1)}, u32[]{:S(2)}, u32[]{:S(2)}) %collective-permute-start.17) | collective-permute-done | bytes 720928 | tf_op jit(solution)/shard_map/ppermute | solution.py:21
  141.2 5.1 %all-to-all-start.1 = ((bf16[4,704,352]{2,1,0:T(8,128)(2,1)}), bf16[4,704,352]{2,1,0:T(8,128)(2,1)}, u32[]{:S(2)}, u32[]{:S(2)}) async-start(bf16[4,704,352]{2,1,0:T(8,128)(2,1)} %copy-done.7), calls=%async_computation.1 | async-start | bytes 4325376 | tf_op jit(solution)/shard_map/all_to_all | solution.py:502
  146.5 2.0 slice.128
  149.1 2.0 slice.129
  152.7 6.1 %shard_map.121 = (bf16[4,704,704]{2,1,0:T(8,128)(2,1)S(1)}, bf16[4,704,704]{2,1,0:T(8,128)(2,1)}) custom-call(s32[2]{0:T(128)S(1)} %pad_add_fusion.places, bf16[4,704,352]{2,1,0:T(8,128)(2,1)} %all-to-all-done.mine, bf16[4,704,352]{2,1,0:T(8,128)(2,1)} %collective-permute-done.19.other), custom_call_target="tpu_custom_call" | custom-call | tf_op jit(solution)/shard_map/pallas_call | solution.py:94
  158.8 2.0 copy-done.11
  160.9 6.5 %collective-permute-done.15.refs_3_ = bf16[2,704,256]{2,1,0:T(8,128)(2,1)} collective-permute-done((bf16[2,704,256]{2,1,0:T(8,128)(2,1)}, bf16[2,704,256]{2,1,0:T(8,128)(2,1)}, u32[]{:S(2)}, u32[]{:S(2)}) %collective-permute-start.15) | collective-permute-done | bytes 720928 | tf_op jit(solution)/shard_map/ppermute | solution.py:21
  167.3 2.4 collective-permute-done.16.refs_4_
  169.7 10.5 %shard_map.122 = (f32[704,1024]{1,0:T(8,128)S(1)}, f32[704,1024]{1,0:T(8,128)}, f32[704,2]{1,0:T(8,128)S(1)}) custom-call(s32[2]{0:T(128)S(1)} %pad_add_fusion.places, bf16[4,704,256]{2,1,0:T(8,128)(2,1)S(1)} %copy-done.2, bf16[4,704,256]{2,1,0:T(8,128)(2,1)} %collective-permute-done.13.refs_1_, bf16[4,704,256]{2,1,0:T(8,128)(2,1)} %collective-permute-done.14.refs_2_, ...), custom_call_target="tpu_custom_call" | custom-call | tf_op jit(solution)/shard_map/pallas_call | solution.py:94
  182.5 3.0 collective-permute-done.20
  187.0 2.1 collective-permute-done.21
  189.1 4.6 %all-to-all-done.1.mine = bf16[4,704,352]{2,1,0:T(8,128)(2,1)} async-done(((bf16[4,704,352]{2,1,0:T(8,128)(2,1)}), bf16[4,704,352]{2,1,0:T(8,128)(2,1)}, u32[]{:S(2)}, u32[]{:S(2)}) %all-to-all-start.1) | async-done | bytes 1982496 | tf_op jit(solution)/shard_map/all_to_all | solution.py:502
  194.9 3.5 collective-permute-done.23
  198.5 4.4 collective-permute-done.24
  202.9 5.4 %shard_map.124 = (bf16[4,704,704]{2,1,0:T(8,128)(2,1)S(1)}, bf16[4,704,704]{2,1,0:T(8,128)(2,1)}) custom-call(s32[2]{0:T(128)S(1)} %pad_add_fusion.places, bf16[4,704,352]{2,1,0:T(8,128)(2,1)} %all-to-all-done.1.mine, bf16[4,704,352]{2,1,0:T(8,128)(2,1)S(1)} %collective-permute-done.22.other), custom_call_target="tpu_custom_call" | custom-call | tf_op jit(solution)/shard_map/pallas_call | solution.py:94
  208.3 2.0 copy-done.10
  210.3 8.8 %shard_map.125 = (f32[704,1024]{1,0:T(8,128)S(1)}, f32[704,2]{1,0:T(8,128)S(1)}) custom-call(s32[2]{0:T(128)S(1)} %pad_add_fusion.places, bf16[4,704,256]{2,1,0:T(8,128)(2,1)S(1)} %pad_maximum_fusion.1.refs_0_, bf16[4,704,256]{2,1,0:T(8,128)(2,1)} %collective-permute-done.11.refs_1_, bf16[4,704,256]{2,1,0:T(8,128)(2,1)} %collective-permute-done.12.refs_2_, ...), custom_call_target="tpu_custom_call" | custom-call | tf_op jit(solution)/shard_map/pallas_call | solution.py:94
  220.9 10.0 %shard_map.126 = (bf16[704,1024]{1,0:T(8,128)(2,1)S(1)}, bf16[2,2,704,256]{3,2,1,0:T(8,128)(2,1)S(1)}, bf16[2,2,704,256]{3,2,1,0:T(8,128)(2,1)S(1)}, bf16[2,2,70...) custom-call(s32[2]{0:T(128)S(1)} %pad_add_fusion.places, f32[704,1024]{1,0:T(8,128)} %copy-done.14, ...), custom_call_target="tpu_custom_call" | custom-call | tf_op jit(solution)/shard_map/pallas_call | solution.py:94
  234.3 1.8 shard_map.127.refs_0_.left
  236.1 8.4 %shard_map.129 = (bf16[4,704,352]{2,1,0:T(8,128)(2,1)S(1)}, bf16[4,704,352]{2,1,0:T(8,128)(2,1)}) custom-call(s32[2]{0:T(128)S(1)} %pad_add_fusion.places, bf16[704,1024]{1,0:T(8,128)(2,1)S(1)} %shard_map.127.refs_0_.left, bf16[4,704,256]{2,1,0:T(8,128)(2,1)S(1)} %pad_maximum_fusion.1.refs_0_, bf16[4,704,256]{2,1,0:T(8,128)(2,1)} %collective-permute-done.11.refs_1_, ...), custom_call_target="tpu_custom_call" | custom-call | tf_op jit(solution)/shard_map/pallas_call | solution.py:94
  244.5 4.5 %collective-permute-done.33.got = bf16[4,704,352]{2,1,0:T(8,128)(2,1)S(1)} collective-permute-done((bf16[4,704,352]{2,1,0:T(8,128)(2,1)}, bf16[4,704,352]{2,1,0:T(8,128)(2,1)S(1)}, u32[]{:S(2)}, u32[]{:S(2)}) %collective-permute-start.33) | collective-permute-done | bytes 1982496 | tf_op jit(solution)/shard_map/ppermute | solution.py:21
  251.4 4.8 %all-to-all-start.2 = ((bf16[4,704,352]{2,1,0:T(8,128)(2,1)}), bf16[4,704,352]{2,1,0:T(8,128)(2,1)}, u32[]{:S(2)}, u32[]{:S(2)}) async-start(bf16[4,704,352]{2,1,0:T(8,128)(2,1)} %copy-done.6), calls=%async_computation.2 | async-start | bytes 4325376 | tf_op jit(solution)/shard_map/all_to_all | solution.py:526
  258.3 8.1 %shard_map.128 = (bf16[704,1024]{1,0:T(8,128)(2,1)}, bf16[2,2,704,256]{3,2,1,0:T(8,128)(2,1)S(1)}, bf16[2,2,704,256]{3,2,1,0:T(8,128)(2,1)}, bf16[2,2,704,256]{3...) custom-call(s32[2]{0:T(128)S(1)} %pad_add_fusion.places, bf16[704,1024]{1,0:T(8,128)(2,1)S(1)} %copy-done.5, ...), custom_call_target="tpu_custom_call" | custom-call | tf_op jit(solution)/shard_map/pallas_call | solution.py:94
  268.7 8.4 %shard_map.130 = (bf16[4,704,352]{2,1,0:T(8,128)(2,1)S(1)}, bf16[4,704,352]{2,1,0:T(8,128)(2,1)}) custom-call(s32[2]{0:T(128)S(1)} %pad_add_fusion.places, bf16[704,1024]{1,0:T(8,128)(2,1)S(1)} %copy-done.21, bf16[4,704,256]{2,1,0:T(8,128)(2,1)S(1)} %copy-done.3, bf16[4,704,256]{2,1,0:T(8,128)(2,1)} %collective-permute-done.13.refs_1_, ...), custom_call_target="tpu_custom_call" | custom-call | tf_op jit(solution)/shard_map/pallas_call | solution.py:94
  277.1 13.0 %collective-permute-done.27 = bf16[2,2,704,256]{3,2,1,0:T(8,128)(2,1)S(1)} collective-permute-done((bf16[2,2,704,256]{3,2,1,0:T(8,128)(2,1)}, bf16[2,2,704,256]{3,2,1,0:T(8,128)(2,1)S(1)}, u32[]{:S(2)}, u32[]{:S(2)}) %collective-permute-start.27) | collective-permute-done | bytes 1441824 | tf_op jit(solution)/shard_map/ppermute | solution.py:21
  295.5 12.6 %collective-permute-done.28 = bf16[1,2,704,256]{3,2,1,0:T(8,128)(2,1)S(1)} collective-permute-done((bf16[1,2,704,256]{3,2,1,0:T(8,128)(2,1)S(1)}, bf16[1,2,704,256]{3,2,1,0:T(8,128)(2,1)S(1)}, u32[]{:S(2)}, u32[]{:S(2)}) %collective-permute-start.28) | collective-permute-done | bytes 720928 | tf_op jit(solution)/shard_map/ppermute | solution.py:21
  310.5 1.9 collective-permute-done.26
  312.4 13.5 %collective-permute-done.34 = bf16[2,704,256]{2,1,0:T(8,128)(2,1)S(1)} collective-permute-done((bf16[2,704,256]{2,1,0:T(8,128)(2,1)}, bf16[2,704,256]{2,1,0:T(8,128)(2,1)S(1)}, u32[]{:S(2)}, u32[]{:S(2)}) %collective-permute-start.34) | collective-permute-done | bytes 720928 | tf_op jit(solution)/shard_map/ppermute | solution.py:21
  325.9 1.9 convert_add_fusion.4
  328.4 2.0 collective-permute-start.35
  332.0 12.8 %collective-permute-done.35 = bf16[1,704,256]{2,1,0:T(8,128)(2,1)S(1)} collective-permute-done((bf16[1,704,256]{2,1,0:T(8,128)(2,1)S(1)}, bf16[1,704,256]{2,1,0:T(8,128)(2,1)S(1)}, u32[]{:S(2)}, u32[]{:S(2)}) %collective-permute-start.35) | collective-permute-done | bytes 360480 | tf_op jit(solution)/shard_map/ppermute | solution.py:21
  345.8 2.3 copy.21
  349.6 2.8 collective-permute-start.37
  354.0 3.6 shard_map.133
  359.3 1.7 convert_add_fusion
  365.0 3.6 all-to-all-start.3
  370.3 1.8 convert_add_fusion.1
  372.9 6.4 %collective-permute-done.32 = bf16[1,2,704,256]{3,2,1,0:T(8,128)(2,1)} collective-permute-done((bf16[1,2,704,256]{3,2,1,0:T(8,128)(2,1)}, bf16[1,2,704,256]{3,2,1,0:T(8,128)(2,1)}, u32[]{:S(2)}, u32[]{:S(2)}) %collective-permute-start.32) | collective-permute-done | bytes 720928 | tf_op jit(solution)/shard_map/ppermute | solution.py:21
  380.7 3.6 collective-permute-start.40
  385.9 2.7 collective-permute-done.40.low
  388.5 7.8 %collective-permute-done.41.high = bf16[3,2,32,704]{3,2,1,0:T(8,128)(2,1)S(1)} collective-permute-done((bf16[3,2,32,704]{3,2,1,0:T(8,128)(2,1)S(1)}, bf16[3,2,32,704]{3,2,1,0:T(8,128)(2,1)S(1)}, u32[]{:S(2)}, u32[]{:S(2)}) %collective-permute-start.41) | collective-permute-done | bytes 270368 | tf_op jit(solution)/shard_map/ppermute | solution.py:353
  396.3 6.7 %shard_map.136 = f32[7,7,704]{2,1,0:T(8,128)S(1)} custom-call(s32[2]{0:T(128)S(1)} %pad_add_fusion.places, bf16[3,2,32,704]{3,2,1,0:T(8,128)(2,1)S(1)} %copy-done.31, bf16[4,2,32,704]{3,2,1,0:T(8,128)(2,1)S(1)} %copy-done.9, bf16[3,2,32,704]{3,2,1,0:T(8,128)(2,1)S(1)} %copy-done.33, f32[4,2,32,704]{3,2,1,0:T(8,128)S(1)} %get-tuple-element.96.mid.grad), custom_call_target="tpu_custom_call" | custom-call | tf_op jit(solution)/shard_map/pallas_call | solution.py:441
  403.2 8.0 %shard_map.132 = bf16[4,2,32,704]{3,2,1,0:T(8,128)(2,1)} custom-call(s32[2]{0:T(128)S(1)} %pad_add_fusion.places, bf16[3,2,32,704]{3,2,1,0:T(8,128)(2,1)S(1)} %collective-permute-done.40.low, f32[4,2,32,704]{3,2,1,0:T(8,128)S(1)} %get-tuple-element.96.mid.grad, bf16[3,2,32,704]{3,2,1,0:T(8,128)(2,1)S(1)} %collective-permute-done.41.high, ...), custom_call_target="tpu_custom_call" | custom-call | tf_op jit(solution)/shard_map/pallas_call | solution.py:403
  412.6 6.1 %collective-permute-done.39 = bf16[2,704,256]{2,1,0:T(8,128)(2,1)S(1)} collective-permute-done((bf16[2,704,256]{2,1,0:T(8,128)(2,1)S(1)}, bf16[2,704,256]{2,1,0:T(8,128)(2,1)S(1)}, u32[]{:S(2)}, u32[]{:S(2)}) %collective-permute-start.39) | collective-permute-done | bytes 720928 | tf_op jit(solution)/shard_map/ppermute | solution.py:21
  419.0 3.5 collective-permute-start.42
  423.5 4.1 shard_map.135
  428.3 7.3 %collective-permute-done.42 = bf16[1,704,256]{2,1,0:T(8,128)(2,1)S(1)} collective-permute-done((bf16[1,704,256]{2,1,0:T(8,128)(2,1)S(1)}, bf16[1,704,256]{2,1,0:T(8,128)(2,1)S(1)}, u32[]{:S(2)}, u32[]{:S(2)}) %collective-permute-start.42) | collective-permute-done | bytes 360480 | tf_op jit(solution)/shard_map/ppermute | solution.py:21
  436.5 2.3 copy.23
  440.8 3.1 shard_map.134
  (198 shorter events, 76.7 us)
Async XLA Ops:
  4.3 22.0 %copy-start.34 = (f32[7,7,704]{2,1,0:T(8,128)S(1)}, f32[7,7,704]{2,1,0:T(8,128)}, u32[]{:S(2)}) copy-start(f32[7,7,704]{2,1,0:T(8,128)} %kern.3) | copy-start | bytes 413956
  6.9 11.1 %collective-permute-start = (bf16[3,2,32,704]{3,2,1,0:T(8,128)(2,1)S(1)}, bf16[3,2,32,704]{3,2,1,0:T(8,128)(2,1)S(1)}, u32[]{:S(2)}, u32[]{:S(2)}) collective-permute-start(bf16[3,2,32,704]{3,2,1,0:T(8,128)(2,1)S(1)} %get-tuple-element.51), channel_id=1, source_target_pairs={{0,4},{4,8},{8,12},{1,5},{5,9},{9,13},{2,6},{6,10},{10,14},{3,7},{... | collective-permute-start | bytes 811016 | tf_op jit(solution)/shard_map/ppermute | solution.py:353
  11.8 14.5 %collective-permute-start.1 = (bf16[3,2,32,704]{3,2,1,0:T(8,128)(2,1)S(1)}, bf16[3,2,32,704]{3,2,1,0:T(8,128)(2,1)S(1)}, u32[]{:S(2)}, u32[]{:S(2)}) collective-permute-start(bf16[3,2,32,704]{3,2,1,0:T(8,128)(2,1)S(1)} %get-tuple-element.52), channel_id=1, source_target_pairs={{4,0},{8,4},{12,8},{5,1},{9,5},{13,9},{6,2},{10,6},{14,10},{7,3},{... | collective-permute-start | bytes 811016 | tf_op jit(solution)/shard_map/ppermute | solution.py:353
  13.1 21.9 %collective-permute-start.2 = (bf16[704,256]{1,0:T(8,128)(2,1)S(1)}, bf16[704,256]{1,0:T(8,128)(2,1)S(1)}, u32[]{:S(2)}, u32[]{:S(2)}) collective-permute-start(bf16[704,256]{1,0:T(8,128)(2,1)S(1)} %get-tuple-element.53), channel_id=1, source_target_pairs={{0,1},{1,0},{2,3},{3,2},{4,5},{5,4},{6,7},{7,6},{8,9},{9,8},{10,11... | collective-permute-start | bytes 1081352 | tf_op jit(solution)/shard_map/ppermute | solution.py:21
  14.7 27.7 %collective-permute-start.3 = (bf16[704,256]{1,0:T(8,128)(2,1)S(1)}, bf16[704,256]{1,0:T(8,128)(2,1)S(1)}, u32[]{:S(2)}, u32[]{:S(2)}) collective-permute-start(bf16[704,256]{1,0:T(8,128)(2,1)S(1)} %get-tuple-element.53), channel_id=1, source_target_pairs={{0,2},{1,3},{2,0},{3,1},{4,6},{5,7},{6,4},{7,5},{8,10},{9,11},{10,... | collective-permute-start | bytes 1081352 | tf_op jit(solution)/shard_map/ppermute | solution.py:21
  17.3 25.1 %collective-permute-start.4 = (bf16[704,256]{1,0:T(8,128)(2,1)S(1)}, bf16[704,256]{1,0:T(8,128)(2,1)S(1)}, u32[]{:S(2)}, u32[]{:S(2)}) collective-permute-start(bf16[704,256]{1,0:T(8,128)(2,1)S(1)} %get-tuple-element.53), channel_id=1, source_target_pairs={{0,3},{1,2},{2,1},{3,0},{4,7},{5,6},{6,5},{7,4},{8,11},{9,10},{10,... | collective-permute-start | bytes 1081352 | tf_op jit(solution)/shard_map/ppermute | solution.py:21
  44.5 42.9 %collective-permute-start.11 = (bf16[4,704,256]{2,1,0:T(8,128)(2,1)S(1)}, bf16[4,704,256]{2,1,0:T(8,128)(2,1)}, u32[]{:S(2)}, u32[]{:S(2)}) collective-permute-start(bf16[4,704,256]{2,1,0:T(8,128)(2,1)S(1)} %pad_maximum_fusion.1.refs_0_), channel_id=1, source_target_pairs={{0,4},{4,0},{8,12},{12,8},{1,5},{5,1},{9,13},{13,9},{2,6},{6,2},{1... | collective-permute-start | bytes 4325384 | tf_op jit(solution)/shard_map/ppermute | solution.py:21
  47.2 40.2 %collective-permute-start.12 = (bf16[4,704,256]{2,1,0:T(8,128)(2,1)S(1)}, bf16[4,704,256]{2,1,0:T(8,128)(2,1)}, u32[]{:S(2)}, u32[]{:S(2)}) collective-permute-start(bf16[4,704,256]{2,1,0:T(8,128)(2,1)S(1)} %pad_maximum_fusion.1.refs_0_), channel_id=1, source_target_pairs={{0,8},{4,12},{8,0},{12,4},{1,9},{5,13},{9,1},{13,5},{2,10},{6,14},... | collective-permute-start | bytes 4325384 | tf_op jit(solution)/shard_map/ppermute | solution.py:21
  48.8 8.7 %collective-permute-start.5 = (f32[2,4,2,32]{3,2,1,0:T(2,128)S(1)}, f32[2,4,2,32]{3,2,1,0:T(2,128)S(1)}, u32[]{:S(2)}, u32[]{:S(2)}) collective-permute-start(f32[2,4,2,32]{3,2,1,0:T(2,128)S(1)} %pad_maximum_fusion.2), channel_id=1, source_target_pairs={{0,1},{1,0},{2,3},{3,2},{4,5},{5,4},{6,7},{7,6},{8,9},{9,8},{10,11... | collective-permute-start | bytes 6152 | tf_op jit(solution)/shard_map/ppermute | solution.py:21
  55.0 4.5 %collective-permute-start.6 = (f32[2,4,2,32]{3,2,1,0:T(2,128)S(1)}, f32[2,4,2,32]{3,2,1,0:T(2,128)S(1)}, u32[]{:S(2)}, u32[]{:S(2)}) collective-permute-start(f32[2,4,2,32]{3,2,1,0:T(2,128)S(1)} %pad_maximum_fusion.2), channel_id=1, source_target_pairs={{0,2},{1,3},{2,0},{3,1},{4,6},{5,7},{6,4},{7,5},{8,10},{9,11},{10,... | collective-permute-start | bytes 6152 | tf_op jit(solution)/shard_map/ppermute | solution.py:21
  56.0 5.5 %collective-permute-start.7 = (f32[2,4,2,32]{3,2,1,0:T(2,128)S(1)}, f32[2,4,2,32]{3,2,1,0:T(2,128)S(1)}, u32[]{:S(2)}, u32[]{:S(2)}) collective-permute-start(f32[2,4,2,32]{3,2,1,0:T(2,128)S(1)} %pad_maximum_fusion.2), channel_id=1, source_target_pairs={{0,3},{1,2},{2,1},{3,0},{4,7},{5,6},{6,5},{7,4},{8,11},{9,10},{10,... | collective-permute-start | bytes 6152 | tf_op jit(solution)/shard_map/ppermute | solution.py:21
  62.0 14.8 %collective-permute-start.8 = (bf16[704,256]{1,0:T(8,128)(2,1)S(1)}, bf16[704,256]{1,0:T(8,128)(2,1)S(1)}, u32[]{:S(2)}, u32[]{:S(2)}) collective-permute-start(bf16[704,256]{1,0:T(8,128)(2,1)S(1)} %copy.16), channel_id=1, source_target_pairs={{0,2},{1,3},{2,0},{3,1},{4,6},{5,7},{6,4},{7,5},{8,10},{9,11},{10,... | collective-permute-start | bytes 1081352 | tf_op jit(solution)/shard_map/ppermute | solution.py:21
  62.0 14.8 %collective-permute-start.9 = (bf16[704,256]{1,0:T(8,128)(2,1)S(1)}, bf16[704,256]{1,0:T(8,128)(2,1)S(1)}, u32[]{:S(2)}, u32[]{:S(2)}) collective-permute-start(bf16[704,256]{1,0:T(8,128)(2,1)S(1)} %copy.16), channel_id=1, source_target_pairs={{0,1},{1,0},{2,3},{3,2},{4,5},{5,4},{6,7},{7,6},{8,9},{9,8},{10,11... | collective-permute-start | bytes 1081352 | tf_op jit(solution)/shard_map/ppermute | solution.py:21
  76.8 9.3 %collective-permute-start.10 = (bf16[704,256]{1,0:T(8,128)(2,1)S(1)}, bf16[704,256]{1,0:T(8,128)(2,1)S(1)}, u32[]{:S(2)}, u32[]{:S(2)}) collective-permute-start(bf16[704,256]{1,0:T(8,128)(2,1)S(1)} %collective-permute-done.8), channel_id=1, source_target_pairs={{0,1},{1,0},{2,3},{3,2},{4,5},{5,4},{6,7},{7,6},{8,9},{9,8},{10,11... | collective-permute-start | bytes 1081352 | tf_op jit(solution)/shard_map/ppermute | solution.py:21
  87.5 53.8 %all-to-all-start = ((bf16[4,704,352]{2,1,0:T(8,128)(2,1)}), bf16[4,704,352]{2,1,0:T(8,128)(2,1)}, u32[]{:S(2)}, u32[]{:S(2)}) async-start(bf16[4,704,352]{2,1,0:T(8,128)(2,1)} %copy-done.15), calls=%async_computation | async-start | bytes 4325376 | tf_op jit(solution)/shard_map/all_to_all | solution.py:498
  91.9 49.3 %collective-permute-start.13 = (bf16[4,704,256]{2,1,0:T(8,128)(2,1)}, bf16[4,704,256]{2,1,0:T(8,128)(2,1)}, u32[]{:S(2)}, u32[]{:S(2)}) collective-permute-start(bf16[4,704,256]{2,1,0:T(8,128)(2,1)} %pad_maximum_fusion.refs_0_), channel_id=1, source_target_pairs={{0,4},{4,0},{8,12},{12,8},{1,5},{5,1},{9,13},{13,9},{2,6},{6,2},{1... | collective-permute-start | bytes 4325384 | tf_op jit(solution)/shard_map/ppermute | solution.py:21
  93.4 47.8 %collective-permute-start.14 = (bf16[4,704,256]{2,1,0:T(8,128)(2,1)}, bf16[4,704,256]{2,1,0:T(8,128)(2,1)}, u32[]{:S(2)}, u32[]{:S(2)}) collective-permute-start(bf16[4,704,256]{2,1,0:T(8,128)(2,1)} %pad_maximum_fusion.refs_0_), channel_id=1, source_target_pairs={{0,8},{4,12},{8,0},{12,4},{1,9},{5,13},{9,1},{13,5},{2,10},{6,14},... | collective-permute-start | bytes 4325384 | tf_op jit(solution)/shard_map/ppermute | solution.py:21
  95.0 45.3 %collective-permute-start.17 = (bf16[2,704,256]{2,1,0:T(8,128)(2,1)S(1)}, bf16[2,704,256]{2,1,0:T(8,128)(2,1)S(1)}, u32[]{:S(2)}, u32[]{:S(2)}) collective-permute-start(bf16[2,704,256]{2,1,0:T(8,128)(2,1)S(1)} %slice.130), channel_id=1, source_target_pairs={{0,8},{4,12},{8,0},{12,4},{1,9},{5,13},{9,1},{13,5},{2,10},{6,14},... | collective-permute-start | bytes 2162696 | tf_op jit(solution)/shard_map/ppermute | solution.py:21
  97.8 42.5 %collective-permute-start.18 = (bf16[2,704,256]{2,1,0:T(8,128)(2,1)S(1)}, bf16[2,704,256]{2,1,0:T(8,128)(2,1)S(1)}, u32[]{:S(2)}, u32[]{:S(2)}) collective-permute-start(bf16[2,704,256]{2,1,0:T(8,128)(2,1)S(1)} %slice.131), channel_id=1, source_target_pairs={{0,4},{4,0},{8,12},{12,8},{1,5},{5,1},{9,13},{13,9},{2,6},{6,2},{1... | collective-permute-start | bytes 2162696 | tf_op jit(solution)/shard_map/ppermute | solution.py:21
  141.2 52.5 %all-to-all-start.1 = ((bf16[4,704,352]{2,1,0:T(8,128)(2,1)}), bf16[4,704,352]{2,1,0:T(8,128)(2,1)}, u32[]{:S(2)}, u32[]{:S(2)}) async-start(bf16[4,704,352]{2,1,0:T(8,128)(2,1)} %copy-done.7), calls=%async_computation.1 | async-start | bytes 4325376 | tf_op jit(solution)/shard_map/all_to_all | solution.py:502
  146.4 6.3 %collective-permute-start.19 = (bf16[4,704,352]{2,1,0:T(8,128)(2,1)}, bf16[4,704,352]{2,1,0:T(8,128)(2,1)}, u32[]{:S(2)}, u32[]{:S(2)}) collective-permute-start(bf16[4,704,352]{2,1,0:T(8,128)(2,1)} %all-to-all-done.mine), channel_id=1, source_target_pairs={{0,16},{16,0},{1,17},{17,1},{2,18},{18,2},{3,19},{19,3},{4,20},{20... | collective-permute-start | bytes 5947400 | tf_op jit(solution)/shard_map/ppermute | solution.py:21
  148.5 18.9 %collective-permute-start.15 = (bf16[2,704,256]{2,1,0:T(8,128)(2,1)}, bf16[2,704,256]{2,1,0:T(8,128)(2,1)}, u32[]{:S(2)}, u32[]{:S(2)}) collective-permute-start(bf16[2,704,256]{2,1,0:T(8,128)(2,1)} %slice.128), channel_id=1, source_target_pairs={{0,8},{4,12},{8,0},{12,4},{1,9},{5,13},{9,1},{13,5},{2,10},{6,14},... | collective-permute-start | bytes 2162696 | tf_op jit(solution)/shard_map/ppermute | solution.py:21
  151.1 18.6 %collective-permute-start.16 = (bf16[2,704,256]{2,1,0:T(8,128)(2,1)}, bf16[2,704,256]{2,1,0:T(8,128)(2,1)}, u32[]{:S(2)}, u32[]{:S(2)}) collective-permute-start(bf16[2,704,256]{2,1,0:T(8,128)(2,1)} %slice.129), channel_id=1, source_target_pairs={{0,4},{4,0},{8,12},{12,8},{1,5},{5,1},{9,13},{13,9},{2,6},{6,2},{1... | collective-permute-start | bytes 2162696 | tf_op jit(solution)/shard_map/ppermute | solution.py:21
  152.7 17.0 %copy-start.2 = (bf16[4,704,256]{2,1,0:T(8,128)(2,1)S(1)}, bf16[4,704,256]{2,1,0:T(8,128)(2,1)}, u32[]{:S(2)}) copy-start(bf16[4,704,256]{2,1,0:T(8,128)(2,1)} %pad_maximum_fusion.refs_0_) | copy-start | bytes 4325380
  182.0 3.6 collective-permute-start.20
  185.6 3.5 collective-permute-start.21
  193.7 9.2 %collective-permute-start.22 = (bf16[4,704,352]{2,1,0:T(8,128)(2,1)}, bf16[4,704,352]{2,1,0:T(8,128)(2,1)S(1)}, u32[]{:S(2)}, u32[]{:S(2)}) collective-permute-start(bf16[4,704,352]{2,1,0:T(8,128)(2,1)} %all-to-all-done.1.mine), channel_id=1, source_target_pairs={{0,16},{16,0},{1,17},{17,1},{2,18},{18,2},{3,19},{19,3},{4,20},{20... | collective-permute-start | bytes 5947400 | tf_op jit(solution)/shard_map/ppermute | solution.py:21
  194.9 3.5 collective-permute-start.23
  198.5 4.4 collective-permute-start.24
  202.9 7.4 %copy-start.13 = (bf16[2,704,256]{2,1,0:T(8,128)(2,1)S(1)}, bf16[2,704,256]{2,1,0:T(8,128)(2,1)}, u32[]{:S(2)}) copy-start(bf16[2,704,256]{2,1,0:T(8,128)(2,1)} %copy-done.12) | copy-start | bytes 2162692
  220.9 13.3 %copy-start.1 = (f32[704,1024]{1,0:T(8,128)S(1)}, f32[704,1024]{1,0:T(8,128)}, u32[]{:S(2)}) copy-start(f32[704,1024]{1,0:T(8,128)} %copy-done) | copy-start | bytes 8650756
  236.0 8.4 %copy-start.4 = (bf16[704,1024]{1,0:T(8,128)(2,1)}, bf16[704,1024]{1,0:T(8,128)(2,1)S(1)}, u32[]{:S(2)}) copy-start(bf16[704,1024]{1,0:T(8,128)(2,1)S(1)} %shard_map.127.refs_0_.left) | copy-start | bytes 4325380
  244.5 4.5 %collective-permute-start.33 = (bf16[4,704,352]{2,1,0:T(8,128)(2,1)}, bf16[4,704,352]{2,1,0:T(8,128)(2,1)S(1)}, u32[]{:S(2)}, u32[]{:S(2)}) collective-permute-start(bf16[4,704,352]{2,1,0:T(8,128)(2,1)} %get-tuple-element.78), channel_id=1, source_target_pairs={{0,16},{16,0},{1,17},{17,1},{2,18},{18,2},{3,19},{19,3},{4,20},{20... | collective-permute-start | bytes 5947400 | tf_op jit(solution)/shard_map/ppermute | solution.py:21
  251.4 57.7 %all-to-all-start.2 = ((bf16[4,704,352]{2,1,0:T(8,128)(2,1)}), bf16[4,704,352]{2,1,0:T(8,128)(2,1)}, u32[]{:S(2)}, u32[]{:S(2)}) async-start(bf16[4,704,352]{2,1,0:T(8,128)(2,1)} %copy-done.6), calls=%async_computation.2 | async-start | bytes 4325376 | tf_op jit(solution)/shard_map/all_to_all | solution.py:526
  256.2 33.9 %collective-permute-start.27 = (bf16[2,2,704,256]{3,2,1,0:T(8,128)(2,1)}, bf16[2,2,704,256]{3,2,1,0:T(8,128)(2,1)S(1)}, u32[]{:S(2)}, u32[]{:S(2)}) collective-permute-start(bf16[2,2,704,256]{3,2,1,0:T(8,128)(2,1)} %copy-done.36), channel_id=1, source_target_pairs={{0,8},{4,12},{8,0},{12,4},{1,9},{5,13},{9,1},{13,5},{2,10},{6,14},... | collective-permute-start | bytes 4325384 | tf_op jit(solution)/shard_map/ppermute | solution.py:21
  256.8 35.2 %collective-permute-start.25 = (bf16[2,2,704,256]{3,2,1,0:T(8,128)(2,1)}, bf16[2,2,704,256]{3,2,1,0:T(8,128)(2,1)S(1)}, u32[]{:S(2)}, u32[]{:S(2)}) collective-permute-start(bf16[2,2,704,256]{3,2,1,0:T(8,128)(2,1)} %copy-done.35), channel_id=1, source_target_pairs={{0,4},{4,0},{8,12},{12,8},{1,5},{5,1},{9,13},{13,9},{2,6},{6,2},{1... | collective-permute-start | bytes 4325384 | tf_op jit(solution)/shard_map/ppermute | solution.py:21
  258.3 10.4 %copy-start.3 = (bf16[4,704,256]{2,1,0:T(8,128)(2,1)S(1)}, bf16[4,704,256]{2,1,0:T(8,128)(2,1)}, u32[]{:S(2)}) copy-start(bf16[4,704,256]{2,1,0:T(8,128)(2,1)} %pad_maximum_fusion.refs_0_) | copy-start | bytes 4325380
  258.3 10.4 %copy-start.21 = (bf16[704,1024]{1,0:T(8,128)(2,1)S(1)}, bf16[704,1024]{1,0:T(8,128)(2,1)}, u32[]{:S(2)}) copy-start(bf16[704,1024]{1,0:T(8,128)(2,1)} %copy-done.20) | copy-start | bytes 4325380
  268.7 21.4 %copy-start.29 = (bf16[2,2,704,256]{3,2,1,0:T(8,128)(2,1)S(1)}, bf16[2,2,704,256]{3,2,1,0:T(8,128)(2,1)}, u32[]{:S(2)}) copy-start(bf16[2,2,704,256]{3,2,1,0:T(8,128)(2,1)} %copy-done.28) | copy-start | bytes 4325380
  290.5 17.5 %collective-permute-start.28 = (bf16[1,2,704,256]{3,2,1,0:T(8,128)(2,1)S(1)}, bf16[1,2,704,256]{3,2,1,0:T(8,128)(2,1)S(1)}, u32[]{:S(2)}, u32[]{:S(2)}) collective-permute-start(bf16[1,2,704,256]{3,2,1,0:T(8,128)(2,1)S(1)} %slice.227), channel_id=1, source_target_pairs={{0,4},{4,0},{8,12},{12,8},{1,5},{5,1},{9,13},{13,9},{2,6},{6,2},{1... | collective-permute-start | bytes 2162696 | tf_op jit(solution)/shard_map/ppermute | solution.py:21
  294.8 17.5 %collective-permute-start.26 = (bf16[1,2,704,256]{3,2,1,0:T(8,128)(2,1)}, bf16[1,2,704,256]{3,2,1,0:T(8,128)(2,1)}, u32[]{:S(2)}, u32[]{:S(2)}) collective-permute-start(bf16[1,2,704,256]{3,2,1,0:T(8,128)(2,1)} %slice.228), channel_id=1, source_target_pairs={{0,8},{4,12},{8,0},{12,4},{1,9},{5,13},{9,1},{13,5},{2,10},{6,14},... | collective-permute-start | bytes 2162696 | tf_op jit(solution)/shard_map/ppermute | solution.py:21
  309.1 16.9 %collective-permute-start.34 = (bf16[2,704,256]{2,1,0:T(8,128)(2,1)}, bf16[2,704,256]{2,1,0:T(8,128)(2,1)S(1)}, u32[]{:S(2)}, u32[]{:S(2)}) collective-permute-start(bf16[2,704,256]{2,1,0:T(8,128)(2,1)} %fusion.3), channel_id=1, source_target_pairs={{0,1},{1,0},{2,3},{3,2},{4,5},{5,4},{6,7},{7,6},{8,9},{9,8},{10,11... | collective-permute-start | bytes 2162696 | tf_op jit(solution)/shard_map/ppermute | solution.py:21
  310.5 41.9 %collective-permute-start.43 = (bf16[4,704,352]{2,1,0:T(8,128)(2,1)}, bf16[4,704,352]{2,1,0:T(8,128)(2,1)}, u32[]{:S(2)}, u32[]{:S(2)}) collective-permute-start(bf16[4,704,352]{2,1,0:T(8,128)(2,1)} %get-tuple-element.80), channel_id=1, source_target_pairs={{0,16},{16,0},{1,17},{17,1},{2,18},{18,2},{3,19},{19,3},{4,20},{20... | collective-permute-start | bytes 5947400 | tf_op jit(solution)/shard_map/ppermute | solution.py:21
  327.8 31.5 %collective-permute-start.31 = (bf16[2,2,704,256]{3,2,1,0:T(8,128)(2,1)}, bf16[2,2,704,256]{3,2,1,0:T(8,128)(2,1)}, u32[]{:S(2)}, u32[]{:S(2)}) collective-permute-start(bf16[2,2,704,256]{3,2,1,0:T(8,128)(2,1)} %get-tuple-element.87), channel_id=1, source_target_pairs={{0,8},{4,12},{8,0},{12,4},{1,9},{5,13},{9,1},{13,5},{2,10},{6,14},... | collective-permute-start | bytes 4325384 | tf_op jit(solution)/shard_map/ppermute | solution.py:21
  328.4 16.4 %collective-permute-start.35 = (bf16[1,704,256]{2,1,0:T(8,128)(2,1)S(1)}, bf16[1,704,256]{2,1,0:T(8,128)(2,1)S(1)}, u32[]{:S(2)}, u32[]{:S(2)}) collective-permute-start(bf16[1,704,256]{2,1,0:T(8,128)(2,1)S(1)} %slice.230), channel_id=1, source_target_pairs={{0,2},{1,3},{2,0},{3,1},{4,6},{5,7},{6,4},{7,5},{8,10},{9,11},{10,... | collective-permute-start | bytes 1081352 | tf_op jit(solution)/shard_map/ppermute | solution.py:21
  330.5 39.7 %collective-permute-start.29 = (bf16[2,2,704,256]{3,2,1,0:T(8,128)(2,1)}, bf16[2,2,704,256]{3,2,1,0:T(8,128)(2,1)}, u32[]{:S(2)}, u32[]{:S(2)}) collective-permute-start(bf16[2,2,704,256]{3,2,1,0:T(8,128)(2,1)} %get-tuple-element.85), channel_id=1, source_target_pairs={{0,4},{4,0},{8,12},{12,8},{1,5},{5,1},{9,13},{13,9},{2,6},{6,2},{1... | collective-permute-start | bytes 4325384 | tf_op jit(solution)/shard_map/ppermute | solution.py:21
  349.5 8.0 %collective-permute-start.36 = (f32[2,4,2,32]{3,2,1,0:T(2,128)S(1)}, f32[2,4,2,32]{3,2,1,0:T(2,128)S(1)}, u32[]{:S(2)}, u32[]{:S(2)}) collective-permute-start(f32[2,4,2,32]{3,2,1,0:T(2,128)S(1)} %pad_maximum_fusion.3), channel_id=1, source_target_pairs={{0,1},{1,0},{2,3},{3,2},{4,5},{5,4},{6,7},{7,6},{8,9},{9,8},{10,11... | collective-permute-start | bytes 6152 | tf_op jit(solution)/shard_map/ppermute | solution.py:21
  349.6 8.0 %collective-permute-start.37 = (f32[2,4,2,32]{3,2,1,0:T(2,128)S(1)}, f32[2,4,2,32]{3,2,1,0:T(2,128)S(1)}, u32[]{:S(2)}, u32[]{:S(2)}) collective-permute-start(f32[2,4,2,32]{3,2,1,0:T(2,128)S(1)} %pad_maximum_fusion.3), channel_id=1, source_target_pairs={{0,2},{1,3},{2,0},{3,1},{4,6},{5,7},{6,4},{7,5},{8,10},{9,11},{10,... | collective-permute-start | bytes 6152 | tf_op jit(solution)/shard_map/ppermute | solution.py:21
  352.4 5.4 %collective-permute-start.38 = (f32[2,4,2,32]{3,2,1,0:T(2,128)S(1)}, f32[2,4,2,32]{3,2,1,0:T(2,128)S(1)}, u32[]{:S(2)}, u32[]{:S(2)}) collective-permute-start(f32[2,4,2,32]{3,2,1,0:T(2,128)S(1)} %pad_maximum_fusion.3), channel_id=1, source_target_pairs={{0,3},{1,2},{2,1},{3,0},{4,7},{5,6},{6,5},{7,4},{8,11},{9,10},{10,... | collective-permute-start | bytes 6152 | tf_op jit(solution)/shard_map/ppermute | solution.py:21
  363.6 15.7 %collective-permute-start.32 = (bf16[1,2,704,256]{3,2,1,0:T(8,128)(2,1)}, bf16[1,2,704,256]{3,2,1,0:T(8,128)(2,1)}, u32[]{:S(2)}, u32[]{:S(2)}) collective-permute-start(bf16[1,2,704,256]{3,2,1,0:T(8,128)(2,1)} %slice.225), channel_id=1, source_target_pairs={{0,4},{4,0},{8,12},{12,8},{1,5},{5,1},{9,13},{13,9},{2,6},{6,2},{1... | collective-permute-start | bytes 2162696 | tf_op jit(solution)/shard_map/ppermute | solution.py:21
  365.0 75.8 %all-to-all-start.3 = ((bf16[4,704,352]{2,1,0:T(8,128)(2,1)}), bf16[4,704,352]{2,1,0:T(8,128)(2,1)S(1)}, u32[]{:S(2)}, u32[]{:S(2)}) async-start(bf16[4,704,352]{2,1,0:T(8,128)(2,1)} %shard_map.133), calls=%async_computation.3 | async-start | bytes 4325376 | tf_op jit(solution)/shard_map/all_to_all | solution.py:551
  370.3 9.0 %copy-start.38 = (f32[2,2,704,256]{3,2,1,0:T(8,128)S(1)}, f32[2,2,704,256]{3,2,1,0:T(8,128)}, u32[]{:S(2)}) copy-start(f32[2,2,704,256]{3,2,1,0:T(8,128)} %copy-done.37) | copy-start | bytes 8650756
  372.2 24.1 %copy-start.9 = (bf16[4,2,32,704]{3,2,1,0:T(8,128)(2,1)S(1)}, bf16[4,2,32,704]{3,2,1,0:T(8,128)(2,1)}, u32[]{:S(2)}) copy-start(bf16[4,2,32,704]{3,2,1,0:T(8,128)(2,1)} %mid.3) | copy-start | bytes 1081348
  372.2 24.1 %copy-start.31 = (bf16[3,2,32,704]{3,2,1,0:T(8,128)(2,1)S(1)}, bf16[3,2,32,704]{3,2,1,0:T(8,128)(2,1)}, u32[]{:S(2)}) copy-start(bf16[3,2,32,704]{3,2,1,0:T(8,128)(2,1)} %copy-done.30) | copy-start | bytes 811012
  372.2 24.1 %copy-start.33 = (bf16[3,2,32,704]{3,2,1,0:T(8,128)(2,1)S(1)}, bf16[3,2,32,704]{3,2,1,0:T(8,128)(2,1)}, u32[]{:S(2)}) copy-start(bf16[3,2,32,704]{3,2,1,0:T(8,128)(2,1)} %copy-done.32) | copy-start | bytes 811012
  372.2 46.5 %collective-permute-start.30 = (bf16[1,2,704,256]{3,2,1,0:T(8,128)(2,1)S(1)}, bf16[1,2,704,256]{3,2,1,0:T(8,128)(2,1)S(1)}, u32[]{:S(2)}, u32[]{:S(2)}) collective-permute-start(bf16[1,2,704,256]{3,2,1,0:T(8,128)(2,1)S(1)} %slice.226), channel_id=1, source_target_pairs={{0,8},{4,12},{8,0},{12,4},{1,9},{5,13},{9,1},{13,5},{2,10},{6,14},... | collective-permute-start | bytes 2162696 | tf_op jit(solution)/shard_map/ppermute | solution.py:21
  380.6 38.2 %collective-permute-start.39 = (bf16[2,704,256]{2,1,0:T(8,128)(2,1)S(1)}, bf16[2,704,256]{2,1,0:T(8,128)(2,1)S(1)}, u32[]{:S(2)}, u32[]{:S(2)}) collective-permute-start(bf16[2,704,256]{2,1,0:T(8,128)(2,1)S(1)} %fusion), channel_id=1, source_target_pairs={{0,1},{1,0},{2,3},{3,2},{4,5},{5,4},{6,7},{7,6},{8,9},{9,8},{10,11... | collective-permute-start | bytes 2162696 | tf_op jit(solution)/shard_map/ppermute | solution.py:21
  380.7 22.5 %copy-start.19 = (bf16[4,2,32,704]{3,2,1,0:T(8,128)(2,1)S(1)}, bf16[4,2,32,704]{3,2,1,0:T(8,128)(2,1)}, u32[]{:S(2)}) copy-start(bf16[4,2,32,704]{3,2,1,0:T(8,128)(2,1)} %refs_0_.1) | copy-start | bytes 1081348
  380.7 7.8 %collective-permute-start.40 = (bf16[3,2,32,704]{3,2,1,0:T(8,128)(2,1)S(1)}, bf16[3,2,32,704]{3,2,1,0:T(8,128)(2,1)S(1)}, u32[]{:S(2)}, u32[]{:S(2)}) collective-permute-start(bf16[3,2,32,704]{3,2,1,0:T(8,128)(2,1)S(1)} %get-tuple-element.111), channel_id=1, source_target_pairs={{0,4},{4,8},{8,12},{1,5},{5,9},{9,13},{2,6},{6,10},{10,14},{3,7},{... | collective-permute-start | bytes 811016 | tf_op jit(solution)/shard_map/ppermute | solution.py:353
  384.3 12.0 %collective-permute-start.41 = (bf16[3,2,32,704]{3,2,1,0:T(8,128)(2,1)S(1)}, bf16[3,2,32,704]{3,2,1,0:T(8,128)(2,1)S(1)}, u32[]{:S(2)}, u32[]{:S(2)}) collective-permute-start(bf16[3,2,32,704]{3,2,1,0:T(8,128)(2,1)S(1)} %get-tuple-element.110), channel_id=1, source_target_pairs={{4,0},{8,4},{12,8},{5,1},{9,5},{13,9},{6,2},{10,6},{14,10},{7,3},{... | collective-permute-start | bytes 811016 | tf_op jit(solution)/shard_map/ppermute | solution.py:353
  403.1 8.1 %collective-permute-start.44 = (bf16[7,7,704]{2,1,0:T(8,128)(2,1)S(1)}, bf16[7,7,704]{2,1,0:T(8,128)(2,1)S(1)}, u32[]{:S(2)}, u32[]{:S(2)}) collective-permute-start(bf16[7,7,704]{2,1,0:T(8,128)(2,1)S(1)} %convert_element_type.121), channel_id=1, source_target_pairs={{0,16},{16,0},{1,17},{17,1},{2,18},{18,2},{3,19},{19,3},{4,20},{20... | collective-permute-start | bytes 206984 | tf_op jit(solution)/shard_map/ppermute | solution.py:21
  411.2 11.3 %collective-permute-start.45 = (bf16[7,7,704]{2,1,0:T(8,128)(2,1)S(1)}, bf16[7,7,704]{2,1,0:T(8,128)(2,1)S(1)}, u32[]{:S(2)}, u32[]{:S(2)}) collective-permute-start(bf16[7,7,704]{2,1,0:T(8,128)(2,1)S(1)} %add_convert_fusion.2), channel_id=1, source_target_pairs={{0,4},{4,0},{8,12},{12,8},{1,5},{5,1},{9,13},{13,9},{2,6},{6,2},{1... | collective-permute-start | bytes 206984 | tf_op jit(solution)/shard_map/ppermute | solution.py:21
  419.0 16.6 %collective-permute-start.42 = (bf16[1,704,256]{2,1,0:T(8,128)(2,1)S(1)}, bf16[1,704,256]{2,1,0:T(8,128)(2,1)S(1)}, u32[]{:S(2)}, u32[]{:S(2)}) collective-permute-start(bf16[1,704,256]{2,1,0:T(8,128)(2,1)S(1)} %slice.229), channel_id=1, source_target_pairs={{0,2},{1,3},{2,0},{3,1},{4,6},{5,7},{6,4},{7,5},{8,10},{9,11},{10,... | collective-permute-start | bytes 1081352 | tf_op jit(solution)/shard_map/ppermute | solution.py:21
  422.5 5.1 %collective-permute-start.46 = (bf16[7,7,704]{2,1,0:T(8,128)(2,1)S(1)}, bf16[7,7,704]{2,1,0:T(8,128)(2,1)S(1)}, u32[]{:S(2)}, u32[]{:S(2)}) collective-permute-start(bf16[7,7,704]{2,1,0:T(8,128)(2,1)S(1)} %add_convert_fusion.1), channel_id=1, source_target_pairs={{0,8},{4,12},{8,0},{12,4},{1,9},{5,13},{9,1},{13,5},{2,10},{6,14},... | collective-permute-start | bytes 206984 | tf_op jit(solution)/shard_map/ppermute | solution.py:21
  (29 other events, 53.0 us)
